TPU v7x, 32 devices: a whole 2x2x4 slice. The times are simulated.
32 devices in a mesh: groups: 2 (over y), gx: 4 (over z), ta: 4 (over x, core).
Axes of the slice: x: 2, y: 2, z: 4, core: 2. Of those that a mesh axis runs over, the one named last changes fastest.
Arguments:
- queries: bfloat16 [512, 6144], P(('groups', 'gx'), 'ta'), parts along dimension 0, may hold values from -320 to 320
- new_kv: bfloat16 [2, 512, 1024], P(None, ('groups', 'gx'), 'ta'), parts along dimension 1, may hold values from -6 to 6
- kv_cache: bfloat16 [2, 512, 192, 1024], P(None, ('groups', 'gx'), None, 'ta'), parts along dimension 1, may hold values from -6 to 6
- lengths: int32 [512], P(('groups', 'gx')), parts along dimension 0, may hold values from 2 to 192, as said below
- out_proj: bfloat16 [6144, 3072], P('ta', 'gx'), may hold values from -0.078125 to 0.078125
- norm_gain: float32 [3072], replicated, may hold values from 0.1 to 1.9
- expert_ids: int32 [512, 4], P('groups'), parts along dimension 0, may hold values from 0 to 3, as said below
- gate_weights: float32 [512, 4], P(('groups', 'gx')), parts along dimension 0, may hold values from 0.05 to 0.6
- w_up: bfloat16 [4, 3072, 5376], P('gx', None, 'ta'), may hold values from -0.109375 to 0.109375
- w_down: bfloat16 [4, 5376, 3072], P('gx', 'ta'), may hold values from -0.109375 to 0.109375
Outputs:
- mixture: bfloat16 [512, 3072], P(('groups', 'gx'), 'ta'), parts along dimension 0
There are 2 independent parts, one for each index of `groups`. A program takes and returns all parts, laid end to end along the dimension named above; an argument that names none is the same for every part. Nothing has to cross between parts.
Inputs may be any that keep to these rules, and one draw needn't show every extreme that they name: `lengths`: in every aligned block of 64 rows at least one row has length 192. `expert_ids`: each row names 4 different experts. In every aligned block of 64 rows one expert, the same for all blocks, is named by exactly 64 rows; every other expert by at most 64 rows, and the counts of the other experts in a block differ by at most one.
All inputs are finite; a program needn't handle non-finite values.
Results may differ from a plain program's by a relative error of at most 0.017.
Values may be sent and summed in bfloat16 or wider, within the bound.
No kernel may reach another device: no remote copies, remote signals or barrier semaphores. Data moves between devices by JAX's collectives and lax.ppermute only.
A program may use at most 128 MiB of HBM per device.

v0:
```python
import math

import jax
import jax.numpy as jnp
from jax import lax
from jax.sharding import PartitionSpec as P

HD = 128


def route_tables(expert_ids, expert_count, block_rows, capacity):
    blocks = expert_ids.shape[0] // block_rows
    expert_range = jnp.arange(expert_count, dtype=jnp.int32)
    matches = (expert_ids[:, :, None] == expert_range[None, None, :]).astype(jnp.int32)
    routed = jnp.sum(matches, axis=1).reshape(blocks, block_rows, expert_count)
    position = jnp.cumsum(routed, axis=1) - routed
    slot_range = jnp.arange(capacity, dtype=jnp.int32)
    slot_hits = routed[:, :, :, None] * (
        position[:, :, :, None] == slot_range[None, None, None, :]
    ).astype(jnp.int32)
    row_range = jnp.arange(block_rows, dtype=jnp.int32)
    block_start = (jnp.arange(blocks, dtype=jnp.int32) * block_rows)[:, None, None]
    source_row = jnp.sum(slot_hits * row_range[None, :, None, None], axis=1) + block_start
    filled = jnp.sum(slot_hits, axis=1)
    source_row = jnp.transpose(source_row, (1, 0, 2)).reshape(expert_count, blocks * capacity)
    filled = jnp.transpose(filled, (1, 0, 2)).reshape(expert_count, blocks * capacity)
    pick_slot = jnp.sum(matches * position.reshape(blocks * block_rows, 1, expert_count), axis=2)
    return (source_row, filled, pick_slot)


def attend(queries, cache_keys, cache_values, fresh_keys, fresh_values, lengths):
    row_count = queries.shape[0]
    context = cache_keys.shape[1]
    kv_heads = fresh_keys.shape[1] // HD
    group_size = queries.shape[1] // (HD * kv_heads)
    scale = 1.0 / math.sqrt(HD)
    query_heads = queries.reshape(row_count, kv_heads, group_size, HD)
    key_heads = cache_keys.reshape(row_count, context, kv_heads, HD)
    value_heads = cache_values.reshape(row_count, context, kv_heads, HD)
    fresh_key = fresh_keys.reshape(row_count, kv_heads, HD)
    fresh_value = fresh_values.astype(jnp.float32).reshape(row_count, kv_heads, HD)
    cached = (
        jnp.einsum("rkgd,rckd->rkgc", query_heads, key_heads, preferred_element_type=jnp.float32)
        * scale
    )
    own_score = (
        jnp.einsum("rkgd,rkd->rkg", query_heads, fresh_key, preferred_element_type=jnp.float32)[
            ..., None
        ]
        * scale
    )
    visible = jnp.arange(context, dtype=jnp.int32)[None, :] < lengths[:, None]
    cached = jnp.where(visible[:, None, None, :], cached, -jnp.inf)
    scores = jnp.concatenate([cached, own_score], axis=3)
    largest = jnp.max(scores, axis=3, keepdims=True)
    lifted = jnp.exp(scores - largest)
    probs = (lifted / jnp.sum(lifted, axis=3, keepdims=True)).astype(jnp.bfloat16)
    mixed = jnp.einsum(
        "rkgc,rckd->rkgd", probs[..., :context], value_heads, preferred_element_type=jnp.float32
    )
    mixed = mixed + probs[..., context:].astype(jnp.float32) * fresh_value[:, :, None, :]
    return mixed.reshape(row_count, -1).astype(jnp.bfloat16)


def layer_norm(hidden, norm_gain):
    values = hidden.astype(jnp.float32)
    center = values - jnp.mean(values, axis=1, keepdims=True)
    spread = jnp.mean(center * center, axis=1, keepdims=True)
    return (center * lax.rsqrt(spread + 1e-05) * norm_gain).astype(jnp.bfloat16)


def body(
    queries, new_kv, kv_cache, lengths, out_proj, norm_gain, expert_ids, gate_weights, w_up, w_down
):
    gx_count = lax.axis_size("gx")
    ta_count = lax.axis_size("ta")
    block_rows = queries.shape[0]
    top_count = expert_ids.shape[1]
    capacity = min(block_rows, 2 * block_rows * top_count // gx_count)
    slot_count = gx_count * capacity
    model_width = norm_gain.shape[0]
    width_share = model_width // ta_count
    attended = attend(queries, kv_cache[0], kv_cache[1], new_kv[0], new_kv[1], lengths)
    projected = jnp.dot(
        lax.all_gather(attended, "gx", axis=0, tiled=True),
        out_proj,
        preferred_element_type=jnp.float32,
    ).astype(jnp.bfloat16)
    source_row, filled, pick_slot = route_tables(expert_ids, gx_count, block_rows, capacity)
    live_slots = (filled > 0)[:, :, None]
    widened = lax.optimization_barrier(projected).astype(jnp.float32)
    hidden_share = lax.psum_scatter(
        widened.astype(jnp.bfloat16), "ta", scatter_dimension=1, tiled=True
    )
    outgoing = jnp.where(live_slots, hidden_share[source_row], jnp.zeros((), jnp.bfloat16))[
        :, :, None, :
    ]
    arrived = lax.all_to_all(outgoing, "gx", split_axis=0, concat_axis=2, tiled=True)
    gathered = lax.all_gather(arrived, "ta", axis=3, tiled=True)
    hidden = gathered.reshape(slot_count, model_width)
    normed = layer_norm(hidden, norm_gain)
    raised = jnp.dot(normed, w_up[0], preferred_element_type=jnp.float32)
    active = jax.nn.silu(raised).astype(jnp.bfloat16)
    terms = jnp.dot(active, w_down[0], preferred_element_type=jnp.float32)
    mine = lax.psum_scatter(terms, "ta", scatter_dimension=1, tiled=True)
    result = mine.astype(jnp.bfloat16).reshape(gx_count, capacity, width_share)
    returned = lax.all_to_all(result, "gx", split_axis=0, concat_axis=0, tiled=True)
    first_row = lax.axis_index("gx") * block_rows
    local_ids = lax.dynamic_slice_in_dim(expert_ids, first_row, block_rows, 0)
    local_slot = lax.dynamic_slice_in_dim(pick_slot, first_row, block_rows, 0)
    flat_rows = returned.reshape(gx_count * capacity, width_share)
    picked = flat_rows[local_ids * capacity + local_slot]
    return jnp.sum(picked.astype(jnp.float32) * gate_weights[:, :, None], axis=1).astype(
        jnp.bfloat16
    )


def solution(mesh):
    return jax.shard_map(
        body,
        mesh=mesh,
        in_specs=(
            P(("groups", "gx"), "ta"),
            P(None, ("groups", "gx"), "ta"),
            P(None, ("groups", "gx"), None, "ta"),
            P(("groups", "gx")),
            P("ta", "gx"),
            P(),
            P("groups", None),
            P(("groups", "gx"), None),
            P("gx", None, "ta"),
            P("gx", "ta", None),
        ),
        out_specs=P(("groups", "gx"), "ta"),
        check_vma=False,
    )
```

profile of v0, /device:TPU:0, one launch (start us, length us, event | category | flops | bytes accessed | tf_op | source)
XLA Modules:
  0.0 234.4 jit_solution(11534466579441959941)
XLA Ops:
  6.5 10.8 %fusion.32 = (bf16[1,64,192,256]{3,2,1,0:T(8,128)(2,1)}, bf16[1,64,192,256]{3,2,1,0:T(8,128)(2,1)}) fusion(bf16[2,64,192,256]{3,2,1,0:T(8,128)(2,1)} %param.12), kind=kLoop, calls=%fused_computation.55 | loop fusion | bytes 25165824 | tf_op jit(solution)/shard_map/slice | solution.py:83
  17.4 9.8 %reshape_squeeze.9 = bf16[64,192,2,128]{3,2,1,0:T(2,128)(2,1)} reshape(bf16[1,64,192,256]{3,2,1,0:T(8,128)(2,1)} %get-tuple-element.10) | data formatting | bytes 12582912 | tf_op jit(solution)/shard_map/reshape;squeeze | solution.py:38
  28.1 6.2 %fusion.6 = f32[64,2,6,192]{3,2,1,0:T(8,128)S(1)} fusion(bf16[64,2,6,128]{3,2,1,0:T(8,128)(2,1)} %reshape.157, bf16[64,192,2,128]{3,2,1,0:T(2,128)(2,1)} %reshape_squeeze.9), kind=kOutput, calls=%fused_computation.8 | convolution fusion | flops 37748736 | bytes 7077888 | tf_op jit(solution)/shard_map/rkgd,rckd->rkgc/dot_general | solution.py:43
  34.3 1.4 copy.67
  35.8 2.3 fusion.31
  38.8 1.4 slice_convert_fusion
  40.2 1.4 reshape.189
  42.8 1.5 multiply_bitcast_fusion
  46.2 1.2 fusion.30
  49.9 9.8 %reshape_squeeze.11 = bf16[64,192,2,128]{3,2,1,0:T(2,128)(2,1)} reshape(bf16[1,64,192,256]{3,2,1,0:T(8,128)(2,1)} %get-tuple-element.9) | data formatting | bytes 12582912 | tf_op jit(solution)/shard_map/reshape;squeeze | solution.py:39
  59.8 4.5 %fusion.19 = bf16[64,2,6,128]{3,2,1,0:T(8,128)(2,1)S(1)} fusion(bf16[64,2,6,192]{3,2,1,0:T(8,128)(2,1)S(1)} %copy.72, bf16[64,192,2,128]{3,2,1,0:T(2,128)(2,1)} %reshape_squeeze.11, f32[64,2,128]{2,1,0:T(2,128)S(1)} %reshape.162, f32[64,2,6]{2,1,0:T(2,128)S(1)} %copy.74), kind=kOutput, calls=%fused_computation.21 | convolution fusion | flops 38043648 | bytes 6851584 | tf_op jit(solution)/shard_map/rkgc,rckd->rkgd/dot_general | solution.py:58
  64.5 21.3 %all_gather.6 = bf16[256,1536]{1,0:T(8,128)(2,1)S(1)} all-gather(bf16[64,1536]{1,0:T(8,128)(2,1)S(1)} %convert_element_type.58), channel_id=1, replica_groups=mesh['groups'=2,'gx'=4,'ta'=4] {'gx'}, dimensions={0}, use_global_device_ids=true | all-gather | bytes 983040 | tf_op jit(solution)/shard_map/all_gather | solution.py:85
  88.8 19.1 %reduce-scatter.7.cloned.1.call-done = bf16[192,256]{1,0:T(8,128)(2,1)} async-done(((bf16[768,256]{1,0:T(8,128)(2,1)}), bf16[192,256]{1,0:T(8,128)(2,1)}) %reduce-scatter.7.cloned.1.call-update) | async-done | bytes 98320
  108.9 3.9 %gather_fusion = bf16[1024,192]{1,0:T(8,128)(2,1)S(1)} fusion(bf16[256,192]{1,0:T(8,128)(2,1)S(1)} %copy.85, s32[1024]{0:T(1024)S(1)} %broadcast_clamp_fusion), kind=kCustom, calls=%fused_computation | custom fusion | bytes 790528 | tf_op jit(solution)/shard_map/gather | solution.py:95
  113.1 16.2 %all_to_all.23 = bf16[4,256,1,192]{1,3,2,0:T(8,128)(2,1)} all-to-all(bf16[4,256,1,192]{1,3,2,0:T(8,128)(2,1)S(1)} %broadcast_select_fusion), channel_id=1, replica_groups=mesh['groups'=2,'gx'=4,'ta'=4] {'gx'}, dimensions={0} | all-to-all | bytes 786432 | tf_op jit(solution)/shard_map/all_to_all | solution.py:98
  129.6 17.7 %all-gather.3.cloned.1.call-done = bf16[1,256,4,1,768]{1,4,2,3,0:T(8,128)(2,1)} async-done(((bf16[1,256,4,1,192]{1,4,2,3,0:T(8,128)(2,1)}), bf16[1,256,4,1,768]{1,4,2,3,0:T(8,128)(2,1)}) %all-gather.3.cloned.1.call-update) | async-done | bytes 1572880 | tf_op jit(solution)/shard_map/all_gather | solution.py:99
  147.3 1.9 convert_reduce_fusion
  149.7 1.7 fusion.13
  151.4 16.8 %fusion = f32[256,3072]{1,0:T(8,128)} fusion(bf16[1,1344,3072]{2,1,0:T(8,128)(2,1)} %param.19, bf16[256,3072]{0,1:T(8,128)(2,1)} %bitcast.70, bf16[1,3072,1344]{1,2,0:T(8,128)(2,1)} %param.18), kind=kOutput, calls=%fused_computation.2 | convolution fusion | flops 4229578752 | bytes 21233664 | tf_op jit(solution)/shard_map/dot_general | solution.py:104
  168.2 38.1 %reduce-scatter.5.cloned.1.call-done = f32[256,768]{1,0:T(8,128)} async-done(((f32[256,3072]{1,0:T(8,128)}), f32[256,768]{1,0:T(8,128)}) %reduce-scatter.5.cloned.1.call-update) | async-done | bytes 786448 | tf_op jit(solution)/shard_map/reduce_scatter | solution.py:105
  206.3 1.9 convert_element_type.64
  208.2 4.6 %all-to-all-start.1 = ((bf16[4,64,768]{2,1,0:T(8,128)(2,1)}), bf16[4,64,768]{2,1,0:T(8,128)(2,1)S(1)}, u32[]{:S(2)}, u32[]{:S(2)}) async-start(bf16[4,64,768]{2,1,0:T(8,128)(2,1)} %bitcast.14), calls=%async_computation.2 | async-start | bytes 786432 | tf_op jit(solution)/shard_map/all_to_all | solution.py:107
  213.9 10.6 %all-to-all-done.1 = bf16[4,64,768]{2,1,0:T(8,128)(2,1)S(1)} async-done(((bf16[4,64,768]{2,1,0:T(8,128)(2,1)}), bf16[4,64,768]{2,1,0:T(8,128)(2,1)S(1)}, u32[]{:S(2)}, u32[]{:S(2)}) %all-to-all-start.1) | async-done | bytes 393248 | tf_op jit(solution)/shard_map/all_to_all | solution.py:107
  225.9 1.9 multiply_reduce_fusion
  (73 shorter events, 14.9 us)
Async XLA Ops:
  6.5 79.3 %copy-start = (bf16[1536,768]{1,0:T(8,128)(2,1)S(1)}, bf16[1536,768]{1,0:T(8,128)(2,1)}, u32[]{:S(2)}) copy-start(bf16[1536,768]{1,0:T(8,128)(2,1)} %param.14) | copy-start | bytes 7077892
  6.5 101.4 %reduce-scatter.7.cloned.1.call-start = ((), (), s32[]{:S(2)}) async-start(), calls=%async_computation.6 | async-start | bytes 491520
  17.4 9.8 %copy-start.4 = (bf16[64,1536]{1,0:T(8,128)(2,1)S(1)}, bf16[64,1536]{1,0:T(8,128)(2,1)}, u32[]{:S(2)}) copy-start(bf16[64,1536]{1,0:T(8,128)(2,1)} %param.10) | copy-start | bytes 589828
  28.1 7.7 %copy-start.8 = (s32[64]{0:T(128)S(1)}, s32[64]{0:T(128)}, u32[]{:S(2)}) copy-start(s32[64]{0:T(128)} %param.13) | copy-start | bytes 772
  49.9 9.8 %copy-start.3 = (f32[1,64,256]{2,1,0:T(8,128)S(1)}, f32[1,64,256]{2,1,0:T(8,128)}, u32[]{:S(2)}) copy-start(f32[1,64,256]{2,1,0:T(8,128)} %get-tuple-element.11) | copy-start | bytes 196612
  85.8 1.8 copy-start.5
  87.6 59.7 %all-gather.3.cloned.1.call-start = ((), (), s32[]{:S(2)}) async-start(), calls=%async_computation.5 | async-start | bytes 1966080 | tf_op jit(solution)/shard_map/all_gather | solution.py:99
  112.9 16.7 %copy-start.6 = (f32[3072]{0:T(1024)S(1)}, f32[3072]{0:T(1024)}, u32[]{:S(2)}) copy-start(f32[3072]{0:T(1024)} %param.15) | copy-start | bytes 36868
  129.3 77.0 %reduce-scatter.5.cloned.1.call-start = ((), (), s32[]{:S(2)}) async-start(), calls=%async_computation.4 | async-start | bytes 3932160 | tf_op jit(solution)/shard_map/reduce_scatter | solution.py:105
  147.3 2.0 copy-start.2
  168.2 45.0 %copy-start.7 = (f32[64,4]{0,1:T(4,128)S(1)}, f32[64,4]{0,1:T(4,128)}, u32[]{:S(2)}) copy-start(f32[64,4]{0,1:T(4,128)} %param.17) | copy-start | bytes 3076
  208.2 16.3 %all-to-all-start.1 = ((bf16[4,64,768]{2,1,0:T(8,128)(2,1)}), bf16[4,64,768]{2,1,0:T(8,128)(2,1)S(1)}, u32[]{:S(2)}, u32[]{:S(2)}) async-start(bf16[4,64,768]{2,1,0:T(8,128)(2,1)} %bitcast.14), calls=%async_computation.2 | async-start | bytes 786432 | tf_op jit(solution)/shard_map/all_to_all | solution.py:107
  224.5 3.3 %copy-start.1 = (bf16[1536,768]{1,0:T(8,128)(2,1)S(1)}, bf16[1536,768]{1,0:T(8,128)(2,1)}, u32[]{:S(2)}) copy-start(bf16[1536,768]{1,0:T(8,128)(2,1)} %param.14) | copy-start | bytes 7077892
Sparse Core Ops, SparseCore 0:
  87.7 20.1 reduce-scatter.6
  129.4 17.7 all-gather.2
  168.3 37.9 reduce-scatter.4
where the time goes:
time: 236 us; the launch traced here: 234 us
  waiting for transfers between devices  85.5 us (36%)
  local copies, waits for them, and re-layouts  47.3 us (20%)
  blocking collectives  37.5 us (16%)
  matrix products  29.5 us (12%)
  other arithmetic  16.4 us (7%)
  between operations  13.3 us (6%)
  starting transfers between devices  4.86 us (2%)
    reduce_scatter x1, waiting for transfers between devices, body(): mine = lax.psum_scatter(terms, 'ta', scatter_dimension=1, tiled=True)  38.1 us
    all_gather x1, blocking collectives, body(): lax.all_gather(attended, 'gx', axis=0, tiled=True)  21.3 us
    unnamed x4, waiting for transfers between devices  19.1 us
    all_gather x1, waiting for transfers between devices, body(): gathered = lax.all_gather(arrived, 'ta', axis=3, tiled=True)  17.7 us
    dot_general x1, matrix products, body(): terms = jnp.dot(active, w_down[0], preferred_element_type=jnp.float32)  16.8 us
    all_to_all x1, blocking collectives, body(): lax.all_to_all(outgoing, 'gx', split_axis=0, concat_axis=2, tiled=True)  16.2 us
    slice x1, local copies, waits for them, and re-layouts, body(): kv_cache[1]  10.8 us
    all_to_all x1, waiting for transfers between devices, body(): lax.all_to_all(result, 'gx', split_axis=0, concat_axis=0, tiled=True)  10.6 us
  transfers between devices with their start and end apart: 4, of which 4 were waited for; matrix products, arithmetic and copies ran while one was open for 1% of the time, Pallas kernels for 0%

commit v1 on v0

--- a/solution.py
+++ b/solution.py
@@ -1,11 +1,300 @@
+import functools
 import math
 
 import jax
 import jax.numpy as jnp
 from jax import lax
+from jax.experimental import pallas as pl
+from jax.experimental.pallas import tpu as pltpu
 from jax.sharding import PartitionSpec as P
 
 HD = 128
+MIB = 1 << 20
+VMEM = pl.BlockSpec(memory_space=pltpu.VMEM)
+SMEM = pl.BlockSpec(memory_space=pltpu.SMEM)
+F32 = jnp.float32
+BF16 = jnp.bfloat16
+
+
+def local_call(kernel, out_shape, in_specs, scratch=(), vmem=32, flops=0, moved=0, name=None):
+    several = isinstance(out_shape, (tuple, list))
+    return pl.pallas_call(
+        kernel,
+        out_shape=out_shape,
+        in_specs=in_specs,
+        out_specs=[VMEM] * len(out_shape) if several else VMEM,
+        scratch_shapes=list(scratch),
+        compiler_params=pltpu.CompilerParams(vmem_limit_bytes=vmem * MIB),
+        cost_estimate=pl.CostEstimate(flops=flops, bytes_accessed=moved, transcendentals=0),
+        name=name,
+    )
+
+
+def attend_kernel(
+    kv_heads, group, slots, batch,
+    lengths_ref, q_ref, fresh_ref, cache_ref, out_ref,
+    keys, values, q_rows, scores, own_scores, probs, own_probs, mixed, sems,
+):
+    rows = q_ref.shape[0]
+    context = keys.shape[1]
+    width = kv_heads * HD
+    heads = kv_heads * group
+    steps = rows // batch
+    scale = 1.0 / math.sqrt(HD)
+
+    def fetch(step, kind):
+        part = pl.ds(step * batch, batch)
+        buffer = (keys, values)[kind]
+        return pltpu.make_async_copy(
+            cache_ref.at[kind, part], buffer.at[part], sems.at[kind, step]
+        )
+
+    for step in range(steps):
+        for kind in range(2):
+            fetch(step, kind).start()
+    q_rows[...] = jnp.zeros_like(q_rows)
+    for head in range(heads):
+        q_rows[head // group, pl.ds(head, rows, stride=slots), :] = q_ref[
+            :, head * HD : (head + 1) * HD
+        ].astype(F32)
+    place = lax.broadcasted_iota(jnp.int32, (slots, context), 1)
+    for step in range(steps):
+        fetch(step, 0).wait()
+        for k in range(batch):
+            row = step * batch + k
+            mine = jnp.concatenate(
+                [q_rows[g, row * slots : (row + 1) * slots, :] for g in range(kv_heads)], axis=1
+            )
+            cached = lax.dot_general(
+                mine.astype(BF16), keys[row], (((1,), (1,)), ((), ())),
+                preferred_element_type=F32,
+            )
+            here = slice(k * slots, (k + 1) * slots)
+            scores[here, :] = jnp.where(place < lengths_ref[row], cached * scale, -jnp.inf)
+            fresh_key = fresh_ref[0, row : row + 1, :].astype(F32)
+            own_scores[here, :] = jnp.broadcast_to(
+                jnp.sum(mine * fresh_key, axis=1, keepdims=True) * scale, (slots, HD)
+            )
+        cached = scores[...]
+        own = own_scores[:, :1]
+        largest = jnp.maximum(jnp.max(cached, axis=1, keepdims=True), own)
+        lifted = jnp.exp(cached - largest)
+        own_lifted = jnp.exp(own - largest)
+        total = jnp.sum(lifted, axis=1, keepdims=True) + own_lifted
+        probs[...] = (lifted / total).astype(BF16)
+        own_probs[...] = jnp.broadcast_to(
+            (own_lifted / total).astype(BF16).astype(F32), own_probs.shape
+        )
+        fetch(step, 1).wait()
+        for k in range(batch):
+            row = step * batch + k
+            here = slice(k * slots, (k + 1) * slots)
+            weighted = jnp.dot(probs[here, :], values[row], preferred_element_type=F32)
+            fresh_value = fresh_ref[1, row : row + 1, :].astype(F32)
+            total = weighted + own_probs[here, :1] * fresh_value
+            for g in range(kv_heads):
+                mixed[g, here, :] = total[:, g * HD : (g + 1) * HD]
+        for head in range(heads):
+            out_ref[step * batch : (step + 1) * batch, head * HD : (head + 1) * HD] = mixed[
+                head // group, pl.ds(head, batch, stride=slots), :
+            ].astype(BF16)
+
+
+def attend(queries, new_kv, kv_cache, lengths):
+    rows, features = queries.shape
+    context, width = kv_cache.shape[2:]
+    kv_heads = width // HD
+    heads = features // HD
+    slots = -(-heads // 8) * 8
+    batch = 16
+    return pl.pallas_call(
+        functools.partial(attend_kernel, kv_heads, heads // kv_heads, slots, batch),
+        out_shape=jax.ShapeDtypeStruct(queries.shape, BF16),
+        in_specs=[SMEM, VMEM, VMEM, pl.BlockSpec(memory_space=pl.ANY)],
+        out_specs=VMEM,
+        scratch_shapes=[
+            pltpu.VMEM((rows, context, width), BF16),
+            pltpu.VMEM((rows, context, width), BF16),
+            pltpu.VMEM((kv_heads, rows * slots, HD), F32),
+            pltpu.VMEM((batch * slots, context), F32),
+            pltpu.VMEM((batch * slots, HD), F32),
+            pltpu.VMEM((batch * slots, context), BF16),
+            pltpu.VMEM((batch * slots, HD), F32),
+            pltpu.VMEM((kv_heads, batch * slots, HD), F32),
+            pltpu.SemaphoreType.DMA((2, rows // batch)),
+        ],
+        compiler_params=pltpu.CompilerParams(vmem_limit_bytes=56 * MIB),
+        cost_estimate=pl.CostEstimate(
+            flops=4 * rows * slots * context * width,
+            bytes_accessed=2 * kv_cache.size,
+            transcendentals=rows * slots * context,
+        ),
+        name="attend",
+    )(lengths, queries, new_kv, kv_cache)
+
+
+def project_kernel(parts, place_ref, *refs):
+    shards, weight_ref = refs[:parts], refs[parts]
+    outs, held = refs[parts + 1 : parts + 1 + parts], refs[-1]
+    rows = shards[0].shape[0]
+    turn = place_ref[0] ^ place_ref[1]
+    block = jnp.concatenate([shard[...] for shard in shards], axis=0)
+    pieces = jnp.dot(block, weight_ref[...], preferred_element_type=F32).astype(BF16)
+    for s in range(parts):
+        held[turn ^ s] = pieces[s * rows : (s + 1) * rows, :]
+    for t in range(parts):
+        outs[t][...] = held[t]
+
+
+def add_kernel(*refs):
+    terms, out = refs[:-1], refs[-1]
+    total = terms[0][...].astype(F32)
+    for term in terms[1:]:
+        total = total + term[...].astype(F32)
+    out[...] = total.astype(BF16)
+
+
+def norm_kernel(parts, place_ref, gain_ref, *refs):
+    shards, out, held = refs[:parts], refs[parts], refs[parts + 1]
+    width = shards[0].shape[1]
+    for s in range(parts):
+        first = pl.multiple_of((place_ref[0] ^ s) * width, HD)
+        held[:, pl.ds(first, width)] = shards[s][...].astype(F32)
+    values = held[...]
+    center = values - jnp.mean(values, axis=1, keepdims=True)
+    spread = jnp.mean(center * center, axis=1, keepdims=True)
+    out[...] = (center * lax.rsqrt(spread + 1e-05) * gain_ref[...]).astype(BF16)
+
+
+def expert_kernel(parts, place_ref, *refs):
+    shards, (up_ref, down_ref), outs = refs[:parts], refs[parts : parts + 2], refs[parts + 2 : -2]
+    held, active = refs[-2:]
+    far_ref, cross_ref, own_ref = outs
+    hidden = up_ref.shape[0]
+    share = own_ref.shape[1]
+    rows = shards[0].shape[0]
+    for t in range(parts):
+        first = pl.multiple_of((place_ref[1] ^ t) * rows, rows)
+        held[pl.ds(first, rows), :] = shards[t][...]
+    block = held[...]
+    for first in range(0, hidden, 256):
+        last = min(first + 256, hidden)
+        raised = lax.dot_general(
+            block, up_ref[first:last, :], (((1,), (1,)), ((), ())), preferred_element_type=F32
+        )
+        active[:, first:last] = (raised / (1.0 + jnp.exp(-raised))).astype(BF16)
+
+    def lowered(turn):
+        first = pl.multiple_of((place_ref[1] ^ turn) * share, HD)
+        return jnp.dot(
+            active[...], down_ref[:, pl.ds(first, share)], preferred_element_type=F32
+        )
+
+    far_ref[0] = lowered(1).astype(BF16)
+    far_ref[1] = lowered(3).astype(BF16)
+    cross_ref[...] = lowered(2)
+    own_ref[...] = lowered(0)
+
+
+def cross_kernel(cross_ref, near_ref, out_ref):
+    out_ref[...] = (cross_ref[...] + near_ref[1].astype(F32)).astype(BF16)
+
+
+def split_kernel(parts, place_ref, own_ref, near_ref, cross_ref, *outs):
+    rows = outs[0].shape[0]
+    for s in range(parts):
+        here = pl.ds(pl.multiple_of((place_ref[0] ^ s) * rows, rows), rows)
+        total = own_ref[here, :] + near_ref[0, here, :].astype(F32) + cross_ref[here, :].astype(F32)
+        outs[s][...] = total.astype(BF16)
+
+
+def mix_kernel(parts, place_ref, ids_ref, gates_ref, *refs):
+    terms, out = refs[:parts], refs[parts]
+    rows = out.shape[0]
+    ids = ids_ref[pl.ds(pl.multiple_of(place_ref[0] * rows, rows), rows), :]
+    total = jnp.zeros(out.shape, F32)
+    for s in range(parts):
+        gate = jnp.sum(
+            jnp.where(ids == (place_ref[0] ^ s), gates_ref[...], 0.0), axis=1, keepdims=True
+        )
+        total = total + gate * terms[s][...].astype(F32)
+    out[...] = total.astype(BF16)
+
+
+def trade(array, axis, turn):
+    count = lax.axis_size(axis)
+    return lax.ppermute(array, axis, [(k, k ^ turn) for k in range(count)])
+
+
+def every_row_body(attended, out_proj, norm_gain, expert_ids, gate_weights, w_up, w_down):
+    gx_count = lax.axis_size("gx")
+    ta_count = lax.axis_size("ta")
+    rows = attended.shape[0]
+    width = out_proj.shape[1]
+    model = norm_gain.shape[0]
+    share = model // ta_count
+    all_rows = rows * gx_count
+    place = jnp.stack([lax.axis_index("gx"), lax.axis_index("ta")]).astype(jnp.int32)
+    shape = jax.ShapeDtypeStruct
+    shards = [attended] + [trade(attended, "gx", s) for s in range(1, gx_count)]
+    pieces = local_call(
+        functools.partial(project_kernel, gx_count),
+        [shape((rows, width), BF16)] * ta_count,
+        [SMEM] + [VMEM] * (gx_count + 1),
+        [pltpu.VMEM((ta_count, rows, width), BF16)],
+        flops=2 * all_rows * out_proj.size,
+        moved=2 * out_proj.size,
+        name="project",
+    )(place, *shards, out_proj)
+    pieces = [pieces[0]] + [trade(pieces[t], "ta", t) for t in range(1, ta_count)]
+    hidden = local_call(
+        add_kernel, shape((rows, width), BF16), [VMEM] * ta_count, moved=8 * rows * width, name="add"
+    )(*pieces)
+    hidden = [hidden] + [trade(hidden, "gx", s) for s in range(1, gx_count)]
+    normed = local_call(
+        functools.partial(norm_kernel, gx_count),
+        shape((rows, model), BF16),
+        [SMEM] + [VMEM] * (gx_count + 1),
+        [pltpu.VMEM((rows, model), F32)],
+        moved=4 * rows * model,
+        name="norm",
+    )(place, norm_gain.reshape(1, model), *hidden)
+    over_x = trade(normed, "ta", 2)
+    blocks = [normed, trade(normed, "ta", 1), over_x, trade(over_x, "ta", 1)]
+    far, cross, own = local_call(
+        functools.partial(expert_kernel, ta_count),
+        [
+            shape((2, all_rows, share), BF16),
+            shape((all_rows, share), F32),
+            shape((all_rows, share), F32),
+        ],
+        [SMEM] + [VMEM] * (ta_count + 2),
+        [pltpu.VMEM((all_rows, model), BF16), pltpu.VMEM((all_rows, w_up.shape[2]), BF16)],
+        vmem=40,
+        flops=4 * all_rows * w_up.size,
+        moved=4 * w_up.size,
+        name="experts",
+    )(place, *blocks, jnp.swapaxes(w_up[0], 0, 1), w_down[0])
+    near = trade(far, "ta", 1)
+    crossing = local_call(
+        cross_kernel, shape((all_rows, share), BF16), [VMEM] * 2, moved=8 * all_rows * share, name="cross"
+    )(cross, near)
+    crossed = trade(crossing, "ta", 2)
+    terms = local_call(
+        functools.partial(split_kernel, gx_count),
+        [shape((rows, share), BF16)] * gx_count,
+        [SMEM] + [VMEM] * 3,
+        moved=10 * all_rows * share,
+        name="split",
+    )(place, own, near, crossed)
+    terms = [terms[0]] + [trade(terms[s], "gx", s) for s in range(1, gx_count)]
+    return local_call(
+        functools.partial(mix_kernel, gx_count),
+        shape((rows, share), BF16),
+        [SMEM] + [VMEM] * (gx_count + 2),
+        moved=10 * rows * share,
+        name="mix",
+    )(place, expert_ids, gate_weights, *terms)
 
 
 def route_tables(expert_ids, expert_count, block_rows, capacity):
@@ -28,40 +317,6 @@
     return (source_row, filled, pick_slot)
 
 
-def attend(queries, cache_keys, cache_values, fresh_keys, fresh_values, lengths):
-    row_count = queries.shape[0]
-    context = cache_keys.shape[1]
-    kv_heads = fresh_keys.shape[1] // HD
-    group_size = queries.shape[1] // (HD * kv_heads)
-    scale = 1.0 / math.sqrt(HD)
-    query_heads = queries.reshape(row_count, kv_heads, group_size, HD)
-    key_heads = cache_keys.reshape(row_count, context, kv_heads, HD)
-    value_heads = cache_values.reshape(row_count, context, kv_heads, HD)
-    fresh_key = fresh_keys.reshape(row_count, kv_heads, HD)
-    fresh_value = fresh_values.astype(jnp.float32).reshape(row_count, kv_heads, HD)
-    cached = (
-        jnp.einsum("rkgd,rckd->rkgc", query_heads, key_heads, preferred_element_type=jnp.float32)
-        * scale
-    )
-    own_score = (
-        jnp.einsum("rkgd,rkd->rkg", query_heads, fresh_key, preferred_element_type=jnp.float32)[
-            ..., None
-        ]
-        * scale
-    )
-    visible = jnp.arange(context, dtype=jnp.int32)[None, :] < lengths[:, None]
-    cached = jnp.where(visible[:, None, None, :], cached, -jnp.inf)
-    scores = jnp.concatenate([cached, own_score], axis=3)
-    largest = jnp.max(scores, axis=3, keepdims=True)
-    lifted = jnp.exp(scores - largest)
-    probs = (lifted / jnp.sum(lifted, axis=3, keepdims=True)).astype(jnp.bfloat16)
-    mixed = jnp.einsum(
-        "rkgc,rckd->rkgd", probs[..., :context], value_heads, preferred_element_type=jnp.float32
-    )
-    mixed = mixed + probs[..., context:].astype(jnp.float32) * fresh_value[:, :, None, :]
-    return mixed.reshape(row_count, -1).astype(jnp.bfloat16)
-
-
 def layer_norm(hidden, norm_gain):
     values = hidden.astype(jnp.float32)
     center = values - jnp.mean(values, axis=1, keepdims=True)
@@ -80,7 +335,11 @@
     slot_count = gx_count * capacity
     model_width = norm_gain.shape[0]
     width_share = model_width // ta_count
-    attended = attend(queries, kv_cache[0], kv_cache[1], new_kv[0], new_kv[1], lengths)
+    attended = attend(queries, new_kv, kv_cache, lengths)
+    if gx_count == top_count and ta_count == gx_count == 4:
+        return every_row_body(
+            attended, out_proj, norm_gain, expert_ids, gate_weights, w_up, w_down
+        )
     projected = jnp.dot(
         lax.all_gather(attended, "gx", axis=0, tiled=True),
         out_proj,

time: 236 us -> 105 us (0.44)
  local copies, waits for them, and re-layouts: 47.3 us -> 4.51 us
  blocking collectives: 37.5 us -> 0 us
  matrix products: 29.5 us -> 0 us
  waiting for transfers between devices: 85.5 us -> 56.4 us
  Pallas kernels: 0 us -> 21 us
  starting transfers between devices: 4.86 us -> 22.2 us
  other arithmetic: 16.4 us -> 0.07 us
  between operations: 13.3 us -> 0.09 us
    ppermute x0 -> x17, waiting for transfers between devices: none -> 56.4 us  [trade(): return lax.ppermute(array, axis, [(k, k ^ turn) for k in range(count)])]
    reduce_scatter x1 -> x0, waiting for transfers between devices: 38.1 us -> none  [body(): mine = lax.psum_scatter(terms, 'ta', scatter_dimension=1, tiled=True)]
    dot_general x5 -> x0, matrix products: 29.5 us -> none  [the longest x1 16.8 us: body(): terms = jnp.dot(active, w_down[0], preferred_element_type=jnp.float32)]
    ppermute x0 -> x17, starting transfers between devices: none -> 22.2 us  [trade(): return lax.ppermute(array, axis, [(k, k ^ turn) for k in range(count)])]
    all_gather x1 -> x0, blocking collectives: 21.3 us -> none  [body(): lax.all_gather(attended, 'gx', axis=0, tiled=True)]
    pallas_call x0 -> x8, Pallas kernels: none -> 21 us  [the longest x1 8.66 us: every_row_body(): local_call(functools.partial(expert_kernel, ta_count), [shape((2, all_row...]
    another operation x4 -> x0, local copies, waits for them, and re-layouts: 21 us -> none  [the longest x1 9.79 us: attend(): value_heads = cache_values.reshape(row_count, context, kv_heads, HD)]
    unnamed x4 -> x0, waiting for transfers between devices: 19.1 us -> none
  transfers between devices with their start and end apart: 4 -> 17, of which waited for: 4 -> 12; matrix products, arithmetic and copies ran while one was open for 1% -> 0% of each run, Pallas kernels for 0% -> 0%
where the time goes in v1:
time: 105 us; the launch traced here: 104 us
  waiting for transfers between devices  56.4 us (54%)
  starting transfers between devices  22.2 us (21%)
  Pallas kernels  21 us (20%)
  local copies, waits for them, and re-layouts  4.51 us (4%)
    ppermute x17, waiting for transfers between devices, trade(): return lax.ppermute(array, axis, [(k, k ^ turn) for k in range(count)])  56.4 us
    ppermute x17, starting transfers between devices, trade(): return lax.ppermute(array, axis, [(k, k ^ turn) for k in range(count)])  22.2 us
    pallas_call x1, Pallas kernels, every_row_body(): local_call(functools.partial(expert_kernel, ta_count), [shape((2, all_row...  8.66 us
    pallas_call x1, Pallas kernels, attend(): pl.pallas_call(functools.partial(attend_kernel, kv_heads, heads // kv_hea...  7.98 us
    unnamed x14, local copies, waits for them, and re-layouts  4.51 us
  transfers between devices with their start and end apart: 17, of which 12 were waited for; matrix products, arithmetic and copies ran while one was open for 0% of the time, Pallas kernels for 0%

profile of v1, /device:TPU:0, one launch (start us, length us, event | category | flops | bytes accessed | tf_op | source)
XLA Modules:
  0.0 104.4 jit_solution(7671467516992236005)
XLA Ops:
  0.0 8.0 %attend.1.refs_0_ = bf16[64,1536]{1,0:T(8,128)(2,1)} custom-call(s32[64]{0:T(128)} %lengths_ref.1, bf16[64,1536]{1,0:T(8,128)(2,1)} %q_ref.1, bf16[2,64,256]{2,1,0:T(8,128)(2,1)} %fresh_ref.1, bf16[2,64,192,256]{3,2,1,0:T(8,128)(2,1)} %cache_ref.1), custom_call_target="tpu_custom_call" | custom-call | flops 201326592 | bytes 12582912 | tf_op jit(solution)/shard_map/attend/pallas_call | solution.py:110
  8.0 3.1 %collective-permute-start = (bf16[64,1536]{1,0:T(8,128)(2,1)}, bf16[64,1536]{1,0:T(8,128)(2,1)S(1)}, u32[]{:S(2)}, u32[]{:S(2)}) collective-permute-start(bf16[64,1536]{1,0:T(8,128)(2,1)} %attend.1.refs_0_), channel_id=1, source_target_pairs={{0,4},{4,0},{8,12},{12,8},{1,5},{5,1},{9,13},{13,9},{2,6},{6,2},{1... | collective-permute-start | bytes 589832 | tf_op jit(solution)/shard_map/ppermute | solution.py:226
  11.1 2.6 %collective-permute-start.1 = (bf16[64,1536]{1,0:T(8,128)(2,1)}, bf16[64,1536]{1,0:T(8,128)(2,1)S(1)}, u32[]{:S(2)}, u32[]{:S(2)}) collective-permute-start(bf16[64,1536]{1,0:T(8,128)(2,1)} %attend.1.refs_0_), channel_id=1, source_target_pairs={{0,8},{4,12},{8,0},{12,4},{1,9},{5,13},{9,1},{13,5},{2,10},{6,14},... | collective-permute-start | bytes 589832 | tf_op jit(solution)/shard_map/ppermute | solution.py:226
  13.8 5.9 %collective-permute-done.refs_1_ = bf16[64,1536]{1,0:T(8,128)(2,1)S(1)} collective-permute-done((bf16[64,1536]{1,0:T(8,128)(2,1)}, bf16[64,1536]{1,0:T(8,128)(2,1)S(1)}, u32[]{:S(2)}, u32[]{:S(2)}) %collective-permute-start) | collective-permute-done | bytes 196640 | tf_op jit(solution)/shard_map/ppermute | solution.py:226
  19.6 8.8 %collective-permute-done.1.refs_2_ = bf16[64,1536]{1,0:T(8,128)(2,1)S(1)} collective-permute-done((bf16[64,1536]{1,0:T(8,128)(2,1)}, bf16[64,1536]{1,0:T(8,128)(2,1)S(1)}, u32[]{:S(2)}, u32[]{:S(2)}) %collective-permute-start.1) | collective-permute-done | bytes 196640 | tf_op jit(solution)/shard_map/ppermute | solution.py:226
  29.4 1.3 %project.1 = (bf16[64,768]{1,0:T(8,128)(2,1)S(1)}, bf16[64,768]{1,0:T(8,128)(2,1)S(1)}, bf16[64,768]{1,0:T(8,128)(2,1)S(1)}, bf16[64,768]{1,0:T(8,128)(2,1)S(1)}) custom-call(s32[2]{0:T(128)S(1)} %pad_add_fusion.place_ref, bf16[64,1536]{1,0:T(8,128)(2,1)S(1)} %copy-done.2, bf16[64,1536]{1,0:T(8,128)(2,1)S(1)} %collective-permute-done.refs_1_, ...), custom_call_target="tpu_custom_call" | custom-call | flops 603979776 | bytes 2359296 | tf_op jit(solution)/shard_map/project/pallas_call | solution.py:240
  30.8 1.6 %collective-permute-start.4 = (bf16[64,768]{1,0:T(8,128)(2,1)S(1)}, bf16[64,768]{1,0:T(8,128)(2,1)S(1)}, u32[]{:S(2)}, u32[]{:S(2)}) collective-permute-start(bf16[64,768]{1,0:T(8,128)(2,1)S(1)} %get-tuple-element.18), channel_id=1, source_target_pairs={{0,2},{1,3},{2,0},{3,1},{4,6},{5,7},{6,4},{7,5},{8,10},{9,11},{10,... | collective-permute-start | bytes 294920 | tf_op jit(solution)/shard_map/ppermute | solution.py:226
  32.7 3.8 %collective-permute-done.4.refs_2_ = bf16[64,768]{1,0:T(8,128)(2,1)S(1)} collective-permute-done((bf16[64,768]{1,0:T(8,128)(2,1)S(1)}, bf16[64,768]{1,0:T(8,128)(2,1)S(1)}, u32[]{:S(2)}, u32[]{:S(2)}) %collective-permute-start.4) | collective-permute-done | bytes 98336 | tf_op jit(solution)/shard_map/ppermute | solution.py:226
  37.7 3.4 %collective-permute-start.6 = (bf16[64,768]{1,0:T(8,128)(2,1)S(1)}, bf16[64,768]{1,0:T(8,128)(2,1)S(1)}, u32[]{:S(2)}, u32[]{:S(2)}) collective-permute-start(bf16[64,768]{1,0:T(8,128)(2,1)S(1)} %add.3.refs_0_), channel_id=1, source_target_pairs={{0,4},{4,0},{8,12},{12,8},{1,5},{5,1},{9,13},{13,9},{2,6},{6,2},{1... | collective-permute-start | bytes 294920 | tf_op jit(solution)/shard_map/ppermute | solution.py:226
  42.2 1.4 %collective-permute-start.8 = (bf16[64,768]{1,0:T(8,128)(2,1)S(1)}, bf16[64,768]{1,0:T(8,128)(2,1)S(1)}, u32[]{:S(2)}, u32[]{:S(2)}) collective-permute-start(bf16[64,768]{1,0:T(8,128)(2,1)S(1)} %add.3.refs_0_), channel_id=1, source_target_pairs={{0,12},{4,8},{8,4},{12,0},{1,13},{5,9},{9,5},{13,1},{2,14},{6,10},... | collective-permute-start | bytes 294920 | tf_op jit(solution)/shard_map/ppermute | solution.py:226
  44.4 7.4 %collective-permute-done.7.refs_2_ = bf16[64,768]{1,0:T(8,128)(2,1)S(1)} collective-permute-done((bf16[64,768]{1,0:T(8,128)(2,1)S(1)}, bf16[64,768]{1,0:T(8,128)(2,1)S(1)}, u32[]{:S(2)}, u32[]{:S(2)}) %collective-permute-start.7) | collective-permute-done | bytes 98336 | tf_op jit(solution)/shard_map/ppermute | solution.py:226
  52.7 1.6 %collective-permute-start.10 = (bf16[64,3072]{1,0:T(8,128)(2,1)S(1)}, bf16[64,3072]{1,0:T(8,128)(2,1)S(1)}, u32[]{:S(2)}, u32[]{:S(2)}) collective-permute-start(bf16[64,3072]{1,0:T(8,128)(2,1)S(1)} %norm.1.refs_0_), channel_id=1, source_target_pairs={{0,2},{1,3},{2,0},{3,1},{4,6},{5,7},{6,4},{7,5},{8,10},{9,11},{10,... | collective-permute-start | bytes 1179656 | tf_op jit(solution)/shard_map/ppermute | solution.py:226
  54.3 8.0 %collective-permute-done.10.refs_2_ = bf16[64,3072]{1,0:T(8,128)(2,1)S(1)} collective-permute-done((bf16[64,3072]{1,0:T(8,128)(2,1)S(1)}, bf16[64,3072]{1,0:T(8,128)(2,1)S(1)}, u32[]{:S(2)}, u32[]{:S(2)}) %collective-permute-start.10) | collective-permute-done | bytes 393248 | tf_op jit(solution)/shard_map/ppermute | solution.py:226
  62.3 1.7 %collective-permute-done.11.refs_3_ = bf16[64,3072]{1,0:T(8,128)(2,1)S(1)} collective-permute-done((bf16[64,3072]{1,0:T(8,128)(2,1)S(1)}, bf16[64,3072]{1,0:T(8,128)(2,1)S(1)}, u32[]{:S(2)}, u32[]{:S(2)}) %collective-permute-start.11) | collective-permute-done | bytes 393248 | tf_op jit(solution)/shard_map/ppermute | solution.py:226
  64.0 3.3 %copy-done = bf16[1,3072,1344]{1,2,0:T(8,128)(2,1)S(1)} copy-done((bf16[1,3072,1344]{1,2,0:T(8,128)(2,1)S(1)}, bf16[1,3072,1344]{1,2,0:T(8,128)(2,1)}, u32[]{:S(2)}) %copy-start) | copy-done | bytes 8257560
  67.4 8.7 %experts.1 = (bf16[2,256,768]{2,1,0:T(8,128)(2,1)S(1)}, f32[256,768]{1,0:T(8,128)S(1)}, f32[256,768]{1,0:T(8,128)S(1)}) custom-call(s32[2]{0:T(128)S(1)} %pad_add_fusion.place_ref, bf16[64,3072]{1,0:T(8,128)(2,1)S(1)} %norm.1.refs_0_, bf16[64,3072]{1,0:T(8,128)(2,1)S(1)} %collective-permute-done.9.refs_1_, ...), custom_call_target="tpu_custom_call" | custom-call | flops 4227858432 | bytes 16515072 | tf_op jit(solution)/shard_map/experts/pallas_call | solution.py:264
  76.2 2.2 %collective-permute-done.12.near_ref = bf16[2,256,768]{2,1,0:T(8,128)(2,1)S(1)} collective-permute-done((bf16[2,256,768]{2,1,0:T(8,128)(2,1)S(1)}, bf16[2,256,768]{2,1,0:T(8,128)(2,1)S(1)}, u32[]{:S(2)}, u32[]{:S(2)}) %collective-permute-start.12) | collective-permute-done | bytes 786464 | tf_op jit(solution)/shard_map/ppermute | solution.py:226
  78.4 1.5 %collective-permute-start.13 = (bf16[256,768]{1,0:T(8,128)(2,1)S(1)}, bf16[256,768]{1,0:T(8,128)(2,1)S(1)}, u32[]{:S(2)}, u32[]{:S(2)}) collective-permute-start(bf16[256,768]{1,0:T(8,128)(2,1)S(1)} %cross.1), channel_id=1, source_target_pairs={{0,2},{1,3},{2,0},{3,1},{4,6},{5,7},{6,4},{7,5},{8,10},{9,11},{10,... | collective-permute-start | bytes 1179656 | tf_op jit(solution)/shard_map/ppermute | solution.py:226
  80.0 9.7 %collective-permute-done.13.cross_ref = bf16[256,768]{1,0:T(8,128)(2,1)S(1)} collective-permute-done((bf16[256,768]{1,0:T(8,128)(2,1)S(1)}, bf16[256,768]{1,0:T(8,128)(2,1)S(1)}, u32[]{:S(2)}, u32[]{:S(2)}) %collective-permute-start.13) | collective-permute-done | bytes 393248 | tf_op jit(solution)/shard_map/ppermute | solution.py:226
  90.4 2.7 %collective-permute-start.14 = (bf16[64,768]{1,0:T(8,128)(2,1)S(1)}, bf16[64,768]{1,0:T(8,128)(2,1)S(1)}, u32[]{:S(2)}, u32[]{:S(2)}) collective-permute-start(bf16[64,768]{1,0:T(8,128)(2,1)S(1)} %get-tuple-element.24), channel_id=1, source_target_pairs={{0,4},{4,0},{8,12},{12,8},{1,5},{5,1},{9,13},{13,9},{2,6},{6,2},{1... | collective-permute-start | bytes 294920 | tf_op jit(solution)/shard_map/ppermute | solution.py:226
  93.1 1.3 %collective-permute-start.15 = (bf16[64,768]{1,0:T(8,128)(2,1)S(1)}, bf16[64,768]{1,0:T(8,128)(2,1)S(1)}, u32[]{:S(2)}, u32[]{:S(2)}) collective-permute-start(bf16[64,768]{1,0:T(8,128)(2,1)S(1)} %get-tuple-element.25), channel_id=1, source_target_pairs={{0,8},{4,12},{8,0},{12,4},{1,9},{5,13},{9,1},{13,5},{2,10},{6,14},... | collective-permute-start | bytes 294920 | tf_op jit(solution)/shard_map/ppermute | solution.py:226
  94.4 1.4 %collective-permute-start.16 = (bf16[64,768]{1,0:T(8,128)(2,1)S(1)}, bf16[64,768]{1,0:T(8,128)(2,1)S(1)}, u32[]{:S(2)}, u32[]{:S(2)}) collective-permute-start(bf16[64,768]{1,0:T(8,128)(2,1)S(1)} %get-tuple-element.26), channel_id=1, source_target_pairs={{0,12},{4,8},{8,4},{12,0},{1,13},{5,9},{9,5},{13,1},{2,14},{6,10},... | collective-permute-start | bytes 294920 | tf_op jit(solution)/shard_map/ppermute | solution.py:226
  96.2 6.8 %collective-permute-done.15.refs_2_ = bf16[64,768]{1,0:T(8,128)(2,1)S(1)} collective-permute-done((bf16[64,768]{1,0:T(8,128)(2,1)S(1)}, bf16[64,768]{1,0:T(8,128)(2,1)S(1)}, u32[]{:S(2)}, u32[]{:S(2)}) %collective-permute-start.15) | collective-permute-done | bytes 98336 | tf_op jit(solution)/shard_map/ppermute | solution.py:226
  103.0 1.3 %mix.1 = bf16[64,768]{1,0:T(8,128)(2,1)} custom-call(s32[2]{0:T(128)S(1)} %pad_add_fusion.place_ref, s32[256,4]{1,0:T(8,128)S(1)} %copy.11.ids_ref, f32[64,4]{1,0:T(8,128)S(1)} %copy.12.gates_ref, bf16[64,768]{1,0:T(8,128)(2,1)S(1)} %get-tuple-element.23.refs_0_, bf16[64,768]{1,0:T(8,128)(2,1)S(1)} %collective-permute-done.14.refs_1_, ...), custom_call_target="tpu_custom_call" | custom-call | bytes 491520 | tf_op jit(solution)/shard_map/mix/pallas_call | solution.py:291
  (33 shorter events, 6.8 us)
Async XLA Ops:
  0.0 28.5 %copy-start.1 = (bf16[1536,768]{1,0:T(8,128)(2,1)S(1)}, bf16[1536,768]{1,0:T(8,128)(2,1)}, u32[]{:S(2)}) copy-start(bf16[1536,768]{1,0:T(8,128)(2,1)} %refs_4_.1) | copy-start | bytes 7077892
  0.0 51.8 %copy-start.3 = (f32[3072]{0:T(1024)S(1)}, f32[3072]{0:T(1024)}, u32[]{:S(2)}) copy-start(f32[3072]{0:T(1024)} %param.15) | copy-start | bytes 36868
  8.0 11.6 %collective-permute-start = (bf16[64,1536]{1,0:T(8,128)(2,1)}, bf16[64,1536]{1,0:T(8,128)(2,1)S(1)}, u32[]{:S(2)}, u32[]{:S(2)}) collective-permute-start(bf16[64,1536]{1,0:T(8,128)(2,1)} %attend.1.refs_0_), channel_id=1, source_target_pairs={{0,4},{4,0},{8,12},{12,8},{1,5},{5,1},{9,13},{13,9},{2,6},{6,2},{1... | collective-permute-start | bytes 589832 | tf_op jit(solution)/shard_map/ppermute | solution.py:226
  11.1 17.4 %collective-permute-start.1 = (bf16[64,1536]{1,0:T(8,128)(2,1)}, bf16[64,1536]{1,0:T(8,128)(2,1)S(1)}, u32[]{:S(2)}, u32[]{:S(2)}) collective-permute-start(bf16[64,1536]{1,0:T(8,128)(2,1)} %attend.1.refs_0_), channel_id=1, source_target_pairs={{0,8},{4,12},{8,0},{12,4},{1,9},{5,13},{9,1},{13,5},{2,10},{6,14},... | collective-permute-start | bytes 589832 | tf_op jit(solution)/shard_map/ppermute | solution.py:226
  13.7 14.8 %collective-permute-start.2 = (bf16[64,1536]{1,0:T(8,128)(2,1)}, bf16[64,1536]{1,0:T(8,128)(2,1)S(1)}, u32[]{:S(2)}, u32[]{:S(2)}) collective-permute-start(bf16[64,1536]{1,0:T(8,128)(2,1)} %attend.1.refs_0_), channel_id=1, source_target_pairs={{0,12},{4,8},{8,4},{12,0},{1,13},{5,9},{9,5},{13,1},{2,14},{6,10},... | collective-permute-start | bytes 589832 | tf_op jit(solution)/shard_map/ppermute | solution.py:226
  28.5 0.9 copy-start.2
  30.7 1.9 %collective-permute-start.3 = (bf16[64,768]{1,0:T(8,128)(2,1)S(1)}, bf16[64,768]{1,0:T(8,128)(2,1)S(1)}, u32[]{:S(2)}, u32[]{:S(2)}) collective-permute-start(bf16[64,768]{1,0:T(8,128)(2,1)S(1)} %get-tuple-element.17), channel_id=1, source_target_pairs={{0,1},{1,0},{2,3},{3,2},{4,5},{5,4},{6,7},{7,6},{8,9},{9,8},{10,11... | collective-permute-start | bytes 294920 | tf_op jit(solution)/shard_map/ppermute | solution.py:226
  30.8 5.7 %collective-permute-start.4 = (bf16[64,768]{1,0:T(8,128)(2,1)S(1)}, bf16[64,768]{1,0:T(8,128)(2,1)S(1)}, u32[]{:S(2)}, u32[]{:S(2)}) collective-permute-start(bf16[64,768]{1,0:T(8,128)(2,1)S(1)} %get-tuple-element.18), channel_id=1, source_target_pairs={{0,2},{1,3},{2,0},{3,1},{4,6},{5,7},{6,4},{7,5},{8,10},{9,11},{10,... | collective-permute-start | bytes 294920 | tf_op jit(solution)/shard_map/ppermute | solution.py:226
  32.4 5.3 %collective-permute-start.5 = (bf16[64,768]{1,0:T(8,128)(2,1)S(1)}, bf16[64,768]{1,0:T(8,128)(2,1)S(1)}, u32[]{:S(2)}, u32[]{:S(2)}) collective-permute-start(bf16[64,768]{1,0:T(8,128)(2,1)S(1)} %get-tuple-element.19), channel_id=1, source_target_pairs={{0,3},{1,2},{2,1},{3,0},{4,7},{5,6},{6,5},{7,4},{8,11},{9,10},{10,... | collective-permute-start | bytes 294920 | tf_op jit(solution)/shard_map/ppermute | solution.py:226
  37.7 6.7 %collective-permute-start.6 = (bf16[64,768]{1,0:T(8,128)(2,1)S(1)}, bf16[64,768]{1,0:T(8,128)(2,1)S(1)}, u32[]{:S(2)}, u32[]{:S(2)}) collective-permute-start(bf16[64,768]{1,0:T(8,128)(2,1)S(1)} %add.3.refs_0_), channel_id=1, source_target_pairs={{0,4},{4,0},{8,12},{12,8},{1,5},{5,1},{9,13},{13,9},{2,6},{6,2},{1... | collective-permute-start | bytes 294920 | tf_op jit(solution)/shard_map/ppermute | solution.py:226
  41.2 10.6 %collective-permute-start.7 = (bf16[64,768]{1,0:T(8,128)(2,1)S(1)}, bf16[64,768]{1,0:T(8,128)(2,1)S(1)}, u32[]{:S(2)}, u32[]{:S(2)}) collective-permute-start(bf16[64,768]{1,0:T(8,128)(2,1)S(1)} %add.3.refs_0_), channel_id=1, source_target_pairs={{0,8},{4,12},{8,0},{12,4},{1,9},{5,13},{9,1},{13,5},{2,10},{6,14},... | collective-permute-start | bytes 294920 | tf_op jit(solution)/shard_map/ppermute | solution.py:226
  42.2 9.6 %collective-permute-start.8 = (bf16[64,768]{1,0:T(8,128)(2,1)S(1)}, bf16[64,768]{1,0:T(8,128)(2,1)S(1)}, u32[]{:S(2)}, u32[]{:S(2)}) collective-permute-start(bf16[64,768]{1,0:T(8,128)(2,1)S(1)} %add.3.refs_0_), channel_id=1, source_target_pairs={{0,12},{4,8},{8,4},{12,0},{1,13},{5,9},{9,5},{13,1},{2,14},{6,10},... | collective-permute-start | bytes 294920 | tf_op jit(solution)/shard_map/ppermute | solution.py:226
  52.7 9.6 %collective-permute-start.10 = (bf16[64,3072]{1,0:T(8,128)(2,1)S(1)}, bf16[64,3072]{1,0:T(8,128)(2,1)S(1)}, u32[]{:S(2)}, u32[]{:S(2)}) collective-permute-start(bf16[64,3072]{1,0:T(8,128)(2,1)S(1)} %norm.1.refs_0_), channel_id=1, source_target_pairs={{0,2},{1,3},{2,0},{3,1},{4,6},{5,7},{6,4},{7,5},{8,10},{9,11},{10,... | collective-permute-start | bytes 1179656 | tf_op jit(solution)/shard_map/ppermute | solution.py:226
  54.3 8.0 %collective-permute-start.9 = (bf16[64,3072]{1,0:T(8,128)(2,1)S(1)}, bf16[64,3072]{1,0:T(8,128)(2,1)S(1)}, u32[]{:S(2)}, u32[]{:S(2)}) collective-permute-start(bf16[64,3072]{1,0:T(8,128)(2,1)S(1)} %norm.1.refs_0_), channel_id=1, source_target_pairs={{0,1},{1,0},{2,3},{3,2},{4,5},{5,4},{6,7},{7,6},{8,9},{9,8},{10,11... | collective-permute-start | bytes 1179656 | tf_op jit(solution)/shard_map/ppermute | solution.py:226
  62.3 1.7 %collective-permute-start.11 = (bf16[64,3072]{1,0:T(8,128)(2,1)S(1)}, bf16[64,3072]{1,0:T(8,128)(2,1)S(1)}, u32[]{:S(2)}, u32[]{:S(2)}) collective-permute-start(bf16[64,3072]{1,0:T(8,128)(2,1)S(1)} %collective-permute-done.10.refs_2_), channel_id=1, source_target_pairs={{0,1},{1,0},{2,3},{3,2},{4,5},{5,4},{6,7},{7,6},{8,9},{9,8},{10,11... | collective-permute-start | bytes 1179656 | tf_op jit(solution)/shard_map/ppermute | solution.py:226
  64.0 3.3 %copy-start = (bf16[1,3072,1344]{1,2,0:T(8,128)(2,1)S(1)}, bf16[1,3072,1344]{1,2,0:T(8,128)(2,1)}, u32[]{:S(2)}) copy-start(bf16[1,3072,1344]{1,2,0:T(8,128)(2,1)} %param.18) | copy-start | bytes 24772612
  67.3 28.4 %copy-start.4 = (s32[256,4]{0,1:T(4,128)S(1)}, s32[256,4]{0,1:T(4,128)}, u32[]{:S(2)}) copy-start(s32[256,4]{0,1:T(4,128)} %param.16) | copy-start | bytes 12292
  67.3 28.6 %copy-start.5 = (f32[64,4]{0,1:T(4,128)S(1)}, f32[64,4]{0,1:T(4,128)}, u32[]{:S(2)}) copy-start(f32[64,4]{0,1:T(4,128)} %param.17) | copy-start | bytes 3076
  76.0 2.4 %collective-permute-start.12 = (bf16[2,256,768]{2,1,0:T(8,128)(2,1)S(1)}, bf16[2,256,768]{2,1,0:T(8,128)(2,1)S(1)}, u32[]{:S(2)}, u32[]{:S(2)}) collective-permute-start(bf16[2,256,768]{2,1,0:T(8,128)(2,1)S(1)} %get-tuple-element.21), channel_id=1, source_target_pairs={{0,1},{1,0},{2,3},{3,2},{4,5},{5,4},{6,7},{7,6},{8,9},{9,8},{10,11... | collective-permute-start | bytes 2359304 | tf_op jit(solution)/shard_map/ppermute | solution.py:226
  78.4 11.2 %collective-permute-start.13 = (bf16[256,768]{1,0:T(8,128)(2,1)S(1)}, bf16[256,768]{1,0:T(8,128)(2,1)S(1)}, u32[]{:S(2)}, u32[]{:S(2)}) collective-permute-start(bf16[256,768]{1,0:T(8,128)(2,1)S(1)} %cross.1), channel_id=1, source_target_pairs={{0,2},{1,3},{2,0},{3,1},{4,6},{5,7},{6,4},{7,5},{8,10},{9,11},{10,... | collective-permute-start | bytes 1179656 | tf_op jit(solution)/shard_map/ppermute | solution.py:226
  90.4 5.9 %collective-permute-start.14 = (bf16[64,768]{1,0:T(8,128)(2,1)S(1)}, bf16[64,768]{1,0:T(8,128)(2,1)S(1)}, u32[]{:S(2)}, u32[]{:S(2)}) collective-permute-start(bf16[64,768]{1,0:T(8,128)(2,1)S(1)} %get-tuple-element.24), channel_id=1, source_target_pairs={{0,4},{4,0},{8,12},{12,8},{1,5},{5,1},{9,13},{13,9},{2,6},{6,2},{1... | collective-permute-start | bytes 294920 | tf_op jit(solution)/shard_map/ppermute | solution.py:226
  93.1 10.0 %collective-permute-start.15 = (bf16[64,768]{1,0:T(8,128)(2,1)S(1)}, bf16[64,768]{1,0:T(8,128)(2,1)S(1)}, u32[]{:S(2)}, u32[]{:S(2)}) collective-permute-start(bf16[64,768]{1,0:T(8,128)(2,1)S(1)} %get-tuple-element.25), channel_id=1, source_target_pairs={{0,8},{4,12},{8,0},{12,4},{1,9},{5,13},{9,1},{13,5},{2,10},{6,14},... | collective-permute-start | bytes 294920 | tf_op jit(solution)/shard_map/ppermute | solution.py:226
  94.4 8.6 %collective-permute-start.16 = (bf16[64,768]{1,0:T(8,128)(2,1)S(1)}, bf16[64,768]{1,0:T(8,128)(2,1)S(1)}, u32[]{:S(2)}, u32[]{:S(2)}) collective-permute-start(bf16[64,768]{1,0:T(8,128)(2,1)S(1)} %get-tuple-element.26), channel_id=1, source_target_pairs={{0,12},{4,8},{8,4},{12,0},{1,13},{5,9},{9,5},{13,1},{2,14},{6,10},... | collective-permute-start | bytes 294920 | tf_op jit(solution)/shard_map/ppermute | solution.py:226

commit v2 on v1

v2 whole, which is shorter than its diff:
```python
import functools
import math

import jax
import jax.numpy as jnp
from jax import lax
from jax.experimental import pallas as pl
from jax.experimental.pallas import tpu as pltpu
from jax.sharding import PartitionSpec as P

HD = 128
MIB = 1 << 20
VMEM = pl.BlockSpec(memory_space=pltpu.VMEM)
SMEM = pl.BlockSpec(memory_space=pltpu.SMEM)
F32 = jnp.float32
BF16 = jnp.bfloat16


ANYWHERE = pl.BlockSpec(memory_space=pl.ANY)


def local_call(kernel, out_shape, in_specs, scratch=(), vmem=32, name=None, after=None):
    several = isinstance(out_shape, (tuple, list))
    if after is not None:
        count, inner = len(in_specs), kernel
        in_specs = [*in_specs, ANYWHERE]
        kernel = lambda *refs: inner(*refs[:count], *refs[count + 1 :])
    call = pl.pallas_call(
        kernel,
        out_shape=out_shape,
        in_specs=in_specs,
        out_specs=[VMEM] * len(out_shape) if several else VMEM,
        scratch_shapes=list(scratch),
        compiler_params=pltpu.CompilerParams(vmem_limit_bytes=vmem * MIB),
        cost_estimate=pl.CostEstimate(flops=1024, bytes_accessed=1024, transcendentals=0),
        name=name,
    )
    return call if after is None else lambda *args: call(*args, after)


def attend_kernel(
    kv_heads, group, slots, batch, begin,
    lengths_ref, q_ref, fresh_ref, cache_ref, after_ref, out_ref,
    keys, values, q_rows, scores, own_scores, probs, own_probs, mixed, sems,
):
    rows = out_ref.shape[0]
    context = keys.shape[1]
    width = kv_heads * HD
    heads = kv_heads * group
    steps = rows // batch
    scale = 1.0 / math.sqrt(HD)

    def fetch(step, kind):
        buffer = (keys, values)[kind]
        return pltpu.make_async_copy(
            cache_ref.at[kind, pl.ds(begin + step * batch, batch)],
            buffer.at[pl.ds(step * batch, batch)],
            sems.at[kind, step],
        )

    for step in range(steps):
        for kind in range(2):
            fetch(step, kind).start()
    q_rows[...] = jnp.zeros_like(q_rows)
    for head in range(heads):
        q_rows[head // group, pl.ds(head, rows, stride=slots), :] = q_ref[
            begin : begin + rows, head * HD : (head + 1) * HD
        ].astype(F32)
    place = lax.broadcasted_iota(jnp.int32, (slots, context), 1)
    for step in range(steps):
        fetch(step, 0).wait()
        for k in range(batch):
            row = step * batch + k
            mine = jnp.concatenate(
                [q_rows[g, row * slots : (row + 1) * slots, :] for g in range(kv_heads)], axis=1
            )
            cached = lax.dot_general(
                mine.astype(BF16), keys[row], (((1,), (1,)), ((), ())),
                preferred_element_type=F32,
            )
            here = slice(k * slots, (k + 1) * slots)
            scores[here, :] = jnp.where(place < lengths_ref[begin + row], cached * scale, -jnp.inf)
            fresh_key = fresh_ref[0, begin + row : begin + row + 1, :].astype(F32)
            own_scores[here, :] = jnp.broadcast_to(
                jnp.sum(mine * fresh_key, axis=1, keepdims=True) * scale, (slots, HD)
            )
        cached = scores[...]
        own = own_scores[:, :1]
        largest = jnp.maximum(jnp.max(cached, axis=1, keepdims=True), own)
        lifted = jnp.exp(cached - largest)
        own_lifted = jnp.exp(own - largest)
        total = jnp.sum(lifted, axis=1, keepdims=True) + own_lifted
        probs[...] = (lifted / total).astype(BF16)
        own_probs[...] = jnp.broadcast_to(
            (own_lifted / total).astype(BF16).astype(F32), own_probs.shape
        )
        fetch(step, 1).wait()
        for k in range(batch):
            row = step * batch + k
            here = slice(k * slots, (k + 1) * slots)
            weighted = jnp.dot(probs[here, :], values[row], preferred_element_type=F32)
            fresh_value = fresh_ref[1, begin + row : begin + row + 1, :].astype(F32)
            total = weighted + own_probs[here, :1] * fresh_value
            for g in range(kv_heads):
                mixed[g, here, :] = total[:, g * HD : (g + 1) * HD]
        for head in range(heads):
            out_ref[step * batch : (step + 1) * batch, head * HD : (head + 1) * HD] = mixed[
                head // group, pl.ds(head, batch, stride=slots), :
            ].astype(BF16)


def attend(queries, new_kv, kv_cache, lengths, begin, rows, after):
    features = queries.shape[1]
    context, width = kv_cache.shape[2:]
    kv_heads = width // HD
    heads = features // HD
    slots = -(-heads // 8) * 8
    batch = 16
    return pl.pallas_call(
        functools.partial(attend_kernel, kv_heads, heads // kv_heads, slots, batch, begin),
        out_shape=jax.ShapeDtypeStruct((rows, features), BF16),
        in_specs=[SMEM, VMEM, VMEM, ANYWHERE, ANYWHERE],
        out_specs=VMEM,
        scratch_shapes=[
            pltpu.VMEM((rows, context, width), BF16),
            pltpu.VMEM((rows, context, width), BF16),
            pltpu.VMEM((kv_heads, rows * slots, HD), F32),
            pltpu.VMEM((batch * slots, context), F32),
            pltpu.VMEM((batch * slots, HD), F32),
            pltpu.VMEM((batch * slots, context), BF16),
            pltpu.VMEM((batch * slots, HD), F32),
            pltpu.VMEM((kv_heads, batch * slots, HD), F32),
            pltpu.SemaphoreType.DMA((2, rows // batch)),
        ],
        compiler_params=pltpu.CompilerParams(vmem_limit_bytes=53 * MIB),
        cost_estimate=pl.CostEstimate(flops=1024, bytes_accessed=1024, transcendentals=0),
        name="attend",
    )(lengths, queries, new_kv, kv_cache, after)


def pair_kernel(own_ref, other_ref, out_ref):
    out_ref[0] = own_ref[...]
    out_ref[1] = other_ref[...]


def gather_pair(owned, others, after):
    pairs = []
    for own, other in zip(owned, others):
        out = jax.ShapeDtypeStruct((2, *own.shape), own.dtype)
        after = pairs[-1] if pairs else after
        pairs.append(local_call(pair_kernel, out, [VMEM] * 2, name="pair", after=after)(own, other))
    return pairs


def by_distance(pair_ref, second_ref):
    return pair_ref.at[0], second_ref.at[0], pair_ref.at[1], second_ref.at[1]


def project_kernel(
    place_ref, pair_ref, second_ref, weight_ref, own_ref, cross_ref, far_ref, held
):
    shards = by_distance(pair_ref, second_ref)
    rows = own_ref.shape[0]
    turn = place_ref[0] ^ place_ref[1]
    block = jnp.concatenate([shard[...] for shard in shards], axis=0)
    pieces = jnp.dot(block, weight_ref[...], preferred_element_type=F32)
    for s in range(len(shards)):
        held[turn ^ s] = pieces[s * rows : (s + 1) * rows, :]
    own_ref[...] = held[0]
    cross_ref[...] = held[2]
    far_ref[0] = held[1].astype(BF16)
    far_ref[1] = held[3].astype(BF16)


def cross_kernel(cross_ref, near_ref, out_ref):
    out_ref[...] = (cross_ref[...] + near_ref[1].astype(F32)).astype(BF16)


def close_kernel(own_ref, near_ref, crossed_ref, out_ref):
    total = own_ref[...] + near_ref[0].astype(F32) + crossed_ref[...].astype(F32)
    out_ref[...] = total.astype(BF16)


def norm_kernel(place_ref, gain_ref, pair_ref, second_ref, out, held):
    width = pair_ref.shape[2]
    for s, shard in enumerate(by_distance(pair_ref, second_ref)):
        first = pl.multiple_of((place_ref[0] ^ s) * width, HD)
        held[:, pl.ds(first, width)] = shard[...].astype(F32)
    values = held[...]
    center = values - jnp.mean(values, axis=1, keepdims=True)
    spread = jnp.mean(center * center, axis=1, keepdims=True)
    out[...] = (center * lax.rsqrt(spread + 1e-05) * gain_ref[...]).astype(BF16)


def lift_kernel(chunks, place_ref, *refs):
    count = 2 * chunks
    shards, (up_hbm, down_hbm) = refs[:count], refs[count : count + 2]
    active_ref, far_ref, held, up, down, sems = refs[count + 2 :]
    hidden = active_ref.shape[1]
    share = far_ref.shape[2]
    rows = shards[0].shape[1]
    tile = up.shape[0] // (sems.shape[0] - 2)
    tiles = hidden // tile

    def fetch(k):
        part = pl.ds(k * tile, tile)
        return pltpu.make_async_copy(up_hbm.at[part], up.at[part], sems.at[k])

    def fetch_down(k):
        first = pl.multiple_of((place_ref[1] ^ (2 * k + 1)) * share, HD)
        return pltpu.make_async_copy(
            down_hbm.at[:, pl.ds(first, share)], down.at[k], sems.at[tiles + k]
        )

    for k in range(tiles):
        fetch(k).start()
    for k in range(2):
        fetch_down(k).start()
    for c in range(chunks):
        for t, shard in enumerate(by_distance(*shards[2 * c : 2 * c + 2])):
            first = pl.multiple_of(((place_ref[1] ^ t) * chunks + c) * rows, rows)
            held[pl.ds(first, rows), :] = shard[...]
    for k in range(tiles):
        fetch(k).wait()
        raised = lax.dot_general(
            held[...], up[k * tile : (k + 1) * tile, :], (((1,), (1,)), ((), ())),
            preferred_element_type=F32,
        )
        active_ref[:, k * tile : (k + 1) * tile] = (raised / (1.0 + jnp.exp(-raised))).astype(BF16)
    for k in range(2):
        fetch_down(k).wait()
        far_ref[k] = jnp.dot(active_ref[...], down[k], preferred_element_type=F32).astype(BF16)


def lower_kernel(place_ref, active_ref, down_hbm, cross_ref, own_ref, down, sems):
    share = own_ref.shape[1]

    def fetch(k):
        first = pl.multiple_of((place_ref[1] ^ (2 - 2 * k)) * share, HD)
        return pltpu.make_async_copy(down_hbm.at[:, pl.ds(first, share)], down.at[k], sems.at[k])

    for k in range(2):
        fetch(k).start()
    for k, out_ref in enumerate((cross_ref, own_ref)):
        fetch(k).wait()
        out_ref[...] = jnp.dot(active_ref[...], down[k], preferred_element_type=F32)


def turn_kernel(place_ref, cross_ref, near_ref, far_ref, close_ref):
    half = far_ref.shape[0]
    mine = place_ref[0] // 2
    for out_ref, side in ((far_ref, 1 - mine), (close_ref, mine)):
        here = pl.ds(pl.multiple_of(side * half, half), half)
        out_ref[...] = (cross_ref[here, :] + near_ref[1, here, :].astype(F32)).astype(BF16)


def split_kernel(side, place_ref, own_ref, near_ref, crossed_ref, *outs):
    rows = outs[0].shape[0]
    for s, out_ref in enumerate(outs):
        z = place_ref[0] ^ (2 * side + s)
        here = pl.ds(pl.multiple_of(z * rows, rows), rows)
        there = pl.ds(pl.multiple_of(z % 2 * rows, rows), rows)
        total = own_ref[here, :] + near_ref[0, here, :].astype(F32)
        out_ref[...] = (total + crossed_ref[there, :].astype(F32)).astype(BF16)


def mix_kernel(parts, place_ref, ids_ref, gates_ref, *refs):
    terms, out = refs[:parts], refs[parts]
    rows = out.shape[0]
    ids = ids_ref[pl.ds(pl.multiple_of(place_ref[0] * rows, rows), rows), :]
    total = jnp.zeros(out.shape, F32)
    for s in range(parts):
        gate = jnp.sum(
            jnp.where(ids == (place_ref[0] ^ s), gates_ref[...], 0.0), axis=1, keepdims=True
        )
        total = total + gate * terms[s][...].astype(F32)
    out[...] = total.astype(BF16)


def trade(array, axis, turn):
    count = lax.axis_size(axis)
    return lax.ppermute(array, axis, [(k, k ^ turn) for k in range(count)])


def every_row_body(
    queries, new_kv, kv_cache, lengths, out_proj, norm_gain, expert_ids, gate_weights, w_up, w_down
):
    gx_count = lax.axis_size("gx")
    ta_count = lax.axis_size("ta")
    chunks = 2
    block_rows = queries.shape[0]
    rows = block_rows // chunks
    width = out_proj.shape[1]
    model = norm_gain.shape[0]
    hidden_share = w_up.shape[2]
    share = model // ta_count
    all_rows = block_rows * gx_count
    place = jnp.stack([lax.axis_index("gx"), lax.axis_index("ta")]).astype(jnp.int32)
    shape = jax.ShapeDtypeStruct
    gain = norm_gain.reshape(1, model)
    attended = []
    for c in range(chunks):
        after = attended[-1] if attended else lengths
        attended.append(attend(queries, new_kv, kv_cache, lengths, c * rows, rows, after))
    first = [trade(part, "gx", 2) for part in attended]
    pairs = gather_pair(attended, first, attended[-1])
    second = [trade(pair, "gx", 1) for pair in pairs]
    pieces, nears, crossings, hidden, normed = [], [], [], [], []
    for c in range(chunks):
        pieces.append(
            local_call(
                project_kernel,
                [shape((rows, width), F32), shape((rows, width), F32), shape((2, rows, width), BF16)],
                [SMEM] + [VMEM] * 3,
                [pltpu.VMEM((ta_count, rows, width), F32)],
                name="project",
                after=pieces[-1][0] if pieces else None,
            )(place, pairs[c], second[c], out_proj)
        )
        nears.append(trade(pieces[c][2], "ta", 1))
    for c in range(chunks):
        crossings.append(
            local_call(
                cross_kernel,
                shape((rows, width), BF16),
                [VMEM] * 2,
                name="cross",
                after=crossings[-1] if crossings else None,
            )(pieces[c][1], nears[c])
        )
    crossed = [trade(part, "ta", 2) for part in crossings]
    for c in range(chunks):
        hidden.append(
            local_call(
                close_kernel,
                shape((rows, width), BF16),
                [VMEM] * 3,
                name="close",
                after=hidden[-1] if hidden else None,
            )(pieces[c][0], nears[c], crossed[c])
        )
    first = [trade(part, "gx", 2) for part in hidden]
    pairs = gather_pair(hidden, first, None)
    second = [trade(pair, "gx", 1) for pair in pairs]
    blocks, after = [], None
    for c in range(chunks):
        normed = local_call(
            norm_kernel,
            shape((rows, model), BF16),
            [SMEM] + [VMEM] * 3,
            [pltpu.VMEM((rows, model), F32)],
            name="norm",
            after=after,
        )(place, gain, pairs[c], second[c])
        (pair,) = gather_pair([normed], [trade(normed, "ta", 2)], None)
        blocks += [pair, trade(pair, "ta", 1)]
        after = pair
    tile = math.gcd(hidden_share, 7 * 64)
    down = w_down[0]
    active, far = local_call(
        functools.partial(lift_kernel, chunks),
        [shape((all_rows, hidden_share), BF16), shape((2, all_rows, share), BF16)],
        [SMEM] + [VMEM] * (2 * chunks) + [ANYWHERE] * 2,
        [
            pltpu.VMEM((all_rows, model), BF16),
            pltpu.VMEM((hidden_share, model), BF16),
            pltpu.VMEM((2, hidden_share, share), BF16),
            pltpu.SemaphoreType.DMA((hidden_share // tile + 2,)),
        ],
        vmem=48,
        name="lift",
    )(place, *blocks, jnp.swapaxes(w_up[0], 0, 1), down)
    near = trade(far, "ta", 1)
    cross, own = local_call(
        lower_kernel,
        [shape((all_rows, share), F32)] * 2,
        [SMEM, VMEM, ANYWHERE],
        [pltpu.VMEM((2, hidden_share, share), BF16), pltpu.SemaphoreType.DMA((2,))],
        vmem=48,
        name="lower",
    )(place, active, down)
    half = all_rows // 2
    far_side, close_side = local_call(
        turn_kernel,
        [shape((half, share), BF16)] * 2,
        [SMEM] + [VMEM] * 2,
        name="turn",
    )(place, cross, near)
    terms = {}
    for side, crossing in ((1, far_side), (0, close_side)):
        crossed = trade(crossing, "ta", 2)
        terms[2 * side], terms[2 * side + 1] = local_call(
            functools.partial(split_kernel, side),
            [shape((block_rows, share), BF16)] * 2,
            [SMEM] + [VMEM] * 3,
            name="split",
        )(place, own, near, crossed)
    terms = [terms[s] if s == 0 else trade(terms[s], "gx", s) for s in range(gx_count)]
    return local_call(
        functools.partial(mix_kernel, gx_count),
        shape((block_rows, share), BF16),
        [SMEM] + [VMEM] * (gx_count + 2),
        name="mix",
    )(place, expert_ids, gate_weights, *terms)


def route_tables(expert_ids, expert_count, block_rows, capacity):
    blocks = expert_ids.shape[0] // block_rows
    expert_range = jnp.arange(expert_count, dtype=jnp.int32)
    matches = (expert_ids[:, :, None] == expert_range[None, None, :]).astype(jnp.int32)
    routed = jnp.sum(matches, axis=1).reshape(blocks, block_rows, expert_count)
    position = jnp.cumsum(routed, axis=1) - routed
    slot_range = jnp.arange(capacity, dtype=jnp.int32)
    slot_hits = routed[:, :, :, None] * (
        position[:, :, :, None] == slot_range[None, None, None, :]
    ).astype(jnp.int32)
    row_range = jnp.arange(block_rows, dtype=jnp.int32)
    block_start = (jnp.arange(blocks, dtype=jnp.int32) * block_rows)[:, None, None]
    source_row = jnp.sum(slot_hits * row_range[None, :, None, None], axis=1) + block_start
    filled = jnp.sum(slot_hits, axis=1)
    source_row = jnp.transpose(source_row, (1, 0, 2)).reshape(expert_count, blocks * capacity)
    filled = jnp.transpose(filled, (1, 0, 2)).reshape(expert_count, blocks * capacity)
    pick_slot = jnp.sum(matches * position.reshape(blocks * block_rows, 1, expert_count), axis=2)
    return (source_row, filled, pick_slot)


def layer_norm(hidden, norm_gain):
    values = hidden.astype(jnp.float32)
    center = values - jnp.mean(values, axis=1, keepdims=True)
    spread = jnp.mean(center * center, axis=1, keepdims=True)
    return (center * lax.rsqrt(spread + 1e-05) * norm_gain).astype(jnp.bfloat16)


def body(
    queries, new_kv, kv_cache, lengths, out_proj, norm_gain, expert_ids, gate_weights, w_up, w_down
):
    gx_count = lax.axis_size("gx")
    ta_count = lax.axis_size("ta")
    block_rows = queries.shape[0]
    top_count = expert_ids.shape[1]
    capacity = min(block_rows, 2 * block_rows * top_count // gx_count)
    slot_count = gx_count * capacity
    model_width = norm_gain.shape[0]
    width_share = model_width // ta_count
    if gx_count == top_count and ta_count == gx_count == 4:
        return every_row_body(
            queries, new_kv, kv_cache, lengths, out_proj, norm_gain, expert_ids, gate_weights,
            w_up, w_down,
        )
    attended = attend(queries, new_kv, kv_cache, lengths, 0, block_rows, lengths)
    projected = jnp.dot(
        lax.all_gather(attended, "gx", axis=0, tiled=True),
        out_proj,
        preferred_element_type=jnp.float32,
    ).astype(jnp.bfloat16)
    source_row, filled, pick_slot = route_tables(expert_ids, gx_count, block_rows, capacity)
    live_slots = (filled > 0)[:, :, None]
    widened = lax.optimization_barrier(projected).astype(jnp.float32)
    hidden_share = lax.psum_scatter(
        widened.astype(jnp.bfloat16), "ta", scatter_dimension=1, tiled=True
    )
    outgoing = jnp.where(live_slots, hidden_share[source_row], jnp.zeros((), jnp.bfloat16))[
        :, :, None, :
    ]
    arrived = lax.all_to_all(outgoing, "gx", split_axis=0, concat_axis=2, tiled=True)
    gathered = lax.all_gather(arrived, "ta", axis=3, tiled=True)
    hidden = gathered.reshape(slot_count, model_width)
    normed = layer_norm(hidden, norm_gain)
    raised = jnp.dot(normed, w_up[0], preferred_element_type=jnp.float32)
    active = jax.nn.silu(raised).astype(jnp.bfloat16)
    terms = jnp.dot(active, w_down[0], preferred_element_type=jnp.float32)
    mine = lax.psum_scatter(terms, "ta", scatter_dimension=1, tiled=True)
    result = mine.astype(jnp.bfloat16).reshape(gx_count, capacity, width_share)
    returned = lax.all_to_all(result, "gx", split_axis=0, concat_axis=0, tiled=True)
    first_row = lax.axis_index("gx") * block_rows
    local_ids = lax.dynamic_slice_in_dim(expert_ids, first_row, block_rows, 0)
    local_slot = lax.dynamic_slice_in_dim(pick_slot, first_row, block_rows, 0)
    flat_rows = returned.reshape(gx_count * capacity, width_share)
    picked = flat_rows[local_ids * capacity + local_slot]
    return jnp.sum(picked.astype(jnp.float32) * gate_weights[:, :, None], axis=1).astype(
        jnp.bfloat16
    )


def solution(mesh):
    return jax.shard_map(
        body,
        mesh=mesh,
        in_specs=(
            P(("groups", "gx"), "ta"),
            P(None, ("groups", "gx"), "ta"),
            P(None, ("groups", "gx"), None, "ta"),
            P(("groups", "gx")),
            P("ta", "gx"),
            P(),
            P("groups", None),
            P(("groups", "gx"), None),
            P("gx", None, "ta"),
            P("gx", "ta", None),
        ),
        out_specs=P(("groups", "gx"), "ta"),
        check_vma=False,
    )
```

time: 105 us -> 96.1 us (0.915)
  waiting for transfers between devices: 56.4 us -> 34.7 us
  starting transfers between devices: 22.2 us -> 30.6 us
  Pallas kernels: 21 us -> 27.5 us
  local copies, waits for them, and re-layouts: 4.51 us -> 2.67 us
    ppermute x17 -> x22, waiting for transfers between devices: 56.4 us -> 34.7 us  [trade(): return lax.ppermute(array, axis, [(k, k ^ turn) for k in range(count)])]
    ppermute x17 -> x22, starting transfers between devices: 22.2 us -> 30.6 us  [trade(): return lax.ppermute(array, axis, [(k, k ^ turn) for k in range(count)])]
    pallas_call x7 -> x20, Pallas kernels: 13.1 us -> 18.8 us  [the longest x1 7.62 us: every_row_body(): local_call(functools.partial(lift_kernel, chunks), [shape((all_rows, hidd...]
    unnamed x14 -> x16, local copies, waits for them, and re-layouts: 4.51 us -> 2.67 us
    pallas_call x1 -> x2, Pallas kernels: 7.98 us -> 8.71 us  [attend(): pl.pallas_call(functools.partial(attend_kernel, kv_heads, heads // kv_hea...]
  transfers between devices with their start and end apart: 17 -> 22, of which waited for: 12 -> 13; matrix products, arithmetic and copies ran while one was open for 0% -> 0% of each run, Pallas kernels for 0% -> 12%
where the time goes in v2:
time: 96.1 us; the launch traced here: 95.9 us
  waiting for transfers between devices  34.7 us (36%)
  starting transfers between devices  30.6 us (32%)
  Pallas kernels  27.5 us (29%)
  local copies, waits for them, and re-layouts  2.67 us (3%)
    ppermute x22, waiting for transfers between devices, trade(): return lax.ppermute(array, axis, [(k, k ^ turn) for k in range(count)])  34.7 us
    ppermute x22, starting transfers between devices, trade(): return lax.ppermute(array, axis, [(k, k ^ turn) for k in range(count)])  30.6 us
    pallas_call x2, Pallas kernels, attend(): pl.pallas_call(functools.partial(attend_kernel, kv_heads, heads // kv_hea...  8.71 us
    pallas_call x1, Pallas kernels, every_row_body(): local_call(functools.partial(lift_kernel, chunks), [shape((all_rows, hidd...  7.62 us
    pallas_call x1, Pallas kernels, every_row_body(): local_call(lower_kernel, [shape((all_rows, share), F32)] * 2, [SMEM, VMEM...  4.13 us
    unnamed x16, local copies, waits for them, and re-layouts  2.67 us
    pallas_call x7, Pallas kernels, local_call(): return call if after is None else lambda *args: call(*args, after)  1.94 us
  transfers between devices with their start and end apart: 22, of which 13 were waited for; matrix products, arithmetic and copies ran while one was open for 0% of the time, Pallas kernels for 12%

profile of v2, /device:TPU:0, one launch (start us, length us, event | category | flops | bytes accessed | tf_op | source)
XLA Modules:
  0.0 95.9 jit_solution(940534610394489431)
XLA Ops:
  2.4 4.4 %attend.2.after_ref.refs_0_ = bf16[32,1536]{1,0:T(8,128)(2,1)S(1)} custom-call(s32[64]{0:T(128)S(1)} %copy-done.4, bf16[64,1536]{1,0:T(8,128)(2,1)S(1)} %copy-done.1, bf16[2,64,256]{2,1,0:T(8,128)(2,1)S(1)} %copy-done.2, bf16[2,64,192,256]{3,2,1,0:T(8,128)(2,1)} %cache_ref.3, s32[64]{0:T(128)S(1)} %copy-done.4), custom_call_target="tpu_custom_call" | custom-call | flops 1024 | bytes 1024 | tf_op jit(solution)/shard_map/attend/pallas_call | solution.py:119
  6.8 4.1 %collective-permute-start = (bf16[32,1536]{1,0:T(8,128)(2,1)S(1)}, bf16[32,1536]{1,0:T(8,128)(2,1)S(1)}, u32[]{:S(2)}, u32[]{:S(2)}) collective-permute-start(bf16[32,1536]{1,0:T(8,128)(2,1)S(1)} %attend.2.after_ref.refs_0_), channel_id=1, source_target_pairs={{0,8},{4,12},{8,0},{12,4},{1,9},{5,13},{9,1},{13,5},{2,10},{6,14},... | collective-permute-start | bytes 294920 | tf_op jit(solution)/shard_map/ppermute | solution.py:282
  10.9 4.4 %attend.3.refs_2_.refs_0_ = bf16[32,1536]{1,0:T(8,128)(2,1)S(1)} custom-call(s32[64]{0:T(128)S(1)} %copy-done.4, bf16[64,1536]{1,0:T(8,128)(2,1)S(1)} %copy-done.1, bf16[2,64,256]{2,1,0:T(8,128)(2,1)S(1)} %copy-done.2, bf16[2,64,192,256]{3,2,1,0:T(8,128)(2,1)} %cache_ref.3, bf16[32,1536]{1,0:T(8,128)(2,1)S(1)} %attend.2.after_ref.refs_0_), custom_call_target="tpu_custom_call" | custom-call | flops 1024 | bytes 1024 | tf_op jit(solution)/shard_map/attend/pallas_call | solution.py:119
  16.9 3.0 %collective-permute-start.8 = (bf16[32,1536]{1,0:T(8,128)(2,1)S(1)}, bf16[32,1536]{1,0:T(8,128)(2,1)S(1)}, u32[]{:S(2)}, u32[]{:S(2)}) collective-permute-start(bf16[32,1536]{1,0:T(8,128)(2,1)S(1)} %attend.3.refs_2_.refs_0_), channel_id=1, source_target_pairs={{0,8},{4,12},{8,0},{12,4},{1,9},{5,13},{9,1},{13,5},{2,10},{6,14},... | collective-permute-start | bytes 294920 | tf_op jit(solution)/shard_map/ppermute | solution.py:282
  20.1 3.0 %collective-permute-done.8.refs_1_ = bf16[32,1536]{1,0:T(8,128)(2,1)S(1)} collective-permute-done((bf16[32,1536]{1,0:T(8,128)(2,1)S(1)}, bf16[32,1536]{1,0:T(8,128)(2,1)S(1)}, u32[]{:S(2)}, u32[]{:S(2)}) %collective-permute-start.8) | collective-permute-done | bytes 98336 | tf_op jit(solution)/shard_map/ppermute | solution.py:282
  25.2 3.2 %collective-permute-start.9 = (bf16[2,32,1536]{2,1,0:T(8,128)(2,1)S(1)}, bf16[2,32,1536]{2,1,0:T(8,128)(2,1)S(1)}, u32[]{:S(2)}, u32[]{:S(2)}) collective-permute-start(bf16[2,32,1536]{2,1,0:T(8,128)(2,1)S(1)} %pair.9.refs_1_), channel_id=1, source_target_pairs={{0,4},{4,0},{8,12},{12,8},{1,5},{5,1},{9,13},{13,9},{2,6},{6,2},{1... | collective-permute-start | bytes 589832 | tf_op jit(solution)/shard_map/ppermute | solution.py:282
  28.4 1.6 %collective-permute-start.3 = (bf16[32,768]{1,0:T(8,128)(2,1)S(1)}, bf16[32,768]{1,0:T(8,128)(2,1)S(1)}, u32[]{:S(2)}, u32[]{:S(2)}) collective-permute-start(bf16[32,768]{1,0:T(8,128)(2,1)S(1)} %cross.2.refs_2_), channel_id=1, source_target_pairs={{0,2},{1,3},{2,0},{3,1},{4,6},{5,7},{6,4},{7,5},{8,10},{9,11},{10,... | collective-permute-start | bytes 147464 | tf_op jit(solution)/shard_map/ppermute | solution.py:282
  30.0 2.6 %collective-permute-done.3.crossed_ref = bf16[32,768]{1,0:T(8,128)(2,1)S(1)} collective-permute-done((bf16[32,768]{1,0:T(8,128)(2,1)S(1)}, bf16[32,768]{1,0:T(8,128)(2,1)S(1)}, u32[]{:S(2)}, u32[]{:S(2)}) %collective-permute-start.3) | collective-permute-done | bytes 49184 | tf_op jit(solution)/shard_map/ppermute | solution.py:282
  32.6 1.8 %collective-permute-start.4 = (bf16[32,768]{1,0:T(8,128)(2,1)S(1)}, bf16[32,768]{1,0:T(8,128)(2,1)S(1)}, u32[]{:S(2)}, u32[]{:S(2)}) collective-permute-start(bf16[32,768]{1,0:T(8,128)(2,1)S(1)} %close.2.own_ref.refs_3_), channel_id=1, source_target_pairs={{0,8},{4,12},{8,0},{12,4},{1,9},{5,13},{9,1},{13,5},{2,10},{6,14},... | collective-permute-start | bytes 147464 | tf_op jit(solution)/shard_map/ppermute | solution.py:282
  35.5 2.2 %collective-permute-done.4.other_ref = bf16[32,768]{1,0:T(8,128)(2,1)S(1)} collective-permute-done((bf16[32,768]{1,0:T(8,128)(2,1)S(1)}, bf16[32,768]{1,0:T(8,128)(2,1)S(1)}, u32[]{:S(2)}, u32[]{:S(2)}) %collective-permute-start.4) | collective-permute-done | bytes 49184 | tf_op jit(solution)/shard_map/ppermute | solution.py:282
  39.0 1.6 %collective-permute-start.11 = (bf16[32,768]{1,0:T(8,128)(2,1)S(1)}, bf16[32,768]{1,0:T(8,128)(2,1)S(1)}, u32[]{:S(2)}, u32[]{:S(2)}) collective-permute-start(bf16[32,768]{1,0:T(8,128)(2,1)S(1)} %cross.3), channel_id=1, source_target_pairs={{0,2},{1,3},{2,0},{3,1},{4,6},{5,7},{6,4},{7,5},{8,10},{9,11},{10,... | collective-permute-start | bytes 147464 | tf_op jit(solution)/shard_map/ppermute | solution.py:282
  40.5 1.8 %collective-permute-done.5.second_ref = bf16[2,32,768]{2,1,0:T(8,128)(2,1)S(1)} collective-permute-done((bf16[2,32,768]{2,1,0:T(8,128)(2,1)S(1)}, bf16[2,32,768]{2,1,0:T(8,128)(2,1)S(1)}, u32[]{:S(2)}, u32[]{:S(2)}) %collective-permute-start.5) | collective-permute-done | bytes 98336 | tf_op jit(solution)/shard_map/ppermute | solution.py:282
  44.8 1.9 %collective-permute-start.12 = (bf16[32,768]{1,0:T(8,128)(2,1)S(1)}, bf16[32,768]{1,0:T(8,128)(2,1)S(1)}, u32[]{:S(2)}, u32[]{:S(2)}) collective-permute-start(bf16[32,768]{1,0:T(8,128)(2,1)S(1)} %close.3.refs_0_), channel_id=1, source_target_pairs={{0,8},{4,12},{8,0},{12,4},{1,9},{5,13},{9,1},{13,5},{2,10},{6,14},... | collective-permute-start | bytes 147464 | tf_op jit(solution)/shard_map/ppermute | solution.py:282
  46.7 3.2 %collective-permute-done.12.refs_1_ = bf16[32,768]{1,0:T(8,128)(2,1)S(1)} collective-permute-done((bf16[32,768]{1,0:T(8,128)(2,1)S(1)}, bf16[32,768]{1,0:T(8,128)(2,1)S(1)}, u32[]{:S(2)}, u32[]{:S(2)}) %collective-permute-start.12) | collective-permute-done | bytes 49184 | tf_op jit(solution)/shard_map/ppermute | solution.py:282
  49.9 1.7 %collective-permute-start.13 = (bf16[2,32,768]{2,1,0:T(8,128)(2,1)S(1)}, bf16[2,32,768]{2,1,0:T(8,128)(2,1)S(1)}, u32[]{:S(2)}, u32[]{:S(2)}) collective-permute-start(bf16[2,32,768]{2,1,0:T(8,128)(2,1)S(1)} %pair.10.refs_2_), channel_id=1, source_target_pairs={{0,4},{4,0},{8,12},{12,8},{1,5},{5,1},{9,13},{13,9},{2,6},{6,2},{1... | collective-permute-start | bytes 294920 | tf_op jit(solution)/shard_map/ppermute | solution.py:282
  51.6 2.9 %collective-permute-done.13.refs_3_ = bf16[2,32,768]{2,1,0:T(8,128)(2,1)S(1)} collective-permute-done((bf16[2,32,768]{2,1,0:T(8,128)(2,1)S(1)}, bf16[2,32,768]{2,1,0:T(8,128)(2,1)S(1)}, u32[]{:S(2)}, u32[]{:S(2)}) %collective-permute-start.13) | collective-permute-done | bytes 98336 | tf_op jit(solution)/shard_map/ppermute | solution.py:282
  56.0 5.1 %collective-permute-done.14.other_ref = bf16[32,3072]{1,0:T(8,128)(2,1)S(1)} collective-permute-done((bf16[32,3072]{1,0:T(8,128)(2,1)S(1)}, bf16[32,3072]{1,0:T(8,128)(2,1)S(1)}, u32[]{:S(2)}, u32[]{:S(2)}) %collective-permute-start.14) | collective-permute-done | bytes 196640 | tf_op jit(solution)/shard_map/ppermute | solution.py:282
  61.2 1.7 %collective-permute-done.15.refs_3_ = bf16[2,32,3072]{2,1,0:T(8,128)(2,1)S(1)} collective-permute-done((bf16[2,32,3072]{2,1,0:T(8,128)(2,1)S(1)}, bf16[2,32,3072]{2,1,0:T(8,128)(2,1)S(1)}, u32[]{:S(2)}, u32[]{:S(2)}) %collective-permute-start.15) | collective-permute-done | bytes 393248 | tf_op jit(solution)/shard_map/ppermute | solution.py:282
  62.9 7.6 %lift.1 = (bf16[256,1344]{1,0:T(8,128)(2,1)S(1)}, bf16[2,256,768]{2,1,0:T(8,128)(2,1)S(1)}) custom-call(s32[2]{0:T(128)S(1)} %pad_add_fusion.place_ref.refs_0_, bf16[2,32,3072]{2,1,0:T(8,128)(2,1)S(1)} %pair.8.refs_4_.refs_0_, bf16[2,32,3072]{2,1,0:T(8,128)(2,1)S(1)} %collective-permute-done.7.refs_1_, bf16[2,32,3072]{2,1,0:T(8,128)(2,1)S(1)} %pair.11.refs_2_, ...), custom_call_target="tpu_custom_call" | custom-call | flops 1024 | bytes 1024 | tf_op jit(solution)/shard_map/lift/pallas_call | solution.py:360
  70.8 4.1 %lower.1 = (f32[256,768]{1,0:T(8,128)S(1)}, f32[256,768]{1,0:T(8,128)S(1)}) custom-call(s32[2]{0:T(128)S(1)} %pad_add_fusion.place_ref.refs_0_, bf16[256,1344]{1,0:T(8,128)(2,1)S(1)} %get-tuple-element.27.active_ref, bf16[1344,3072]{1,0:T(8,128)(2,1)} %bitcast.10), custom_call_target="tpu_custom_call" | custom-call | flops 1024 | bytes 1024 | tf_op jit(solution)/shard_map/lower/pallas_call | solution.py:374
  77.7 5.7 %collective-permute-done.19.crossed_ref = bf16[128,768]{1,0:T(8,128)(2,1)S(1)} collective-permute-done((bf16[128,768]{1,0:T(8,128)(2,1)S(1)}, bf16[128,768]{1,0:T(8,128)(2,1)S(1)}, u32[]{:S(2)}, u32[]{:S(2)}) %collective-permute-start.19) | collective-permute-done | bytes 196640 | tf_op jit(solution)/shard_map/ppermute | solution.py:282
  84.0 2.4 %collective-permute-start.20 = (bf16[64,768]{1,0:T(8,128)(2,1)S(1)}, bf16[64,768]{1,0:T(8,128)(2,1)S(1)}, u32[]{:S(2)}, u32[]{:S(2)}) collective-permute-start(bf16[64,768]{1,0:T(8,128)(2,1)S(1)} %get-tuple-element.35), channel_id=1, source_target_pairs={{0,8},{4,12},{8,0},{12,4},{1,9},{5,13},{9,1},{13,5},{2,10},{6,14},... | collective-permute-start | bytes 294920 | tf_op jit(solution)/shard_map/ppermute | solution.py:282
  86.3 1.7 %collective-permute-start.21 = (bf16[64,768]{1,0:T(8,128)(2,1)S(1)}, bf16[64,768]{1,0:T(8,128)(2,1)S(1)}, u32[]{:S(2)}, u32[]{:S(2)}) collective-permute-start(bf16[64,768]{1,0:T(8,128)(2,1)S(1)} %get-tuple-element.36), channel_id=1, source_target_pairs={{0,12},{4,8},{8,4},{12,0},{1,13},{5,9},{9,5},{13,1},{2,14},{6,10},... | collective-permute-start | bytes 294920 | tf_op jit(solution)/shard_map/ppermute | solution.py:282
  89.6 4.3 %collective-permute-done.20.refs_2_ = bf16[64,768]{1,0:T(8,128)(2,1)S(1)} collective-permute-done((bf16[64,768]{1,0:T(8,128)(2,1)S(1)}, bf16[64,768]{1,0:T(8,128)(2,1)S(1)}, u32[]{:S(2)}, u32[]{:S(2)}) %collective-permute-start.20) | collective-permute-done | bytes 98336 | tf_op jit(solution)/shard_map/ppermute | solution.py:282
  (59 shorter events, 19.8 us)
Async XLA Ops:
  6.8 35.6 %copy-start.3 = (f32[3072]{0:T(1024)S(1)}, f32[3072]{0:T(1024)}, u32[]{:S(2)}) copy-start(f32[3072]{0:T(1024)} %param.15) | copy-start | bytes 36868
  6.8 9.0 %collective-permute-start = (bf16[32,1536]{1,0:T(8,128)(2,1)S(1)}, bf16[32,1536]{1,0:T(8,128)(2,1)S(1)}, u32[]{:S(2)}, u32[]{:S(2)}) collective-permute-start(bf16[32,1536]{1,0:T(8,128)(2,1)S(1)} %attend.2.after_ref.refs_0_), channel_id=1, source_target_pairs={{0,8},{4,12},{8,0},{12,4},{1,9},{5,13},{9,1},{13,5},{2,10},{6,14},... | collective-permute-start | bytes 294920 | tf_op jit(solution)/shard_map/ppermute | solution.py:282
  15.8 8.3 %collective-permute-start.1 = (bf16[2,32,1536]{2,1,0:T(8,128)(2,1)S(1)}, bf16[2,32,1536]{2,1,0:T(8,128)(2,1)S(1)}, u32[]{:S(2)}, u32[]{:S(2)}) collective-permute-start(bf16[2,32,1536]{2,1,0:T(8,128)(2,1)S(1)} %pair.6.pair_ref.refs_2_), channel_id=1, source_target_pairs={{0,4},{4,0},{8,12},{12,8},{1,5},{5,1},{9,13},{13,9},{2,6},{6,2},{1... | collective-permute-start | bytes 589832 | tf_op jit(solution)/shard_map/ppermute | solution.py:282
  16.9 6.1 %collective-permute-start.8 = (bf16[32,1536]{1,0:T(8,128)(2,1)S(1)}, bf16[32,1536]{1,0:T(8,128)(2,1)S(1)}, u32[]{:S(2)}, u32[]{:S(2)}) collective-permute-start(bf16[32,1536]{1,0:T(8,128)(2,1)S(1)} %attend.3.refs_2_.refs_0_), channel_id=1, source_target_pairs={{0,8},{4,12},{8,0},{12,4},{1,9},{5,13},{9,1},{13,5},{2,10},{6,14},... | collective-permute-start | bytes 294920 | tf_op jit(solution)/shard_map/ppermute | solution.py:282
  25.1 3.3 %collective-permute-start.2 = (bf16[2,32,768]{2,1,0:T(8,128)(2,1)S(1)}, bf16[2,32,768]{2,1,0:T(8,128)(2,1)S(1)}, u32[]{:S(2)}, u32[]{:S(2)}) collective-permute-start(bf16[2,32,768]{2,1,0:T(8,128)(2,1)S(1)} %get-tuple-element.22), channel_id=1, source_target_pairs={{0,1},{1,0},{2,3},{3,2},{4,5},{5,4},{6,7},{7,6},{8,9},{9,8},{10,11... | collective-permute-start | bytes 294920 | tf_op jit(solution)/shard_map/ppermute | solution.py:282
  25.2 9.2 %collective-permute-start.9 = (bf16[2,32,1536]{2,1,0:T(8,128)(2,1)S(1)}, bf16[2,32,1536]{2,1,0:T(8,128)(2,1)S(1)}, u32[]{:S(2)}, u32[]{:S(2)}) collective-permute-start(bf16[2,32,1536]{2,1,0:T(8,128)(2,1)S(1)} %pair.9.refs_1_), channel_id=1, source_target_pairs={{0,4},{4,0},{8,12},{12,8},{1,5},{5,1},{9,13},{13,9},{2,6},{6,2},{1... | collective-permute-start | bytes 589832 | tf_op jit(solution)/shard_map/ppermute | solution.py:282
  28.4 4.2 %collective-permute-start.3 = (bf16[32,768]{1,0:T(8,128)(2,1)S(1)}, bf16[32,768]{1,0:T(8,128)(2,1)S(1)}, u32[]{:S(2)}, u32[]{:S(2)}) collective-permute-start(bf16[32,768]{1,0:T(8,128)(2,1)S(1)} %cross.2.refs_2_), channel_id=1, source_target_pairs={{0,2},{1,3},{2,0},{3,1},{4,6},{5,7},{6,4},{7,5},{8,10},{9,11},{10,... | collective-permute-start | bytes 147464 | tf_op jit(solution)/shard_map/ppermute | solution.py:282
  32.6 5.1 %collective-permute-start.4 = (bf16[32,768]{1,0:T(8,128)(2,1)S(1)}, bf16[32,768]{1,0:T(8,128)(2,1)S(1)}, u32[]{:S(2)}, u32[]{:S(2)}) collective-permute-start(bf16[32,768]{1,0:T(8,128)(2,1)S(1)} %close.2.own_ref.refs_3_), channel_id=1, source_target_pairs={{0,8},{4,12},{8,0},{12,4},{1,9},{5,13},{9,1},{13,5},{2,10},{6,14},... | collective-permute-start | bytes 147464 | tf_op jit(solution)/shard_map/ppermute | solution.py:282
  35.4 3.5 %collective-permute-start.10 = (bf16[2,32,768]{2,1,0:T(8,128)(2,1)S(1)}, bf16[2,32,768]{2,1,0:T(8,128)(2,1)S(1)}, u32[]{:S(2)}, u32[]{:S(2)}) collective-permute-start(bf16[2,32,768]{2,1,0:T(8,128)(2,1)S(1)} %get-tuple-element.25), channel_id=1, source_target_pairs={{0,1},{1,0},{2,3},{3,2},{4,5},{5,4},{6,7},{7,6},{8,9},{9,8},{10,11... | collective-permute-start | bytes 294920 | tf_op jit(solution)/shard_map/ppermute | solution.py:282
  37.7 4.7 %collective-permute-start.5 = (bf16[2,32,768]{2,1,0:T(8,128)(2,1)S(1)}, bf16[2,32,768]{2,1,0:T(8,128)(2,1)S(1)}, u32[]{:S(2)}, u32[]{:S(2)}) collective-permute-start(bf16[2,32,768]{2,1,0:T(8,128)(2,1)S(1)} %pair.7.pair_ref.refs_2_), channel_id=1, source_target_pairs={{0,4},{4,0},{8,12},{12,8},{1,5},{5,1},{9,13},{13,9},{2,6},{6,2},{1... | collective-permute-start | bytes 294920 | tf_op jit(solution)/shard_map/ppermute | solution.py:282
  39.0 5.8 %collective-permute-start.11 = (bf16[32,768]{1,0:T(8,128)(2,1)S(1)}, bf16[32,768]{1,0:T(8,128)(2,1)S(1)}, u32[]{:S(2)}, u32[]{:S(2)}) collective-permute-start(bf16[32,768]{1,0:T(8,128)(2,1)S(1)} %cross.3), channel_id=1, source_target_pairs={{0,2},{1,3},{2,0},{3,1},{4,6},{5,7},{6,4},{7,5},{8,10},{9,11},{10,... | collective-permute-start | bytes 147464 | tf_op jit(solution)/shard_map/ppermute | solution.py:282
  43.2 8.4 %collective-permute-start.6 = (bf16[32,3072]{1,0:T(8,128)(2,1)S(1)}, bf16[32,3072]{1,0:T(8,128)(2,1)S(1)}, u32[]{:S(2)}, u32[]{:S(2)}) collective-permute-start(bf16[32,3072]{1,0:T(8,128)(2,1)S(1)} %norm.2.own_ref), channel_id=1, source_target_pairs={{0,2},{1,3},{2,0},{3,1},{4,6},{5,7},{6,4},{7,5},{8,10},{9,11},{10,... | collective-permute-start | bytes 589832 | tf_op jit(solution)/shard_map/ppermute | solution.py:282
  44.8 5.1 %collective-permute-start.12 = (bf16[32,768]{1,0:T(8,128)(2,1)S(1)}, bf16[32,768]{1,0:T(8,128)(2,1)S(1)}, u32[]{:S(2)}, u32[]{:S(2)}) collective-permute-start(bf16[32,768]{1,0:T(8,128)(2,1)S(1)} %close.3.refs_0_), channel_id=1, source_target_pairs={{0,8},{4,12},{8,0},{12,4},{1,9},{5,13},{9,1},{13,5},{2,10},{6,14},... | collective-permute-start | bytes 147464 | tf_op jit(solution)/shard_map/ppermute | solution.py:282
  49.9 4.7 %collective-permute-start.13 = (bf16[2,32,768]{2,1,0:T(8,128)(2,1)S(1)}, bf16[2,32,768]{2,1,0:T(8,128)(2,1)S(1)}, u32[]{:S(2)}, u32[]{:S(2)}) collective-permute-start(bf16[2,32,768]{2,1,0:T(8,128)(2,1)S(1)} %pair.10.refs_2_), channel_id=1, source_target_pairs={{0,4},{4,0},{8,12},{12,8},{1,5},{5,1},{9,13},{13,9},{2,6},{6,2},{1... | collective-permute-start | bytes 294920 | tf_op jit(solution)/shard_map/ppermute | solution.py:282
  55.4 5.7 %collective-permute-start.14 = (bf16[32,3072]{1,0:T(8,128)(2,1)S(1)}, bf16[32,3072]{1,0:T(8,128)(2,1)S(1)}, u32[]{:S(2)}, u32[]{:S(2)}) collective-permute-start(bf16[32,3072]{1,0:T(8,128)(2,1)S(1)} %norm.3.own_ref), channel_id=1, source_target_pairs={{0,2},{1,3},{2,0},{3,1},{4,6},{5,7},{6,4},{7,5},{8,10},{9,11},{10,... | collective-permute-start | bytes 589832 | tf_op jit(solution)/shard_map/ppermute | solution.py:282
  56.0 5.2 %collective-permute-start.7 = (bf16[2,32,3072]{2,1,0:T(8,128)(2,1)S(1)}, bf16[2,32,3072]{2,1,0:T(8,128)(2,1)S(1)}, u32[]{:S(2)}, u32[]{:S(2)}) collective-permute-start(bf16[2,32,3072]{2,1,0:T(8,128)(2,1)S(1)} %pair.8.refs_4_.refs_0_), channel_id=1, source_target_pairs={{0,1},{1,0},{2,3},{3,2},{4,5},{5,4},{6,7},{7,6},{8,9},{9,8},{10,11... | collective-permute-start | bytes 1179656 | tf_op jit(solution)/shard_map/ppermute | solution.py:282
  61.2 1.8 %collective-permute-start.15 = (bf16[2,32,3072]{2,1,0:T(8,128)(2,1)S(1)}, bf16[2,32,3072]{2,1,0:T(8,128)(2,1)S(1)}, u32[]{:S(2)}, u32[]{:S(2)}) collective-permute-start(bf16[2,32,3072]{2,1,0:T(8,128)(2,1)S(1)} %pair.11.refs_2_), channel_id=1, source_target_pairs={{0,1},{1,0},{2,3},{3,2},{4,5},{5,4},{6,7},{7,6},{8,9},{9,8},{10,11... | collective-permute-start | bytes 1179656 | tf_op jit(solution)/shard_map/ppermute | solution.py:282
  70.6 18.9 %copy-start.6 = (f32[64,4]{0,1:T(4,128)S(1)}, f32[64,4]{0,1:T(4,128)}, u32[]{:S(2)}) copy-start(f32[64,4]{0,1:T(4,128)} %param.17) | copy-start | bytes 3076
  70.6 4.3 %collective-permute-start.16 = (bf16[2,256,768]{2,1,0:T(8,128)(2,1)S(1)}, bf16[2,256,768]{2,1,0:T(8,128)(2,1)S(1)}, u32[]{:S(2)}, u32[]{:S(2)}) collective-permute-start(bf16[2,256,768]{2,1,0:T(8,128)(2,1)S(1)} %get-tuple-element.29), channel_id=1, source_target_pairs={{0,1},{1,0},{2,3},{3,2},{4,5},{5,4},{6,7},{7,6},{8,9},{9,8},{10,11... | collective-permute-start | bytes 2359304 | tf_op jit(solution)/shard_map/ppermute | solution.py:282
  75.6 7.8 %collective-permute-start.19 = (bf16[128,768]{1,0:T(8,128)(2,1)S(1)}, bf16[128,768]{1,0:T(8,128)(2,1)S(1)}, u32[]{:S(2)}, u32[]{:S(2)}) collective-permute-start(bf16[128,768]{1,0:T(8,128)(2,1)S(1)} %get-tuple-element.34), channel_id=1, source_target_pairs={{0,2},{1,3},{2,0},{3,1},{4,6},{5,7},{6,4},{7,5},{8,10},{9,11},{10,... | collective-permute-start | bytes 589832 | tf_op jit(solution)/shard_map/ppermute | solution.py:282
  76.2 11.9 %collective-permute-start.17 = (bf16[128,768]{1,0:T(8,128)(2,1)S(1)}, bf16[128,768]{1,0:T(8,128)(2,1)S(1)}, u32[]{:S(2)}, u32[]{:S(2)}) collective-permute-start(bf16[128,768]{1,0:T(8,128)(2,1)S(1)} %get-tuple-element.31), channel_id=1, source_target_pairs={{0,2},{1,3},{2,0},{3,1},{4,6},{5,7},{6,4},{7,5},{8,10},{9,11},{10,... | collective-permute-start | bytes 589832 | tf_op jit(solution)/shard_map/ppermute | solution.py:282
  84.0 9.9 %collective-permute-start.20 = (bf16[64,768]{1,0:T(8,128)(2,1)S(1)}, bf16[64,768]{1,0:T(8,128)(2,1)S(1)}, u32[]{:S(2)}, u32[]{:S(2)}) collective-permute-start(bf16[64,768]{1,0:T(8,128)(2,1)S(1)} %get-tuple-element.35), channel_id=1, source_target_pairs={{0,8},{4,12},{8,0},{12,4},{1,9},{5,13},{9,1},{13,5},{2,10},{6,14},... | collective-permute-start | bytes 294920 | tf_op jit(solution)/shard_map/ppermute | solution.py:282
  86.3 7.6 %collective-permute-start.21 = (bf16[64,768]{1,0:T(8,128)(2,1)S(1)}, bf16[64,768]{1,0:T(8,128)(2,1)S(1)}, u32[]{:S(2)}, u32[]{:S(2)}) collective-permute-start(bf16[64,768]{1,0:T(8,128)(2,1)S(1)} %get-tuple-element.36), channel_id=1, source_target_pairs={{0,12},{4,8},{8,4},{12,0},{1,13},{5,9},{9,5},{13,1},{2,14},{6,10},... | collective-permute-start | bytes 294920 | tf_op jit(solution)/shard_map/ppermute | solution.py:282
  88.7 5.9 %collective-permute-start.18 = (bf16[64,768]{1,0:T(8,128)(2,1)S(1)}, bf16[64,768]{1,0:T(8,128)(2,1)S(1)}, u32[]{:S(2)}, u32[]{:S(2)}) collective-permute-start(bf16[64,768]{1,0:T(8,128)(2,1)S(1)} %get-tuple-element.33), channel_id=1, source_target_pairs={{0,4},{4,0},{8,12},{12,8},{1,5},{5,1},{9,13},{13,9},{2,6},{6,2},{1... | collective-permute-start | bytes 294920 | tf_op jit(solution)/shard_map/ppermute | solution.py:282
  (5 other events, 38.5 us)

commit v3 on v2

--- a/solution.py
+++ b/solution.py
@@ -19,7 +19,7 @@
 ANYWHERE = pl.BlockSpec(memory_space=pl.ANY)
 
 
-def local_call(kernel, out_shape, in_specs, scratch=(), vmem=32, name=None, after=None):
+def local_call(kernel, out_shape, in_specs, scratch=(), vmem=12, name=None, after=None):
     several = isinstance(out_shape, (tuple, list))
     if after is not None:
         count, inner = len(in_specs), kernel
@@ -40,7 +40,7 @@
 
 def attend_kernel(
     kv_heads, group, slots, batch, begin,
-    lengths_ref, q_ref, fresh_ref, cache_ref, after_ref, out_ref,
+    lengths_ref, q_ref, fresh_ref, cache_ref, after_ref, out_ref, again_ref,
     keys, values, q_rows, scores, own_scores, probs, own_probs, mixed, sems,
 ):
     rows = out_ref.shape[0]
@@ -104,9 +104,10 @@
             for g in range(kv_heads):
                 mixed[g, here, :] = total[:, g * HD : (g + 1) * HD]
         for head in range(heads):
-            out_ref[step * batch : (step + 1) * batch, head * HD : (head + 1) * HD] = mixed[
-                head // group, pl.ds(head, batch, stride=slots), :
-            ].astype(BF16)
+            there = (slice(step * batch, (step + 1) * batch), slice(head * HD, (head + 1) * HD))
+            done = mixed[head // group, pl.ds(head, batch, stride=slots), :].astype(BF16)
+            out_ref[there] = done
+            again_ref[there] = done
 
 
 def attend(queries, new_kv, kv_cache, lengths, begin, rows, after):
@@ -118,9 +119,9 @@
     batch = 16
     return pl.pallas_call(
         functools.partial(attend_kernel, kv_heads, heads // kv_heads, slots, batch, begin),
-        out_shape=jax.ShapeDtypeStruct((rows, features), BF16),
+        out_shape=[jax.ShapeDtypeStruct((rows, features), BF16)] * 2,
         in_specs=[SMEM, VMEM, VMEM, ANYWHERE, ANYWHERE],
-        out_specs=VMEM,
+        out_specs=[VMEM] * 2,
         scratch_shapes=[
             pltpu.VMEM((rows, context, width), BF16),
             pltpu.VMEM((rows, context, width), BF16),
@@ -132,7 +133,7 @@
             pltpu.VMEM((kv_heads, batch * slots, HD), F32),
             pltpu.SemaphoreType.DMA((2, rows // batch)),
         ],
-        compiler_params=pltpu.CompilerParams(vmem_limit_bytes=53 * MIB),
+        compiler_params=pltpu.CompilerParams(vmem_limit_bytes=58 * MIB),
         cost_estimate=pl.CostEstimate(flops=1024, bytes_accessed=1024, transcendentals=0),
         name="attend",
     )(lengths, queries, new_kv, kv_cache, after)
@@ -143,107 +144,102 @@
     out_ref[1] = other_ref[...]
 
 
-def gather_pair(owned, others, after):
-    pairs = []
-    for own, other in zip(owned, others):
-        out = jax.ShapeDtypeStruct((2, *own.shape), own.dtype)
-        after = pairs[-1] if pairs else after
-        pairs.append(local_call(pair_kernel, out, [VMEM] * 2, name="pair", after=after)(own, other))
-    return pairs
-
-
-def by_distance(pair_ref, second_ref):
-    return pair_ref.at[0], second_ref.at[0], pair_ref.at[1], second_ref.at[1]
-
-
-def project_kernel(
-    place_ref, pair_ref, second_ref, weight_ref, own_ref, cross_ref, far_ref, held
-):
-    shards = by_distance(pair_ref, second_ref)
-    rows = own_ref.shape[0]
+def gate_kernel(place_ref, ids_ref, gates_ref, gate_ref):
+    parts, rows, lanes = gate_ref.shape
+    ids = ids_ref[pl.ds(pl.multiple_of(place_ref[0] * rows, rows), rows), :]
+    for s in range(parts):
+        gate = jnp.sum(
+            jnp.where(ids == (place_ref[0] ^ s), gates_ref[...], 0.0), axis=1, keepdims=True
+        )
+        gate_ref[s] = jnp.broadcast_to(gate, (rows, lanes))
+
+
+def project_kernel(parts, place_ref, *refs):
+    shards, weight_ref = refs[:parts], refs[parts]
+    outs, held = refs[parts + 1 : -1], refs[-1]
+    rows = shards[0].shape[0]
     turn = place_ref[0] ^ place_ref[1]
     block = jnp.concatenate([shard[...] for shard in shards], axis=0)
-    pieces = jnp.dot(block, weight_ref[...], preferred_element_type=F32)
-    for s in range(len(shards)):
+    pieces = jnp.dot(block, weight_ref[...], preferred_element_type=F32).astype(BF16)
+    for s in range(parts):
         held[turn ^ s] = pieces[s * rows : (s + 1) * rows, :]
-    own_ref[...] = held[0]
-    cross_ref[...] = held[2]
-    far_ref[0] = held[1].astype(BF16)
-    far_ref[1] = held[3].astype(BF16)
-
-
-def cross_kernel(cross_ref, near_ref, out_ref):
-    out_ref[...] = (cross_ref[...] + near_ref[1].astype(F32)).astype(BF16)
-
-
-def close_kernel(own_ref, near_ref, crossed_ref, out_ref):
-    total = own_ref[...] + near_ref[0].astype(F32) + crossed_ref[...].astype(F32)
-    out_ref[...] = total.astype(BF16)
-
-
-def norm_kernel(place_ref, gain_ref, pair_ref, second_ref, out, held):
-    width = pair_ref.shape[2]
-    for s, shard in enumerate(by_distance(pair_ref, second_ref)):
+    for t in range(parts):
+        outs[t][...] = held[t]
+
+
+def add_kernel(*refs):
+    terms, out = refs[:-1], refs[-1]
+    total = terms[0][...].astype(F32)
+    for term in terms[1:]:
+        total = total + term[...].astype(F32)
+    out[...] = total.astype(BF16)
+
+
+def norm_kernel(parts, place_ref, gain_ref, *refs):
+    shards, out, held = refs[:parts], refs[parts], refs[parts + 1]
+    width = shards[0].shape[1]
+    for s in range(parts):
         first = pl.multiple_of((place_ref[0] ^ s) * width, HD)
-        held[:, pl.ds(first, width)] = shard[...].astype(F32)
+        held[:, pl.ds(first, width)] = shards[s][...].astype(F32)
     values = held[...]
     center = values - jnp.mean(values, axis=1, keepdims=True)
     spread = jnp.mean(center * center, axis=1, keepdims=True)
     out[...] = (center * lax.rsqrt(spread + 1e-05) * gain_ref[...]).astype(BF16)
 
 
-def lift_kernel(chunks, place_ref, *refs):
+def by_distance(pair_ref, second_ref):
+    return pair_ref.at[0], second_ref.at[0], pair_ref.at[1], second_ref.at[1]
+
+
+def lift_kernel(chunks, tile, place_ref, *refs):
     count = 2 * chunks
     shards, (up_hbm, down_hbm) = refs[:count], refs[count : count + 2]
-    active_ref, far_ref, held, up, down, sems = refs[count + 2 :]
+    active_ref, far_ref, rest_ref, held, up, down, up_sems, down_sems = refs[count + 2 :]
     hidden = active_ref.shape[1]
     share = far_ref.shape[2]
     rows = shards[0].shape[1]
-    tile = up.shape[0] // (sems.shape[0] - 2)
-    tiles = hidden // tile
-
-    def fetch(k):
-        part = pl.ds(k * tile, tile)
-        return pltpu.make_async_copy(up_hbm.at[part], up.at[part], sems.at[k])
-
-    def fetch_down(k):
-        first = pl.multiple_of((place_ref[1] ^ (2 * k + 1)) * share, HD)
+
+    def fetch_up(first):
+        part = pl.ds(first, tile)
         return pltpu.make_async_copy(
-            down_hbm.at[:, pl.ds(first, share)], down.at[k], sems.at[tiles + k]
-        )
-
-    for k in range(tiles):
-        fetch(k).start()
-    for k in range(2):
-        fetch_down(k).start()
+            up_hbm.at[part], up.at[part], up_sems.at[first // tile]
+        )
+
+    def fetch_down(k, turn, into):
+        first = pl.multiple_of((place_ref[1] ^ turn) * share, HD)
+        return pltpu.make_async_copy(
+            down_hbm.at[:, pl.ds(first, share)], into, down_sems.at[k]
+        )
+
+    ups = [fetch_up(first) for first in range(0, hidden, tile)]
+    downs = [fetch_down(k, 2 * k + 1, down.at[k]) for k in range(2)]
+    rests = [fetch_down(2 + k, 2 - 2 * k, rest_ref.at[k]) for k in range(2)]
+    for copy in ups + downs + rests:
+        copy.start()
     for c in range(chunks):
         for t, shard in enumerate(by_distance(*shards[2 * c : 2 * c + 2])):
             first = pl.multiple_of(((place_ref[1] ^ t) * chunks + c) * rows, rows)
             held[pl.ds(first, rows), :] = shard[...]
-    for k in range(tiles):
-        fetch(k).wait()
+    arrived = 0
+    for first in range(0, hidden, 2 * HD):
+        last = min(first + 2 * HD, hidden)
+        while arrived < last:
+            ups[arrived // tile].wait()
+            arrived += tile
         raised = lax.dot_general(
-            held[...], up[k * tile : (k + 1) * tile, :], (((1,), (1,)), ((), ())),
-            preferred_element_type=F32,
-        )
-        active_ref[:, k * tile : (k + 1) * tile] = (raised / (1.0 + jnp.exp(-raised))).astype(BF16)
+            up[first:last, :], held[...], (((1,), (1,)), ((), ())), preferred_element_type=F32
+        )
+        active_ref[:, first:last] = (raised / (1.0 + jnp.exp(-raised))).T.astype(BF16)
     for k in range(2):
-        fetch_down(k).wait()
+        downs[k].wait()
         far_ref[k] = jnp.dot(active_ref[...], down[k], preferred_element_type=F32).astype(BF16)
-
-
-def lower_kernel(place_ref, active_ref, down_hbm, cross_ref, own_ref, down, sems):
-    share = own_ref.shape[1]
-
-    def fetch(k):
-        first = pl.multiple_of((place_ref[1] ^ (2 - 2 * k)) * share, HD)
-        return pltpu.make_async_copy(down_hbm.at[:, pl.ds(first, share)], down.at[k], sems.at[k])
-
-    for k in range(2):
-        fetch(k).start()
+    for copy in rests:
+        copy.wait()
+
+
+def lower_kernel(active_ref, rest_ref, cross_ref, own_ref):
     for k, out_ref in enumerate((cross_ref, own_ref)):
-        fetch(k).wait()
-        out_ref[...] = jnp.dot(active_ref[...], down[k], preferred_element_type=F32)
+        out_ref[...] = jnp.dot(active_ref[...], rest_ref[k], preferred_element_type=F32)
 
 
 def turn_kernel(place_ref, cross_ref, near_ref, far_ref, close_ref):
@@ -264,17 +260,15 @@
         out_ref[...] = (total + crossed_ref[there, :].astype(F32)).astype(BF16)
 
 
-def mix_kernel(parts, place_ref, ids_ref, gates_ref, *refs):
+def mix_kernel(parts, gate_ref, *refs):
     terms, out = refs[:parts], refs[parts]
-    rows = out.shape[0]
-    ids = ids_ref[pl.ds(pl.multiple_of(place_ref[0] * rows, rows), rows), :]
-    total = jnp.zeros(out.shape, F32)
-    for s in range(parts):
-        gate = jnp.sum(
-            jnp.where(ids == (place_ref[0] ^ s), gates_ref[...], 0.0), axis=1, keepdims=True
-        )
-        total = total + gate * terms[s][...].astype(F32)
-    out[...] = total.astype(BF16)
+    lanes = gate_ref.shape[2]
+    for first in range(0, out.shape[1], lanes):
+        part = slice(first, first + lanes)
+        total = gate_ref[0] * terms[0][:, part].astype(F32)
+        for s in range(1, parts):
+            total = total + gate_ref[s] * terms[s][:, part].astype(F32)
+        out[:, part] = total.astype(BF16)
 
 
 def trade(array, axis, turn):
@@ -300,85 +294,96 @@
     gain = norm_gain.reshape(1, model)
     attended = []
     for c in range(chunks):
-        after = attended[-1] if attended else lengths
+        after = attended[-1][1] if attended else lengths
         attended.append(attend(queries, new_kv, kv_cache, lengths, c * rows, rows, after))
-    first = [trade(part, "gx", 2) for part in attended]
-    pairs = gather_pair(attended, first, attended[-1])
-    second = [trade(pair, "gx", 1) for pair in pairs]
-    pieces, nears, crossings, hidden, normed = [], [], [], [], []
+    order = [s for s in range(gx_count - 1, 0, -1)]
+
+    def spread(array, axis):
+        parts = {0: array, **{s: trade(array, axis, s) for s in order}}
+        return [parts[s] for s in range(len(parts))]
+
+    shards = [[kept] + spread(sent, "gx")[1:] for sent, kept in attended]
+    gates = local_call(
+        gate_kernel,
+        shape((gx_count, block_rows, HD), F32),
+        [SMEM, VMEM, VMEM],
+        name="gates",
+        after=attended[-1][1],
+    )(place, expert_ids, gate_weights)
+    pieces, hidden = [], []
     for c in range(chunks):
         pieces.append(
             local_call(
-                project_kernel,
-                [shape((rows, width), F32), shape((rows, width), F32), shape((2, rows, width), BF16)],
-                [SMEM] + [VMEM] * 3,
-                [pltpu.VMEM((ta_count, rows, width), F32)],
+                functools.partial(project_kernel, gx_count),
+                [shape((rows, width), BF16)] * ta_count,
+                [SMEM] + [VMEM] * (gx_count + 1),
+                [pltpu.VMEM((ta_count, rows, width), BF16)],
                 name="project",
-                after=pieces[-1][0] if pieces else None,
-            )(place, pairs[c], second[c], out_proj)
-        )
-        nears.append(trade(pieces[c][2], "ta", 1))
+                after=pieces[-1][0] if pieces else gates,
+            )(place, *shards[c], out_proj)
+        )
     for c in range(chunks):
-        crossings.append(
-            local_call(
-                cross_kernel,
-                shape((rows, width), BF16),
-                [VMEM] * 2,
-                name="cross",
-                after=crossings[-1] if crossings else None,
-            )(pieces[c][1], nears[c])
-        )
-    crossed = [trade(part, "ta", 2) for part in crossings]
-    for c in range(chunks):
+        parts = [pieces[c][0]] + [trade(pieces[c][t], "ta", t) for t in range(1, ta_count)]
         hidden.append(
             local_call(
-                close_kernel,
+                add_kernel,
                 shape((rows, width), BF16),
-                [VMEM] * 3,
-                name="close",
-                after=hidden[-1] if hidden else None,
-            )(pieces[c][0], nears[c], crossed[c])
-        )
-    first = [trade(part, "gx", 2) for part in hidden]
-    pairs = gather_pair(hidden, first, None)
-    second = [trade(pair, "gx", 1) for pair in pairs]
-    blocks, after = [], None
+                [VMEM] * ta_count,
+                name="add",
+                after=hidden[-1] if hidden else pieces[-1][0],
+            )(*parts)
+        )
+    shards = [spread(part, "gx") for part in hidden]
+    normed, pairs = [], []
     for c in range(chunks):
-        normed = local_call(
-            norm_kernel,
-            shape((rows, model), BF16),
-            [SMEM] + [VMEM] * 3,
-            [pltpu.VMEM((rows, model), F32)],
-            name="norm",
-            after=after,
-        )(place, gain, pairs[c], second[c])
-        (pair,) = gather_pair([normed], [trade(normed, "ta", 2)], None)
-        blocks += [pair, trade(pair, "ta", 1)]
-        after = pair
-    tile = math.gcd(hidden_share, 7 * 64)
-    down = w_down[0]
-    active, far = local_call(
-        functools.partial(lift_kernel, chunks),
-        [shape((all_rows, hidden_share), BF16), shape((2, all_rows, share), BF16)],
+        normed.append(
+            local_call(
+                functools.partial(norm_kernel, gx_count),
+                shape((rows, model), BF16),
+                [SMEM] + [VMEM] * (gx_count + 1),
+                [pltpu.VMEM((rows, model), F32)],
+                name="norm",
+                after=normed[-1] if normed else hidden[-1],
+            )(place, gain, *shards[c])
+        )
+    for c in range(chunks):
+        pairs.append(
+            local_call(
+                pair_kernel,
+                shape((2, rows, model), BF16),
+                [VMEM] * 2,
+                name="pair",
+                after=pairs[-1] if pairs else normed[-1],
+            )(normed[c], trade(normed[c], "ta", 2))
+        )
+    blocks = [block for pair in pairs for block in (pair, trade(pair, "ta", 1))]
+    tile = math.gcd(hidden_share, 3 * 64)
+    active, far, rest = local_call(
+        functools.partial(lift_kernel, chunks, tile),
+        [
+            shape((all_rows, hidden_share), BF16),
+            shape((2, all_rows, share), BF16),
+            shape((2, hidden_share, share), BF16),
+        ],
         [SMEM] + [VMEM] * (2 * chunks) + [ANYWHERE] * 2,
         [
             pltpu.VMEM((all_rows, model), BF16),
             pltpu.VMEM((hidden_share, model), BF16),
             pltpu.VMEM((2, hidden_share, share), BF16),
-            pltpu.SemaphoreType.DMA((hidden_share // tile + 2,)),
+            pltpu.SemaphoreType.DMA((hidden_share // tile,)),
+            pltpu.SemaphoreType.DMA((4,)),
         ],
-        vmem=48,
+        vmem=40,
         name="lift",
-    )(place, *blocks, jnp.swapaxes(w_up[0], 0, 1), down)
+    )(place, *blocks, jnp.swapaxes(w_up[0], 0, 1), w_down[0])
     near = trade(far, "ta", 1)
     cross, own = local_call(
         lower_kernel,
         [shape((all_rows, share), F32)] * 2,
-        [SMEM, VMEM, ANYWHERE],
-        [pltpu.VMEM((2, hidden_share, share), BF16), pltpu.SemaphoreType.DMA((2,))],
-        vmem=48,
+        [VMEM, VMEM],
+        vmem=16,
         name="lower",
-    )(place, active, down)
+    )(active, rest)
     half = all_rows // 2
     far_side, close_side = local_call(
         turn_kernel,
@@ -399,9 +404,9 @@
     return local_call(
         functools.partial(mix_kernel, gx_count),
         shape((block_rows, share), BF16),
-        [SMEM] + [VMEM] * (gx_count + 2),
+        [VMEM] * (gx_count + 1),
         name="mix",
-    )(place, expert_ids, gate_weights, *terms)
+    )(gates, *terms)
 
 
 def route_tables(expert_ids, expert_count, block_rows, capacity):
@@ -447,7 +452,7 @@
             queries, new_kv, kv_cache, lengths, out_proj, norm_gain, expert_ids, gate_weights,
             w_up, w_down,
         )
-    attended = attend(queries, new_kv, kv_cache, lengths, 0, block_rows, lengths)
+    attended, _ = attend(queries, new_kv, kv_cache, lengths, 0, block_rows, lengths)
     projected = jnp.dot(
         lax.all_gather(attended, "gx", axis=0, tiled=True),
         out_proj,

time: 96.1 us -> 88.3 us (0.919)
  waiting for transfers between devices: 34.7 us -> 26 us
  local copies, waits for them, and re-layouts: 2.67 us -> 1.15 us
  Pallas kernels: 27.5 us -> 29 us
  starting transfers between devices: 30.6 us -> 31.7 us
    ppermute x22 -> x28, waiting for transfers between devices: 34.7 us -> 26 us  [trade(): return lax.ppermute(array, axis, [(k, k ^ turn) for k in range(count)])]
    pallas_call x9 -> x2, Pallas kernels: 13.7 us -> 11.1 us  [the longest x1 9.72 us: every_row_body(): local_call(functools.partial(lift_kernel, chunks, tile), [shape((all_rows...]
    pallas_call x7 -> x9, Pallas kernels: 1.94 us -> 4.47 us  [local_call(): return call if after is None else lambda *args: call(*args, after)]
    pallas_call x2, Pallas kernels: 8.71 us -> 10.9 us  [attend(): pl.pallas_call(functools.partial(attend_kernel, kv_heads, heads // kv_hea...]
    unnamed x16 -> x14, local copies, waits for them, and re-layouts: 2.67 us -> 1.15 us
    ppermute x22 -> x28, starting transfers between devices: 30.6 us -> 31.7 us  [trade(): return lax.ppermute(array, axis, [(k, k ^ turn) for k in range(count)])]
  transfers between devices with their start and end apart: 22 -> 28, of which waited for: 13 -> 10; matrix products, arithmetic and copies ran while one was open for 0% -> 0% of each run, Pallas kernels for 12% -> 14%
where the time goes in v3:
time: 88.3 us; the launch traced here: 88.2 us
  starting transfers between devices  31.7 us (36%)
  Pallas kernels  29 us (33%)
  waiting for transfers between devices  26 us (29%)
  local copies, waits for them, and re-layouts  1.15 us (1%)
    ppermute x28, starting transfers between devices, trade(): return lax.ppermute(array, axis, [(k, k ^ turn) for k in range(count)])  31.7 us
    ppermute x28, waiting for transfers between devices, trade(): return lax.ppermute(array, axis, [(k, k ^ turn) for k in range(count)])  26 us
    pallas_call x2, Pallas kernels, attend(): pl.pallas_call(functools.partial(attend_kernel, kv_heads, heads // kv_hea...  10.9 us
    pallas_call x1, Pallas kernels, every_row_body(): local_call(functools.partial(lift_kernel, chunks, tile), [shape((all_rows...  9.72 us
    pallas_call x9, Pallas kernels, local_call(): return call if after is None else lambda *args: call(*args, after)  4.47 us
  transfers between devices with their start and end apart: 28, of which 10 were waited for; matrix products, arithmetic and copies ran while one was open for 0% of the time, Pallas kernels for 14%

profile of v3, /device:TPU:0, one launch (start us, length us, event | category | flops | bytes accessed | tf_op | source)
XLA Modules:
  0.0 88.2 jit_solution(17357182320435566057)
XLA Ops:
  0.0 5.4 %attend.2 = (bf16[32,1536]{1,0:T(8,128)(2,1)}, bf16[32,1536]{1,0:T(8,128)(2,1)}) custom-call(s32[64]{0:T(128)} %lengths_ref.3, bf16[64,1536]{1,0:T(8,128)(2,1)} %q_ref.3, bf16[2,64,256]{2,1,0:T(8,128)(2,1)} %fresh_ref.3, bf16[2,64,192,256]{3,2,1,0:T(8,128)(2,1)} %cache_ref.3, s32[64]{0:T(128)} %lengths_ref.3), custom_call_target="tpu_custom_call" | custom-call | flops 1024 | bytes 1024 | tf_op jit(solution)/shard_map/attend/pallas_call | solution.py:120
  5.5 5.1 %collective-permute-start.2 = (bf16[32,1536]{1,0:T(8,128)(2,1)}, bf16[32,1536]{1,0:T(8,128)(2,1)S(1)}, u32[]{:S(2)}, u32[]{:S(2)}) collective-permute-start(bf16[32,1536]{1,0:T(8,128)(2,1)} %get-tuple-element.30), channel_id=1, source_target_pairs={{0,12},{4,8},{8,4},{12,0},{1,13},{5,9},{9,5},{13,1},{2,14},{6,10},... | collective-permute-start | bytes 294920 | tf_op jit(solution)/shard_map/ppermute | solution.py:276
  11.3 5.4 %attend.3 = (bf16[32,1536]{1,0:T(8,128)(2,1)}, bf16[32,1536]{1,0:T(8,128)(2,1)}) custom-call(s32[64]{0:T(128)} %lengths_ref.3, bf16[64,1536]{1,0:T(8,128)(2,1)} %q_ref.3, bf16[2,64,256]{2,1,0:T(8,128)(2,1)} %fresh_ref.3, bf16[2,64,192,256]{3,2,1,0:T(8,128)(2,1)} %cache_ref.3, bf16[32,1536]{1,0:T(8,128)(2,1)} %get-tuple-element.28.after_ref.refs_1_), custom_call_target="tpu_custom_call" | custom-call | flops 1024 | bytes 1024 | tf_op jit(solution)/shard_map/attend/pallas_call | solution.py:120
  16.7 3.8 %collective-permute-start.8 = (bf16[32,1536]{1,0:T(8,128)(2,1)}, bf16[32,1536]{1,0:T(8,128)(2,1)S(1)}, u32[]{:S(2)}, u32[]{:S(2)}) collective-permute-start(bf16[32,1536]{1,0:T(8,128)(2,1)} %get-tuple-element.35), channel_id=1, source_target_pairs={{0,12},{4,8},{8,4},{12,0},{1,13},{5,9},{9,5},{13,1},{2,14},{6,10},... | collective-permute-start | bytes 294920 | tf_op jit(solution)/shard_map/ppermute | solution.py:276
  23.1 1.0 %project.2 = (bf16[32,768]{1,0:T(8,128)(2,1)S(1)}, bf16[32,768]{1,0:T(8,128)(2,1)S(1)}, bf16[32,768]{1,0:T(8,128)(2,1)S(1)}, bf16[32,768]{1,0:T(8,128)(2,1)S(1)}) custom-call(s32[2]{0:T(128)S(1)} %pad_add_fusion.refs_0_.place_ref, bf16[32,1536]{1,0:T(8,128)(2,1)S(1)} %copy-done.1, bf16[32,1536]{1,0:T(8,128)(2,1)S(1)} %collective-permute-done.refs_2_, ...), custom_call_target="tpu_custom_call" | custom-call | flops 1024 | bytes 1024 | tf_op jit(solution)/shard_map/project/pallas_call | solution.py:38
  24.2 1.7 %collective-permute-start.4 = (bf16[32,768]{1,0:T(8,128)(2,1)S(1)}, bf16[32,768]{1,0:T(8,128)(2,1)S(1)}, u32[]{:S(2)}, u32[]{:S(2)}) collective-permute-start(bf16[32,768]{1,0:T(8,128)(2,1)S(1)} %get-tuple-element.33), channel_id=1, source_target_pairs={{0,2},{1,3},{2,0},{3,1},{4,6},{5,7},{6,4},{7,5},{8,10},{9,11},{10,... | collective-permute-start | bytes 147464 | tf_op jit(solution)/shard_map/ppermute | solution.py:276
  26.1 2.0 %collective-permute-done.7.refs_3_ = bf16[32,1536]{1,0:T(8,128)(2,1)S(1)} collective-permute-done((bf16[32,1536]{1,0:T(8,128)(2,1)}, bf16[32,1536]{1,0:T(8,128)(2,1)S(1)}, u32[]{:S(2)}, u32[]{:S(2)}) %collective-permute-start.7) | collective-permute-done | bytes 98336 | tf_op jit(solution)/shard_map/ppermute | solution.py:276
  29.2 1.6 %collective-permute-start.13 = (bf16[32,768]{1,0:T(8,128)(2,1)S(1)}, bf16[32,768]{1,0:T(8,128)(2,1)S(1)}, u32[]{:S(2)}, u32[]{:S(2)}) collective-permute-start(bf16[32,768]{1,0:T(8,128)(2,1)S(1)} %get-tuple-element.38), channel_id=1, source_target_pairs={{0,2},{1,3},{2,0},{3,1},{4,6},{5,7},{6,4},{7,5},{8,10},{9,11},{10,... | collective-permute-start | bytes 147464 | tf_op jit(solution)/shard_map/ppermute | solution.py:276
  31.1 2.6 %collective-permute-start.11 = (bf16[32,768]{1,0:T(8,128)(2,1)S(1)}, bf16[32,768]{1,0:T(8,128)(2,1)S(1)}, u32[]{:S(2)}, u32[]{:S(2)}) collective-permute-start(bf16[32,768]{1,0:T(8,128)(2,1)S(1)} %add.4.refs_4_.refs_2_), channel_id=1, source_target_pairs={{0,12},{4,8},{8,4},{12,0},{1,13},{5,9},{9,5},{13,1},{2,14},{6,10},... | collective-permute-start | bytes 147464 | tf_op jit(solution)/shard_map/ppermute | solution.py:276
  33.8 1.8 %collective-permute-start.9 = (bf16[32,768]{1,0:T(8,128)(2,1)S(1)}, bf16[32,768]{1,0:T(8,128)(2,1)S(1)}, u32[]{:S(2)}, u32[]{:S(2)}) collective-permute-start(bf16[32,768]{1,0:T(8,128)(2,1)S(1)} %add.4.refs_4_.refs_2_), channel_id=1, source_target_pairs={{0,4},{4,0},{8,12},{12,8},{1,5},{5,1},{9,13},{13,9},{2,6},{6,2},{1... | collective-permute-start | bytes 147464 | tf_op jit(solution)/shard_map/ppermute | solution.py:276
  35.6 2.6 %collective-permute-start.18 = (bf16[32,768]{1,0:T(8,128)(2,1)S(1)}, bf16[32,768]{1,0:T(8,128)(2,1)S(1)}, u32[]{:S(2)}, u32[]{:S(2)}) collective-permute-start(bf16[32,768]{1,0:T(8,128)(2,1)S(1)} %add.5.refs_6_.refs_2_), channel_id=1, source_target_pairs={{0,12},{4,8},{8,4},{12,0},{1,13},{5,9},{9,5},{13,1},{2,14},{6,10},... | collective-permute-start | bytes 147464 | tf_op jit(solution)/shard_map/ppermute | solution.py:276
  38.3 1.8 %collective-permute-start.16 = (bf16[32,768]{1,0:T(8,128)(2,1)S(1)}, bf16[32,768]{1,0:T(8,128)(2,1)S(1)}, u32[]{:S(2)}, u32[]{:S(2)}) collective-permute-start(bf16[32,768]{1,0:T(8,128)(2,1)S(1)} %add.5.refs_6_.refs_2_), channel_id=1, source_target_pairs={{0,4},{4,0},{8,12},{12,8},{1,5},{5,1},{9,13},{13,9},{2,6},{6,2},{1... | collective-permute-start | bytes 147464 | tf_op jit(solution)/shard_map/ppermute | solution.py:276
  40.9 1.6 %collective-permute-start.15 = (bf16[32,3072]{1,0:T(8,128)(2,1)S(1)}, bf16[32,3072]{1,0:T(8,128)(2,1)S(1)}, u32[]{:S(2)}, u32[]{:S(2)}) collective-permute-start(bf16[32,3072]{1,0:T(8,128)(2,1)S(1)} %norm.2.refs_6_.refs_0_), channel_id=1, source_target_pairs={{0,2},{1,3},{2,0},{3,1},{4,6},{5,7},{6,4},{7,5},{8,10},{9,11},{10,... | collective-permute-start | bytes 589832 | tf_op jit(solution)/shard_map/ppermute | solution.py:276
  44.2 1.6 %collective-permute-start.20 = (bf16[32,3072]{1,0:T(8,128)(2,1)S(1)}, bf16[32,3072]{1,0:T(8,128)(2,1)S(1)}, u32[]{:S(2)}, u32[]{:S(2)}) collective-permute-start(bf16[32,3072]{1,0:T(8,128)(2,1)S(1)} %norm.3.refs_2_.refs_0_), channel_id=1, source_target_pairs={{0,2},{1,3},{2,0},{3,1},{4,6},{5,7},{6,4},{7,5},{8,10},{9,11},{10,... | collective-permute-start | bytes 589832 | tf_op jit(solution)/shard_map/ppermute | solution.py:276
  45.8 1.4 %collective-permute-done.15.refs_1_ = bf16[32,3072]{1,0:T(8,128)(2,1)S(1)} collective-permute-done((bf16[32,3072]{1,0:T(8,128)(2,1)S(1)}, bf16[32,3072]{1,0:T(8,128)(2,1)S(1)}, u32[]{:S(2)}, u32[]{:S(2)}) %collective-permute-start.15) | collective-permute-done | bytes 196640 | tf_op jit(solution)/shard_map/ppermute | solution.py:276
  47.2 3.9 %collective-permute-done.20.refs_1_ = bf16[32,3072]{1,0:T(8,128)(2,1)S(1)} collective-permute-done((bf16[32,3072]{1,0:T(8,128)(2,1)S(1)}, bf16[32,3072]{1,0:T(8,128)(2,1)S(1)}, u32[]{:S(2)}, u32[]{:S(2)}) %collective-permute-start.20) | collective-permute-done | bytes 196640 | tf_op jit(solution)/shard_map/ppermute | solution.py:276
  51.7 1.2 %collective-permute-done.21.refs_3_ = bf16[2,32,3072]{2,1,0:T(8,128)(2,1)S(1)} collective-permute-done((bf16[2,32,3072]{2,1,0:T(8,128)(2,1)S(1)}, bf16[2,32,3072]{2,1,0:T(8,128)(2,1)S(1)}, u32[]{:S(2)}, u32[]{:S(2)}) %collective-permute-start.21) | collective-permute-done | bytes 393248 | tf_op jit(solution)/shard_map/ppermute | solution.py:276
  53.5 9.7 %lift.1 = (bf16[256,1344]{1,0:T(8,128)(2,1)S(1)}, bf16[2,256,768]{2,1,0:T(8,128)(2,1)S(1)}, bf16[2,1344,768]{2,1,0:T(8,128)(2,1)S(1)}) custom-call(s32[2]{0:T(128)S(1)} %pad_add_fusion.refs_0_.place_ref, bf16[2,32,3072]{2,1,0:T(8,128)(2,1)S(1)} %pair.2.refs_2_.refs_0_, bf16[2,32,3072]{2,1,0:T(8,128)(2,1)S(1)} %collective-permute-done.19.refs_1_, ...), custom_call_target="tpu_custom_call" | custom-call | flops 1024 | bytes 1024 | tf_op jit(solution)/shard_map/lift/pallas_call | solution.py:361
  63.4 1.4 %lower.1 = (f32[256,768]{1,0:T(8,128)S(1)}, f32[256,768]{1,0:T(8,128)S(1)}) custom-call(bf16[256,1344]{1,0:T(8,128)(2,1)S(1)} %get-tuple-element.40.active_ref, bf16[2,1344,768]{2,1,0:T(8,128)(2,1)S(1)} %get-tuple-element.41.rest_ref), custom_call_target="tpu_custom_call" | custom-call | flops 1024 | bytes 1024 | tf_op jit(solution)/shard_map/lower/pallas_call | solution.py:380
  66.2 1.4 %collective-permute-start.23 = (bf16[128,768]{1,0:T(8,128)(2,1)S(1)}, bf16[128,768]{1,0:T(8,128)(2,1)S(1)}, u32[]{:S(2)}, u32[]{:S(2)}) collective-permute-start(bf16[128,768]{1,0:T(8,128)(2,1)S(1)} %get-tuple-element.45), channel_id=1, source_target_pairs={{0,2},{1,3},{2,0},{3,1},{4,6},{5,7},{6,4},{7,5},{8,10},{9,11},{10,... | collective-permute-start | bytes 589832 | tf_op jit(solution)/shard_map/ppermute | solution.py:276
  68.3 5.7 %collective-permute-done.23.crossed_ref = bf16[128,768]{1,0:T(8,128)(2,1)S(1)} collective-permute-done((bf16[128,768]{1,0:T(8,128)(2,1)S(1)}, bf16[128,768]{1,0:T(8,128)(2,1)S(1)}, u32[]{:S(2)}, u32[]{:S(2)}) %collective-permute-start.23) | collective-permute-done | bytes 196640 | tf_op jit(solution)/shard_map/ppermute | solution.py:276
  74.8 2.7 %collective-permute-done.25.crossed_ref = bf16[128,768]{1,0:T(8,128)(2,1)S(1)} collective-permute-done((bf16[128,768]{1,0:T(8,128)(2,1)S(1)}, bf16[128,768]{1,0:T(8,128)(2,1)S(1)}, u32[]{:S(2)}, u32[]{:S(2)}) %collective-permute-start.25) | collective-permute-done | bytes 196640 | tf_op jit(solution)/shard_map/ppermute | solution.py:276
  79.1 1.6 %collective-permute-start.27 = (bf16[64,768]{1,0:T(8,128)(2,1)S(1)}, bf16[64,768]{1,0:T(8,128)(2,1)S(1)}, u32[]{:S(2)}, u32[]{:S(2)}) collective-permute-start(bf16[64,768]{1,0:T(8,128)(2,1)S(1)} %get-tuple-element.50), channel_id=1, source_target_pairs={{0,12},{4,8},{8,4},{12,0},{1,13},{5,9},{9,5},{13,1},{2,14},{6,10},... | collective-permute-start | bytes 294920 | tf_op jit(solution)/shard_map/ppermute | solution.py:276
  80.7 6.7 %collective-permute-done.26.refs_2_ = bf16[64,768]{1,0:T(8,128)(2,1)S(1)} collective-permute-done((bf16[64,768]{1,0:T(8,128)(2,1)S(1)}, bf16[64,768]{1,0:T(8,128)(2,1)S(1)}, u32[]{:S(2)}, u32[]{:S(2)}) %collective-permute-start.26) | collective-permute-done | bytes 98336 | tf_op jit(solution)/shard_map/ppermute | solution.py:276
  (64 shorter events, 14.1 us)
Async XLA Ops:
  5.5 15.0 %collective-permute-start.2 = (bf16[32,1536]{1,0:T(8,128)(2,1)}, bf16[32,1536]{1,0:T(8,128)(2,1)S(1)}, u32[]{:S(2)}, u32[]{:S(2)}) collective-permute-start(bf16[32,1536]{1,0:T(8,128)(2,1)} %get-tuple-element.30), channel_id=1, source_target_pairs={{0,12},{4,8},{8,4},{12,0},{1,13},{5,9},{9,5},{13,1},{2,14},{6,10},... | collective-permute-start | bytes 294920 | tf_op jit(solution)/shard_map/ppermute | solution.py:276
  10.6 12.4 %collective-permute-start.1 = (bf16[32,1536]{1,0:T(8,128)(2,1)}, bf16[32,1536]{1,0:T(8,128)(2,1)S(1)}, u32[]{:S(2)}, u32[]{:S(2)}) collective-permute-start(bf16[32,1536]{1,0:T(8,128)(2,1)} %get-tuple-element.30), channel_id=1, source_target_pairs={{0,8},{4,12},{8,0},{12,4},{1,9},{5,13},{9,1},{13,5},{2,10},{6,14},... | collective-permute-start | bytes 294920 | tf_op jit(solution)/shard_map/ppermute | solution.py:276
  10.6 12.4 %collective-permute-start = (bf16[32,1536]{1,0:T(8,128)(2,1)}, bf16[32,1536]{1,0:T(8,128)(2,1)S(1)}, u32[]{:S(2)}, u32[]{:S(2)}) collective-permute-start(bf16[32,1536]{1,0:T(8,128)(2,1)} %get-tuple-element.30), channel_id=1, source_target_pairs={{0,4},{4,0},{8,12},{12,8},{1,5},{5,1},{9,13},{13,9},{2,6},{6,2},{1... | collective-permute-start | bytes 294920 | tf_op jit(solution)/shard_map/ppermute | solution.py:276
  16.7 9.2 %collective-permute-start.8 = (bf16[32,1536]{1,0:T(8,128)(2,1)}, bf16[32,1536]{1,0:T(8,128)(2,1)S(1)}, u32[]{:S(2)}, u32[]{:S(2)}) collective-permute-start(bf16[32,1536]{1,0:T(8,128)(2,1)} %get-tuple-element.35), channel_id=1, source_target_pairs={{0,12},{4,8},{8,4},{12,0},{1,13},{5,9},{9,5},{13,1},{2,14},{6,10},... | collective-permute-start | bytes 294920 | tf_op jit(solution)/shard_map/ppermute | solution.py:276
  20.5 7.6 %collective-permute-start.7 = (bf16[32,1536]{1,0:T(8,128)(2,1)}, bf16[32,1536]{1,0:T(8,128)(2,1)S(1)}, u32[]{:S(2)}, u32[]{:S(2)}) collective-permute-start(bf16[32,1536]{1,0:T(8,128)(2,1)} %get-tuple-element.35), channel_id=1, source_target_pairs={{0,8},{4,12},{8,0},{12,4},{1,9},{5,13},{9,1},{13,5},{2,10},{6,14},... | collective-permute-start | bytes 294920 | tf_op jit(solution)/shard_map/ppermute | solution.py:276
  20.5 7.6 %collective-permute-start.6 = (bf16[32,1536]{1,0:T(8,128)(2,1)}, bf16[32,1536]{1,0:T(8,128)(2,1)S(1)}, u32[]{:S(2)}, u32[]{:S(2)}) collective-permute-start(bf16[32,1536]{1,0:T(8,128)(2,1)} %get-tuple-element.35), channel_id=1, source_target_pairs={{0,4},{4,0},{8,12},{12,8},{1,5},{5,1},{9,13},{13,9},{2,6},{6,2},{1... | collective-permute-start | bytes 294920 | tf_op jit(solution)/shard_map/ppermute | solution.py:276
  24.1 6.7 %collective-permute-start.3 = (bf16[32,768]{1,0:T(8,128)(2,1)S(1)}, bf16[32,768]{1,0:T(8,128)(2,1)S(1)}, u32[]{:S(2)}, u32[]{:S(2)}) collective-permute-start(bf16[32,768]{1,0:T(8,128)(2,1)S(1)} %get-tuple-element.32), channel_id=1, source_target_pairs={{0,1},{1,0},{2,3},{3,2},{4,5},{5,4},{6,7},{7,6},{8,9},{9,8},{10,11... | collective-permute-start | bytes 147464 | tf_op jit(solution)/shard_map/ppermute | solution.py:276
  24.2 6.9 %collective-permute-start.4 = (bf16[32,768]{1,0:T(8,128)(2,1)S(1)}, bf16[32,768]{1,0:T(8,128)(2,1)S(1)}, u32[]{:S(2)}, u32[]{:S(2)}) collective-permute-start(bf16[32,768]{1,0:T(8,128)(2,1)S(1)} %get-tuple-element.33), channel_id=1, source_target_pairs={{0,2},{1,3},{2,0},{3,1},{4,6},{5,7},{6,4},{7,5},{8,10},{9,11},{10,... | collective-permute-start | bytes 147464 | tf_op jit(solution)/shard_map/ppermute | solution.py:276
  25.9 5.2 %collective-permute-start.5 = (bf16[32,768]{1,0:T(8,128)(2,1)S(1)}, bf16[32,768]{1,0:T(8,128)(2,1)S(1)}, u32[]{:S(2)}, u32[]{:S(2)}) collective-permute-start(bf16[32,768]{1,0:T(8,128)(2,1)S(1)} %get-tuple-element.34), channel_id=1, source_target_pairs={{0,3},{1,2},{2,1},{3,0},{4,7},{5,6},{6,5},{7,4},{8,11},{9,10},{10,... | collective-permute-start | bytes 147464 | tf_op jit(solution)/shard_map/ppermute | solution.py:276
  29.2 6.4 %collective-permute-start.13 = (bf16[32,768]{1,0:T(8,128)(2,1)S(1)}, bf16[32,768]{1,0:T(8,128)(2,1)S(1)}, u32[]{:S(2)}, u32[]{:S(2)}) collective-permute-start(bf16[32,768]{1,0:T(8,128)(2,1)S(1)} %get-tuple-element.38), channel_id=1, source_target_pairs={{0,2},{1,3},{2,0},{3,1},{4,6},{5,7},{6,4},{7,5},{8,10},{9,11},{10,... | collective-permute-start | bytes 147464 | tf_op jit(solution)/shard_map/ppermute | solution.py:276
  30.8 4.8 %collective-permute-start.14 = (bf16[32,768]{1,0:T(8,128)(2,1)S(1)}, bf16[32,768]{1,0:T(8,128)(2,1)S(1)}, u32[]{:S(2)}, u32[]{:S(2)}) collective-permute-start(bf16[32,768]{1,0:T(8,128)(2,1)S(1)} %get-tuple-element.39), channel_id=1, source_target_pairs={{0,3},{1,2},{2,1},{3,0},{4,7},{5,6},{6,5},{7,4},{8,11},{9,10},{10,... | collective-permute-start | bytes 147464 | tf_op jit(solution)/shard_map/ppermute | solution.py:276
  31.1 7.1 %collective-permute-start.11 = (bf16[32,768]{1,0:T(8,128)(2,1)S(1)}, bf16[32,768]{1,0:T(8,128)(2,1)S(1)}, u32[]{:S(2)}, u32[]{:S(2)}) collective-permute-start(bf16[32,768]{1,0:T(8,128)(2,1)S(1)} %add.4.refs_4_.refs_2_), channel_id=1, source_target_pairs={{0,12},{4,8},{8,4},{12,0},{1,13},{5,9},{9,5},{13,1},{2,14},{6,10},... | collective-permute-start | bytes 147464 | tf_op jit(solution)/shard_map/ppermute | solution.py:276
  33.8 6.3 %collective-permute-start.10 = (bf16[32,768]{1,0:T(8,128)(2,1)S(1)}, bf16[32,768]{1,0:T(8,128)(2,1)S(1)}, u32[]{:S(2)}, u32[]{:S(2)}) collective-permute-start(bf16[32,768]{1,0:T(8,128)(2,1)S(1)} %add.4.refs_4_.refs_2_), channel_id=1, source_target_pairs={{0,8},{4,12},{8,0},{12,4},{1,9},{5,13},{9,1},{13,5},{2,10},{6,14},... | collective-permute-start | bytes 147464 | tf_op jit(solution)/shard_map/ppermute | solution.py:276
  33.8 6.3 %collective-permute-start.9 = (bf16[32,768]{1,0:T(8,128)(2,1)S(1)}, bf16[32,768]{1,0:T(8,128)(2,1)S(1)}, u32[]{:S(2)}, u32[]{:S(2)}) collective-permute-start(bf16[32,768]{1,0:T(8,128)(2,1)S(1)} %add.4.refs_4_.refs_2_), channel_id=1, source_target_pairs={{0,4},{4,0},{8,12},{12,8},{1,5},{5,1},{9,13},{13,9},{2,6},{6,2},{1... | collective-permute-start | bytes 147464 | tf_op jit(solution)/shard_map/ppermute | solution.py:276
  35.6 6.9 %collective-permute-start.18 = (bf16[32,768]{1,0:T(8,128)(2,1)S(1)}, bf16[32,768]{1,0:T(8,128)(2,1)S(1)}, u32[]{:S(2)}, u32[]{:S(2)}) collective-permute-start(bf16[32,768]{1,0:T(8,128)(2,1)S(1)} %add.5.refs_6_.refs_2_), channel_id=1, source_target_pairs={{0,12},{4,8},{8,4},{12,0},{1,13},{5,9},{9,5},{13,1},{2,14},{6,10},... | collective-permute-start | bytes 147464 | tf_op jit(solution)/shard_map/ppermute | solution.py:276
  38.3 5.2 %collective-permute-start.17 = (bf16[32,768]{1,0:T(8,128)(2,1)S(1)}, bf16[32,768]{1,0:T(8,128)(2,1)S(1)}, u32[]{:S(2)}, u32[]{:S(2)}) collective-permute-start(bf16[32,768]{1,0:T(8,128)(2,1)S(1)} %add.5.refs_6_.refs_2_), channel_id=1, source_target_pairs={{0,8},{4,12},{8,0},{12,4},{1,9},{5,13},{9,1},{13,5},{2,10},{6,14},... | collective-permute-start | bytes 147464 | tf_op jit(solution)/shard_map/ppermute | solution.py:276
  38.3 5.1 %collective-permute-start.16 = (bf16[32,768]{1,0:T(8,128)(2,1)S(1)}, bf16[32,768]{1,0:T(8,128)(2,1)S(1)}, u32[]{:S(2)}, u32[]{:S(2)}) collective-permute-start(bf16[32,768]{1,0:T(8,128)(2,1)S(1)} %add.5.refs_6_.refs_2_), channel_id=1, source_target_pairs={{0,4},{4,0},{8,12},{12,8},{1,5},{5,1},{9,13},{13,9},{2,6},{6,2},{1... | collective-permute-start | bytes 147464 | tf_op jit(solution)/shard_map/ppermute | solution.py:276
  40.9 6.3 %collective-permute-start.15 = (bf16[32,3072]{1,0:T(8,128)(2,1)S(1)}, bf16[32,3072]{1,0:T(8,128)(2,1)S(1)}, u32[]{:S(2)}, u32[]{:S(2)}) collective-permute-start(bf16[32,3072]{1,0:T(8,128)(2,1)S(1)} %norm.2.refs_6_.refs_0_), channel_id=1, source_target_pairs={{0,2},{1,3},{2,0},{3,1},{4,6},{5,7},{6,4},{7,5},{8,10},{9,11},{10,... | collective-permute-start | bytes 589832 | tf_op jit(solution)/shard_map/ppermute | solution.py:276
  44.2 6.9 %collective-permute-start.20 = (bf16[32,3072]{1,0:T(8,128)(2,1)S(1)}, bf16[32,3072]{1,0:T(8,128)(2,1)S(1)}, u32[]{:S(2)}, u32[]{:S(2)}) collective-permute-start(bf16[32,3072]{1,0:T(8,128)(2,1)S(1)} %norm.3.refs_2_.refs_0_), channel_id=1, source_target_pairs={{0,2},{1,3},{2,0},{3,1},{4,6},{5,7},{6,4},{7,5},{8,10},{9,11},{10,... | collective-permute-start | bytes 589832 | tf_op jit(solution)/shard_map/ppermute | solution.py:276
  66.2 7.8 %collective-permute-start.23 = (bf16[128,768]{1,0:T(8,128)(2,1)S(1)}, bf16[128,768]{1,0:T(8,128)(2,1)S(1)}, u32[]{:S(2)}, u32[]{:S(2)}) collective-permute-start(bf16[128,768]{1,0:T(8,128)(2,1)S(1)} %get-tuple-element.45), channel_id=1, source_target_pairs={{0,2},{1,3},{2,0},{3,1},{4,6},{5,7},{6,4},{7,5},{8,10},{9,11},{10,... | collective-permute-start | bytes 589832 | tf_op jit(solution)/shard_map/ppermute | solution.py:276
  67.6 9.9 %collective-permute-start.25 = (bf16[128,768]{1,0:T(8,128)(2,1)S(1)}, bf16[128,768]{1,0:T(8,128)(2,1)S(1)}, u32[]{:S(2)}, u32[]{:S(2)}) collective-permute-start(bf16[128,768]{1,0:T(8,128)(2,1)S(1)} %get-tuple-element.48), channel_id=1, source_target_pairs={{0,2},{1,3},{2,0},{3,1},{4,6},{5,7},{6,4},{7,5},{8,10},{9,11},{10,... | collective-permute-start | bytes 589832 | tf_op jit(solution)/shard_map/ppermute | solution.py:276
  74.7 6.0 %collective-permute-start.24 = (bf16[64,768]{1,0:T(8,128)(2,1)S(1)}, bf16[64,768]{1,0:T(8,128)(2,1)S(1)}, u32[]{:S(2)}, u32[]{:S(2)}) collective-permute-start(bf16[64,768]{1,0:T(8,128)(2,1)S(1)} %get-tuple-element.47), channel_id=1, source_target_pairs={{0,4},{4,0},{8,12},{12,8},{1,5},{5,1},{9,13},{13,9},{2,6},{6,2},{1... | collective-permute-start | bytes 294920 | tf_op jit(solution)/shard_map/ppermute | solution.py:276
  78.1 9.4 %collective-permute-start.26 = (bf16[64,768]{1,0:T(8,128)(2,1)S(1)}, bf16[64,768]{1,0:T(8,128)(2,1)S(1)}, u32[]{:S(2)}, u32[]{:S(2)}) collective-permute-start(bf16[64,768]{1,0:T(8,128)(2,1)S(1)} %get-tuple-element.49), channel_id=1, source_target_pairs={{0,8},{4,12},{8,0},{12,4},{1,9},{5,13},{9,1},{13,5},{2,10},{6,14},... | collective-permute-start | bytes 294920 | tf_op jit(solution)/shard_map/ppermute | solution.py:276
  79.1 8.3 %collective-permute-start.27 = (bf16[64,768]{1,0:T(8,128)(2,1)S(1)}, bf16[64,768]{1,0:T(8,128)(2,1)S(1)}, u32[]{:S(2)}, u32[]{:S(2)}) collective-permute-start(bf16[64,768]{1,0:T(8,128)(2,1)S(1)} %get-tuple-element.50), channel_id=1, source_target_pairs={{0,12},{4,8},{8,4},{12,0},{1,13},{5,9},{9,5},{13,1},{2,14},{6,10},... | collective-permute-start | bytes 294920 | tf_op jit(solution)/shard_map/ppermute | solution.py:276
  (10 other events, 107.6 us)

commit v4 on v3

--- a/solution.py
+++ b/solution.py
@@ -10,6 +10,7 @@
 
 HD = 128
 MIB = 1 << 20
+MIX_COST = 1 << 22
 VMEM = pl.BlockSpec(memory_space=pltpu.VMEM)
 SMEM = pl.BlockSpec(memory_space=pltpu.SMEM)
 F32 = jnp.float32
@@ -19,7 +20,7 @@
 ANYWHERE = pl.BlockSpec(memory_space=pl.ANY)
 
 
-def local_call(kernel, out_shape, in_specs, scratch=(), vmem=12, name=None, after=None):
+def local_call(kernel, out_shape, in_specs, scratch=(), vmem=8, name=None, after=None, cost=1024):
     several = isinstance(out_shape, (tuple, list))
     if after is not None:
         count, inner = len(in_specs), kernel
@@ -32,7 +33,7 @@
         out_specs=[VMEM] * len(out_shape) if several else VMEM,
         scratch_shapes=list(scratch),
         compiler_params=pltpu.CompilerParams(vmem_limit_bytes=vmem * MIB),
-        cost_estimate=pl.CostEstimate(flops=1024, bytes_accessed=1024, transcendentals=0),
+        cost_estimate=pl.CostEstimate(flops=1024, bytes_accessed=cost, transcendentals=0),
         name=name,
     )
     return call if after is None else lambda *args: call(*args, after)
@@ -40,8 +41,9 @@
 
 def attend_kernel(
     kv_heads, group, slots, batch, begin,
-    lengths_ref, q_ref, fresh_ref, cache_ref, after_ref, out_ref, again_ref,
-    keys, values, q_rows, scores, own_scores, probs, own_probs, mixed, sems,
+    lengths_hbm, q_hbm, fresh_hbm, cache_ref, after_ref, out_ref, again_ref,
+    lengths_ref, q_ref, fresh_ref, keys, values, q_rows, scores, own_scores, probs, own_probs,
+    mixed, sems, small_sems,
 ):
     rows = out_ref.shape[0]
     context = keys.shape[1]
@@ -58,13 +60,23 @@
             sems.at[kind, step],
         )
 
+    part = pl.ds(begin, rows)
+    small = [
+        pltpu.make_async_copy(q_hbm.at[part], q_ref, small_sems.at[0]),
+        pltpu.make_async_copy(lengths_hbm, lengths_ref, small_sems.at[1]),
+        pltpu.make_async_copy(fresh_hbm.at[:, part], fresh_ref, small_sems.at[2]),
+    ]
+    for copy in small:
+        copy.start()
     for step in range(steps):
         for kind in range(2):
             fetch(step, kind).start()
     q_rows[...] = jnp.zeros_like(q_rows)
+    for copy in small:
+        copy.wait()
     for head in range(heads):
         q_rows[head // group, pl.ds(head, rows, stride=slots), :] = q_ref[
-            begin : begin + rows, head * HD : (head + 1) * HD
+            :, head * HD : (head + 1) * HD
         ].astype(F32)
     place = lax.broadcasted_iota(jnp.int32, (slots, context), 1)
     for step in range(steps):
@@ -80,7 +92,7 @@
             )
             here = slice(k * slots, (k + 1) * slots)
             scores[here, :] = jnp.where(place < lengths_ref[begin + row], cached * scale, -jnp.inf)
-            fresh_key = fresh_ref[0, begin + row : begin + row + 1, :].astype(F32)
+            fresh_key = fresh_ref[0, row : row + 1, :].astype(F32)
             own_scores[here, :] = jnp.broadcast_to(
                 jnp.sum(mine * fresh_key, axis=1, keepdims=True) * scale, (slots, HD)
             )
@@ -99,7 +111,7 @@
             row = step * batch + k
             here = slice(k * slots, (k + 1) * slots)
             weighted = jnp.dot(probs[here, :], values[row], preferred_element_type=F32)
-            fresh_value = fresh_ref[1, begin + row : begin + row + 1, :].astype(F32)
+            fresh_value = fresh_ref[1, row : row + 1, :].astype(F32)
             total = weighted + own_probs[here, :1] * fresh_value
             for g in range(kv_heads):
                 mixed[g, here, :] = total[:, g * HD : (g + 1) * HD]
@@ -120,9 +132,12 @@
     return pl.pallas_call(
         functools.partial(attend_kernel, kv_heads, heads // kv_heads, slots, batch, begin),
         out_shape=[jax.ShapeDtypeStruct((rows, features), BF16)] * 2,
-        in_specs=[SMEM, VMEM, VMEM, ANYWHERE, ANYWHERE],
+        in_specs=[ANYWHERE] * 5,
         out_specs=[VMEM] * 2,
         scratch_shapes=[
+            pltpu.SMEM(lengths.shape, jnp.int32),
+            pltpu.VMEM((rows, features), BF16),
+            pltpu.VMEM((2, rows, width), BF16),
             pltpu.VMEM((rows, context, width), BF16),
             pltpu.VMEM((rows, context, width), BF16),
             pltpu.VMEM((kv_heads, rows * slots, HD), F32),
@@ -132,6 +147,7 @@
             pltpu.VMEM((batch * slots, HD), F32),
             pltpu.VMEM((kv_heads, batch * slots, HD), F32),
             pltpu.SemaphoreType.DMA((2, rows // batch)),
+            pltpu.SemaphoreType.DMA((3,)),
         ],
         compiler_params=pltpu.CompilerParams(vmem_limit_bytes=58 * MIB),
         cost_estimate=pl.CostEstimate(flops=1024, bytes_accessed=1024, transcendentals=0),
@@ -191,55 +207,52 @@
     return pair_ref.at[0], second_ref.at[0], pair_ref.at[1], second_ref.at[1]
 
 
+def load_kernel(source_hbm, out_ref, sem):
+    copy = pltpu.make_async_copy(source_hbm, out_ref, sem)
+    copy.start()
+    copy.wait()
+
+
 def lift_kernel(chunks, tile, place_ref, *refs):
     count = 2 * chunks
-    shards, (up_hbm, down_hbm) = refs[:count], refs[count : count + 2]
-    active_ref, far_ref, rest_ref, held, up, down, up_sems, down_sems = refs[count + 2 :]
+    shards, (up_ref, down_hbm) = refs[:count], refs[count : count + 2]
+    active_ref, far_ref, down_ref, held, sems = refs[count + 2 :]
     hidden = active_ref.shape[1]
     share = far_ref.shape[2]
     rows = shards[0].shape[1]
-
-    def fetch_up(first):
+    copies = []
+    for first in range(0, hidden, tile):
         part = pl.ds(first, tile)
-        return pltpu.make_async_copy(
-            up_hbm.at[part], up.at[part], up_sems.at[first // tile]
-        )
-
-    def fetch_down(k, turn, into):
-        first = pl.multiple_of((place_ref[1] ^ turn) * share, HD)
-        return pltpu.make_async_copy(
-            down_hbm.at[:, pl.ds(first, share)], into, down_sems.at[k]
-        )
-
-    ups = [fetch_up(first) for first in range(0, hidden, tile)]
-    downs = [fetch_down(k, 2 * k + 1, down.at[k]) for k in range(2)]
-    rests = [fetch_down(2 + k, 2 - 2 * k, rest_ref.at[k]) for k in range(2)]
-    for copy in ups + downs + rests:
-        copy.start()
+        copies.append(
+            pltpu.make_async_copy(down_hbm.at[part], down_ref.at[part], sems.at[first // tile])
+        )
+        copies[-1].start()
     for c in range(chunks):
         for t, shard in enumerate(by_distance(*shards[2 * c : 2 * c + 2])):
             first = pl.multiple_of(((place_ref[1] ^ t) * chunks + c) * rows, rows)
             held[pl.ds(first, rows), :] = shard[...]
-    arrived = 0
     for first in range(0, hidden, 2 * HD):
         last = min(first + 2 * HD, hidden)
-        while arrived < last:
-            ups[arrived // tile].wait()
-            arrived += tile
         raised = lax.dot_general(
-            up[first:last, :], held[...], (((1,), (1,)), ((), ())), preferred_element_type=F32
+            up_ref[first:last, :], held[...], (((1,), (1,)), ((), ())), preferred_element_type=F32
         )
         active_ref[:, first:last] = (raised / (1.0 + jnp.exp(-raised))).T.astype(BF16)
+    for copy in copies:
+        copy.wait()
     for k in range(2):
-        downs[k].wait()
-        far_ref[k] = jnp.dot(active_ref[...], down[k], preferred_element_type=F32).astype(BF16)
-    for copy in rests:
-        copy.wait()
-
-
-def lower_kernel(active_ref, rest_ref, cross_ref, own_ref):
-    for k, out_ref in enumerate((cross_ref, own_ref)):
-        out_ref[...] = jnp.dot(active_ref[...], rest_ref[k], preferred_element_type=F32)
+        first = pl.multiple_of((place_ref[1] ^ (2 * k + 1)) * share, HD)
+        far_ref[k] = jnp.dot(
+            active_ref[...], down_ref[:, pl.ds(first, share)], preferred_element_type=F32
+        ).astype(BF16)
+
+
+def lower_kernel(place_ref, active_ref, down_ref, cross_ref, own_ref):
+    share = own_ref.shape[1]
+    for out_ref, turn in ((cross_ref, 2), (own_ref, 0)):
+        first = pl.multiple_of((place_ref[1] ^ turn) * share, HD)
+        out_ref[...] = jnp.dot(
+            active_ref[...], down_ref[:, pl.ds(first, share)], preferred_element_type=F32
+        )
 
 
 def turn_kernel(place_ref, cross_ref, near_ref, far_ref, close_ref):
@@ -260,15 +273,18 @@
         out_ref[...] = (total + crossed_ref[there, :].astype(F32)).astype(BF16)
 
 
-def mix_kernel(parts, gate_ref, *refs):
-    terms, out = refs[:parts], refs[parts]
+def mix_kernel(first, gate_ref, *refs):
+    out = refs[-1]
+    terms = refs[:2]
+    earlier = refs[2:-1]
     lanes = gate_ref.shape[2]
-    for first in range(0, out.shape[1], lanes):
-        part = slice(first, first + lanes)
-        total = gate_ref[0] * terms[0][:, part].astype(F32)
-        for s in range(1, parts):
-            total = total + gate_ref[s] * terms[s][:, part].astype(F32)
-        out[:, part] = total.astype(BF16)
+    for begin in range(0, out.shape[1], lanes):
+        part = slice(begin, begin + lanes)
+        total = gate_ref[first] * terms[0][:, part].astype(F32)
+        total = total + gate_ref[first + 1] * terms[1][:, part].astype(F32)
+        for ref in earlier:
+            total = total + ref[:, part]
+        out[:, part] = total.astype(out.dtype)
 
 
 def trade(array, axis, turn):
@@ -303,13 +319,6 @@
         return [parts[s] for s in range(len(parts))]
 
     shards = [[kept] + spread(sent, "gx")[1:] for sent, kept in attended]
-    gates = local_call(
-        gate_kernel,
-        shape((gx_count, block_rows, HD), F32),
-        [SMEM, VMEM, VMEM],
-        name="gates",
-        after=attended[-1][1],
-    )(place, expert_ids, gate_weights)
     pieces, hidden = [], []
     for c in range(chunks):
         pieces.append(
@@ -319,7 +328,7 @@
                 [SMEM] + [VMEM] * (gx_count + 1),
                 [pltpu.VMEM((ta_count, rows, width), BF16)],
                 name="project",
-                after=pieces[-1][0] if pieces else gates,
+                after=pieces[-1][0] if pieces else attended[-1][1],
             )(place, *shards[c], out_proj)
         )
     for c in range(chunks):
@@ -346,6 +355,22 @@
                 after=normed[-1] if normed else hidden[-1],
             )(place, gain, *shards[c])
         )
+    gates = local_call(
+        gate_kernel,
+        shape((gx_count, block_rows, HD), F32),
+        [SMEM, VMEM, VMEM],
+        name="gates",
+        after=normed[-1],
+    )(place, expert_ids, gate_weights)
+    up = local_call(
+        load_kernel,
+        shape((hidden_share, model), BF16),
+        [ANYWHERE],
+        [pltpu.SemaphoreType.DMA],
+        vmem=40,
+        name="load",
+        after=gates,
+    )(jnp.swapaxes(w_up[0], 0, 1))
     for c in range(chunks):
         pairs.append(
             local_call(
@@ -353,37 +378,34 @@
                 shape((2, rows, model), BF16),
                 [VMEM] * 2,
                 name="pair",
-                after=pairs[-1] if pairs else normed[-1],
+                after=pairs[-1] if pairs else up,
             )(normed[c], trade(normed[c], "ta", 2))
         )
     blocks = [block for pair in pairs for block in (pair, trade(pair, "ta", 1))]
     tile = math.gcd(hidden_share, 3 * 64)
-    active, far, rest = local_call(
+    active, far, down = local_call(
         functools.partial(lift_kernel, chunks, tile),
         [
             shape((all_rows, hidden_share), BF16),
             shape((2, all_rows, share), BF16),
-            shape((2, hidden_share, share), BF16),
+            shape((hidden_share, model), BF16),
         ],
-        [SMEM] + [VMEM] * (2 * chunks) + [ANYWHERE] * 2,
+        [SMEM] + [VMEM] * (2 * chunks + 1) + [ANYWHERE],
         [
             pltpu.VMEM((all_rows, model), BF16),
-            pltpu.VMEM((hidden_share, model), BF16),
-            pltpu.VMEM((2, hidden_share, share), BF16),
             pltpu.SemaphoreType.DMA((hidden_share // tile,)),
-            pltpu.SemaphoreType.DMA((4,)),
         ],
-        vmem=40,
+        vmem=30,
         name="lift",
-    )(place, *blocks, jnp.swapaxes(w_up[0], 0, 1), w_down[0])
+    )(place, *blocks, up, w_down[0])
     near = trade(far, "ta", 1)
     cross, own = local_call(
         lower_kernel,
         [shape((all_rows, share), F32)] * 2,
-        [VMEM, VMEM],
+        [SMEM, VMEM, VMEM],
         vmem=16,
         name="lower",
-    )(active, rest)
+    )(place, active, down)
     half = all_rows // 2
     far_side, close_side = local_call(
         turn_kernel,
@@ -391,7 +413,7 @@
         [SMEM] + [VMEM] * 2,
         name="turn",
     )(place, cross, near)
-    terms = {}
+    terms, after = {}, None
     for side, crossing in ((1, far_side), (0, close_side)):
         crossed = trade(crossing, "ta", 2)
         terms[2 * side], terms[2 * side + 1] = local_call(
@@ -399,14 +421,23 @@
             [shape((block_rows, share), BF16)] * 2,
             [SMEM] + [VMEM] * 3,
             name="split",
+            after=after,
         )(place, own, near, crossed)
+        after = terms[2 * side]
     terms = [terms[s] if s == 0 else trade(terms[s], "gx", s) for s in range(gx_count)]
+    far_sum = local_call(
+        functools.partial(mix_kernel, 2),
+        shape((block_rows, share), F32),
+        [VMEM] * 3,
+        name="mix_far",
+        cost=MIX_COST,
+    )(gates, *terms[2:])
     return local_call(
-        functools.partial(mix_kernel, gx_count),
+        functools.partial(mix_kernel, 0),
         shape((block_rows, share), BF16),
-        [VMEM] * (gx_count + 1),
+        [VMEM] * 4,
         name="mix",
-    )(gates, *terms)
+    )(gates, *terms[:2], far_sum)
 
 
 def route_tables(expert_ids, expert_count, block_rows, capacity):

time: 88.3 us -> 81.9 us (0.928)
  waiting for transfers between devices: 26 us -> 18.5 us
  starting transfers between devices: 31.7 us -> 33.1 us
    ppermute x28, waiting for transfers between devices: 26 us -> 18.5 us  [trade(): return lax.ppermute(array, axis, [(k, k ^ turn) for k in range(count)])]
    pallas_call x1, Pallas kernels: 9.72 us -> 5.48 us  [every_row_body(): local_call(functools.partial(lift_kernel, chunks, tile), [shape((all_rows...]
    pallas_call x9 -> x11, Pallas kernels: 4.47 us -> 8.44 us  [local_call(): return call if after is None else lambda *args: call(*args, after)]
    ppermute x28, starting transfers between devices: 31.7 us -> 33.1 us  [trade(): return lax.ppermute(array, axis, [(k, k ^ turn) for k in range(count)])]
    pallas_call x2 -> x3, Pallas kernels: 2.1 us -> 2.7 us  [the longest x1 1.96 us: every_row_body(): local_call(lower_kernel, [shape((all_rows, share), F32)] * 2, [SMEM, VMEM...]
  transfers between devices with their start and end apart: 28 -> 28, of which waited for: 10 -> 11; matrix products, arithmetic and copies ran while one was open for 0% -> 0% of each run, Pallas kernels for 14% -> 20%
where the time goes in v4:
time: 81.9 us; the launch traced here: 81.7 us
  starting transfers between devices  33.1 us (40%)
  Pallas kernels  28.7 us (35%)
  waiting for transfers between devices  18.5 us (23%)
  local copies, waits for them, and re-layouts  1.14 us (1%)
    ppermute x28, starting transfers between devices, trade(): return lax.ppermute(array, axis, [(k, k ^ turn) for k in range(count)])  33.1 us
    ppermute x28, waiting for transfers between devices, trade(): return lax.ppermute(array, axis, [(k, k ^ turn) for k in range(count)])  18.5 us
    pallas_call x2, Pallas kernels, attend(): pl.pallas_call(functools.partial(attend_kernel, kv_heads, heads // kv_hea...  10.8 us
    pallas_call x11, Pallas kernels, local_call(): return call if after is None else lambda *args: call(*args, after)  8.44 us
    pallas_call x1, Pallas kernels, every_row_body(): local_call(functools.partial(lift_kernel, chunks, tile), [shape((all_rows...  5.48 us
    pallas_call x1, Pallas kernels, every_row_body(): local_call(lower_kernel, [shape((all_rows, share), F32)] * 2, [SMEM, VMEM...  1.96 us
  transfers between devices with their start and end apart: 28, of which 11 were waited for; matrix products, arithmetic and copies ran while one was open for 0% of the time, Pallas kernels for 20%

profile of v4, /device:TPU:0, one launch (start us, length us, event | category | flops | bytes accessed | tf_op | source)
XLA Modules:
  0.0 81.7 jit_solution(7118968541541297013)
XLA Ops:
  0.0 5.4 %attend.2 = (bf16[32,1536]{1,0:T(8,128)(2,1)}, bf16[32,1536]{1,0:T(8,128)(2,1)}) custom-call(s32[64]{0:T(128)} %lengths_hbm.3, bf16[64,1536]{1,0:T(8,128)(2,1)} %q_hbm.3, bf16[2,64,256]{2,1,0:T(8,128)(2,1)} %fresh_hbm.3, bf16[2,64,192,256]{3,2,1,0:T(8,128)(2,1)} %cache_ref.3, s32[64]{0:T(128)} %lengths_hbm.3), custom_call_target="tpu_custom_call" | custom-call | flops 1024 | bytes 1024 | tf_op jit(solution)/shard_map/attend/pallas_call | solution.py:132
  5.4 5.1 %collective-permute-start.5 = (bf16[32,1536]{1,0:T(8,128)(2,1)}, bf16[32,1536]{1,0:T(8,128)(2,1)S(1)}, u32[]{:S(2)}, u32[]{:S(2)}) collective-permute-start(bf16[32,1536]{1,0:T(8,128)(2,1)} %get-tuple-element.31), channel_id=1, source_target_pairs={{0,12},{4,8},{8,4},{12,0},{1,13},{5,9},{9,5},{13,1},{2,14},{6,10},... | collective-permute-start | bytes 294920 | tf_op jit(solution)/shard_map/ppermute | solution.py:292
  11.2 5.4 %attend.3 = (bf16[32,1536]{1,0:T(8,128)(2,1)}, bf16[32,1536]{1,0:T(8,128)(2,1)}) custom-call(s32[64]{0:T(128)} %lengths_hbm.3, bf16[64,1536]{1,0:T(8,128)(2,1)} %q_hbm.3, bf16[2,64,256]{2,1,0:T(8,128)(2,1)} %fresh_hbm.3, bf16[2,64,192,256]{3,2,1,0:T(8,128)(2,1)} %cache_ref.3, bf16[32,1536]{1,0:T(8,128)(2,1)} %get-tuple-element.28.after_ref.refs_1_), custom_call_target="tpu_custom_call" | custom-call | flops 1024 | bytes 1024 | tf_op jit(solution)/shard_map/attend/pallas_call | solution.py:132
  16.6 3.8 %collective-permute-start.2 = (bf16[32,1536]{1,0:T(8,128)(2,1)}, bf16[32,1536]{1,0:T(8,128)(2,1)S(1)}, u32[]{:S(2)}, u32[]{:S(2)}) collective-permute-start(bf16[32,1536]{1,0:T(8,128)(2,1)} %get-tuple-element.30), channel_id=1, source_target_pairs={{0,12},{4,8},{8,4},{12,0},{1,13},{5,9},{9,5},{13,1},{2,14},{6,10},... | collective-permute-start | bytes 294920 | tf_op jit(solution)/shard_map/ppermute | solution.py:292
  22.1 1.0 %project.2 = (bf16[32,768]{1,0:T(8,128)(2,1)S(1)}, bf16[32,768]{1,0:T(8,128)(2,1)S(1)}, bf16[32,768]{1,0:T(8,128)(2,1)S(1)}, bf16[32,768]{1,0:T(8,128)(2,1)S(1)}) custom-call(s32[2]{0:T(128)S(1)} %pad_add_fusion.refs_0_.place_ref, bf16[32,1536]{1,0:T(8,128)(2,1)S(1)} %copy-done.1, bf16[32,1536]{1,0:T(8,128)(2,1)S(1)} %collective-permute-done.3.refs_2_, ...), custom_call_target="tpu_custom_call" | custom-call | flops 1024 | bytes 1024 | tf_op jit(solution)/shard_map/project/pallas_call | solution.py:39
  23.2 1.7 %collective-permute-start.10 = (bf16[32,768]{1,0:T(8,128)(2,1)S(1)}, bf16[32,768]{1,0:T(8,128)(2,1)S(1)}, u32[]{:S(2)}, u32[]{:S(2)}) collective-permute-start(bf16[32,768]{1,0:T(8,128)(2,1)S(1)} %get-tuple-element.38), channel_id=1, source_target_pairs={{0,2},{1,3},{2,0},{3,1},{4,6},{5,7},{6,4},{7,5},{8,10},{9,11},{10,... | collective-permute-start | bytes 147464 | tf_op jit(solution)/shard_map/ppermute | solution.py:292
  25.1 3.0 %collective-permute-done.1.refs_3_ = bf16[32,1536]{1,0:T(8,128)(2,1)S(1)} collective-permute-done((bf16[32,1536]{1,0:T(8,128)(2,1)}, bf16[32,1536]{1,0:T(8,128)(2,1)S(1)}, u32[]{:S(2)}, u32[]{:S(2)}) %collective-permute-start.1) | collective-permute-done | bytes 98336 | tf_op jit(solution)/shard_map/ppermute | solution.py:292
  29.2 1.6 %collective-permute-start.7 = (bf16[32,768]{1,0:T(8,128)(2,1)S(1)}, bf16[32,768]{1,0:T(8,128)(2,1)S(1)}, u32[]{:S(2)}, u32[]{:S(2)}) collective-permute-start(bf16[32,768]{1,0:T(8,128)(2,1)S(1)} %get-tuple-element.35), channel_id=1, source_target_pairs={{0,2},{1,3},{2,0},{3,1},{4,6},{5,7},{6,4},{7,5},{8,10},{9,11},{10,... | collective-permute-start | bytes 147464 | tf_op jit(solution)/shard_map/ppermute | solution.py:292
  31.1 2.6 %collective-permute-start.17 = (bf16[32,768]{1,0:T(8,128)(2,1)S(1)}, bf16[32,768]{1,0:T(8,128)(2,1)S(1)}, u32[]{:S(2)}, u32[]{:S(2)}) collective-permute-start(bf16[32,768]{1,0:T(8,128)(2,1)S(1)} %add.4.refs_4_.refs_2_), channel_id=1, source_target_pairs={{0,12},{4,8},{8,4},{12,0},{1,13},{5,9},{9,5},{13,1},{2,14},{6,10},... | collective-permute-start | bytes 147464 | tf_op jit(solution)/shard_map/ppermute | solution.py:292
  33.7 1.8 %collective-permute-start.15 = (bf16[32,768]{1,0:T(8,128)(2,1)S(1)}, bf16[32,768]{1,0:T(8,128)(2,1)S(1)}, u32[]{:S(2)}, u32[]{:S(2)}) collective-permute-start(bf16[32,768]{1,0:T(8,128)(2,1)S(1)} %add.4.refs_4_.refs_2_), channel_id=1, source_target_pairs={{0,4},{4,0},{8,12},{12,8},{1,5},{5,1},{9,13},{13,9},{2,6},{6,2},{1... | collective-permute-start | bytes 147464 | tf_op jit(solution)/shard_map/ppermute | solution.py:292
  35.6 2.6 %collective-permute-start.14 = (bf16[32,768]{1,0:T(8,128)(2,1)S(1)}, bf16[32,768]{1,0:T(8,128)(2,1)S(1)}, u32[]{:S(2)}, u32[]{:S(2)}) collective-permute-start(bf16[32,768]{1,0:T(8,128)(2,1)S(1)} %add.5.refs_6_.refs_2_), channel_id=1, source_target_pairs={{0,12},{4,8},{8,4},{12,0},{1,13},{5,9},{9,5},{13,1},{2,14},{6,10},... | collective-permute-start | bytes 147464 | tf_op jit(solution)/shard_map/ppermute | solution.py:292
  38.2 1.8 %collective-permute-start.12 = (bf16[32,768]{1,0:T(8,128)(2,1)S(1)}, bf16[32,768]{1,0:T(8,128)(2,1)S(1)}, u32[]{:S(2)}, u32[]{:S(2)}) collective-permute-start(bf16[32,768]{1,0:T(8,128)(2,1)S(1)} %add.5.refs_6_.refs_2_), channel_id=1, source_target_pairs={{0,4},{4,0},{8,12},{12,8},{1,5},{5,1},{9,13},{13,9},{2,6},{6,2},{1... | collective-permute-start | bytes 147464 | tf_op jit(solution)/shard_map/ppermute | solution.py:292
  40.9 1.6 %collective-permute-start.18 = (bf16[32,3072]{1,0:T(8,128)(2,1)S(1)}, bf16[32,3072]{1,0:T(8,128)(2,1)S(1)}, u32[]{:S(2)}, u32[]{:S(2)}) collective-permute-start(bf16[32,3072]{1,0:T(8,128)(2,1)S(1)} %norm.2.refs_6_.refs_0_), channel_id=1, source_target_pairs={{0,2},{1,3},{2,0},{3,1},{4,6},{5,7},{6,4},{7,5},{8,10},{9,11},{10,... | collective-permute-start | bytes 589832 | tf_op jit(solution)/shard_map/ppermute | solution.py:292
  44.2 1.6 %collective-permute-start.20 = (bf16[32,3072]{1,0:T(8,128)(2,1)S(1)}, bf16[32,3072]{1,0:T(8,128)(2,1)S(1)}, u32[]{:S(2)}, u32[]{:S(2)}) collective-permute-start(bf16[32,3072]{1,0:T(8,128)(2,1)S(1)} %norm.3.refs_3_.refs_0_), channel_id=1, source_target_pairs={{0,2},{1,3},{2,0},{3,1},{4,6},{5,7},{6,4},{7,5},{8,10},{9,11},{10,... | collective-permute-start | bytes 589832 | tf_op jit(solution)/shard_map/ppermute | solution.py:292
  46.6 3.4 %load.1.refs_2_.refs_4_ = bf16[1344,3072]{1,0:T(8,128)(2,1)S(1)} custom-call(bf16[1344,3072]{1,0:T(8,128)(2,1)} %bitcast.9, f32[4,64,128]{2,1,0:T(8,128)S(1)} %gates.1.refs_1_.gate_ref), custom_call_target="tpu_custom_call" | custom-call | flops 1024 | bytes 1024 | tf_op jit(solution)/shard_map/load/pallas_call | solution.py:39
  51.7 1.2 %collective-permute-done.21.refs_3_ = bf16[2,32,3072]{2,1,0:T(8,128)(2,1)S(1)} collective-permute-done((bf16[2,32,3072]{2,1,0:T(8,128)(2,1)S(1)}, bf16[2,32,3072]{2,1,0:T(8,128)(2,1)S(1)}, u32[]{:S(2)}, u32[]{:S(2)}) %collective-permute-start.21) | collective-permute-done | bytes 393248 | tf_op jit(solution)/shard_map/ppermute | solution.py:292
  53.5 5.5 %lift.1 = (bf16[256,1344]{1,0:T(8,128)(2,1)S(1)}, bf16[2,256,768]{2,1,0:T(8,128)(2,1)S(1)}, bf16[1344,3072]{1,0:T(8,128)(2,1)S(1)}) custom-call(s32[2]{0:T(128)S(1)} %pad_add_fusion.refs_0_.place_ref, bf16[2,32,3072]{2,1,0:T(8,128)(2,1)S(1)} %pair.2.refs_2_.refs_0_, bf16[2,32,3072]{2,1,0:T(8,128)(2,1)S(1)} %collective-permute-done.19.refs_1_, ...), custom_call_target="tpu_custom_call" | custom-call | flops 1024 | bytes 1024 | tf_op jit(solution)/shard_map/lift/pallas_call | solution.py:386
  59.1 2.0 %lower.1 = (f32[256,768]{1,0:T(8,128)S(1)}, f32[256,768]{1,0:T(8,128)S(1)}) custom-call(s32[2]{0:T(128)S(1)} %pad_add_fusion.refs_0_.place_ref, bf16[256,1344]{1,0:T(8,128)(2,1)S(1)} %get-tuple-element.40.active_ref, bf16[1344,3072]{1,0:T(8,128)(2,1)S(1)} %get-tuple-element.41.down_ref), custom_call_target="tpu_custom_call" | custom-call | flops 1024 | bytes 1024 | tf_op jit(solution)/shard_map/lower/pallas_call | solution.py:402
  61.9 1.4 %collective-permute-start.24 = (bf16[128,768]{1,0:T(8,128)(2,1)S(1)}, bf16[128,768]{1,0:T(8,128)(2,1)S(1)}, u32[]{:S(2)}, u32[]{:S(2)}) collective-permute-start(bf16[128,768]{1,0:T(8,128)(2,1)S(1)} %get-tuple-element.46), channel_id=1, source_target_pairs={{0,2},{1,3},{2,0},{3,1},{4,6},{5,7},{6,4},{7,5},{8,10},{9,11},{10,... | collective-permute-start | bytes 589832 | tf_op jit(solution)/shard_map/ppermute | solution.py:292
  64.0 5.7 %collective-permute-done.24.crossed_ref = bf16[128,768]{1,0:T(8,128)(2,1)S(1)} collective-permute-done((bf16[128,768]{1,0:T(8,128)(2,1)S(1)}, bf16[128,768]{1,0:T(8,128)(2,1)S(1)}, u32[]{:S(2)}, u32[]{:S(2)}) %collective-permute-start.24) | collective-permute-done | bytes 196640 | tf_op jit(solution)/shard_map/ppermute | solution.py:292
  70.3 2.5 %collective-permute-start.27 = (bf16[64,768]{1,0:T(8,128)(2,1)S(1)}, bf16[64,768]{1,0:T(8,128)(2,1)S(1)}, u32[]{:S(2)}, u32[]{:S(2)}) collective-permute-start(bf16[64,768]{1,0:T(8,128)(2,1)S(1)} %get-tuple-element.50), channel_id=1, source_target_pairs={{0,12},{4,8},{8,4},{12,0},{1,13},{5,9},{9,5},{13,1},{2,14},{6,10},... | collective-permute-start | bytes 294920 | tf_op jit(solution)/shard_map/ppermute | solution.py:292
  73.9 1.6 %collective-permute-start.25 = (bf16[64,768]{1,0:T(8,128)(2,1)S(1)}, bf16[64,768]{1,0:T(8,128)(2,1)S(1)}, u32[]{:S(2)}, u32[]{:S(2)}) collective-permute-start(bf16[64,768]{1,0:T(8,128)(2,1)S(1)} %get-tuple-element.49), channel_id=1, source_target_pairs={{0,4},{4,0},{8,12},{12,8},{1,5},{5,1},{9,13},{13,9},{2,6},{6,2},{1... | collective-permute-start | bytes 294920 | tf_op jit(solution)/shard_map/ppermute | solution.py:292
  75.5 1.5 %collective-permute-done.27.refs_1_ = bf16[64,768]{1,0:T(8,128)(2,1)S(1)} collective-permute-done((bf16[64,768]{1,0:T(8,128)(2,1)S(1)}, bf16[64,768]{1,0:T(8,128)(2,1)S(1)}, u32[]{:S(2)}, u32[]{:S(2)}) %collective-permute-start.27) | collective-permute-done | bytes 98336 | tf_op jit(solution)/shard_map/ppermute | solution.py:292
  77.0 3.9 %collective-permute-done.26.refs_0_ = bf16[64,768]{1,0:T(8,128)(2,1)S(1)} collective-permute-done((bf16[64,768]{1,0:T(8,128)(2,1)S(1)}, bf16[64,768]{1,0:T(8,128)(2,1)S(1)}, u32[]{:S(2)}, u32[]{:S(2)}) %collective-permute-start.26) | collective-permute-done | bytes 98336 | tf_op jit(solution)/shard_map/ppermute | solution.py:292
  (66 shorter events, 13.9 us)
Async XLA Ops:
  5.4 15.0 %collective-permute-start.5 = (bf16[32,1536]{1,0:T(8,128)(2,1)}, bf16[32,1536]{1,0:T(8,128)(2,1)S(1)}, u32[]{:S(2)}, u32[]{:S(2)}) collective-permute-start(bf16[32,1536]{1,0:T(8,128)(2,1)} %get-tuple-element.31), channel_id=1, source_target_pairs={{0,12},{4,8},{8,4},{12,0},{1,13},{5,9},{9,5},{13,1},{2,14},{6,10},... | collective-permute-start | bytes 294920 | tf_op jit(solution)/shard_map/ppermute | solution.py:292
  10.5 10.6 %collective-permute-start.4 = (bf16[32,1536]{1,0:T(8,128)(2,1)}, bf16[32,1536]{1,0:T(8,128)(2,1)S(1)}, u32[]{:S(2)}, u32[]{:S(2)}) collective-permute-start(bf16[32,1536]{1,0:T(8,128)(2,1)} %get-tuple-element.31), channel_id=1, source_target_pairs={{0,8},{4,12},{8,0},{12,4},{1,9},{5,13},{9,1},{13,5},{2,10},{6,14},... | collective-permute-start | bytes 294920 | tf_op jit(solution)/shard_map/ppermute | solution.py:292
  10.5 10.6 %collective-permute-start.3 = (bf16[32,1536]{1,0:T(8,128)(2,1)}, bf16[32,1536]{1,0:T(8,128)(2,1)S(1)}, u32[]{:S(2)}, u32[]{:S(2)}) collective-permute-start(bf16[32,1536]{1,0:T(8,128)(2,1)} %get-tuple-element.31), channel_id=1, source_target_pairs={{0,4},{4,0},{8,12},{12,8},{1,5},{5,1},{9,13},{13,9},{2,6},{6,2},{1... | collective-permute-start | bytes 294920 | tf_op jit(solution)/shard_map/ppermute | solution.py:292
  16.6 8.3 %collective-permute-start.2 = (bf16[32,1536]{1,0:T(8,128)(2,1)}, bf16[32,1536]{1,0:T(8,128)(2,1)S(1)}, u32[]{:S(2)}, u32[]{:S(2)}) collective-permute-start(bf16[32,1536]{1,0:T(8,128)(2,1)} %get-tuple-element.30), channel_id=1, source_target_pairs={{0,12},{4,8},{8,4},{12,0},{1,13},{5,9},{9,5},{13,1},{2,14},{6,10},... | collective-permute-start | bytes 294920 | tf_op jit(solution)/shard_map/ppermute | solution.py:292
  20.5 7.6 %collective-permute-start.1 = (bf16[32,1536]{1,0:T(8,128)(2,1)}, bf16[32,1536]{1,0:T(8,128)(2,1)S(1)}, u32[]{:S(2)}, u32[]{:S(2)}) collective-permute-start(bf16[32,1536]{1,0:T(8,128)(2,1)} %get-tuple-element.30), channel_id=1, source_target_pairs={{0,8},{4,12},{8,0},{12,4},{1,9},{5,13},{9,1},{13,5},{2,10},{6,14},... | collective-permute-start | bytes 294920 | tf_op jit(solution)/shard_map/ppermute | solution.py:292
  20.5 7.6 %collective-permute-start = (bf16[32,1536]{1,0:T(8,128)(2,1)}, bf16[32,1536]{1,0:T(8,128)(2,1)S(1)}, u32[]{:S(2)}, u32[]{:S(2)}) collective-permute-start(bf16[32,1536]{1,0:T(8,128)(2,1)} %get-tuple-element.30), channel_id=1, source_target_pairs={{0,4},{4,0},{8,12},{12,8},{1,5},{5,1},{9,13},{13,9},{2,6},{6,2},{1... | collective-permute-start | bytes 294920 | tf_op jit(solution)/shard_map/ppermute | solution.py:292
  23.1 7.6 %collective-permute-start.9 = (bf16[32,768]{1,0:T(8,128)(2,1)S(1)}, bf16[32,768]{1,0:T(8,128)(2,1)S(1)}, u32[]{:S(2)}, u32[]{:S(2)}) collective-permute-start(bf16[32,768]{1,0:T(8,128)(2,1)S(1)} %get-tuple-element.37), channel_id=1, source_target_pairs={{0,1},{1,0},{2,3},{3,2},{4,5},{5,4},{6,7},{7,6},{8,9},{9,8},{10,11... | collective-permute-start | bytes 147464 | tf_op jit(solution)/shard_map/ppermute | solution.py:292
  23.2 7.8 %collective-permute-start.10 = (bf16[32,768]{1,0:T(8,128)(2,1)S(1)}, bf16[32,768]{1,0:T(8,128)(2,1)S(1)}, u32[]{:S(2)}, u32[]{:S(2)}) collective-permute-start(bf16[32,768]{1,0:T(8,128)(2,1)S(1)} %get-tuple-element.38), channel_id=1, source_target_pairs={{0,2},{1,3},{2,0},{3,1},{4,6},{5,7},{6,4},{7,5},{8,10},{9,11},{10,... | collective-permute-start | bytes 147464 | tf_op jit(solution)/shard_map/ppermute | solution.py:292
  24.9 6.1 %collective-permute-start.11 = (bf16[32,768]{1,0:T(8,128)(2,1)S(1)}, bf16[32,768]{1,0:T(8,128)(2,1)S(1)}, u32[]{:S(2)}, u32[]{:S(2)}) collective-permute-start(bf16[32,768]{1,0:T(8,128)(2,1)S(1)} %get-tuple-element.39), channel_id=1, source_target_pairs={{0,3},{1,2},{2,1},{3,0},{4,7},{5,6},{6,5},{7,4},{8,11},{9,10},{10,... | collective-permute-start | bytes 147464 | tf_op jit(solution)/shard_map/ppermute | solution.py:292
  29.2 6.4 %collective-permute-start.7 = (bf16[32,768]{1,0:T(8,128)(2,1)S(1)}, bf16[32,768]{1,0:T(8,128)(2,1)S(1)}, u32[]{:S(2)}, u32[]{:S(2)}) collective-permute-start(bf16[32,768]{1,0:T(8,128)(2,1)S(1)} %get-tuple-element.35), channel_id=1, source_target_pairs={{0,2},{1,3},{2,0},{3,1},{4,6},{5,7},{6,4},{7,5},{8,10},{9,11},{10,... | collective-permute-start | bytes 147464 | tf_op jit(solution)/shard_map/ppermute | solution.py:292
  30.7 4.8 %collective-permute-start.8 = (bf16[32,768]{1,0:T(8,128)(2,1)S(1)}, bf16[32,768]{1,0:T(8,128)(2,1)S(1)}, u32[]{:S(2)}, u32[]{:S(2)}) collective-permute-start(bf16[32,768]{1,0:T(8,128)(2,1)S(1)} %get-tuple-element.36), channel_id=1, source_target_pairs={{0,3},{1,2},{2,1},{3,0},{4,7},{5,6},{6,5},{7,4},{8,11},{9,10},{10,... | collective-permute-start | bytes 147464 | tf_op jit(solution)/shard_map/ppermute | solution.py:292
  31.1 7.1 %collective-permute-start.17 = (bf16[32,768]{1,0:T(8,128)(2,1)S(1)}, bf16[32,768]{1,0:T(8,128)(2,1)S(1)}, u32[]{:S(2)}, u32[]{:S(2)}) collective-permute-start(bf16[32,768]{1,0:T(8,128)(2,1)S(1)} %add.4.refs_4_.refs_2_), channel_id=1, source_target_pairs={{0,12},{4,8},{8,4},{12,0},{1,13},{5,9},{9,5},{13,1},{2,14},{6,10},... | collective-permute-start | bytes 147464 | tf_op jit(solution)/shard_map/ppermute | solution.py:292
  33.7 6.3 %collective-permute-start.16 = (bf16[32,768]{1,0:T(8,128)(2,1)S(1)}, bf16[32,768]{1,0:T(8,128)(2,1)S(1)}, u32[]{:S(2)}, u32[]{:S(2)}) collective-permute-start(bf16[32,768]{1,0:T(8,128)(2,1)S(1)} %add.4.refs_4_.refs_2_), channel_id=1, source_target_pairs={{0,8},{4,12},{8,0},{12,4},{1,9},{5,13},{9,1},{13,5},{2,10},{6,14},... | collective-permute-start | bytes 147464 | tf_op jit(solution)/shard_map/ppermute | solution.py:292
  33.7 6.3 %collective-permute-start.15 = (bf16[32,768]{1,0:T(8,128)(2,1)S(1)}, bf16[32,768]{1,0:T(8,128)(2,1)S(1)}, u32[]{:S(2)}, u32[]{:S(2)}) collective-permute-start(bf16[32,768]{1,0:T(8,128)(2,1)S(1)} %add.4.refs_4_.refs_2_), channel_id=1, source_target_pairs={{0,4},{4,0},{8,12},{12,8},{1,5},{5,1},{9,13},{13,9},{2,6},{6,2},{1... | collective-permute-start | bytes 147464 | tf_op jit(solution)/shard_map/ppermute | solution.py:292
  35.6 6.9 %collective-permute-start.14 = (bf16[32,768]{1,0:T(8,128)(2,1)S(1)}, bf16[32,768]{1,0:T(8,128)(2,1)S(1)}, u32[]{:S(2)}, u32[]{:S(2)}) collective-permute-start(bf16[32,768]{1,0:T(8,128)(2,1)S(1)} %add.5.refs_6_.refs_2_), channel_id=1, source_target_pairs={{0,12},{4,8},{8,4},{12,0},{1,13},{5,9},{9,5},{13,1},{2,14},{6,10},... | collective-permute-start | bytes 147464 | tf_op jit(solution)/shard_map/ppermute | solution.py:292
  38.2 5.2 %collective-permute-start.13 = (bf16[32,768]{1,0:T(8,128)(2,1)S(1)}, bf16[32,768]{1,0:T(8,128)(2,1)S(1)}, u32[]{:S(2)}, u32[]{:S(2)}) collective-permute-start(bf16[32,768]{1,0:T(8,128)(2,1)S(1)} %add.5.refs_6_.refs_2_), channel_id=1, source_target_pairs={{0,8},{4,12},{8,0},{12,4},{1,9},{5,13},{9,1},{13,5},{2,10},{6,14},... | collective-permute-start | bytes 147464 | tf_op jit(solution)/shard_map/ppermute | solution.py:292
  38.2 5.1 %collective-permute-start.12 = (bf16[32,768]{1,0:T(8,128)(2,1)S(1)}, bf16[32,768]{1,0:T(8,128)(2,1)S(1)}, u32[]{:S(2)}, u32[]{:S(2)}) collective-permute-start(bf16[32,768]{1,0:T(8,128)(2,1)S(1)} %add.5.refs_6_.refs_2_), channel_id=1, source_target_pairs={{0,4},{4,0},{8,12},{12,8},{1,5},{5,1},{9,13},{13,9},{2,6},{6,2},{1... | collective-permute-start | bytes 147464 | tf_op jit(solution)/shard_map/ppermute | solution.py:292
  40.9 9.1 %collective-permute-start.18 = (bf16[32,3072]{1,0:T(8,128)(2,1)S(1)}, bf16[32,3072]{1,0:T(8,128)(2,1)S(1)}, u32[]{:S(2)}, u32[]{:S(2)}) collective-permute-start(bf16[32,3072]{1,0:T(8,128)(2,1)S(1)} %norm.2.refs_6_.refs_0_), channel_id=1, source_target_pairs={{0,2},{1,3},{2,0},{3,1},{4,6},{5,7},{6,4},{7,5},{8,10},{9,11},{10,... | collective-permute-start | bytes 589832 | tf_op jit(solution)/shard_map/ppermute | solution.py:292
  44.2 6.9 %collective-permute-start.20 = (bf16[32,3072]{1,0:T(8,128)(2,1)S(1)}, bf16[32,3072]{1,0:T(8,128)(2,1)S(1)}, u32[]{:S(2)}, u32[]{:S(2)}) collective-permute-start(bf16[32,3072]{1,0:T(8,128)(2,1)S(1)} %norm.3.refs_3_.refs_0_), channel_id=1, source_target_pairs={{0,2},{1,3},{2,0},{3,1},{4,6},{5,7},{6,4},{7,5},{8,10},{9,11},{10,... | collective-permute-start | bytes 589832 | tf_op jit(solution)/shard_map/ppermute | solution.py:292
  61.9 7.8 %collective-permute-start.24 = (bf16[128,768]{1,0:T(8,128)(2,1)S(1)}, bf16[128,768]{1,0:T(8,128)(2,1)S(1)}, u32[]{:S(2)}, u32[]{:S(2)}) collective-permute-start(bf16[128,768]{1,0:T(8,128)(2,1)S(1)} %get-tuple-element.46), channel_id=1, source_target_pairs={{0,2},{1,3},{2,0},{3,1},{4,6},{5,7},{6,4},{7,5},{8,10},{9,11},{10,... | collective-permute-start | bytes 589832 | tf_op jit(solution)/shard_map/ppermute | solution.py:292
  63.3 10.0 %collective-permute-start.23 = (bf16[128,768]{1,0:T(8,128)(2,1)S(1)}, bf16[128,768]{1,0:T(8,128)(2,1)S(1)}, u32[]{:S(2)}, u32[]{:S(2)}) collective-permute-start(bf16[128,768]{1,0:T(8,128)(2,1)S(1)} %get-tuple-element.45), channel_id=1, source_target_pairs={{0,2},{1,3},{2,0},{3,1},{4,6},{5,7},{6,4},{7,5},{8,10},{9,11},{10,... | collective-permute-start | bytes 589832 | tf_op jit(solution)/shard_map/ppermute | solution.py:292
  70.3 6.6 %collective-permute-start.27 = (bf16[64,768]{1,0:T(8,128)(2,1)S(1)}, bf16[64,768]{1,0:T(8,128)(2,1)S(1)}, u32[]{:S(2)}, u32[]{:S(2)}) collective-permute-start(bf16[64,768]{1,0:T(8,128)(2,1)S(1)} %get-tuple-element.50), channel_id=1, source_target_pairs={{0,12},{4,8},{8,4},{12,0},{1,13},{5,9},{9,5},{13,1},{2,14},{6,10},... | collective-permute-start | bytes 294920 | tf_op jit(solution)/shard_map/ppermute | solution.py:292
  72.9 8.0 %collective-permute-start.26 = (bf16[64,768]{1,0:T(8,128)(2,1)S(1)}, bf16[64,768]{1,0:T(8,128)(2,1)S(1)}, u32[]{:S(2)}, u32[]{:S(2)}) collective-permute-start(bf16[64,768]{1,0:T(8,128)(2,1)S(1)} %get-tuple-element.47.refs_4_), channel_id=1, source_target_pairs={{0,8},{4,12},{8,0},{12,4},{1,9},{5,13},{9,1},{13,5},{2,10},{6,14},... | collective-permute-start | bytes 294920 | tf_op jit(solution)/shard_map/ppermute | solution.py:292
  73.9 7.2 %collective-permute-start.25 = (bf16[64,768]{1,0:T(8,128)(2,1)S(1)}, bf16[64,768]{1,0:T(8,128)(2,1)S(1)}, u32[]{:S(2)}, u32[]{:S(2)}) collective-permute-start(bf16[64,768]{1,0:T(8,128)(2,1)S(1)} %get-tuple-element.49), channel_id=1, source_target_pairs={{0,4},{4,0},{8,12},{12,8},{1,5},{5,1},{9,13},{13,9},{2,6},{6,2},{1... | collective-permute-start | bytes 294920 | tf_op jit(solution)/shard_map/ppermute | solution.py:292
  (10 other events, 141.5 us)

commit v5 on v4

--- a/solution.py
+++ b/solution.py
@@ -41,9 +41,8 @@
 
 def attend_kernel(
     kv_heads, group, slots, batch, begin,
-    lengths_hbm, q_hbm, fresh_hbm, cache_ref, after_ref, out_ref, again_ref,
-    lengths_ref, q_ref, fresh_ref, keys, values, q_rows, scores, own_scores, probs, own_probs,
-    mixed, sems, small_sems,
+    small_ref, cache_ref, after_ref, out_ref,
+    keys, values, q_rows, scores, own_scores, probs, own_probs, mixed, sems,
 ):
     rows = out_ref.shape[0]
     context = keys.shape[1]
@@ -51,6 +50,8 @@
     heads = kv_heads * group
     steps = rows // batch
     scale = 1.0 / math.sqrt(HD)
+    fresh = [slice(heads * HD + k * width, heads * HD + (k + 1) * width) for k in range(2)]
+    spans = slice(heads * HD + 2 * width, heads * HD + 2 * width + context)
 
     def fetch(step, kind):
         buffer = (keys, values)[kind]
@@ -60,29 +61,20 @@
             sems.at[kind, step],
         )
 
-    part = pl.ds(begin, rows)
-    small = [
-        pltpu.make_async_copy(q_hbm.at[part], q_ref, small_sems.at[0]),
-        pltpu.make_async_copy(lengths_hbm, lengths_ref, small_sems.at[1]),
-        pltpu.make_async_copy(fresh_hbm.at[:, part], fresh_ref, small_sems.at[2]),
-    ]
-    for copy in small:
-        copy.start()
     for step in range(steps):
         for kind in range(2):
             fetch(step, kind).start()
     q_rows[...] = jnp.zeros_like(q_rows)
-    for copy in small:
-        copy.wait()
     for head in range(heads):
-        q_rows[head // group, pl.ds(head, rows, stride=slots), :] = q_ref[
-            :, head * HD : (head + 1) * HD
+        q_rows[head // group, pl.ds(head, rows, stride=slots), :] = small_ref[
+            begin : begin + rows, head * HD : (head + 1) * HD
         ].astype(F32)
-    place = lax.broadcasted_iota(jnp.int32, (slots, context), 1)
+    place = lax.broadcasted_iota(jnp.int32, (slots, context), 1).astype(F32)
     for step in range(steps):
         fetch(step, 0).wait()
         for k in range(batch):
             row = step * batch + k
+            whole = slice(begin + row, begin + row + 1)
             mine = jnp.concatenate(
                 [q_rows[g, row * slots : (row + 1) * slots, :] for g in range(kv_heads)], axis=1
             )
@@ -91,8 +83,9 @@
                 preferred_element_type=F32,
             )
             here = slice(k * slots, (k + 1) * slots)
-            scores[here, :] = jnp.where(place < lengths_ref[begin + row], cached * scale, -jnp.inf)
-            fresh_key = fresh_ref[0, row : row + 1, :].astype(F32)
+            seen = place < small_ref[whole, spans].astype(F32)
+            scores[here, :] = jnp.where(seen, cached * scale, -jnp.inf)
+            fresh_key = small_ref[whole, fresh[0]].astype(F32)
             own_scores[here, :] = jnp.broadcast_to(
                 jnp.sum(mine * fresh_key, axis=1, keepdims=True) * scale, (slots, HD)
             )
@@ -109,35 +102,37 @@
         fetch(step, 1).wait()
         for k in range(batch):
             row = step * batch + k
+            whole = slice(begin + row, begin + row + 1)
             here = slice(k * slots, (k + 1) * slots)
             weighted = jnp.dot(probs[here, :], values[row], preferred_element_type=F32)
-            fresh_value = fresh_ref[1, row : row + 1, :].astype(F32)
+            fresh_value = small_ref[whole, fresh[1]].astype(F32)
             total = weighted + own_probs[here, :1] * fresh_value
             for g in range(kv_heads):
                 mixed[g, here, :] = total[:, g * HD : (g + 1) * HD]
         for head in range(heads):
-            there = (slice(step * batch, (step + 1) * batch), slice(head * HD, (head + 1) * HD))
-            done = mixed[head // group, pl.ds(head, batch, stride=slots), :].astype(BF16)
-            out_ref[there] = done
-            again_ref[there] = done
-
-
-def attend(queries, new_kv, kv_cache, lengths, begin, rows, after):
-    features = queries.shape[1]
+            out_ref[step * batch : (step + 1) * batch, head * HD : (head + 1) * HD] = mixed[
+                head // group, pl.ds(head, batch, stride=slots), :
+            ].astype(BF16)
+
+
+def beside(queries, new_kv, lengths, context):
+    lanes = -(-context // HD) * HD
+    spans = jnp.broadcast_to(lengths.astype(BF16)[:, None], (lengths.shape[0], lanes))
+    return jnp.concatenate([queries, new_kv[0], new_kv[1], spans], axis=1)
+
+
+def attend(small, kv_cache, heads, begin, rows, after):
     context, width = kv_cache.shape[2:]
     kv_heads = width // HD
-    heads = features // HD
     slots = -(-heads // 8) * 8
     batch = 16
+    shape = jax.ShapeDtypeStruct((rows, heads * HD), BF16)
     return pl.pallas_call(
         functools.partial(attend_kernel, kv_heads, heads // kv_heads, slots, batch, begin),
-        out_shape=[jax.ShapeDtypeStruct((rows, features), BF16)] * 2,
-        in_specs=[ANYWHERE] * 5,
-        out_specs=[VMEM] * 2,
+        out_shape=shape,
+        in_specs=[VMEM, ANYWHERE, ANYWHERE],
+        out_specs=VMEM,
         scratch_shapes=[
-            pltpu.SMEM(lengths.shape, jnp.int32),
-            pltpu.VMEM((rows, features), BF16),
-            pltpu.VMEM((2, rows, width), BF16),
             pltpu.VMEM((rows, context, width), BF16),
             pltpu.VMEM((rows, context, width), BF16),
             pltpu.VMEM((kv_heads, rows * slots, HD), F32),
@@ -147,12 +142,11 @@
             pltpu.VMEM((batch * slots, HD), F32),
             pltpu.VMEM((kv_heads, batch * slots, HD), F32),
             pltpu.SemaphoreType.DMA((2, rows // batch)),
-            pltpu.SemaphoreType.DMA((3,)),
         ],
-        compiler_params=pltpu.CompilerParams(vmem_limit_bytes=58 * MIB),
+        compiler_params=pltpu.CompilerParams(vmem_limit_bytes=50 * MIB),
         cost_estimate=pl.CostEstimate(flops=1024, bytes_accessed=1024, transcendentals=0),
         name="attend",
-    )(lengths, queries, new_kv, kv_cache, after)
+    )(small, kv_cache, after)
 
 
 def pair_kernel(own_ref, other_ref, out_ref):
@@ -192,41 +186,39 @@
 
 
 def norm_kernel(parts, place_ref, gain_ref, *refs):
-    shards, out, held = refs[:parts], refs[parts], refs[parts + 1]
+    shards, out = refs[:parts], refs[parts]
     width = shards[0].shape[1]
+    values = [shard[...].astype(F32) for shard in shards]
+    center = sum(jnp.sum(part, axis=1, keepdims=True) for part in values) / out.shape[1]
+    values = [part - center for part in values]
+    spread = sum(jnp.sum(part * part, axis=1, keepdims=True) for part in values) / out.shape[1]
+    scale = lax.rsqrt(spread + 1e-05)
     for s in range(parts):
-        first = pl.multiple_of((place_ref[0] ^ s) * width, HD)
-        held[:, pl.ds(first, width)] = shards[s][...].astype(F32)
-    values = held[...]
-    center = values - jnp.mean(values, axis=1, keepdims=True)
-    spread = jnp.mean(center * center, axis=1, keepdims=True)
-    out[...] = (center * lax.rsqrt(spread + 1e-05) * gain_ref[...]).astype(BF16)
+        here = pl.ds(pl.multiple_of((place_ref[0] ^ s) * width, HD), width)
+        out[:, here] = (values[s] * scale * gain_ref[:, here]).astype(BF16)
 
 
 def by_distance(pair_ref, second_ref):
     return pair_ref.at[0], second_ref.at[0], pair_ref.at[1], second_ref.at[1]
 
 
-def load_kernel(source_hbm, out_ref, sem):
-    copy = pltpu.make_async_copy(source_hbm, out_ref, sem)
+def load_kernel(rows, source_hbm, out_ref, sem):
+    copy = pltpu.make_async_copy(source_hbm.at[pl.ds(0, rows)], out_ref, sem)
     copy.start()
     copy.wait()
 
 
-def lift_kernel(chunks, tile, place_ref, *refs):
+def lift_kernel(chunks, place_ref, *refs):
     count = 2 * chunks
-    shards, (up_ref, down_hbm) = refs[:count], refs[count : count + 2]
-    active_ref, far_ref, down_ref, held, sems = refs[count + 2 :]
+    shards, (up_ref, down_ref, down_hbm) = refs[:count], refs[count : count + 3]
+    active_ref, far_ref, close_ref, rest_ref, held, passed, sem = refs[count + 3 :]
     hidden = active_ref.shape[1]
     share = far_ref.shape[2]
+    half = far_ref.shape[1]
     rows = shards[0].shape[1]
-    copies = []
-    for first in range(0, hidden, tile):
-        part = pl.ds(first, tile)
-        copies.append(
-            pltpu.make_async_copy(down_hbm.at[part], down_ref.at[part], sems.at[first // tile])
-        )
-        copies[-1].start()
+    cut = down_ref.shape[0]
+    copy = pltpu.make_async_copy(down_hbm.at[pl.ds(cut, hidden - cut)], rest_ref, sem)
+    copy.start()
     for c in range(chunks):
         for t, shard in enumerate(by_distance(*shards[2 * c : 2 * c + 2])):
             first = pl.multiple_of(((place_ref[1] ^ t) * chunks + c) * rows, rows)
@@ -237,52 +229,55 @@
             up_ref[first:last, :], held[...], (((1,), (1,)), ((), ())), preferred_element_type=F32
         )
         active_ref[:, first:last] = (raised / (1.0 + jnp.exp(-raised))).T.astype(BF16)
-    for copy in copies:
-        copy.wait()
+    copy.wait()
+    mine = place_ref[0] // 2
     for k in range(2):
-        first = pl.multiple_of((place_ref[1] ^ (2 * k + 1)) * share, HD)
-        far_ref[k] = jnp.dot(
-            active_ref[...], down_ref[:, pl.ds(first, share)], preferred_element_type=F32
-        ).astype(BF16)
-
-
-def lower_kernel(place_ref, active_ref, down_ref, cross_ref, own_ref):
-    share = own_ref.shape[1]
-    for out_ref, turn in ((cross_ref, 2), (own_ref, 0)):
-        first = pl.multiple_of((place_ref[1] ^ turn) * share, HD)
-        out_ref[...] = jnp.dot(
-            active_ref[...], down_ref[:, pl.ds(first, share)], preferred_element_type=F32
-        )
-
-
-def turn_kernel(place_ref, cross_ref, near_ref, far_ref, close_ref):
-    half = far_ref.shape[0]
-    mine = place_ref[0] // 2
-    for out_ref, side in ((far_ref, 1 - mine), (close_ref, mine)):
-        here = pl.ds(pl.multiple_of(side * half, half), half)
-        out_ref[...] = (cross_ref[here, :] + near_ref[1, here, :].astype(F32)).astype(BF16)
-
-
-def split_kernel(side, place_ref, own_ref, near_ref, crossed_ref, *outs):
+        passed[...] = lowered(place_ref, 2 * k + 1, active_ref, down_ref, rest_ref, share).astype(BF16)
+        for out_ref, side in ((far_ref, 1 - mine), (close_ref, mine)):
+            out_ref[k] = passed[pl.ds(pl.multiple_of(side * half, half), half), :]
+
+
+def lowered(place_ref, turn, active_ref, down_ref, rest_ref, share):
+    cut = down_ref.shape[0]
+    here = pl.ds(pl.multiple_of((place_ref[1] ^ turn) * share, HD), share)
+    return jnp.dot(
+        active_ref[:, :cut], down_ref[:, here], preferred_element_type=F32
+    ) + jnp.dot(active_ref[:, cut:], rest_ref[:, here], preferred_element_type=F32)
+
+
+def lower_kernel(turn, place_ref, active_ref, down_ref, rest_ref, out_ref):
+    out_ref[...] = lowered(place_ref, turn, active_ref, down_ref, rest_ref, out_ref.shape[1])
+
+
+def turn_kernel(distances, place_ref, cross_ref, near_ref, *outs):
     rows = outs[0].shape[0]
-    for s, out_ref in enumerate(outs):
-        z = place_ref[0] ^ (2 * side + s)
+    for distance, out_ref in zip(distances, outs):
+        z = place_ref[0] ^ distance
         here = pl.ds(pl.multiple_of(z * rows, rows), rows)
         there = pl.ds(pl.multiple_of(z % 2 * rows, rows), rows)
-        total = own_ref[here, :] + near_ref[0, here, :].astype(F32)
-        out_ref[...] = (total + crossed_ref[there, :].astype(F32)).astype(BF16)
-
-
-def mix_kernel(first, gate_ref, *refs):
+        out_ref[...] = (cross_ref[here, :] + near_ref[1, there, :].astype(F32)).astype(BF16)
+
+
+def split_kernel(distances, place_ref, own_ref, near_ref, *refs):
+    count = len(distances)
+    rows = refs[0].shape[0]
+    for distance, crossed_ref, out_ref in zip(distances, refs[:count], refs[count:]):
+        z = place_ref[0] ^ distance
+        here = pl.ds(pl.multiple_of(z * rows, rows), rows)
+        there = pl.ds(pl.multiple_of(z % 2 * rows, rows), rows)
+        total = own_ref[here, :] + near_ref[0, there, :].astype(F32)
+        out_ref[...] = (total + crossed_ref[...].astype(F32)).astype(BF16)
+
+
+def mix_kernel(distances, gate_ref, *refs):
     out = refs[-1]
-    terms = refs[:2]
-    earlier = refs[2:-1]
     lanes = gate_ref.shape[2]
     for begin in range(0, out.shape[1], lanes):
         part = slice(begin, begin + lanes)
-        total = gate_ref[first] * terms[0][:, part].astype(F32)
-        total = total + gate_ref[first + 1] * terms[1][:, part].astype(F32)
-        for ref in earlier:
+        total = sum(
+            gate_ref[s] * term[:, part].astype(F32) for s, term in zip(distances, refs)
+        )
+        for ref in refs[len(distances) : -1]:
             total = total + ref[:, part]
         out[:, part] = total.astype(out.dtype)
 
@@ -308,17 +303,19 @@
     place = jnp.stack([lax.axis_index("gx"), lax.axis_index("ta")]).astype(jnp.int32)
     shape = jax.ShapeDtypeStruct
     gain = norm_gain.reshape(1, model)
+    heads = queries.shape[1] // HD
+    small = beside(queries, new_kv, lengths, kv_cache.shape[2])
     attended = []
     for c in range(chunks):
-        after = attended[-1][1] if attended else lengths
-        attended.append(attend(queries, new_kv, kv_cache, lengths, c * rows, rows, after))
+        after = attended[-1] if attended else small
+        attended.append(attend(small, kv_cache, heads, c * rows, rows, after))
     order = [s for s in range(gx_count - 1, 0, -1)]
 
     def spread(array, axis):
         parts = {0: array, **{s: trade(array, axis, s) for s in order}}
         return [parts[s] for s in range(len(parts))]
 
-    shards = [[kept] + spread(sent, "gx")[1:] for sent, kept in attended]
+    shards = [spread(part, "gx") for part in attended]
     pieces, hidden = [], []
     for c in range(chunks):
         pieces.append(
@@ -328,7 +325,7 @@
                 [SMEM] + [VMEM] * (gx_count + 1),
                 [pltpu.VMEM((ta_count, rows, width), BF16)],
                 name="project",
-                after=pieces[-1][0] if pieces else attended[-1][1],
+                after=pieces[-1][0] if pieces else attended[-1],
             )(place, *shards[c], out_proj)
         )
     for c in range(chunks):
@@ -350,7 +347,6 @@
                 functools.partial(norm_kernel, gx_count),
                 shape((rows, model), BF16),
                 [SMEM] + [VMEM] * (gx_count + 1),
-                [pltpu.VMEM((rows, model), F32)],
                 name="norm",
                 after=normed[-1] if normed else hidden[-1],
             )(place, gain, *shards[c])
@@ -363,12 +359,12 @@
         after=normed[-1],
     )(place, expert_ids, gate_weights)
     up = local_call(
-        load_kernel,
+        functools.partial(load_kernel, hidden_share),
         shape((hidden_share, model), BF16),
         [ANYWHERE],
         [pltpu.SemaphoreType.DMA],
         vmem=40,
-        name="load",
+        name="load_up",
         after=gates,
     )(jnp.swapaxes(w_up[0], 0, 1))
     for c in range(chunks):
@@ -382,62 +378,84 @@
             )(normed[c], trade(normed[c], "ta", 2))
         )
     blocks = [block for pair in pairs for block in (pair, trade(pair, "ta", 1))]
-    tile = math.gcd(hidden_share, 3 * 64)
-    active, far, down = local_call(
-        functools.partial(lift_kernel, chunks, tile),
+    cut = -(-hidden_share // (4 * HD)) * 2 * HD
+    part = local_call(
+        functools.partial(load_kernel, cut),
+        shape((cut, model), BF16),
+        [ANYWHERE],
+        [pltpu.SemaphoreType.DMA],
+        vmem=37,
+        name="load_down",
+        after=pairs[-1],
+    )(w_down[0])
+    half = all_rows // 2
+    active, far, close, rest = local_call(
+        functools.partial(lift_kernel, chunks),
         [
             shape((all_rows, hidden_share), BF16),
-            shape((2, all_rows, share), BF16),
-            shape((hidden_share, model), BF16),
+            shape((2, half, share), BF16),
+            shape((2, half, share), BF16),
+            shape((hidden_share - cut, model), BF16),
         ],
-        [SMEM] + [VMEM] * (2 * chunks + 1) + [ANYWHERE],
+        [SMEM] + [VMEM] * (2 * chunks + 2) + [ANYWHERE],
         [
             pltpu.VMEM((all_rows, model), BF16),
-            pltpu.SemaphoreType.DMA((hidden_share // tile,)),
+            pltpu.VMEM((all_rows, share), BF16),
+            pltpu.SemaphoreType.DMA,
         ],
         vmem=30,
         name="lift",
-    )(place, *blocks, up, w_down[0])
-    near = trade(far, "ta", 1)
-    cross, own = local_call(
-        lower_kernel,
-        [shape((all_rows, share), F32)] * 2,
-        [SMEM, VMEM, VMEM],
-        vmem=16,
-        name="lower",
-    )(place, active, down)
-    half = all_rows // 2
-    far_side, close_side = local_call(
-        turn_kernel,
-        [shape((half, share), BF16)] * 2,
-        [SMEM] + [VMEM] * 2,
-        name="turn",
-    )(place, cross, near)
-    terms, after = {}, None
-    for side, crossing in ((1, far_side), (0, close_side)):
-        crossed = trade(crossing, "ta", 2)
-        terms[2 * side], terms[2 * side + 1] = local_call(
-            functools.partial(split_kernel, side),
-            [shape((block_rows, share), BF16)] * 2,
+    )(place, *blocks, up, part, w_down[0])
+    near = {1: trade(far, "ta", 1), 0: trade(close, "ta", 1)}
+
+    def lower(turn, after):
+        return local_call(
+            functools.partial(lower_kernel, turn),
+            shape((all_rows, share), F32),
             [SMEM] + [VMEM] * 3,
-            name="split",
+            name="lower",
             after=after,
-        )(place, own, near, crossed)
-        after = terms[2 * side]
-    terms = [terms[s] if s == 0 else trade(terms[s], "gx", s) for s in range(gx_count)]
-    far_sum = local_call(
-        functools.partial(mix_kernel, 2),
-        shape((block_rows, share), F32),
-        [VMEM] * 3,
-        name="mix_far",
-        cost=MIX_COST,
-    )(gates, *terms[2:])
-    return local_call(
-        functools.partial(mix_kernel, 0),
-        shape((block_rows, share), BF16),
-        [VMEM] * 4,
-        name="mix",
-    )(gates, *terms[:2], far_sum)
+        )(place, active, part, rest)
+
+    def on_rows(kernel, distances, after, *arrays):
+        return local_call(
+            functools.partial(kernel, distances),
+            [shape((block_rows, share), BF16)] * len(distances),
+            [SMEM] + [VMEM] * len(arrays),
+            name=kernel.__name__[:-7],
+            after=after,
+        )(place, *arrays)
+
+    cross = lower(2, None)
+    groups = ((3,), (2,), (1, 0))
+    turned = [cross]
+    crossed = {}
+    for distances in groups:
+        sums = on_rows(turn_kernel, distances, turned[0], cross, near[distances[0] // 2])
+        turned = sums
+        crossed.update({s: trade(part, "ta", 2) for s, part in zip(distances, sums)})
+    own = lower(0, turned[0])
+    gathered, total, after = {}, [], None
+    for distances in groups:
+        terms = on_rows(
+            split_kernel, distances, after, own, near[distances[0] // 2],
+            *[crossed[s] for s in distances],
+        )
+        after = terms[0]
+        for s, term in zip(distances, terms):
+            gathered[s] = trade(term, "gx", s) if s else term
+    for distances in groups:
+        last = 0 in distances
+        total = [
+            local_call(
+                functools.partial(mix_kernel, distances),
+                shape((block_rows, share), BF16 if last else F32),
+                [VMEM] * (1 + len(distances) + len(total)),
+                name="mix",
+                cost=1024 if last else MIX_COST,
+            )(gates, *[gathered[s] for s in distances], *total)
+        ]
+    return total[0]
 
 
 def route_tables(expert_ids, expert_count, block_rows, capacity):
@@ -483,7 +501,8 @@
             queries, new_kv, kv_cache, lengths, out_proj, norm_gain, expert_ids, gate_weights,
             w_up, w_down,
         )
-    attended, _ = attend(queries, new_kv, kv_cache, lengths, 0, block_rows, lengths)
+    small = beside(queries, new_kv, lengths, kv_cache.shape[2])
+    attended = attend(small, kv_cache, queries.shape[1] // HD, 0, block_rows, small)
     projected = jnp.dot(
         lax.all_gather(attended, "gx", axis=0, tiled=True),
         out_proj,

time: 81.9 us -> 86.7 us (1.059)
  local copies, waits for them, and re-layouts: 1.14 us -> 4.45 us
  other arithmetic: 0.07 us -> 1.68 us
  Pallas kernels: 28.7 us -> 27.7 us
  starting transfers between devices: 33.1 us -> 34 us
    pallas_call x11 -> x17, Pallas kernels: 8.44 us -> 12.4 us  [local_call(): return call if after is None else lambda *args: call(*args, after)]
    pallas_call x2, Pallas kernels: 10.8 us -> 7.63 us  [attend(): pl.pallas_call(functools.partial(attend_kernel, kv_heads, heads // kv_hea...]
    unnamed x14 -> x12, local copies, waits for them, and re-layouts: 1.14 us -> 3.6 us
    pallas_call x6, Pallas kernels: 9.4 us -> 7.68 us  [the longest x1 5.05 us: every_row_body(): local_call(functools.partial(lift_kernel, chunks), [shape((all_rows, hidd...]
    concatenate x0 -> x1, other arithmetic: none -> 0.95 us  [beside(): return jnp.concatenate([queries, new_kv[0], new_kv[1], spans], axis=1)]
    ppermute x28 -> x31, starting transfers between devices: 33.1 us -> 34 us  [trade(): return lax.ppermute(array, axis, [(k, k ^ turn) for k in range(count)])]
    ppermute x28 -> x31, waiting for transfers between devices: 18.5 us -> 18.4 us  [trade(): return lax.ppermute(array, axis, [(k, k ^ turn) for k in range(count)])]
  transfers between devices with their start and end apart: 28 -> 31, of which waited for: 11 -> 11; matrix products, arithmetic and copies ran while one was open for 0% -> 0% of each run, Pallas kernels for 20% -> 21%
where the time goes in v5:
time: 86.7 us; the launch traced here: 86.4 us
  starting transfers between devices  34 us (39%)
  Pallas kernels  27.7 us (32%)
  waiting for transfers between devices  18.4 us (21%)
  local copies, waits for them, and re-layouts  4.45 us (5%)
  other arithmetic  1.68 us (2%)
    ppermute x31, starting transfers between devices, trade(): return lax.ppermute(array, axis, [(k, k ^ turn) for k in range(count)])  34 us
    ppermute x31, waiting for transfers between devices, trade(): return lax.ppermute(array, axis, [(k, k ^ turn) for k in range(count)])  18.4 us
    pallas_call x17, Pallas kernels, local_call(): return call if after is None else lambda *args: call(*args, after)  12.4 us
    pallas_call x2, Pallas kernels, attend(): pl.pallas_call(functools.partial(attend_kernel, kv_heads, heads // kv_hea...  7.63 us
    pallas_call x1, Pallas kernels, every_row_body(): local_call(functools.partial(lift_kernel, chunks), [shape((all_rows, hidd...  5.05 us
    unnamed x12, local copies, waits for them, and re-layouts  3.6 us
  transfers between devices with their start and end apart: 31, of which 11 were waited for; matrix products, arithmetic and copies ran while one was open for 0% of the time, Pallas kernels for 21%

profile of v5, /device:TPU:0, one launch (start us, length us, event | category | flops | bytes accessed | tf_op | source)
XLA Modules:
  0.0 86.4 jit_solution(397639425237605864)
XLA Ops:
  2.5 3.8 %attend.2.after_ref.refs_1_ = bf16[32,1536]{1,0:T(8,128)(2,1)S(1)} custom-call(bf16[64,2304]{1,0:T(8,128)(2,1)S(1)} %pad_maximum_fusion.small_ref.after_ref, bf16[2,64,192,256]{3,2,1,0:T(8,128)(2,1)} %cache_ref.3, bf16[64,2304]{1,0:T(8,128)(2,1)S(1)} %pad_maximum_fusion.small_ref.after_ref), custom_call_target="tpu_custom_call" | custom-call | flops 1024 | bytes 1024 | tf_op jit(solution)/shard_map/attend/pallas_call | solution.py:130
  6.3 5.1 %collective-permute-start.5 = (bf16[32,1536]{1,0:T(8,128)(2,1)S(1)}, bf16[32,1536]{1,0:T(8,128)(2,1)S(1)}, u32[]{:S(2)}, u32[]{:S(2)}) collective-permute-start(bf16[32,1536]{1,0:T(8,128)(2,1)S(1)} %attend.2.after_ref.refs_1_), channel_id=1, source_target_pairs={{0,12},{4,8},{8,4},{12,0},{1,13},{5,9},{9,5},{13,1},{2,14},{6,10},... | collective-permute-start | bytes 294920 | tf_op jit(solution)/shard_map/ppermute | solution.py:287
  11.5 3.8 %attend.3.refs_6_.refs_1_ = bf16[32,1536]{1,0:T(8,128)(2,1)S(1)} custom-call(bf16[64,2304]{1,0:T(8,128)(2,1)S(1)} %pad_maximum_fusion.small_ref.after_ref, bf16[2,64,192,256]{3,2,1,0:T(8,128)(2,1)} %cache_ref.3, bf16[32,1536]{1,0:T(8,128)(2,1)S(1)} %attend.2.after_ref.refs_1_), custom_call_target="tpu_custom_call" | custom-call | flops 1024 | bytes 1024 | tf_op jit(solution)/shard_map/attend/pallas_call | solution.py:130
  16.4 3.4 %collective-permute-start = (bf16[32,1536]{1,0:T(8,128)(2,1)S(1)}, bf16[32,1536]{1,0:T(8,128)(2,1)S(1)}, u32[]{:S(2)}, u32[]{:S(2)}) collective-permute-start(bf16[32,1536]{1,0:T(8,128)(2,1)S(1)} %attend.3.refs_6_.refs_1_), channel_id=1, source_target_pairs={{0,4},{4,0},{8,12},{12,8},{1,5},{5,1},{9,13},{13,9},{2,6},{6,2},{1... | collective-permute-start | bytes 294920 | tf_op jit(solution)/shard_map/ppermute | solution.py:287
  20.5 8.9 %collective-permute-done.4.refs_3_ = bf16[32,1536]{1,0:T(8,128)(2,1)S(1)} collective-permute-done((bf16[32,1536]{1,0:T(8,128)(2,1)S(1)}, bf16[32,1536]{1,0:T(8,128)(2,1)S(1)}, u32[]{:S(2)}, u32[]{:S(2)}) %collective-permute-start.4) | collective-permute-done | bytes 98336 | tf_op jit(solution)/shard_map/ppermute | solution.py:287
  30.6 1.6 %collective-permute-start.10 = (bf16[32,768]{1,0:T(8,128)(2,1)S(1)}, bf16[32,768]{1,0:T(8,128)(2,1)S(1)}, u32[]{:S(2)}, u32[]{:S(2)}) collective-permute-start(bf16[32,768]{1,0:T(8,128)(2,1)S(1)} %get-tuple-element.27), channel_id=1, source_target_pairs={{0,2},{1,3},{2,0},{3,1},{4,6},{5,7},{6,4},{7,5},{8,10},{9,11},{10,... | collective-permute-start | bytes 147464 | tf_op jit(solution)/shard_map/ppermute | solution.py:287
  33.9 1.5 %collective-permute-start.7 = (bf16[32,768]{1,0:T(8,128)(2,1)S(1)}, bf16[32,768]{1,0:T(8,128)(2,1)S(1)}, u32[]{:S(2)}, u32[]{:S(2)}) collective-permute-start(bf16[32,768]{1,0:T(8,128)(2,1)S(1)} %get-tuple-element.24), channel_id=1, source_target_pairs={{0,2},{1,3},{2,0},{3,1},{4,6},{5,7},{6,4},{7,5},{8,10},{9,11},{10,... | collective-permute-start | bytes 147464 | tf_op jit(solution)/shard_map/ppermute | solution.py:287
  35.9 1.6 %collective-permute-start.17 = (bf16[32,768]{1,0:T(8,128)(2,1)S(1)}, bf16[32,768]{1,0:T(8,128)(2,1)S(1)}, u32[]{:S(2)}, u32[]{:S(2)}) collective-permute-start(bf16[32,768]{1,0:T(8,128)(2,1)S(1)} %add.4.refs_4_.refs_2_), channel_id=1, source_target_pairs={{0,12},{4,8},{8,4},{12,0},{1,13},{5,9},{9,5},{13,1},{2,14},{6,10},... | collective-permute-start | bytes 147464 | tf_op jit(solution)/shard_map/ppermute | solution.py:287
  37.5 2.8 %collective-permute-start.15 = (bf16[32,768]{1,0:T(8,128)(2,1)S(1)}, bf16[32,768]{1,0:T(8,128)(2,1)S(1)}, u32[]{:S(2)}, u32[]{:S(2)}) collective-permute-start(bf16[32,768]{1,0:T(8,128)(2,1)S(1)} %add.4.refs_4_.refs_2_), channel_id=1, source_target_pairs={{0,4},{4,0},{8,12},{12,8},{1,5},{5,1},{9,13},{13,9},{2,6},{6,2},{1... | collective-permute-start | bytes 147464 | tf_op jit(solution)/shard_map/ppermute | solution.py:287
  40.4 1.6 %collective-permute-start.14 = (bf16[32,768]{1,0:T(8,128)(2,1)S(1)}, bf16[32,768]{1,0:T(8,128)(2,1)S(1)}, u32[]{:S(2)}, u32[]{:S(2)}) collective-permute-start(bf16[32,768]{1,0:T(8,128)(2,1)S(1)} %add.5.refs_6_.refs_2_), channel_id=1, source_target_pairs={{0,12},{4,8},{8,4},{12,0},{1,13},{5,9},{9,5},{13,1},{2,14},{6,10},... | collective-permute-start | bytes 147464 | tf_op jit(solution)/shard_map/ppermute | solution.py:287
  42.3 2.6 %collective-permute-start.12 = (bf16[32,768]{1,0:T(8,128)(2,1)S(1)}, bf16[32,768]{1,0:T(8,128)(2,1)S(1)}, u32[]{:S(2)}, u32[]{:S(2)}) collective-permute-start(bf16[32,768]{1,0:T(8,128)(2,1)S(1)} %add.5.refs_6_.refs_2_), channel_id=1, source_target_pairs={{0,4},{4,0},{8,12},{12,8},{1,5},{5,1},{9,13},{13,9},{2,6},{6,2},{1... | collective-permute-start | bytes 147464 | tf_op jit(solution)/shard_map/ppermute | solution.py:287
  45.7 1.1 %collective-permute-start.18 = (bf16[32,3072]{1,0:T(8,128)(2,1)S(1)}, bf16[32,3072]{1,0:T(8,128)(2,1)S(1)}, u32[]{:S(2)}, u32[]{:S(2)}) collective-permute-start(bf16[32,3072]{1,0:T(8,128)(2,1)S(1)} %norm.2.refs_6_.refs_0_), channel_id=1, source_target_pairs={{0,2},{1,3},{2,0},{3,1},{4,6},{5,7},{6,4},{7,5},{8,10},{9,11},{10,... | collective-permute-start | bytes 589832 | tf_op jit(solution)/shard_map/ppermute | solution.py:287
  48.8 1.6 %collective-permute-start.20 = (bf16[32,3072]{1,0:T(8,128)(2,1)S(1)}, bf16[32,3072]{1,0:T(8,128)(2,1)S(1)}, u32[]{:S(2)}, u32[]{:S(2)}) collective-permute-start(bf16[32,3072]{1,0:T(8,128)(2,1)S(1)} %norm.3.refs_3_.refs_0_), channel_id=1, source_target_pairs={{0,2},{1,3},{2,0},{3,1},{4,6},{5,7},{6,4},{7,5},{8,10},{9,11},{10,... | collective-permute-start | bytes 589832 | tf_op jit(solution)/shard_map/ppermute | solution.py:287
  51.2 3.4 %load_up.1.refs_2_.refs_4_ = bf16[1344,3072]{1,0:T(8,128)(2,1)S(1)} custom-call(bf16[1344,3072]{1,0:T(8,128)(2,1)} %bitcast.15, f32[4,64,128]{2,1,0:T(8,128)S(1)} %gates.1.refs_1_.gate_ref), custom_call_target="tpu_custom_call" | custom-call | flops 1024 | bytes 1024 | tf_op jit(solution)/shard_map/load_up/pallas_call | solution.py:39
  56.3 3.3 %copy-done = bf16[1,1344,3072]{2,1,0:T(8,128)(2,1)S(1)} copy-done((bf16[1,1344,3072]{2,1,0:T(8,128)(2,1)S(1)}, bf16[1,1344,3072]{2,1,0:T(8,128)(2,1)}, u32[]{:S(2)}) %copy-start) | copy-done | bytes 8257560
  60.0 5.0 %lift.1 = (bf16[256,1344]{1,0:T(8,128)(2,1)S(1)}, bf16[2,128,768]{2,1,0:T(8,128)(2,1)S(1)}, bf16[2,128,768]{2,1,0:T(8,128)(2,1)S(1)}, bf16[576,3072]{1,0:T(8,128)(2,1)S(1)}) custom-call(s32[2]{0:T(128)S(1)} %pad_add_fusion.refs_0_.place_ref, bf16[2,32,3072]{2,1,0:T(8,128)(2,1)S(1)} %pair.2.refs_2_.refs_0_, ...), custom_call_target="tpu_custom_call" | custom-call | flops 1024 | bytes 1024 | tf_op jit(solution)/shard_map/lift/pallas_call | solution.py:392
  65.6 1.3 %lower.2.refs_1_.refs_3_ = f32[256,768]{1,0:T(8,128)S(1)} custom-call(s32[2]{0:T(128)S(1)} %pad_add_fusion.refs_0_.place_ref, bf16[256,1344]{1,0:T(8,128)(2,1)S(1)} %get-tuple-element.29.active_ref.refs_1_, bf16[768,3072]{1,0:T(8,128)(2,1)S(1)} %load_down.1.refs_5_.down_ref.refs_2_, bf16[576,3072]{1,0:T(8,128)(2,1)S(1)} %get-tuple-element.30.rest_ref.refs_3_), custom_call_target="tpu_custom_call" | custom-call | flops 1024 | bytes 1024 | tf_op jit(solution)/shard_map/lower/pallas_call | solution.py:412
  67.5 1.6 %collective-permute-start.27 = (bf16[64,768]{1,0:T(8,128)(2,1)S(1)}, bf16[64,768]{1,0:T(8,128)(2,1)S(1)}, u32[]{:S(2)}, u32[]{:S(2)}) collective-permute-start(bf16[64,768]{1,0:T(8,128)(2,1)S(1)} %turn.3.refs_3_), channel_id=1, source_target_pairs={{0,2},{1,3},{2,0},{3,1},{4,6},{5,7},{6,4},{7,5},{8,10},{9,11},{10,... | collective-permute-start | bytes 294920 | tf_op jit(solution)/shard_map/ppermute | solution.py:287
  70.8 1.6 %collective-permute-start.25 = (bf16[64,768]{1,0:T(8,128)(2,1)S(1)}, bf16[64,768]{1,0:T(8,128)(2,1)S(1)}, u32[]{:S(2)}, u32[]{:S(2)}) collective-permute-start(bf16[64,768]{1,0:T(8,128)(2,1)S(1)} %get-tuple-element.34), channel_id=1, source_target_pairs={{0,2},{1,3},{2,0},{3,1},{4,6},{5,7},{6,4},{7,5},{8,10},{9,11},{10,... | collective-permute-start | bytes 294920 | tf_op jit(solution)/shard_map/ppermute | solution.py:287
  72.9 1.3 %lower.3.own_ref.refs_1_ = f32[256,768]{1,0:T(8,128)S(1)} custom-call(s32[2]{0:T(128)S(1)} %pad_add_fusion.refs_0_.place_ref, bf16[256,1344]{1,0:T(8,128)(2,1)S(1)} %get-tuple-element.29.active_ref.refs_1_, bf16[768,3072]{1,0:T(8,128)(2,1)S(1)} %load_down.1.refs_5_.down_ref.refs_2_, bf16[576,3072]{1,0:T(8,128)(2,1)S(1)} %get-tuple-element.30.rest_ref.refs_3_, ...), custom_call_target="tpu_custom_call" | custom-call | flops 1024 | bytes 1024 | tf_op jit(solution)/shard_map/lower/pallas_call | solution.py:39
  74.9 1.6 %collective-permute-start.30 = (bf16[64,768]{1,0:T(8,128)(2,1)S(1)}, bf16[64,768]{1,0:T(8,128)(2,1)S(1)}, u32[]{:S(2)}, u32[]{:S(2)}) collective-permute-start(bf16[64,768]{1,0:T(8,128)(2,1)S(1)} %split.3.refs_4_), channel_id=1, source_target_pairs={{0,12},{4,8},{8,4},{12,0},{1,13},{5,9},{9,5},{13,1},{2,14},{6,10},... | collective-permute-start | bytes 294920 | tf_op jit(solution)/shard_map/ppermute | solution.py:287
  79.3 1.4 %collective-permute-start.28 = (bf16[64,768]{1,0:T(8,128)(2,1)S(1)}, bf16[64,768]{1,0:T(8,128)(2,1)S(1)}, u32[]{:S(2)}, u32[]{:S(2)}) collective-permute-start(bf16[64,768]{1,0:T(8,128)(2,1)S(1)} %get-tuple-element.35), channel_id=1, source_target_pairs={{0,4},{4,0},{8,12},{12,8},{1,5},{5,1},{9,13},{13,9},{2,6},{6,2},{1... | collective-permute-start | bytes 294920 | tf_op jit(solution)/shard_map/ppermute | solution.py:287
  80.7 1.1 %collective-permute-done.30.refs_0_ = bf16[64,768]{1,0:T(8,128)(2,1)S(1)} collective-permute-done((bf16[64,768]{1,0:T(8,128)(2,1)S(1)}, bf16[64,768]{1,0:T(8,128)(2,1)S(1)}, u32[]{:S(2)}, u32[]{:S(2)}) %collective-permute-start.30) | collective-permute-done | bytes 98336 | tf_op jit(solution)/shard_map/ppermute | solution.py:287
  81.8 3.6 %collective-permute-done.29.refs_0_ = bf16[64,768]{1,0:T(8,128)(2,1)S(1)} collective-permute-done((bf16[64,768]{1,0:T(8,128)(2,1)S(1)}, bf16[64,768]{1,0:T(8,128)(2,1)S(1)}, u32[]{:S(2)}, u32[]{:S(2)}) %collective-permute-start.29) | collective-permute-done | bytes 98336 | tf_op jit(solution)/shard_map/ppermute | solution.py:287
  (80 shorter events, 21.4 us)
Async XLA Ops:
  6.3 13.4 %collective-permute-start.5 = (bf16[32,1536]{1,0:T(8,128)(2,1)S(1)}, bf16[32,1536]{1,0:T(8,128)(2,1)S(1)}, u32[]{:S(2)}, u32[]{:S(2)}) collective-permute-start(bf16[32,1536]{1,0:T(8,128)(2,1)S(1)} %attend.2.after_ref.refs_1_), channel_id=1, source_target_pairs={{0,12},{4,8},{8,4},{12,0},{1,13},{5,9},{9,5},{13,1},{2,14},{6,10},... | collective-permute-start | bytes 294920 | tf_op jit(solution)/shard_map/ppermute | solution.py:287
  15.3 16.9 %collective-permute-start.2 = (bf16[32,1536]{1,0:T(8,128)(2,1)S(1)}, bf16[32,1536]{1,0:T(8,128)(2,1)S(1)}, u32[]{:S(2)}, u32[]{:S(2)}) collective-permute-start(bf16[32,1536]{1,0:T(8,128)(2,1)S(1)} %attend.3.refs_6_.refs_1_), channel_id=1, source_target_pairs={{0,12},{4,8},{8,4},{12,0},{1,13},{5,9},{9,5},{13,1},{2,14},{6,10},... | collective-permute-start | bytes 294920 | tf_op jit(solution)/shard_map/ppermute | solution.py:287
  15.5 17.0 %collective-permute-start.1 = (bf16[32,1536]{1,0:T(8,128)(2,1)S(1)}, bf16[32,1536]{1,0:T(8,128)(2,1)S(1)}, u32[]{:S(2)}, u32[]{:S(2)}) collective-permute-start(bf16[32,1536]{1,0:T(8,128)(2,1)S(1)} %attend.3.refs_6_.refs_1_), channel_id=1, source_target_pairs={{0,8},{4,12},{8,0},{12,4},{1,9},{5,13},{9,1},{13,5},{2,10},{6,14},... | collective-permute-start | bytes 294920 | tf_op jit(solution)/shard_map/ppermute | solution.py:287
  16.4 16.1 %collective-permute-start = (bf16[32,1536]{1,0:T(8,128)(2,1)S(1)}, bf16[32,1536]{1,0:T(8,128)(2,1)S(1)}, u32[]{:S(2)}, u32[]{:S(2)}) collective-permute-start(bf16[32,1536]{1,0:T(8,128)(2,1)S(1)} %attend.3.refs_6_.refs_1_), channel_id=1, source_target_pairs={{0,4},{4,0},{8,12},{12,8},{1,5},{5,1},{9,13},{13,9},{2,6},{6,2},{1... | collective-permute-start | bytes 294920 | tf_op jit(solution)/shard_map/ppermute | solution.py:287
  19.7 9.7 %collective-permute-start.4 = (bf16[32,1536]{1,0:T(8,128)(2,1)S(1)}, bf16[32,1536]{1,0:T(8,128)(2,1)S(1)}, u32[]{:S(2)}, u32[]{:S(2)}) collective-permute-start(bf16[32,1536]{1,0:T(8,128)(2,1)S(1)} %attend.2.after_ref.refs_1_), channel_id=1, source_target_pairs={{0,8},{4,12},{8,0},{12,4},{1,9},{5,13},{9,1},{13,5},{2,10},{6,14},... | collective-permute-start | bytes 294920 | tf_op jit(solution)/shard_map/ppermute | solution.py:287
  19.7 9.7 %collective-permute-start.3 = (bf16[32,1536]{1,0:T(8,128)(2,1)S(1)}, bf16[32,1536]{1,0:T(8,128)(2,1)S(1)}, u32[]{:S(2)}, u32[]{:S(2)}) collective-permute-start(bf16[32,1536]{1,0:T(8,128)(2,1)S(1)} %attend.2.after_ref.refs_1_), channel_id=1, source_target_pairs={{0,4},{4,0},{8,12},{12,8},{1,5},{5,1},{9,13},{13,9},{2,6},{6,2},{1... | collective-permute-start | bytes 294920 | tf_op jit(solution)/shard_map/ppermute | solution.py:287
  33.9 6.4 %collective-permute-start.7 = (bf16[32,768]{1,0:T(8,128)(2,1)S(1)}, bf16[32,768]{1,0:T(8,128)(2,1)S(1)}, u32[]{:S(2)}, u32[]{:S(2)}) collective-permute-start(bf16[32,768]{1,0:T(8,128)(2,1)S(1)} %get-tuple-element.24), channel_id=1, source_target_pairs={{0,2},{1,3},{2,0},{3,1},{4,6},{5,7},{6,4},{7,5},{8,10},{9,11},{10,... | collective-permute-start | bytes 147464 | tf_op jit(solution)/shard_map/ppermute | solution.py:287
  35.4 4.9 %collective-permute-start.8 = (bf16[32,768]{1,0:T(8,128)(2,1)S(1)}, bf16[32,768]{1,0:T(8,128)(2,1)S(1)}, u32[]{:S(2)}, u32[]{:S(2)}) collective-permute-start(bf16[32,768]{1,0:T(8,128)(2,1)S(1)} %get-tuple-element.25), channel_id=1, source_target_pairs={{0,3},{1,2},{2,1},{3,0},{4,7},{5,6},{6,5},{7,4},{8,11},{9,10},{10,... | collective-permute-start | bytes 147464 | tf_op jit(solution)/shard_map/ppermute | solution.py:287
  35.9 6.4 %collective-permute-start.17 = (bf16[32,768]{1,0:T(8,128)(2,1)S(1)}, bf16[32,768]{1,0:T(8,128)(2,1)S(1)}, u32[]{:S(2)}, u32[]{:S(2)}) collective-permute-start(bf16[32,768]{1,0:T(8,128)(2,1)S(1)} %add.4.refs_4_.refs_2_), channel_id=1, source_target_pairs={{0,12},{4,8},{8,4},{12,0},{1,13},{5,9},{9,5},{13,1},{2,14},{6,10},... | collective-permute-start | bytes 147464 | tf_op jit(solution)/shard_map/ppermute | solution.py:287
  37.5 7.4 %collective-permute-start.16 = (bf16[32,768]{1,0:T(8,128)(2,1)S(1)}, bf16[32,768]{1,0:T(8,128)(2,1)S(1)}, u32[]{:S(2)}, u32[]{:S(2)}) collective-permute-start(bf16[32,768]{1,0:T(8,128)(2,1)S(1)} %add.4.refs_4_.refs_2_), channel_id=1, source_target_pairs={{0,8},{4,12},{8,0},{12,4},{1,9},{5,13},{9,1},{13,5},{2,10},{6,14},... | collective-permute-start | bytes 147464 | tf_op jit(solution)/shard_map/ppermute | solution.py:287
  37.5 7.3 %collective-permute-start.15 = (bf16[32,768]{1,0:T(8,128)(2,1)S(1)}, bf16[32,768]{1,0:T(8,128)(2,1)S(1)}, u32[]{:S(2)}, u32[]{:S(2)}) collective-permute-start(bf16[32,768]{1,0:T(8,128)(2,1)S(1)} %add.4.refs_4_.refs_2_), channel_id=1, source_target_pairs={{0,4},{4,0},{8,12},{12,8},{1,5},{5,1},{9,13},{13,9},{2,6},{6,2},{1... | collective-permute-start | bytes 147464 | tf_op jit(solution)/shard_map/ppermute | solution.py:287
  40.4 6.5 %collective-permute-start.14 = (bf16[32,768]{1,0:T(8,128)(2,1)S(1)}, bf16[32,768]{1,0:T(8,128)(2,1)S(1)}, u32[]{:S(2)}, u32[]{:S(2)}) collective-permute-start(bf16[32,768]{1,0:T(8,128)(2,1)S(1)} %add.5.refs_6_.refs_2_), channel_id=1, source_target_pairs={{0,12},{4,8},{8,4},{12,0},{1,13},{5,9},{9,5},{13,1},{2,14},{6,10},... | collective-permute-start | bytes 147464 | tf_op jit(solution)/shard_map/ppermute | solution.py:287
  42.0 5.9 %collective-permute-start.13 = (bf16[32,768]{1,0:T(8,128)(2,1)S(1)}, bf16[32,768]{1,0:T(8,128)(2,1)S(1)}, u32[]{:S(2)}, u32[]{:S(2)}) collective-permute-start(bf16[32,768]{1,0:T(8,128)(2,1)S(1)} %add.5.refs_6_.refs_2_), channel_id=1, source_target_pairs={{0,8},{4,12},{8,0},{12,4},{1,9},{5,13},{9,1},{13,5},{2,10},{6,14},... | collective-permute-start | bytes 147464 | tf_op jit(solution)/shard_map/ppermute | solution.py:287
  42.3 5.7 %collective-permute-start.12 = (bf16[32,768]{1,0:T(8,128)(2,1)S(1)}, bf16[32,768]{1,0:T(8,128)(2,1)S(1)}, u32[]{:S(2)}, u32[]{:S(2)}) collective-permute-start(bf16[32,768]{1,0:T(8,128)(2,1)S(1)} %add.5.refs_6_.refs_2_), channel_id=1, source_target_pairs={{0,4},{4,0},{8,12},{12,8},{1,5},{5,1},{9,13},{13,9},{2,6},{6,2},{1... | collective-permute-start | bytes 147464 | tf_op jit(solution)/shard_map/ppermute | solution.py:287
  45.7 8.9 %collective-permute-start.18 = (bf16[32,3072]{1,0:T(8,128)(2,1)S(1)}, bf16[32,3072]{1,0:T(8,128)(2,1)S(1)}, u32[]{:S(2)}, u32[]{:S(2)}) collective-permute-start(bf16[32,3072]{1,0:T(8,128)(2,1)S(1)} %norm.2.refs_6_.refs_0_), channel_id=1, source_target_pairs={{0,2},{1,3},{2,0},{3,1},{4,6},{5,7},{6,4},{7,5},{8,10},{9,11},{10,... | collective-permute-start | bytes 589832 | tf_op jit(solution)/shard_map/ppermute | solution.py:287
  48.8 6.9 %collective-permute-start.20 = (bf16[32,3072]{1,0:T(8,128)(2,1)S(1)}, bf16[32,3072]{1,0:T(8,128)(2,1)S(1)}, u32[]{:S(2)}, u32[]{:S(2)}) collective-permute-start(bf16[32,3072]{1,0:T(8,128)(2,1)S(1)} %norm.3.refs_3_.refs_0_), channel_id=1, source_target_pairs={{0,2},{1,3},{2,0},{3,1},{4,6},{5,7},{6,4},{7,5},{8,10},{9,11},{10,... | collective-permute-start | bytes 589832 | tf_op jit(solution)/shard_map/ppermute | solution.py:287
  65.1 5.1 %collective-permute-start.22 = (bf16[2,128,768]{2,1,0:T(8,128)(2,1)S(1)}, bf16[2,128,768]{2,1,0:T(8,128)(2,1)S(1)}, u32[]{:S(2)}, u32[]{:S(2)}) collective-permute-start(bf16[2,128,768]{2,1,0:T(8,128)(2,1)S(1)} %get-tuple-element.31), channel_id=1, source_target_pairs={{0,1},{1,0},{2,3},{3,2},{4,5},{5,4},{6,7},{7,6},{8,9},{9,8},{10,11... | collective-permute-start | bytes 1179656 | tf_op jit(solution)/shard_map/ppermute | solution.py:287
  67.5 6.7 %collective-permute-start.27 = (bf16[64,768]{1,0:T(8,128)(2,1)S(1)}, bf16[64,768]{1,0:T(8,128)(2,1)S(1)}, u32[]{:S(2)}, u32[]{:S(2)}) collective-permute-start(bf16[64,768]{1,0:T(8,128)(2,1)S(1)} %turn.3.refs_3_), channel_id=1, source_target_pairs={{0,2},{1,3},{2,0},{3,1},{4,6},{5,7},{6,4},{7,5},{8,10},{9,11},{10,... | collective-permute-start | bytes 294920 | tf_op jit(solution)/shard_map/ppermute | solution.py:287
  69.7 6.8 %collective-permute-start.26 = (bf16[64,768]{1,0:T(8,128)(2,1)S(1)}, bf16[64,768]{1,0:T(8,128)(2,1)S(1)}, u32[]{:S(2)}, u32[]{:S(2)}) collective-permute-start(bf16[64,768]{1,0:T(8,128)(2,1)S(1)} %turn.4.refs_3_), channel_id=1, source_target_pairs={{0,2},{1,3},{2,0},{3,1},{4,6},{5,7},{6,4},{7,5},{8,10},{9,11},{10,... | collective-permute-start | bytes 294920 | tf_op jit(solution)/shard_map/ppermute | solution.py:287
  70.8 6.7 %collective-permute-start.25 = (bf16[64,768]{1,0:T(8,128)(2,1)S(1)}, bf16[64,768]{1,0:T(8,128)(2,1)S(1)}, u32[]{:S(2)}, u32[]{:S(2)}) collective-permute-start(bf16[64,768]{1,0:T(8,128)(2,1)S(1)} %get-tuple-element.34), channel_id=1, source_target_pairs={{0,2},{1,3},{2,0},{3,1},{4,6},{5,7},{6,4},{7,5},{8,10},{9,11},{10,... | collective-permute-start | bytes 294920 | tf_op jit(solution)/shard_map/ppermute | solution.py:287
  72.4 6.2 %collective-permute-start.24 = (bf16[64,768]{1,0:T(8,128)(2,1)S(1)}, bf16[64,768]{1,0:T(8,128)(2,1)S(1)}, u32[]{:S(2)}, u32[]{:S(2)}) collective-permute-start(bf16[64,768]{1,0:T(8,128)(2,1)S(1)} %get-tuple-element.33.refs_4_), channel_id=1, source_target_pairs={{0,2},{1,3},{2,0},{3,1},{4,6},{5,7},{6,4},{7,5},{8,10},{9,11},{10,... | collective-permute-start | bytes 294920 | tf_op jit(solution)/shard_map/ppermute | solution.py:287
  74.9 6.9 %collective-permute-start.30 = (bf16[64,768]{1,0:T(8,128)(2,1)S(1)}, bf16[64,768]{1,0:T(8,128)(2,1)S(1)}, u32[]{:S(2)}, u32[]{:S(2)}) collective-permute-start(bf16[64,768]{1,0:T(8,128)(2,1)S(1)} %split.3.refs_4_), channel_id=1, source_target_pairs={{0,12},{4,8},{8,4},{12,0},{1,13},{5,9},{9,5},{13,1},{2,14},{6,10},... | collective-permute-start | bytes 294920 | tf_op jit(solution)/shard_map/ppermute | solution.py:287
  77.1 8.3 %collective-permute-start.29 = (bf16[64,768]{1,0:T(8,128)(2,1)S(1)}, bf16[64,768]{1,0:T(8,128)(2,1)S(1)}, u32[]{:S(2)}, u32[]{:S(2)}) collective-permute-start(bf16[64,768]{1,0:T(8,128)(2,1)S(1)} %split.4.refs_5_), channel_id=1, source_target_pairs={{0,8},{4,12},{8,0},{12,4},{1,9},{5,13},{9,1},{13,5},{2,10},{6,14},... | collective-permute-start | bytes 294920 | tf_op jit(solution)/shard_map/ppermute | solution.py:287
  79.3 6.5 %collective-permute-start.28 = (bf16[64,768]{1,0:T(8,128)(2,1)S(1)}, bf16[64,768]{1,0:T(8,128)(2,1)S(1)}, u32[]{:S(2)}, u32[]{:S(2)}) collective-permute-start(bf16[64,768]{1,0:T(8,128)(2,1)S(1)} %get-tuple-element.35), channel_id=1, source_target_pairs={{0,4},{4,0},{8,12},{12,8},{1,5},{5,1},{9,13},{13,9},{2,6},{6,2},{1... | collective-permute-start | bytes 294920 | tf_op jit(solution)/shard_map/ppermute | solution.py:287
  (12 other events, 181.0 us)

commit v6 on v5

--- a/solution.py
+++ b/solution.py
@@ -11,8 +11,8 @@
 HD = 128
 MIB = 1 << 20
 MIX_COST = 1 << 22
+PROJECT_COST = 1 << 21
 VMEM = pl.BlockSpec(memory_space=pltpu.VMEM)
-SMEM = pl.BlockSpec(memory_space=pltpu.SMEM)
 F32 = jnp.float32
 BF16 = jnp.bfloat16
 
@@ -154,21 +154,21 @@
     out_ref[1] = other_ref[...]
 
 
-def gate_kernel(place_ref, ids_ref, gates_ref, gate_ref):
+def gate_kernel(ids_ref, gates_ref, gate_ref):
     parts, rows, lanes = gate_ref.shape
-    ids = ids_ref[pl.ds(pl.multiple_of(place_ref[0] * rows, rows), rows), :]
+    ids = ids_ref[pl.ds(pl.multiple_of(lax.axis_index("gx") * rows, rows), rows), :]
     for s in range(parts):
         gate = jnp.sum(
-            jnp.where(ids == (place_ref[0] ^ s), gates_ref[...], 0.0), axis=1, keepdims=True
+            jnp.where(ids == (lax.axis_index("gx") ^ s), gates_ref[...], 0.0), axis=1, keepdims=True
         )
         gate_ref[s] = jnp.broadcast_to(gate, (rows, lanes))
 
 
-def project_kernel(parts, place_ref, *refs):
+def project_kernel(parts, *refs):
     shards, weight_ref = refs[:parts], refs[parts]
     outs, held = refs[parts + 1 : -1], refs[-1]
     rows = shards[0].shape[0]
-    turn = place_ref[0] ^ place_ref[1]
+    turn = lax.axis_index("gx") ^ lax.axis_index("ta")
     block = jnp.concatenate([shard[...] for shard in shards], axis=0)
     pieces = jnp.dot(block, weight_ref[...], preferred_element_type=F32).astype(BF16)
     for s in range(parts):
@@ -185,7 +185,7 @@
     out[...] = total.astype(BF16)
 
 
-def norm_kernel(parts, place_ref, gain_ref, *refs):
+def norm_kernel(parts, gain_ref, *refs):
     shards, out = refs[:parts], refs[parts]
     width = shards[0].shape[1]
     values = [shard[...].astype(F32) for shard in shards]
@@ -194,7 +194,7 @@
     spread = sum(jnp.sum(part * part, axis=1, keepdims=True) for part in values) / out.shape[1]
     scale = lax.rsqrt(spread + 1e-05)
     for s in range(parts):
-        here = pl.ds(pl.multiple_of((place_ref[0] ^ s) * width, HD), width)
+        here = pl.ds(pl.multiple_of((lax.axis_index("gx") ^ s) * width, HD), width)
         out[:, here] = (values[s] * scale * gain_ref[:, here]).astype(BF16)
 
 
@@ -208,7 +208,7 @@
     copy.wait()
 
 
-def lift_kernel(chunks, place_ref, *refs):
+def lift_kernel(chunks, *refs):
     count = 2 * chunks
     shards, (up_ref, down_ref, down_hbm) = refs[:count], refs[count : count + 3]
     active_ref, far_ref, close_ref, rest_ref, held, passed, sem = refs[count + 3 :]
@@ -221,7 +221,7 @@
     copy.start()
     for c in range(chunks):
         for t, shard in enumerate(by_distance(*shards[2 * c : 2 * c + 2])):
-            first = pl.multiple_of(((place_ref[1] ^ t) * chunks + c) * rows, rows)
+            first = pl.multiple_of(((lax.axis_index("ta") ^ t) * chunks + c) * rows, rows)
             held[pl.ds(first, rows), :] = shard[...]
     for first in range(0, hidden, 2 * HD):
         last = min(first + 2 * HD, hidden)
@@ -230,39 +230,39 @@
         )
         active_ref[:, first:last] = (raised / (1.0 + jnp.exp(-raised))).T.astype(BF16)
     copy.wait()
-    mine = place_ref[0] // 2
+    mine = lax.axis_index("gx") // 2
     for k in range(2):
-        passed[...] = lowered(place_ref, 2 * k + 1, active_ref, down_ref, rest_ref, share).astype(BF16)
+        passed[...] = lowered(2 * k + 1, active_ref, down_ref, rest_ref, share).astype(BF16)
         for out_ref, side in ((far_ref, 1 - mine), (close_ref, mine)):
             out_ref[k] = passed[pl.ds(pl.multiple_of(side * half, half), half), :]
 
 
-def lowered(place_ref, turn, active_ref, down_ref, rest_ref, share):
+def lowered(turn, active_ref, down_ref, rest_ref, share):
     cut = down_ref.shape[0]
-    here = pl.ds(pl.multiple_of((place_ref[1] ^ turn) * share, HD), share)
+    here = pl.ds(pl.multiple_of((lax.axis_index("ta") ^ turn) * share, HD), share)
     return jnp.dot(
         active_ref[:, :cut], down_ref[:, here], preferred_element_type=F32
     ) + jnp.dot(active_ref[:, cut:], rest_ref[:, here], preferred_element_type=F32)
 
 
-def lower_kernel(turn, place_ref, active_ref, down_ref, rest_ref, out_ref):
-    out_ref[...] = lowered(place_ref, turn, active_ref, down_ref, rest_ref, out_ref.shape[1])
-
-
-def turn_kernel(distances, place_ref, cross_ref, near_ref, *outs):
+def lower_kernel(turn, active_ref, down_ref, rest_ref, out_ref):
+    out_ref[...] = lowered(turn, active_ref, down_ref, rest_ref, out_ref.shape[1])
+
+
+def turn_kernel(distances, cross_ref, near_ref, *outs):
     rows = outs[0].shape[0]
     for distance, out_ref in zip(distances, outs):
-        z = place_ref[0] ^ distance
+        z = lax.axis_index("gx") ^ distance
         here = pl.ds(pl.multiple_of(z * rows, rows), rows)
         there = pl.ds(pl.multiple_of(z % 2 * rows, rows), rows)
         out_ref[...] = (cross_ref[here, :] + near_ref[1, there, :].astype(F32)).astype(BF16)
 
 
-def split_kernel(distances, place_ref, own_ref, near_ref, *refs):
+def split_kernel(distances, own_ref, near_ref, *refs):
     count = len(distances)
     rows = refs[0].shape[0]
     for distance, crossed_ref, out_ref in zip(distances, refs[:count], refs[count:]):
-        z = place_ref[0] ^ distance
+        z = lax.axis_index("gx") ^ distance
         here = pl.ds(pl.multiple_of(z * rows, rows), rows)
         there = pl.ds(pl.multiple_of(z % 2 * rows, rows), rows)
         total = own_ref[here, :] + near_ref[0, there, :].astype(F32)
@@ -300,7 +300,6 @@
     hidden_share = w_up.shape[2]
     share = model // ta_count
     all_rows = block_rows * gx_count
-    place = jnp.stack([lax.axis_index("gx"), lax.axis_index("ta")]).astype(jnp.int32)
     shape = jax.ShapeDtypeStruct
     gain = norm_gain.reshape(1, model)
     heads = queries.shape[1] // HD
@@ -322,11 +321,12 @@
             local_call(
                 functools.partial(project_kernel, gx_count),
                 [shape((rows, width), BF16)] * ta_count,
-                [SMEM] + [VMEM] * (gx_count + 1),
+                [VMEM] * (gx_count + 1),
                 [pltpu.VMEM((ta_count, rows, width), BF16)],
                 name="project",
                 after=pieces[-1][0] if pieces else attended[-1],
-            )(place, *shards[c], out_proj)
+                cost=PROJECT_COST,
+            )(*shards[c], out_proj)
         )
     for c in range(chunks):
         parts = [pieces[c][0]] + [trade(pieces[c][t], "ta", t) for t in range(1, ta_count)]
@@ -346,18 +346,18 @@
             local_call(
                 functools.partial(norm_kernel, gx_count),
                 shape((rows, model), BF16),
-                [SMEM] + [VMEM] * (gx_count + 1),
+                [VMEM] * (gx_count + 1),
                 name="norm",
                 after=normed[-1] if normed else hidden[-1],
-            )(place, gain, *shards[c])
+            )(gain, *shards[c])
         )
     gates = local_call(
         gate_kernel,
         shape((gx_count, block_rows, HD), F32),
-        [SMEM, VMEM, VMEM],
+        [VMEM, VMEM],
         name="gates",
         after=normed[-1],
-    )(place, expert_ids, gate_weights)
+    )(expert_ids, gate_weights)
     up = local_call(
         functools.partial(load_kernel, hidden_share),
         shape((hidden_share, model), BF16),
@@ -384,7 +384,7 @@
         shape((cut, model), BF16),
         [ANYWHERE],
         [pltpu.SemaphoreType.DMA],
-        vmem=37,
+        vmem=42,
         name="load_down",
         after=pairs[-1],
     )(w_down[0])
@@ -397,7 +397,7 @@
             shape((2, half, share), BF16),
             shape((hidden_share - cut, model), BF16),
         ],
-        [SMEM] + [VMEM] * (2 * chunks + 2) + [ANYWHERE],
+        [VMEM] * (2 * chunks + 2) + [ANYWHERE],
         [
             pltpu.VMEM((all_rows, model), BF16),
             pltpu.VMEM((all_rows, share), BF16),
@@ -405,26 +405,26 @@
         ],
         vmem=30,
         name="lift",
-    )(place, *blocks, up, part, w_down[0])
+    )(*blocks, up, part, w_down[0])
     near = {1: trade(far, "ta", 1), 0: trade(close, "ta", 1)}
 
     def lower(turn, after):
         return local_call(
             functools.partial(lower_kernel, turn),
             shape((all_rows, share), F32),
-            [SMEM] + [VMEM] * 3,
+            [VMEM] * 3,
             name="lower",
             after=after,
-        )(place, active, part, rest)
+        )(active, part, rest)
 
     def on_rows(kernel, distances, after, *arrays):
         return local_call(
             functools.partial(kernel, distances),
             [shape((block_rows, share), BF16)] * len(distances),
-            [SMEM] + [VMEM] * len(arrays),
+            [VMEM] * len(arrays),
             name=kernel.__name__[:-7],
             after=after,
-        )(place, *arrays)
+        )(*arrays)
 
     cross = lower(2, None)
     groups = ((3,), (2,), (1, 0))

time: 86.7 us -> 77.8 us (0.90)
  Pallas kernels: 27.7 us -> 22 us
  local copies, waits for them, and re-layouts: 4.45 us -> 1.1 us
    pallas_call x17, Pallas kernels: 12.4 us -> 8.39 us  [local_call(): return call if after is None else lambda *args: call(*args, after)]
    unnamed x12 -> x10, local copies, waits for them, and re-layouts: 3.6 us -> 0.25 us
  transfers between devices with their start and end apart: 31 -> 31, of which waited for: 11 -> 12; matrix products, arithmetic and copies ran while one was open for 0% -> 0% of each run, Pallas kernels for 21% -> 17%
where the time goes in v6:
time: 77.8 us; the launch traced here: 77.5 us
  starting transfers between devices  34.1 us (44%)
  Pallas kernels  22 us (28%)
  waiting for transfers between devices  18.4 us (24%)
  other arithmetic  1.61 us (2%)
  local copies, waits for them, and re-layouts  1.1 us (1%)
    ppermute x31, starting transfers between devices, trade(): return lax.ppermute(array, axis, [(k, k ^ turn) for k in range(count)])  34.1 us
    ppermute x31, waiting for transfers between devices, trade(): return lax.ppermute(array, axis, [(k, k ^ turn) for k in range(count)])  18.4 us
    pallas_call x17, Pallas kernels, local_call(): return call if after is None else lambda *args: call(*args, after)  8.39 us
    pallas_call x2, Pallas kernels, attend(): pl.pallas_call(functools.partial(attend_kernel, kv_heads, heads // kv_hea...  7.63 us
    pallas_call x1, Pallas kernels, every_row_body(): local_call(functools.partial(lift_kernel, chunks), [shape((all_rows, hidd...  4.47 us
  transfers between devices with their start and end apart: 31, of which 12 were waited for; matrix products, arithmetic and copies ran while one was open for 0% of the time, Pallas kernels for 17%

profile of v6, /device:TPU:0, one launch (start us, length us, event | category | flops | bytes accessed | tf_op | source)
XLA Modules:
  0.0 77.5 jit_solution(10126561056872705645)
XLA Ops:
  2.5 3.8 %attend.2.after_ref.refs_0_ = bf16[32,1536]{1,0:T(8,128)(2,1)S(1)} custom-call(bf16[64,2304]{1,0:T(8,128)(2,1)S(1)} %pad_maximum_fusion.small_ref.after_ref, bf16[2,64,192,256]{3,2,1,0:T(8,128)(2,1)} %cache_ref.3, bf16[64,2304]{1,0:T(8,128)(2,1)S(1)} %pad_maximum_fusion.small_ref.after_ref), custom_call_target="tpu_custom_call" | custom-call | flops 1024 | bytes 1024 | tf_op jit(solution)/shard_map/attend/pallas_call | solution.py:130
  6.3 5.1 %collective-permute-start.5 = (bf16[32,1536]{1,0:T(8,128)(2,1)S(1)}, bf16[32,1536]{1,0:T(8,128)(2,1)S(1)}, u32[]{:S(2)}, u32[]{:S(2)}) collective-permute-start(bf16[32,1536]{1,0:T(8,128)(2,1)S(1)} %attend.2.after_ref.refs_0_), channel_id=1, source_target_pairs={{0,12},{4,8},{8,4},{12,0},{1,13},{5,9},{9,5},{13,1},{2,14},{6,10},... | collective-permute-start | bytes 294920 | tf_op jit(solution)/shard_map/ppermute | solution.py:287
  12.1 3.8 %attend.3.refs_5_.refs_0_ = bf16[32,1536]{1,0:T(8,128)(2,1)S(1)} custom-call(bf16[64,2304]{1,0:T(8,128)(2,1)S(1)} %pad_maximum_fusion.small_ref.after_ref, bf16[2,64,192,256]{3,2,1,0:T(8,128)(2,1)} %cache_ref.3, bf16[32,1536]{1,0:T(8,128)(2,1)S(1)} %attend.2.after_ref.refs_0_), custom_call_target="tpu_custom_call" | custom-call | flops 1024 | bytes 1024 | tf_op jit(solution)/shard_map/attend/pallas_call | solution.py:130
  15.9 3.8 %collective-permute-start.2 = (bf16[32,1536]{1,0:T(8,128)(2,1)S(1)}, bf16[32,1536]{1,0:T(8,128)(2,1)S(1)}, u32[]{:S(2)}, u32[]{:S(2)}) collective-permute-start(bf16[32,1536]{1,0:T(8,128)(2,1)S(1)} %attend.3.refs_5_.refs_0_), channel_id=1, source_target_pairs={{0,12},{4,8},{8,4},{12,0},{1,13},{5,9},{9,5},{13,1},{2,14},{6,10},... | collective-permute-start | bytes 294920 | tf_op jit(solution)/shard_map/ppermute | solution.py:287
  20.4 4.5 %collective-permute-done.4.refs_2_ = bf16[32,1536]{1,0:T(8,128)(2,1)S(1)} collective-permute-done((bf16[32,1536]{1,0:T(8,128)(2,1)S(1)}, bf16[32,1536]{1,0:T(8,128)(2,1)S(1)}, u32[]{:S(2)}, u32[]{:S(2)}) %collective-permute-start.4) | collective-permute-done | bytes 98336 | tf_op jit(solution)/shard_map/ppermute | solution.py:287
  25.5 1.6 %collective-permute-start.10 = (bf16[32,768]{1,0:T(8,128)(2,1)S(1)}, bf16[32,768]{1,0:T(8,128)(2,1)S(1)}, u32[]{:S(2)}, u32[]{:S(2)}) collective-permute-start(bf16[32,768]{1,0:T(8,128)(2,1)S(1)} %get-tuple-element.27), channel_id=1, source_target_pairs={{0,2},{1,3},{2,0},{3,1},{4,6},{5,7},{6,4},{7,5},{8,10},{9,11},{10,... | collective-permute-start | bytes 147464 | tf_op jit(solution)/shard_map/ppermute | solution.py:287
  28.7 1.6 %collective-permute-start.7 = (bf16[32,768]{1,0:T(8,128)(2,1)S(1)}, bf16[32,768]{1,0:T(8,128)(2,1)S(1)}, u32[]{:S(2)}, u32[]{:S(2)}) collective-permute-start(bf16[32,768]{1,0:T(8,128)(2,1)S(1)} %get-tuple-element.24), channel_id=1, source_target_pairs={{0,2},{1,3},{2,0},{3,1},{4,6},{5,7},{6,4},{7,5},{8,10},{9,11},{10,... | collective-permute-start | bytes 147464 | tf_op jit(solution)/shard_map/ppermute | solution.py:287
  30.8 2.4 %collective-permute-start.17 = (bf16[32,768]{1,0:T(8,128)(2,1)S(1)}, bf16[32,768]{1,0:T(8,128)(2,1)S(1)}, u32[]{:S(2)}, u32[]{:S(2)}) collective-permute-start(bf16[32,768]{1,0:T(8,128)(2,1)S(1)} %add.2.refs_4_.refs_1_), channel_id=1, source_target_pairs={{0,12},{4,8},{8,4},{12,0},{1,13},{5,9},{9,5},{13,1},{2,14},{6,10},... | collective-permute-start | bytes 147464 | tf_op jit(solution)/shard_map/ppermute | solution.py:287
  33.2 2.0 %collective-permute-start.15 = (bf16[32,768]{1,0:T(8,128)(2,1)S(1)}, bf16[32,768]{1,0:T(8,128)(2,1)S(1)}, u32[]{:S(2)}, u32[]{:S(2)}) collective-permute-start(bf16[32,768]{1,0:T(8,128)(2,1)S(1)} %add.2.refs_4_.refs_1_), channel_id=1, source_target_pairs={{0,4},{4,0},{8,12},{12,8},{1,5},{5,1},{9,13},{13,9},{2,6},{6,2},{1... | collective-permute-start | bytes 147464 | tf_op jit(solution)/shard_map/ppermute | solution.py:287
  35.3 2.4 %collective-permute-start.14 = (bf16[32,768]{1,0:T(8,128)(2,1)S(1)}, bf16[32,768]{1,0:T(8,128)(2,1)S(1)}, u32[]{:S(2)}, u32[]{:S(2)}) collective-permute-start(bf16[32,768]{1,0:T(8,128)(2,1)S(1)} %add.3.refs_5_.refs_1_), channel_id=1, source_target_pairs={{0,12},{4,8},{8,4},{12,0},{1,13},{5,9},{9,5},{13,1},{2,14},{6,10},... | collective-permute-start | bytes 147464 | tf_op jit(solution)/shard_map/ppermute | solution.py:287
  37.7 2.0 %collective-permute-start.12 = (bf16[32,768]{1,0:T(8,128)(2,1)S(1)}, bf16[32,768]{1,0:T(8,128)(2,1)S(1)}, u32[]{:S(2)}, u32[]{:S(2)}) collective-permute-start(bf16[32,768]{1,0:T(8,128)(2,1)S(1)} %add.3.refs_5_.refs_1_), channel_id=1, source_target_pairs={{0,4},{4,0},{8,12},{12,8},{1,5},{5,1},{9,13},{13,9},{2,6},{6,2},{1... | collective-permute-start | bytes 147464 | tf_op jit(solution)/shard_map/ppermute | solution.py:287
  40.0 1.4 %collective-permute-start.18 = (bf16[32,3072]{1,0:T(8,128)(2,1)S(1)}, bf16[32,3072]{1,0:T(8,128)(2,1)S(1)}, u32[]{:S(2)}, u32[]{:S(2)}) collective-permute-start(bf16[32,3072]{1,0:T(8,128)(2,1)S(1)} %norm.2.refs_5_.refs_0_), channel_id=1, source_target_pairs={{0,2},{1,3},{2,0},{3,1},{4,6},{5,7},{6,4},{7,5},{8,10},{9,11},{10,... | collective-permute-start | bytes 589832 | tf_op jit(solution)/shard_map/ppermute | solution.py:287
  41.4 1.6 %collective-permute-done.13.refs_3_ = bf16[32,768]{1,0:T(8,128)(2,1)S(1)} collective-permute-done((bf16[32,768]{1,0:T(8,128)(2,1)S(1)}, bf16[32,768]{1,0:T(8,128)(2,1)S(1)}, u32[]{:S(2)}, u32[]{:S(2)}) %collective-permute-start.13) | collective-permute-done | bytes 49184 | tf_op jit(solution)/shard_map/ppermute | solution.py:287
  43.3 1.4 %collective-permute-start.20 = (bf16[32,3072]{1,0:T(8,128)(2,1)S(1)}, bf16[32,3072]{1,0:T(8,128)(2,1)S(1)}, u32[]{:S(2)}, u32[]{:S(2)}) collective-permute-start(bf16[32,3072]{1,0:T(8,128)(2,1)S(1)} %norm.3.refs_2_.refs_0_), channel_id=1, source_target_pairs={{0,2},{1,3},{2,0},{3,1},{4,6},{5,7},{6,4},{7,5},{8,10},{9,11},{10,... | collective-permute-start | bytes 589832 | tf_op jit(solution)/shard_map/ppermute | solution.py:287
  45.0 3.4 %load_up.1.refs_2_.refs_4_ = bf16[1344,3072]{1,0:T(8,128)(2,1)S(1)} custom-call(bf16[1344,3072]{1,0:T(8,128)(2,1)} %bitcast.13, f32[4,64,128]{2,1,0:T(8,128)S(1)} %gates.1.refs_1_.gate_ref), custom_call_target="tpu_custom_call" | custom-call | flops 1024 | bytes 1024 | tf_op jit(solution)/shard_map/load_up/pallas_call | solution.py:39
  48.5 1.8 %collective-permute-done.20.refs_1_ = bf16[32,3072]{1,0:T(8,128)(2,1)S(1)} collective-permute-done((bf16[32,3072]{1,0:T(8,128)(2,1)S(1)}, bf16[32,3072]{1,0:T(8,128)(2,1)S(1)}, u32[]{:S(2)}, u32[]{:S(2)}) %collective-permute-start.20) | collective-permute-done | bytes 196640 | tf_op jit(solution)/shard_map/ppermute | solution.py:287
  50.8 2.3 %load_down.1.refs_5_.down_ref.refs_1_ = bf16[768,3072]{1,0:T(8,128)(2,1)S(1)} custom-call(bf16[1344,3072]{1,0:T(8,128)(2,1)} %bitcast.11, bf16[2,32,3072]{2,1,0:T(8,128)(2,1)S(1)} %pair.3.refs_1_.refs_2_), custom_call_target="tpu_custom_call" | custom-call | flops 1024 | bytes 1024 | tf_op jit(solution)/shard_map/load_down/pallas_call | solution.py:39
  53.2 4.5 %lift.1 = (bf16[256,1344]{1,0:T(8,128)(2,1)S(1)}, bf16[2,128,768]{2,1,0:T(8,128)(2,1)S(1)}, bf16[2,128,768]{2,1,0:T(8,128)(2,1)S(1)}, bf16[576,3072]{1,0:T(8,128)(2,1)S(1)}) custom-call(bf16[2,32,3072]{2,1,0:T(8,128)(2,1)S(1)} %pair.2.refs_2_.refs_0_, bf16[2,32,3072]{2,1,0:T(8,128)(2,1)S(1)} %collective-permute-done.19.refs_1_, ...), custom_call_target="tpu_custom_call" | custom-call | flops 1024 | bytes 1024 | tf_op jit(solution)/shard_map/lift/pallas_call | solution.py:392
  59.5 1.3 %collective-permute-start.27 = (bf16[64,768]{1,0:T(8,128)(2,1)S(1)}, bf16[64,768]{1,0:T(8,128)(2,1)S(1)}, u32[]{:S(2)}, u32[]{:S(2)}) collective-permute-start(bf16[64,768]{1,0:T(8,128)(2,1)S(1)} %turn.3.refs_2_), channel_id=1, source_target_pairs={{0,2},{1,3},{2,0},{3,1},{4,6},{5,7},{6,4},{7,5},{8,10},{9,11},{10,... | collective-permute-start | bytes 294920 | tf_op jit(solution)/shard_map/ppermute | solution.py:287
  61.7 1.3 %collective-permute-start.25 = (bf16[64,768]{1,0:T(8,128)(2,1)S(1)}, bf16[64,768]{1,0:T(8,128)(2,1)S(1)}, u32[]{:S(2)}, u32[]{:S(2)}) collective-permute-start(bf16[64,768]{1,0:T(8,128)(2,1)S(1)} %get-tuple-element.34), channel_id=1, source_target_pairs={{0,2},{1,3},{2,0},{3,1},{4,6},{5,7},{6,4},{7,5},{8,10},{9,11},{10,... | collective-permute-start | bytes 294920 | tf_op jit(solution)/shard_map/ppermute | solution.py:287
  65.2 2.3 %collective-permute-start.30 = (bf16[64,768]{1,0:T(8,128)(2,1)S(1)}, bf16[64,768]{1,0:T(8,128)(2,1)S(1)}, u32[]{:S(2)}, u32[]{:S(2)}) collective-permute-start(bf16[64,768]{1,0:T(8,128)(2,1)S(1)} %split.3.refs_3_), channel_id=1, source_target_pairs={{0,12},{4,8},{8,4},{12,0},{1,13},{5,9},{9,5},{13,1},{2,14},{6,10},... | collective-permute-start | bytes 294920 | tf_op jit(solution)/shard_map/ppermute | solution.py:287
  68.2 1.3 %collective-permute-done.25.refs_3_ = bf16[64,768]{1,0:T(8,128)(2,1)S(1)} collective-permute-done((bf16[64,768]{1,0:T(8,128)(2,1)S(1)}, bf16[64,768]{1,0:T(8,128)(2,1)S(1)}, u32[]{:S(2)}, u32[]{:S(2)}) %collective-permute-start.25) | collective-permute-done | bytes 98336 | tf_op jit(solution)/shard_map/ppermute | solution.py:287
  69.4 1.3 %collective-permute-done.24.refs_2_ = bf16[64,768]{1,0:T(8,128)(2,1)S(1)} collective-permute-done((bf16[64,768]{1,0:T(8,128)(2,1)S(1)}, bf16[64,768]{1,0:T(8,128)(2,1)S(1)}, u32[]{:S(2)}, u32[]{:S(2)}) %collective-permute-start.24) | collective-permute-done | bytes 98336 | tf_op jit(solution)/shard_map/ppermute | solution.py:287
  71.7 3.9 %collective-permute-done.29.refs_0_ = bf16[64,768]{1,0:T(8,128)(2,1)S(1)} collective-permute-done((bf16[64,768]{1,0:T(8,128)(2,1)S(1)}, bf16[64,768]{1,0:T(8,128)(2,1)S(1)}, u32[]{:S(2)}, u32[]{:S(2)}) %collective-permute-start.29) | collective-permute-done | bytes 98336 | tf_op jit(solution)/shard_map/ppermute | solution.py:287
  (77 shorter events, 16.5 us)
Async XLA Ops:
  6.3 13.4 %collective-permute-start.5 = (bf16[32,1536]{1,0:T(8,128)(2,1)S(1)}, bf16[32,1536]{1,0:T(8,128)(2,1)S(1)}, u32[]{:S(2)}, u32[]{:S(2)}) collective-permute-start(bf16[32,1536]{1,0:T(8,128)(2,1)S(1)} %attend.2.after_ref.refs_0_), channel_id=1, source_target_pairs={{0,12},{4,8},{8,4},{12,0},{1,13},{5,9},{9,5},{13,1},{2,14},{6,10},... | collective-permute-start | bytes 294920 | tf_op jit(solution)/shard_map/ppermute | solution.py:287
  11.5 13.4 %collective-permute-start.4 = (bf16[32,1536]{1,0:T(8,128)(2,1)S(1)}, bf16[32,1536]{1,0:T(8,128)(2,1)S(1)}, u32[]{:S(2)}, u32[]{:S(2)}) collective-permute-start(bf16[32,1536]{1,0:T(8,128)(2,1)S(1)} %attend.2.after_ref.refs_0_), channel_id=1, source_target_pairs={{0,8},{4,12},{8,0},{12,4},{1,9},{5,13},{9,1},{13,5},{2,10},{6,14},... | collective-permute-start | bytes 294920 | tf_op jit(solution)/shard_map/ppermute | solution.py:287
  11.5 13.4 %collective-permute-start.3 = (bf16[32,1536]{1,0:T(8,128)(2,1)S(1)}, bf16[32,1536]{1,0:T(8,128)(2,1)S(1)}, u32[]{:S(2)}, u32[]{:S(2)}) collective-permute-start(bf16[32,1536]{1,0:T(8,128)(2,1)S(1)} %attend.2.after_ref.refs_0_), channel_id=1, source_target_pairs={{0,4},{4,0},{8,12},{12,8},{1,5},{5,1},{9,13},{13,9},{2,6},{6,2},{1... | collective-permute-start | bytes 294920 | tf_op jit(solution)/shard_map/ppermute | solution.py:287
  15.9 11.1 %collective-permute-start.2 = (bf16[32,1536]{1,0:T(8,128)(2,1)S(1)}, bf16[32,1536]{1,0:T(8,128)(2,1)S(1)}, u32[]{:S(2)}, u32[]{:S(2)}) collective-permute-start(bf16[32,1536]{1,0:T(8,128)(2,1)S(1)} %attend.3.refs_5_.refs_0_), channel_id=1, source_target_pairs={{0,12},{4,8},{8,4},{12,0},{1,13},{5,9},{9,5},{13,1},{2,14},{6,10},... | collective-permute-start | bytes 294920 | tf_op jit(solution)/shard_map/ppermute | solution.py:287
  19.7 8.4 %collective-permute-start.1 = (bf16[32,1536]{1,0:T(8,128)(2,1)S(1)}, bf16[32,1536]{1,0:T(8,128)(2,1)S(1)}, u32[]{:S(2)}, u32[]{:S(2)}) collective-permute-start(bf16[32,1536]{1,0:T(8,128)(2,1)S(1)} %attend.3.refs_5_.refs_0_), channel_id=1, source_target_pairs={{0,8},{4,12},{8,0},{12,4},{1,9},{5,13},{9,1},{13,5},{2,10},{6,14},... | collective-permute-start | bytes 294920 | tf_op jit(solution)/shard_map/ppermute | solution.py:287
  19.7 8.4 %collective-permute-start = (bf16[32,1536]{1,0:T(8,128)(2,1)S(1)}, bf16[32,1536]{1,0:T(8,128)(2,1)S(1)}, u32[]{:S(2)}, u32[]{:S(2)}) collective-permute-start(bf16[32,1536]{1,0:T(8,128)(2,1)S(1)} %attend.3.refs_5_.refs_0_), channel_id=1, source_target_pairs={{0,4},{4,0},{8,12},{12,8},{1,5},{5,1},{9,13},{13,9},{2,6},{6,2},{1... | collective-permute-start | bytes 294920 | tf_op jit(solution)/shard_map/ppermute | solution.py:287
  25.5 5.1 %collective-permute-start.10 = (bf16[32,768]{1,0:T(8,128)(2,1)S(1)}, bf16[32,768]{1,0:T(8,128)(2,1)S(1)}, u32[]{:S(2)}, u32[]{:S(2)}) collective-permute-start(bf16[32,768]{1,0:T(8,128)(2,1)S(1)} %get-tuple-element.27), channel_id=1, source_target_pairs={{0,2},{1,3},{2,0},{3,1},{4,6},{5,7},{6,4},{7,5},{8,10},{9,11},{10,... | collective-permute-start | bytes 147464 | tf_op jit(solution)/shard_map/ppermute | solution.py:287
  28.7 6.5 %collective-permute-start.7 = (bf16[32,768]{1,0:T(8,128)(2,1)S(1)}, bf16[32,768]{1,0:T(8,128)(2,1)S(1)}, u32[]{:S(2)}, u32[]{:S(2)}) collective-permute-start(bf16[32,768]{1,0:T(8,128)(2,1)S(1)} %get-tuple-element.24), channel_id=1, source_target_pairs={{0,2},{1,3},{2,0},{3,1},{4,6},{5,7},{6,4},{7,5},{8,10},{9,11},{10,... | collective-permute-start | bytes 147464 | tf_op jit(solution)/shard_map/ppermute | solution.py:287
  30.3 4.9 %collective-permute-start.8 = (bf16[32,768]{1,0:T(8,128)(2,1)S(1)}, bf16[32,768]{1,0:T(8,128)(2,1)S(1)}, u32[]{:S(2)}, u32[]{:S(2)}) collective-permute-start(bf16[32,768]{1,0:T(8,128)(2,1)S(1)} %get-tuple-element.25), channel_id=1, source_target_pairs={{0,3},{1,2},{2,1},{3,0},{4,7},{5,6},{6,5},{7,4},{8,11},{9,10},{10,... | collective-permute-start | bytes 147464 | tf_op jit(solution)/shard_map/ppermute | solution.py:287
  30.8 7.0 %collective-permute-start.17 = (bf16[32,768]{1,0:T(8,128)(2,1)S(1)}, bf16[32,768]{1,0:T(8,128)(2,1)S(1)}, u32[]{:S(2)}, u32[]{:S(2)}) collective-permute-start(bf16[32,768]{1,0:T(8,128)(2,1)S(1)} %add.2.refs_4_.refs_1_), channel_id=1, source_target_pairs={{0,12},{4,8},{8,4},{12,0},{1,13},{5,9},{9,5},{13,1},{2,14},{6,10},... | collective-permute-start | bytes 147464 | tf_op jit(solution)/shard_map/ppermute | solution.py:287
  33.2 6.5 %collective-permute-start.16 = (bf16[32,768]{1,0:T(8,128)(2,1)S(1)}, bf16[32,768]{1,0:T(8,128)(2,1)S(1)}, u32[]{:S(2)}, u32[]{:S(2)}) collective-permute-start(bf16[32,768]{1,0:T(8,128)(2,1)S(1)} %add.2.refs_4_.refs_1_), channel_id=1, source_target_pairs={{0,8},{4,12},{8,0},{12,4},{1,9},{5,13},{9,1},{13,5},{2,10},{6,14},... | collective-permute-start | bytes 147464 | tf_op jit(solution)/shard_map/ppermute | solution.py:287
  33.2 6.5 %collective-permute-start.15 = (bf16[32,768]{1,0:T(8,128)(2,1)S(1)}, bf16[32,768]{1,0:T(8,128)(2,1)S(1)}, u32[]{:S(2)}, u32[]{:S(2)}) collective-permute-start(bf16[32,768]{1,0:T(8,128)(2,1)S(1)} %add.2.refs_4_.refs_1_), channel_id=1, source_target_pairs={{0,4},{4,0},{8,12},{12,8},{1,5},{5,1},{9,13},{13,9},{2,6},{6,2},{1... | collective-permute-start | bytes 147464 | tf_op jit(solution)/shard_map/ppermute | solution.py:287
  35.3 6.2 %collective-permute-start.14 = (bf16[32,768]{1,0:T(8,128)(2,1)S(1)}, bf16[32,768]{1,0:T(8,128)(2,1)S(1)}, u32[]{:S(2)}, u32[]{:S(2)}) collective-permute-start(bf16[32,768]{1,0:T(8,128)(2,1)S(1)} %add.3.refs_5_.refs_1_), channel_id=1, source_target_pairs={{0,12},{4,8},{8,4},{12,0},{1,13},{5,9},{9,5},{13,1},{2,14},{6,10},... | collective-permute-start | bytes 147464 | tf_op jit(solution)/shard_map/ppermute | solution.py:287
  37.7 5.3 %collective-permute-start.13 = (bf16[32,768]{1,0:T(8,128)(2,1)S(1)}, bf16[32,768]{1,0:T(8,128)(2,1)S(1)}, u32[]{:S(2)}, u32[]{:S(2)}) collective-permute-start(bf16[32,768]{1,0:T(8,128)(2,1)S(1)} %add.3.refs_5_.refs_1_), channel_id=1, source_target_pairs={{0,8},{4,12},{8,0},{12,4},{1,9},{5,13},{9,1},{13,5},{2,10},{6,14},... | collective-permute-start | bytes 147464 | tf_op jit(solution)/shard_map/ppermute | solution.py:287
  37.7 5.3 %collective-permute-start.12 = (bf16[32,768]{1,0:T(8,128)(2,1)S(1)}, bf16[32,768]{1,0:T(8,128)(2,1)S(1)}, u32[]{:S(2)}, u32[]{:S(2)}) collective-permute-start(bf16[32,768]{1,0:T(8,128)(2,1)S(1)} %add.3.refs_5_.refs_1_), channel_id=1, source_target_pairs={{0,4},{4,0},{8,12},{12,8},{1,5},{5,1},{9,13},{13,9},{2,6},{6,2},{1... | collective-permute-start | bytes 147464 | tf_op jit(solution)/shard_map/ppermute | solution.py:287
  40.0 8.4 %collective-permute-start.18 = (bf16[32,3072]{1,0:T(8,128)(2,1)S(1)}, bf16[32,3072]{1,0:T(8,128)(2,1)S(1)}, u32[]{:S(2)}, u32[]{:S(2)}) collective-permute-start(bf16[32,3072]{1,0:T(8,128)(2,1)S(1)} %norm.2.refs_5_.refs_0_), channel_id=1, source_target_pairs={{0,2},{1,3},{2,0},{3,1},{4,6},{5,7},{6,4},{7,5},{8,10},{9,11},{10,... | collective-permute-start | bytes 589832 | tf_op jit(solution)/shard_map/ppermute | solution.py:287
  43.3 6.9 %collective-permute-start.20 = (bf16[32,3072]{1,0:T(8,128)(2,1)S(1)}, bf16[32,3072]{1,0:T(8,128)(2,1)S(1)}, u32[]{:S(2)}, u32[]{:S(2)}) collective-permute-start(bf16[32,3072]{1,0:T(8,128)(2,1)S(1)} %norm.3.refs_2_.refs_0_), channel_id=1, source_target_pairs={{0,2},{1,3},{2,0},{3,1},{4,6},{5,7},{6,4},{7,5},{8,10},{9,11},{10,... | collective-permute-start | bytes 589832 | tf_op jit(solution)/shard_map/ppermute | solution.py:287
  59.5 5.7 %collective-permute-start.27 = (bf16[64,768]{1,0:T(8,128)(2,1)S(1)}, bf16[64,768]{1,0:T(8,128)(2,1)S(1)}, u32[]{:S(2)}, u32[]{:S(2)}) collective-permute-start(bf16[64,768]{1,0:T(8,128)(2,1)S(1)} %turn.3.refs_2_), channel_id=1, source_target_pairs={{0,2},{1,3},{2,0},{3,1},{4,6},{5,7},{6,4},{7,5},{8,10},{9,11},{10,... | collective-permute-start | bytes 294920 | tf_op jit(solution)/shard_map/ppermute | solution.py:287
  60.8 6.8 %collective-permute-start.26 = (bf16[64,768]{1,0:T(8,128)(2,1)S(1)}, bf16[64,768]{1,0:T(8,128)(2,1)S(1)}, u32[]{:S(2)}, u32[]{:S(2)}) collective-permute-start(bf16[64,768]{1,0:T(8,128)(2,1)S(1)} %turn.4.refs_2_), channel_id=1, source_target_pairs={{0,2},{1,3},{2,0},{3,1},{4,6},{5,7},{6,4},{7,5},{8,10},{9,11},{10,... | collective-permute-start | bytes 294920 | tf_op jit(solution)/shard_map/ppermute | solution.py:287
  61.7 7.7 %collective-permute-start.25 = (bf16[64,768]{1,0:T(8,128)(2,1)S(1)}, bf16[64,768]{1,0:T(8,128)(2,1)S(1)}, u32[]{:S(2)}, u32[]{:S(2)}) collective-permute-start(bf16[64,768]{1,0:T(8,128)(2,1)S(1)} %get-tuple-element.34), channel_id=1, source_target_pairs={{0,2},{1,3},{2,0},{3,1},{4,6},{5,7},{6,4},{7,5},{8,10},{9,11},{10,... | collective-permute-start | bytes 294920 | tf_op jit(solution)/shard_map/ppermute | solution.py:287
  63.0 7.7 %collective-permute-start.24 = (bf16[64,768]{1,0:T(8,128)(2,1)S(1)}, bf16[64,768]{1,0:T(8,128)(2,1)S(1)}, u32[]{:S(2)}, u32[]{:S(2)}) collective-permute-start(bf16[64,768]{1,0:T(8,128)(2,1)S(1)} %get-tuple-element.33.refs_3_), channel_id=1, source_target_pairs={{0,2},{1,3},{2,0},{3,1},{4,6},{5,7},{6,4},{7,5},{8,10},{9,11},{10,... | collective-permute-start | bytes 294920 | tf_op jit(solution)/shard_map/ppermute | solution.py:287
  65.2 6.5 %collective-permute-start.30 = (bf16[64,768]{1,0:T(8,128)(2,1)S(1)}, bf16[64,768]{1,0:T(8,128)(2,1)S(1)}, u32[]{:S(2)}, u32[]{:S(2)}) collective-permute-start(bf16[64,768]{1,0:T(8,128)(2,1)S(1)} %split.3.refs_3_), channel_id=1, source_target_pairs={{0,12},{4,8},{8,4},{12,0},{1,13},{5,9},{9,5},{13,1},{2,14},{6,10},... | collective-permute-start | bytes 294920 | tf_op jit(solution)/shard_map/ppermute | solution.py:287
  67.6 8.0 %collective-permute-start.29 = (bf16[64,768]{1,0:T(8,128)(2,1)S(1)}, bf16[64,768]{1,0:T(8,128)(2,1)S(1)}, u32[]{:S(2)}, u32[]{:S(2)}) collective-permute-start(bf16[64,768]{1,0:T(8,128)(2,1)S(1)} %split.4.refs_4_), channel_id=1, source_target_pairs={{0,8},{4,12},{8,0},{12,4},{1,9},{5,13},{9,1},{13,5},{2,10},{6,14},... | collective-permute-start | bytes 294920 | tf_op jit(solution)/shard_map/ppermute | solution.py:287
  70.8 6.0 %collective-permute-start.28 = (bf16[64,768]{1,0:T(8,128)(2,1)S(1)}, bf16[64,768]{1,0:T(8,128)(2,1)S(1)}, u32[]{:S(2)}, u32[]{:S(2)}) collective-permute-start(bf16[64,768]{1,0:T(8,128)(2,1)S(1)} %get-tuple-element.35), channel_id=1, source_target_pairs={{0,4},{4,0},{8,12},{12,8},{1,5},{5,1},{9,13},{13,9},{2,6},{6,2},{1... | collective-permute-start | bytes 294920 | tf_op jit(solution)/shard_map/ppermute | solution.py:287
  (11 other events, 153.5 us)

commit v7 on v6

--- a/solution.py
+++ b/solution.py
@@ -11,7 +11,6 @@
 HD = 128
 MIB = 1 << 20
 MIX_COST = 1 << 22
-PROJECT_COST = 1 << 21
 VMEM = pl.BlockSpec(memory_space=pltpu.VMEM)
 F32 = jnp.float32
 BF16 = jnp.bfloat16
@@ -154,6 +153,10 @@
     out_ref[1] = other_ref[...]
 
 
+def pass_kernel(source_ref, out_ref):
+    out_ref[...] = source_ref[...]
+
+
 def gate_kernel(ids_ref, gates_ref, gate_ref):
     parts, rows, lanes = gate_ref.shape
     ids = ids_ref[pl.ds(pl.multiple_of(lax.axis_index("gx") * rows, rows), rows), :]
@@ -314,43 +317,50 @@
         parts = {0: array, **{s: trade(array, axis, s) for s in order}}
         return [parts[s] for s in range(len(parts))]
 
-    shards = [spread(part, "gx") for part in attended]
-    pieces, hidden = [], []
-    for c in range(chunks):
-        pieces.append(
-            local_call(
-                functools.partial(project_kernel, gx_count),
-                [shape((rows, width), BF16)] * ta_count,
-                [VMEM] * (gx_count + 1),
-                [pltpu.VMEM((ta_count, rows, width), BF16)],
-                name="project",
-                after=pieces[-1][0] if pieces else attended[-1],
-                cost=PROJECT_COST,
-            )(*shards[c], out_proj)
-        )
-    for c in range(chunks):
-        parts = [pieces[c][0]] + [trade(pieces[c][t], "ta", t) for t in range(1, ta_count)]
-        hidden.append(
-            local_call(
-                add_kernel,
-                shape((rows, width), BF16),
-                [VMEM] * ta_count,
-                name="add",
-                after=hidden[-1] if hidden else pieces[-1][0],
-            )(*parts)
-        )
-    shards = [spread(part, "gx") for part in hidden]
-    normed, pairs = [], []
-    for c in range(chunks):
-        normed.append(
-            local_call(
-                functools.partial(norm_kernel, gx_count),
-                shape((rows, model), BF16),
-                [VMEM] * (gx_count + 1),
-                name="norm",
-                after=normed[-1] if normed else hidden[-1],
-            )(gain, *shards[c])
-        )
+    shards = []
+    for part in attended:
+        one, two = trade(part, "gx", 1), trade(part, "gx", 2)
+        onward = local_call(
+            pass_kernel, shape(two.shape, BF16), [VMEM], name="pass", after=one
+        )(two)
+        shards.append([part, one, two, trade(onward, "gx", 1)])
+
+    def project(c, after):
+        pieces = local_call(
+            functools.partial(project_kernel, gx_count),
+            [shape((rows, width), BF16)] * ta_count,
+            [VMEM] * (gx_count + 1),
+            [pltpu.VMEM((ta_count, rows, width), BF16)],
+            name="project",
+            after=after,
+        )(*shards[c], out_proj)
+        return [pieces[0]] + [trade(pieces[t], "ta", t) for t in range(1, ta_count)]
+
+    def close(pieces, after):
+        hidden = local_call(
+            add_kernel,
+            shape((rows, width), BF16),
+            [VMEM] * ta_count,
+            name="add",
+            after=after,
+        )(*pieces)
+        return spread(hidden, "gx")
+
+    def norm(hidden, after):
+        return local_call(
+            functools.partial(norm_kernel, gx_count),
+            shape((rows, model), BF16),
+            [VMEM] * (gx_count + 1),
+            name="norm",
+            after=after,
+        )(gain, *hidden)
+
+    hidden = close(project(0, attended[1]), None)
+    pieces = project(1, hidden[0])
+    normed = [norm(hidden, pieces[0])]
+    hidden = close(pieces, normed[0])
+    normed.append(norm(hidden, None))
+    pairs = []
     gates = local_call(
         gate_kernel,
         shape((gx_count, block_rows, HD), F32),
@@ -378,13 +388,13 @@
             )(normed[c], trade(normed[c], "ta", 2))
         )
     blocks = [block for pair in pairs for block in (pair, trade(pair, "ta", 1))]
-    cut = -(-hidden_share // (4 * HD)) * 2 * HD
+    cut = hidden_share // (4 * HD) * 2 * HD
     part = local_call(
         functools.partial(load_kernel, cut),
         shape((cut, model), BF16),
         [ANYWHERE],
         [pltpu.SemaphoreType.DMA],
-        vmem=42,
+        vmem=46,
         name="load_down",
         after=pairs[-1],
     )(w_down[0])

time: 77.8 us -> 82.5 us (1.060)
  waiting for transfers between devices: 18.4 us -> 26.8 us
  starting transfers between devices: 34.1 us -> 30.8 us
    ppermute x31, waiting for transfers between devices: 18.4 us -> 26.8 us  [trade(): return lax.ppermute(array, axis, [(k, k ^ turn) for k in range(count)])]
    ppermute x31, starting transfers between devices: 34.1 us -> 30.8 us  [trade(): return lax.ppermute(array, axis, [(k, k ^ turn) for k in range(count)])]
  transfers between devices with their start and end apart: 31 -> 31, of which waited for: 12 -> 19; matrix products, arithmetic and copies ran while one was open for 0% -> 0% of each run, Pallas kernels for 17% -> 15%
where the time goes in v7:
time: 82.5 us; the launch traced here: 82.2 us
  starting transfers between devices  30.8 us (37%)
  waiting for transfers between devices  26.8 us (32%)
  Pallas kernels  21.6 us (26%)
  other arithmetic  1.61 us (2%)
  local copies, waits for them, and re-layouts  1.1 us (1%)
    ppermute x31, starting transfers between devices, trade(): return lax.ppermute(array, axis, [(k, k ^ turn) for k in range(count)])  30.8 us
    ppermute x31, waiting for transfers between devices, trade(): return lax.ppermute(array, axis, [(k, k ^ turn) for k in range(count)])  26.8 us
    pallas_call x17, Pallas kernels, local_call(): return call if after is None else lambda *args: call(*args, after)  7.67 us
    pallas_call x2, Pallas kernels, attend(): pl.pallas_call(functools.partial(attend_kernel, kv_heads, heads // kv_hea...  7.63 us
    pallas_call x1, Pallas kernels, every_row_body(): local_call(functools.partial(lift_kernel, chunks), [shape((all_rows, hidd...  4.48 us
  transfers between devices with their start and end apart: 31, of which 19 were waited for; matrix products, arithmetic and copies ran while one was open for 0% of the time, Pallas kernels for 15%

profile of v7, /device:TPU:0, one launch (start us, length us, event | category | flops | bytes accessed | tf_op | source)
XLA Modules:
  0.0 82.2 jit_solution(922032069400705227)
XLA Ops:
  2.5 3.8 %attend.2.after_ref.refs_0_ = bf16[32,1536]{1,0:T(8,128)(2,1)S(1)} custom-call(bf16[64,2304]{1,0:T(8,128)(2,1)S(1)} %pad_maximum_fusion.small_ref.after_ref, bf16[2,64,192,256]{3,2,1,0:T(8,128)(2,1)} %cache_ref.3, bf16[64,2304]{1,0:T(8,128)(2,1)S(1)} %pad_maximum_fusion.small_ref.after_ref), custom_call_target="tpu_custom_call" | custom-call | flops 1024 | bytes 1024 | tf_op jit(solution)/shard_map/attend/pallas_call | solution.py:129
  6.3 4.1 %collective-permute-start.4 = (bf16[32,1536]{1,0:T(8,128)(2,1)S(1)}, bf16[32,1536]{1,0:T(8,128)(2,1)S(1)}, u32[]{:S(2)}, u32[]{:S(2)}) collective-permute-start(bf16[32,1536]{1,0:T(8,128)(2,1)S(1)} %attend.2.after_ref.refs_0_), channel_id=1, source_target_pairs={{0,8},{4,12},{8,0},{12,4},{1,9},{5,13},{9,1},{13,5},{2,10},{6,14},... | collective-permute-start | bytes 294920 | tf_op jit(solution)/shard_map/ppermute | solution.py:290
  10.4 1.6 %collective-permute-start.3 = (bf16[32,1536]{1,0:T(8,128)(2,1)S(1)}, bf16[32,1536]{1,0:T(8,128)(2,1)S(1)}, u32[]{:S(2)}, u32[]{:S(2)}) collective-permute-start(bf16[32,1536]{1,0:T(8,128)(2,1)S(1)} %attend.2.after_ref.refs_0_), channel_id=1, source_target_pairs={{0,4},{4,0},{8,12},{12,8},{1,5},{5,1},{9,13},{13,9},{2,6},{6,2},{1... | collective-permute-start | bytes 294920 | tf_op jit(solution)/shard_map/ppermute | solution.py:290
  12.0 3.8 %attend.3.refs_5_.refs_0_ = bf16[32,1536]{1,0:T(8,128)(2,1)S(1)} custom-call(bf16[64,2304]{1,0:T(8,128)(2,1)S(1)} %pad_maximum_fusion.small_ref.after_ref, bf16[2,64,192,256]{3,2,1,0:T(8,128)(2,1)} %cache_ref.3, bf16[32,1536]{1,0:T(8,128)(2,1)S(1)} %attend.2.after_ref.refs_0_), custom_call_target="tpu_custom_call" | custom-call | flops 1024 | bytes 1024 | tf_op jit(solution)/shard_map/attend/pallas_call | solution.py:129
  16.6 1.8 %collective-permute-start.5 = (bf16[32,1536]{1,0:T(8,128)(2,1)S(1)}, bf16[32,1536]{1,0:T(8,128)(2,1)S(1)}, u32[]{:S(2)}, u32[]{:S(2)}) collective-permute-start(bf16[32,1536]{1,0:T(8,128)(2,1)S(1)} %pass.3), channel_id=1, source_target_pairs={{0,4},{4,0},{8,12},{12,8},{1,5},{5,1},{9,13},{13,9},{2,6},{6,2},{1... | collective-permute-start | bytes 294920 | tf_op jit(solution)/shard_map/ppermute | solution.py:290
  18.4 4.5 %collective-permute-done.1.refs_0_.refs_2_ = bf16[32,1536]{1,0:T(8,128)(2,1)S(1)} collective-permute-done((bf16[32,1536]{1,0:T(8,128)(2,1)S(1)}, bf16[32,1536]{1,0:T(8,128)(2,1)S(1)}, u32[]{:S(2)}, u32[]{:S(2)}) %collective-permute-start.1) | collective-permute-done | bytes 98336 | tf_op jit(solution)/shard_map/ppermute | solution.py:290
  24.8 1.6 %collective-permute-start.7 = (bf16[32,768]{1,0:T(8,128)(2,1)S(1)}, bf16[32,768]{1,0:T(8,128)(2,1)S(1)}, u32[]{:S(2)}, u32[]{:S(2)}) collective-permute-start(bf16[32,768]{1,0:T(8,128)(2,1)S(1)} %get-tuple-element.23), channel_id=1, source_target_pairs={{0,2},{1,3},{2,0},{3,1},{4,6},{5,7},{6,4},{7,5},{8,10},{9,11},{10,... | collective-permute-start | bytes 147464 | tf_op jit(solution)/shard_map/ppermute | solution.py:290
  26.6 2.3 %collective-permute-done.7.refs_2_ = bf16[32,768]{1,0:T(8,128)(2,1)S(1)} collective-permute-done((bf16[32,768]{1,0:T(8,128)(2,1)S(1)}, bf16[32,768]{1,0:T(8,128)(2,1)S(1)}, u32[]{:S(2)}, u32[]{:S(2)}) %collective-permute-start.7) | collective-permute-done | bytes 49184 | tf_op jit(solution)/shard_map/ppermute | solution.py:290
  30.0 2.2 %collective-permute-start.14 = (bf16[32,768]{1,0:T(8,128)(2,1)S(1)}, bf16[32,768]{1,0:T(8,128)(2,1)S(1)}, u32[]{:S(2)}, u32[]{:S(2)}) collective-permute-start(bf16[32,768]{1,0:T(8,128)(2,1)S(1)} %add.2.refs_5_.refs_1_), channel_id=1, source_target_pairs={{0,12},{4,8},{8,4},{12,0},{1,13},{5,9},{9,5},{13,1},{2,14},{6,10},... | collective-permute-start | bytes 147464 | tf_op jit(solution)/shard_map/ppermute | solution.py:290
  32.6 1.9 %collective-permute-start.12 = (bf16[32,768]{1,0:T(8,128)(2,1)S(1)}, bf16[32,768]{1,0:T(8,128)(2,1)S(1)}, u32[]{:S(2)}, u32[]{:S(2)}) collective-permute-start(bf16[32,768]{1,0:T(8,128)(2,1)S(1)} %add.2.refs_5_.refs_1_), channel_id=1, source_target_pairs={{0,4},{4,0},{8,12},{12,8},{1,5},{5,1},{9,13},{13,9},{2,6},{6,2},{1... | collective-permute-start | bytes 147464 | tf_op jit(solution)/shard_map/ppermute | solution.py:290
  40.5 2.0 %collective-permute-start.17 = (bf16[32,768]{1,0:T(8,128)(2,1)S(1)}, bf16[32,768]{1,0:T(8,128)(2,1)S(1)}, u32[]{:S(2)}, u32[]{:S(2)}) collective-permute-start(bf16[32,768]{1,0:T(8,128)(2,1)S(1)} %add.3.refs_0_), channel_id=1, source_target_pairs={{0,12},{4,8},{8,4},{12,0},{1,13},{5,9},{9,5},{13,1},{2,14},{6,10},... | collective-permute-start | bytes 147464 | tf_op jit(solution)/shard_map/ppermute | solution.py:290
  42.5 2.5 %collective-permute-start.15 = (bf16[32,768]{1,0:T(8,128)(2,1)S(1)}, bf16[32,768]{1,0:T(8,128)(2,1)S(1)}, u32[]{:S(2)}, u32[]{:S(2)}) collective-permute-start(bf16[32,768]{1,0:T(8,128)(2,1)S(1)} %add.3.refs_0_), channel_id=1, source_target_pairs={{0,4},{4,0},{8,12},{12,8},{1,5},{5,1},{9,13},{13,9},{2,6},{6,2},{1... | collective-permute-start | bytes 147464 | tf_op jit(solution)/shard_map/ppermute | solution.py:290
  46.7 1.5 %collective-permute-done.16.refs_2_ = bf16[32,768]{1,0:T(8,128)(2,1)S(1)} collective-permute-done((bf16[32,768]{1,0:T(8,128)(2,1)S(1)}, bf16[32,768]{1,0:T(8,128)(2,1)S(1)}, u32[]{:S(2)}, u32[]{:S(2)}) %collective-permute-start.16) | collective-permute-done | bytes 49184 | tf_op jit(solution)/shard_map/ppermute | solution.py:290
  49.8 3.4 %load_up.1.refs_2_.refs_4_ = bf16[1344,3072]{1,0:T(8,128)(2,1)S(1)} custom-call(bf16[1344,3072]{1,0:T(8,128)(2,1)} %bitcast.13, f32[4,64,128]{2,1,0:T(8,128)S(1)} %gates.1.refs_1_.gate_ref), custom_call_target="tpu_custom_call" | custom-call | flops 1024 | bytes 1024 | tf_op jit(solution)/shard_map/load_up/pallas_call | solution.py:38
  53.3 1.9 %collective-permute-done.20.refs_1_ = bf16[32,3072]{1,0:T(8,128)(2,1)S(1)} collective-permute-done((bf16[32,3072]{1,0:T(8,128)(2,1)S(1)}, bf16[32,3072]{1,0:T(8,128)(2,1)S(1)}, u32[]{:S(2)}, u32[]{:S(2)}) %collective-permute-start.20) | collective-permute-done | bytes 196640 | tf_op jit(solution)/shard_map/ppermute | solution.py:290
  55.4 1.9 %load_down.1.refs_5_.down_ref.refs_1_ = bf16[512,3072]{1,0:T(8,128)(2,1)S(1)} custom-call(bf16[1344,3072]{1,0:T(8,128)(2,1)} %bitcast.11, bf16[2,32,3072]{2,1,0:T(8,128)(2,1)S(1)} %pair.3.refs_1_.refs_2_), custom_call_target="tpu_custom_call" | custom-call | flops 1024 | bytes 1024 | tf_op jit(solution)/shard_map/load_down/pallas_call | solution.py:38
  57.3 4.5 %lift.1 = (bf16[256,1344]{1,0:T(8,128)(2,1)S(1)}, bf16[2,128,768]{2,1,0:T(8,128)(2,1)S(1)}, bf16[2,128,768]{2,1,0:T(8,128)(2,1)S(1)}, bf16[832,3072]{1,0:T(8,128)(2,1)S(1)}) custom-call(bf16[2,32,3072]{2,1,0:T(8,128)(2,1)S(1)} %pair.2.refs_2_.refs_0_, bf16[2,32,3072]{2,1,0:T(8,128)(2,1)S(1)} %collective-permute-done.19.refs_1_, ...), custom_call_target="tpu_custom_call" | custom-call | flops 1024 | bytes 1024 | tf_op jit(solution)/shard_map/lift/pallas_call | solution.py:402
  64.5 1.4 %collective-permute-start.26 = (bf16[64,768]{1,0:T(8,128)(2,1)S(1)}, bf16[64,768]{1,0:T(8,128)(2,1)S(1)}, u32[]{:S(2)}, u32[]{:S(2)}) collective-permute-start(bf16[64,768]{1,0:T(8,128)(2,1)S(1)} %turn.4.refs_2_), channel_id=1, source_target_pairs={{0,2},{1,3},{2,0},{3,1},{4,6},{5,7},{6,4},{7,5},{8,10},{9,11},{10,... | collective-permute-start | bytes 294920 | tf_op jit(solution)/shard_map/ppermute | solution.py:290
  66.7 1.4 %collective-permute-start.24 = (bf16[64,768]{1,0:T(8,128)(2,1)S(1)}, bf16[64,768]{1,0:T(8,128)(2,1)S(1)}, u32[]{:S(2)}, u32[]{:S(2)}) collective-permute-start(bf16[64,768]{1,0:T(8,128)(2,1)S(1)} %get-tuple-element.33.refs_3_), channel_id=1, source_target_pairs={{0,2},{1,3},{2,0},{3,1},{4,6},{5,7},{6,4},{7,5},{8,10},{9,11},{10,... | collective-permute-start | bytes 294920 | tf_op jit(solution)/shard_map/ppermute | solution.py:290
  69.4 2.3 %collective-permute-start.30 = (bf16[64,768]{1,0:T(8,128)(2,1)S(1)}, bf16[64,768]{1,0:T(8,128)(2,1)S(1)}, u32[]{:S(2)}, u32[]{:S(2)}) collective-permute-start(bf16[64,768]{1,0:T(8,128)(2,1)S(1)} %split.3.refs_3_), channel_id=1, source_target_pairs={{0,12},{4,8},{8,4},{12,0},{1,13},{5,9},{9,5},{13,1},{2,14},{6,10},... | collective-permute-start | bytes 294920 | tf_op jit(solution)/shard_map/ppermute | solution.py:290
  72.3 1.3 %collective-permute-done.25.refs_3_ = bf16[64,768]{1,0:T(8,128)(2,1)S(1)} collective-permute-done((bf16[64,768]{1,0:T(8,128)(2,1)S(1)}, bf16[64,768]{1,0:T(8,128)(2,1)S(1)}, u32[]{:S(2)}, u32[]{:S(2)}) %collective-permute-start.25) | collective-permute-done | bytes 98336 | tf_op jit(solution)/shard_map/ppermute | solution.py:290
  73.6 1.6 %collective-permute-done.24.refs_2_ = bf16[64,768]{1,0:T(8,128)(2,1)S(1)} collective-permute-done((bf16[64,768]{1,0:T(8,128)(2,1)S(1)}, bf16[64,768]{1,0:T(8,128)(2,1)S(1)}, u32[]{:S(2)}, u32[]{:S(2)}) %collective-permute-start.24) | collective-permute-done | bytes 98336 | tf_op jit(solution)/shard_map/ppermute | solution.py:290
  76.2 4.0 %collective-permute-done.29.refs_0_ = bf16[64,768]{1,0:T(8,128)(2,1)S(1)} collective-permute-done((bf16[64,768]{1,0:T(8,128)(2,1)S(1)}, bf16[64,768]{1,0:T(8,128)(2,1)S(1)}, u32[]{:S(2)}, u32[]{:S(2)}) %collective-permute-start.29) | collective-permute-done | bytes 98336 | tf_op jit(solution)/shard_map/ppermute | solution.py:290
  80.2 1.3 %collective-permute-done.28.refs_0_ = bf16[64,768]{1,0:T(8,128)(2,1)S(1)} collective-permute-done((bf16[64,768]{1,0:T(8,128)(2,1)S(1)}, bf16[64,768]{1,0:T(8,128)(2,1)S(1)}, u32[]{:S(2)}, u32[]{:S(2)}) %collective-permute-start.28) | collective-permute-done | bytes 98336 | tf_op jit(solution)/shard_map/ppermute | solution.py:290
  (79 shorter events, 23.6 us)
Async XLA Ops:
  6.3 10.2 %collective-permute-start.4 = (bf16[32,1536]{1,0:T(8,128)(2,1)S(1)}, bf16[32,1536]{1,0:T(8,128)(2,1)S(1)}, u32[]{:S(2)}, u32[]{:S(2)}) collective-permute-start(bf16[32,1536]{1,0:T(8,128)(2,1)S(1)} %attend.2.after_ref.refs_0_), channel_id=1, source_target_pairs={{0,8},{4,12},{8,0},{12,4},{1,9},{5,13},{9,1},{13,5},{2,10},{6,14},... | collective-permute-start | bytes 294920 | tf_op jit(solution)/shard_map/ppermute | solution.py:290
  10.4 6.1 %collective-permute-start.3 = (bf16[32,1536]{1,0:T(8,128)(2,1)S(1)}, bf16[32,1536]{1,0:T(8,128)(2,1)S(1)}, u32[]{:S(2)}, u32[]{:S(2)}) collective-permute-start(bf16[32,1536]{1,0:T(8,128)(2,1)S(1)} %attend.2.after_ref.refs_0_), channel_id=1, source_target_pairs={{0,4},{4,0},{8,12},{12,8},{1,5},{5,1},{9,13},{13,9},{2,6},{6,2},{1... | collective-permute-start | bytes 294920 | tf_op jit(solution)/shard_map/ppermute | solution.py:290
  15.8 7.0 %collective-permute-start.1 = (bf16[32,1536]{1,0:T(8,128)(2,1)S(1)}, bf16[32,1536]{1,0:T(8,128)(2,1)S(1)}, u32[]{:S(2)}, u32[]{:S(2)}) collective-permute-start(bf16[32,1536]{1,0:T(8,128)(2,1)S(1)} %attend.3.refs_5_.refs_0_), channel_id=1, source_target_pairs={{0,8},{4,12},{8,0},{12,4},{1,9},{5,13},{9,1},{13,5},{2,10},{6,14},... | collective-permute-start | bytes 294920 | tf_op jit(solution)/shard_map/ppermute | solution.py:290
  16.2 6.9 %collective-permute-start = (bf16[32,1536]{1,0:T(8,128)(2,1)S(1)}, bf16[32,1536]{1,0:T(8,128)(2,1)S(1)}, u32[]{:S(2)}, u32[]{:S(2)}) collective-permute-start(bf16[32,1536]{1,0:T(8,128)(2,1)S(1)} %attend.3.refs_5_.refs_0_), channel_id=1, source_target_pairs={{0,4},{4,0},{8,12},{12,8},{1,5},{5,1},{9,13},{13,9},{2,6},{6,2},{1... | collective-permute-start | bytes 294920 | tf_op jit(solution)/shard_map/ppermute | solution.py:290
  16.6 7.6 %collective-permute-start.5 = (bf16[32,1536]{1,0:T(8,128)(2,1)S(1)}, bf16[32,1536]{1,0:T(8,128)(2,1)S(1)}, u32[]{:S(2)}, u32[]{:S(2)}) collective-permute-start(bf16[32,1536]{1,0:T(8,128)(2,1)S(1)} %pass.3), channel_id=1, source_target_pairs={{0,4},{4,0},{8,12},{12,8},{1,5},{5,1},{9,13},{13,9},{2,6},{6,2},{1... | collective-permute-start | bytes 294920 | tf_op jit(solution)/shard_map/ppermute | solution.py:290
  23.1 11.4 %collective-permute-start.2 = (bf16[32,1536]{1,0:T(8,128)(2,1)S(1)}, bf16[32,1536]{1,0:T(8,128)(2,1)S(1)}, u32[]{:S(2)}, u32[]{:S(2)}) collective-permute-start(bf16[32,1536]{1,0:T(8,128)(2,1)S(1)} %pass.2), channel_id=1, source_target_pairs={{0,4},{4,0},{8,12},{12,8},{1,5},{5,1},{9,13},{13,9},{2,6},{6,2},{1... | collective-permute-start | bytes 294920 | tf_op jit(solution)/shard_map/ppermute | solution.py:290
  24.8 4.2 %collective-permute-start.7 = (bf16[32,768]{1,0:T(8,128)(2,1)S(1)}, bf16[32,768]{1,0:T(8,128)(2,1)S(1)}, u32[]{:S(2)}, u32[]{:S(2)}) collective-permute-start(bf16[32,768]{1,0:T(8,128)(2,1)S(1)} %get-tuple-element.23), channel_id=1, source_target_pairs={{0,2},{1,3},{2,0},{3,1},{4,6},{5,7},{6,4},{7,5},{8,10},{9,11},{10,... | collective-permute-start | bytes 147464 | tf_op jit(solution)/shard_map/ppermute | solution.py:290
  30.0 6.4 %collective-permute-start.14 = (bf16[32,768]{1,0:T(8,128)(2,1)S(1)}, bf16[32,768]{1,0:T(8,128)(2,1)S(1)}, u32[]{:S(2)}, u32[]{:S(2)}) collective-permute-start(bf16[32,768]{1,0:T(8,128)(2,1)S(1)} %add.2.refs_5_.refs_1_), channel_id=1, source_target_pairs={{0,12},{4,8},{8,4},{12,0},{1,13},{5,9},{9,5},{13,1},{2,14},{6,10},... | collective-permute-start | bytes 147464 | tf_op jit(solution)/shard_map/ppermute | solution.py:290
  32.2 5.9 %collective-permute-start.13 = (bf16[32,768]{1,0:T(8,128)(2,1)S(1)}, bf16[32,768]{1,0:T(8,128)(2,1)S(1)}, u32[]{:S(2)}, u32[]{:S(2)}) collective-permute-start(bf16[32,768]{1,0:T(8,128)(2,1)S(1)} %add.2.refs_5_.refs_1_), channel_id=1, source_target_pairs={{0,8},{4,12},{8,0},{12,4},{1,9},{5,13},{9,1},{13,5},{2,10},{6,14},... | collective-permute-start | bytes 147464 | tf_op jit(solution)/shard_map/ppermute | solution.py:290
  32.6 5.5 %collective-permute-start.12 = (bf16[32,768]{1,0:T(8,128)(2,1)S(1)}, bf16[32,768]{1,0:T(8,128)(2,1)S(1)}, u32[]{:S(2)}, u32[]{:S(2)}) collective-permute-start(bf16[32,768]{1,0:T(8,128)(2,1)S(1)} %add.2.refs_5_.refs_1_), channel_id=1, source_target_pairs={{0,4},{4,0},{8,12},{12,8},{1,5},{5,1},{9,13},{13,9},{2,6},{6,2},{1... | collective-permute-start | bytes 147464 | tf_op jit(solution)/shard_map/ppermute | solution.py:290
  35.1 4.2 %collective-permute-start.10 = (bf16[32,768]{1,0:T(8,128)(2,1)S(1)}, bf16[32,768]{1,0:T(8,128)(2,1)S(1)}, u32[]{:S(2)}, u32[]{:S(2)}) collective-permute-start(bf16[32,768]{1,0:T(8,128)(2,1)S(1)} %get-tuple-element.27), channel_id=1, source_target_pairs={{0,2},{1,3},{2,0},{3,1},{4,6},{5,7},{6,4},{7,5},{8,10},{9,11},{10,... | collective-permute-start | bytes 147464 | tf_op jit(solution)/shard_map/ppermute | solution.py:290
  40.5 6.3 %collective-permute-start.17 = (bf16[32,768]{1,0:T(8,128)(2,1)S(1)}, bf16[32,768]{1,0:T(8,128)(2,1)S(1)}, u32[]{:S(2)}, u32[]{:S(2)}) collective-permute-start(bf16[32,768]{1,0:T(8,128)(2,1)S(1)} %add.3.refs_0_), channel_id=1, source_target_pairs={{0,12},{4,8},{8,4},{12,0},{1,13},{5,9},{9,5},{13,1},{2,14},{6,10},... | collective-permute-start | bytes 147464 | tf_op jit(solution)/shard_map/ppermute | solution.py:290
  42.5 5.7 %collective-permute-start.16 = (bf16[32,768]{1,0:T(8,128)(2,1)S(1)}, bf16[32,768]{1,0:T(8,128)(2,1)S(1)}, u32[]{:S(2)}, u32[]{:S(2)}) collective-permute-start(bf16[32,768]{1,0:T(8,128)(2,1)S(1)} %add.3.refs_0_), channel_id=1, source_target_pairs={{0,8},{4,12},{8,0},{12,4},{1,9},{5,13},{9,1},{13,5},{2,10},{6,14},... | collective-permute-start | bytes 147464 | tf_op jit(solution)/shard_map/ppermute | solution.py:290
  42.5 5.7 %collective-permute-start.15 = (bf16[32,768]{1,0:T(8,128)(2,1)S(1)}, bf16[32,768]{1,0:T(8,128)(2,1)S(1)}, u32[]{:S(2)}, u32[]{:S(2)}) collective-permute-start(bf16[32,768]{1,0:T(8,128)(2,1)S(1)} %add.3.refs_0_), channel_id=1, source_target_pairs={{0,4},{4,0},{8,12},{12,8},{1,5},{5,1},{9,13},{13,9},{2,6},{6,2},{1... | collective-permute-start | bytes 147464 | tf_op jit(solution)/shard_map/ppermute | solution.py:290
  44.9 8.3 %collective-permute-start.18 = (bf16[32,3072]{1,0:T(8,128)(2,1)S(1)}, bf16[32,3072]{1,0:T(8,128)(2,1)S(1)}, u32[]{:S(2)}, u32[]{:S(2)}) collective-permute-start(bf16[32,3072]{1,0:T(8,128)(2,1)S(1)} %norm.2.refs_4_.refs_0_), channel_id=1, source_target_pairs={{0,2},{1,3},{2,0},{3,1},{4,6},{5,7},{6,4},{7,5},{8,10},{9,11},{10,... | collective-permute-start | bytes 589832 | tf_op jit(solution)/shard_map/ppermute | solution.py:290
  48.5 6.8 %collective-permute-start.20 = (bf16[32,3072]{1,0:T(8,128)(2,1)S(1)}, bf16[32,3072]{1,0:T(8,128)(2,1)S(1)}, u32[]{:S(2)}, u32[]{:S(2)}) collective-permute-start(bf16[32,3072]{1,0:T(8,128)(2,1)S(1)} %norm.3.refs_2_.refs_0_), channel_id=1, source_target_pairs={{0,2},{1,3},{2,0},{3,1},{4,6},{5,7},{6,4},{7,5},{8,10},{9,11},{10,... | collective-permute-start | bytes 589832 | tf_op jit(solution)/shard_map/ppermute | solution.py:290
  53.2 4.0 %collective-permute-start.19 = (bf16[2,32,3072]{2,1,0:T(8,128)(2,1)S(1)}, bf16[2,32,3072]{2,1,0:T(8,128)(2,1)S(1)}, u32[]{:S(2)}, u32[]{:S(2)}) collective-permute-start(bf16[2,32,3072]{2,1,0:T(8,128)(2,1)S(1)} %pair.2.refs_2_.refs_0_), channel_id=1, source_target_pairs={{0,1},{1,0},{2,3},{3,2},{4,5},{5,4},{6,7},{7,6},{8,9},{9,8},{10,11... | collective-permute-start | bytes 1179656 | tf_op jit(solution)/shard_map/ppermute | solution.py:290
  63.7 5.7 %collective-permute-start.27 = (bf16[64,768]{1,0:T(8,128)(2,1)S(1)}, bf16[64,768]{1,0:T(8,128)(2,1)S(1)}, u32[]{:S(2)}, u32[]{:S(2)}) collective-permute-start(bf16[64,768]{1,0:T(8,128)(2,1)S(1)} %turn.3.refs_2_), channel_id=1, source_target_pairs={{0,2},{1,3},{2,0},{3,1},{4,6},{5,7},{6,4},{7,5},{8,10},{9,11},{10,... | collective-permute-start | bytes 294920 | tf_op jit(solution)/shard_map/ppermute | solution.py:290
  64.5 7.3 %collective-permute-start.26 = (bf16[64,768]{1,0:T(8,128)(2,1)S(1)}, bf16[64,768]{1,0:T(8,128)(2,1)S(1)}, u32[]{:S(2)}, u32[]{:S(2)}) collective-permute-start(bf16[64,768]{1,0:T(8,128)(2,1)S(1)} %turn.4.refs_2_), channel_id=1, source_target_pairs={{0,2},{1,3},{2,0},{3,1},{4,6},{5,7},{6,4},{7,5},{8,10},{9,11},{10,... | collective-permute-start | bytes 294920 | tf_op jit(solution)/shard_map/ppermute | solution.py:290
  65.9 7.7 %collective-permute-start.25 = (bf16[64,768]{1,0:T(8,128)(2,1)S(1)}, bf16[64,768]{1,0:T(8,128)(2,1)S(1)}, u32[]{:S(2)}, u32[]{:S(2)}) collective-permute-start(bf16[64,768]{1,0:T(8,128)(2,1)S(1)} %get-tuple-element.34), channel_id=1, source_target_pairs={{0,2},{1,3},{2,0},{3,1},{4,6},{5,7},{6,4},{7,5},{8,10},{9,11},{10,... | collective-permute-start | bytes 294920 | tf_op jit(solution)/shard_map/ppermute | solution.py:290
  66.7 8.5 %collective-permute-start.24 = (bf16[64,768]{1,0:T(8,128)(2,1)S(1)}, bf16[64,768]{1,0:T(8,128)(2,1)S(1)}, u32[]{:S(2)}, u32[]{:S(2)}) collective-permute-start(bf16[64,768]{1,0:T(8,128)(2,1)S(1)} %get-tuple-element.33.refs_3_), channel_id=1, source_target_pairs={{0,2},{1,3},{2,0},{3,1},{4,6},{5,7},{6,4},{7,5},{8,10},{9,11},{10,... | collective-permute-start | bytes 294920 | tf_op jit(solution)/shard_map/ppermute | solution.py:290
  69.4 6.7 %collective-permute-start.30 = (bf16[64,768]{1,0:T(8,128)(2,1)S(1)}, bf16[64,768]{1,0:T(8,128)(2,1)S(1)}, u32[]{:S(2)}, u32[]{:S(2)}) collective-permute-start(bf16[64,768]{1,0:T(8,128)(2,1)S(1)} %split.3.refs_3_), channel_id=1, source_target_pairs={{0,12},{4,8},{8,4},{12,0},{1,13},{5,9},{9,5},{13,1},{2,14},{6,10},... | collective-permute-start | bytes 294920 | tf_op jit(solution)/shard_map/ppermute | solution.py:290
  71.8 8.4 %collective-permute-start.29 = (bf16[64,768]{1,0:T(8,128)(2,1)S(1)}, bf16[64,768]{1,0:T(8,128)(2,1)S(1)}, u32[]{:S(2)}, u32[]{:S(2)}) collective-permute-start(bf16[64,768]{1,0:T(8,128)(2,1)S(1)} %split.4.refs_4_), channel_id=1, source_target_pairs={{0,8},{4,12},{8,0},{12,4},{1,9},{5,13},{9,1},{13,5},{2,10},{6,14},... | collective-permute-start | bytes 294920 | tf_op jit(solution)/shard_map/ppermute | solution.py:290
  75.2 6.3 %collective-permute-start.28 = (bf16[64,768]{1,0:T(8,128)(2,1)S(1)}, bf16[64,768]{1,0:T(8,128)(2,1)S(1)}, u32[]{:S(2)}, u32[]{:S(2)}) collective-permute-start(bf16[64,768]{1,0:T(8,128)(2,1)S(1)} %get-tuple-element.35), channel_id=1, source_target_pairs={{0,4},{4,0},{8,12},{12,8},{1,5},{5,1},{9,13},{13,9},{2,6},{6,2},{1... | collective-permute-start | bytes 294920 | tf_op jit(solution)/shard_map/ppermute | solution.py:290
  (11 other events, 156.6 us)

commit v8 on v6

--- a/solution.py
+++ b/solution.py
@@ -378,13 +378,13 @@
             )(normed[c], trade(normed[c], "ta", 2))
         )
     blocks = [block for pair in pairs for block in (pair, trade(pair, "ta", 1))]
-    cut = -(-hidden_share // (4 * HD)) * 2 * HD
+    cut = hidden_share // (4 * HD) * 2 * HD
     part = local_call(
         functools.partial(load_kernel, cut),
         shape((cut, model), BF16),
         [ANYWHERE],
         [pltpu.SemaphoreType.DMA],
-        vmem=42,
+        vmem=46,
         name="load_down",
         after=pairs[-1],
     )(w_down[0])
@@ -426,36 +426,39 @@
             after=after,
         )(*arrays)
 
-    cross = lower(2, None)
-    groups = ((3,), (2,), (1, 0))
-    turned = [cross]
-    crossed = {}
-    for distances in groups:
-        sums = on_rows(turn_kernel, distances, turned[0], cross, near[distances[0] // 2])
-        turned = sums
-        crossed.update({s: trade(part, "ta", 2) for s, part in zip(distances, sums)})
-    own = lower(0, turned[0])
-    gathered, total, after = {}, [], None
-    for distances in groups:
-        terms = on_rows(
-            split_kernel, distances, after, own, near[distances[0] // 2],
-            *[crossed[s] for s in distances],
-        )
-        after = terms[0]
+    gathered = {}
+
+    def turn(distances, after):
+        sums = on_rows(turn_kernel, distances, after, cross, near[distances[0] // 2])
+        return sums, [trade(part, "ta", 2) for part in sums]
+
+    def split(distances, after, crossed):
+        terms = on_rows(split_kernel, distances, after, own, near[distances[0] // 2], *crossed)
         for s, term in zip(distances, terms):
             gathered[s] = trade(term, "gx", s) if s else term
-    for distances in groups:
-        last = 0 in distances
-        total = [
-            local_call(
-                functools.partial(mix_kernel, distances),
-                shape((block_rows, share), BF16 if last else F32),
-                [VMEM] * (1 + len(distances) + len(total)),
-                name="mix",
-                cost=1024 if last else MIX_COST,
-            )(gates, *[gathered[s] for s in distances], *total)
-        ]
-    return total[0]
+        return terms
+
+    def mix(distances, after, earlier, kind=F32):
+        return local_call(
+            functools.partial(mix_kernel, distances),
+            shape((block_rows, share), kind),
+            [VMEM] * (1 + len(distances) + len(earlier)),
+            name="mix",
+            after=after,
+            cost=1024 if kind == BF16 else MIX_COST,
+        )(gates, *[gathered[s] for s in distances], *earlier)
+
+    cross = lower(2, None)
+    sums, first = turn((3,), None)
+    sums, second = turn((2,), sums[0])
+    own = lower(0, sums[0])
+    terms = split((3,), None, first)
+    sums, third = turn((1, 0), terms[0])
+    terms = split((2,), sums[0], second)
+    partial = mix((3,), terms[0], [])
+    split((1, 0), partial, third)
+    partial = mix((2,), None, [partial])
+    return mix((1, 0), None, [partial], BF16)
 
 
 def route_tables(expert_ids, expert_count, block_rows, capacity):

time: 77.8 us -> 79.1 us (1.017)
  waiting for transfers between devices: 18.4 us -> 20.5 us
    ppermute x31, waiting for transfers between devices: 18.4 us -> 20.5 us  [trade(): return lax.ppermute(array, axis, [(k, k ^ turn) for k in range(count)])]
  transfers between devices with their start and end apart: 31 -> 31, of which waited for: 12 -> 11; matrix products, arithmetic and copies ran while one was open for 0% -> 0% of each run, Pallas kernels for 17% -> 16%
where the time goes in v8:
time: 79.1 us; the launch traced here: 78.8 us
  starting transfers between devices  33.7 us (43%)
  Pallas kernels  21.6 us (27%)
  waiting for transfers between devices  20.5 us (26%)
  other arithmetic  1.61 us (2%)
  local copies, waits for them, and re-layouts  1.1 us (1%)
    ppermute x31, starting transfers between devices, trade(): return lax.ppermute(array, axis, [(k, k ^ turn) for k in range(count)])  33.7 us
    ppermute x31, waiting for transfers between devices, trade(): return lax.ppermute(array, axis, [(k, k ^ turn) for k in range(count)])  20.5 us
    pallas_call x17, Pallas kernels, local_call(): return call if after is None else lambda *args: call(*args, after)  7.95 us
    pallas_call x2, Pallas kernels, attend(): pl.pallas_call(functools.partial(attend_kernel, kv_heads, heads // kv_hea...  7.63 us
    pallas_call x1, Pallas kernels, every_row_body(): local_call(functools.partial(lift_kernel, chunks), [shape((all_rows, hidd...  4.48 us
  transfers between devices with their start and end apart: 31, of which 11 were waited for; matrix products, arithmetic and copies ran while one was open for 0% of the time, Pallas kernels for 16%

profile of v8, /device:TPU:0, one launch (start us, length us, event | category | flops | bytes accessed | tf_op | source)
XLA Modules:
  0.0 78.8 jit_solution(16624096842571271547)
XLA Ops:
  2.5 3.8 %attend.2.after_ref.refs_0_ = bf16[32,1536]{1,0:T(8,128)(2,1)S(1)} custom-call(bf16[64,2304]{1,0:T(8,128)(2,1)S(1)} %pad_maximum_fusion.small_ref.after_ref, bf16[2,64,192,256]{3,2,1,0:T(8,128)(2,1)} %cache_ref.3, bf16[64,2304]{1,0:T(8,128)(2,1)S(1)} %pad_maximum_fusion.small_ref.after_ref), custom_call_target="tpu_custom_call" | custom-call | flops 1024 | bytes 1024 | tf_op jit(solution)/shard_map/attend/pallas_call | solution.py:130
  6.3 5.1 %collective-permute-start.5 = (bf16[32,1536]{1,0:T(8,128)(2,1)S(1)}, bf16[32,1536]{1,0:T(8,128)(2,1)S(1)}, u32[]{:S(2)}, u32[]{:S(2)}) collective-permute-start(bf16[32,1536]{1,0:T(8,128)(2,1)S(1)} %attend.2.after_ref.refs_0_), channel_id=1, source_target_pairs={{0,12},{4,8},{8,4},{12,0},{1,13},{5,9},{9,5},{13,1},{2,14},{6,10},... | collective-permute-start | bytes 294920 | tf_op jit(solution)/shard_map/ppermute | solution.py:287
  12.1 3.8 %attend.3.refs_5_.refs_0_ = bf16[32,1536]{1,0:T(8,128)(2,1)S(1)} custom-call(bf16[64,2304]{1,0:T(8,128)(2,1)S(1)} %pad_maximum_fusion.small_ref.after_ref, bf16[2,64,192,256]{3,2,1,0:T(8,128)(2,1)} %cache_ref.3, bf16[32,1536]{1,0:T(8,128)(2,1)S(1)} %attend.2.after_ref.refs_0_), custom_call_target="tpu_custom_call" | custom-call | flops 1024 | bytes 1024 | tf_op jit(solution)/shard_map/attend/pallas_call | solution.py:130
  15.9 3.8 %collective-permute-start.2 = (bf16[32,1536]{1,0:T(8,128)(2,1)S(1)}, bf16[32,1536]{1,0:T(8,128)(2,1)S(1)}, u32[]{:S(2)}, u32[]{:S(2)}) collective-permute-start(bf16[32,1536]{1,0:T(8,128)(2,1)S(1)} %attend.3.refs_5_.refs_0_), channel_id=1, source_target_pairs={{0,12},{4,8},{8,4},{12,0},{1,13},{5,9},{9,5},{13,1},{2,14},{6,10},... | collective-permute-start | bytes 294920 | tf_op jit(solution)/shard_map/ppermute | solution.py:287
  20.4 4.5 %collective-permute-done.4.refs_2_ = bf16[32,1536]{1,0:T(8,128)(2,1)S(1)} collective-permute-done((bf16[32,1536]{1,0:T(8,128)(2,1)S(1)}, bf16[32,1536]{1,0:T(8,128)(2,1)S(1)}, u32[]{:S(2)}, u32[]{:S(2)}) %collective-permute-start.4) | collective-permute-done | bytes 98336 | tf_op jit(solution)/shard_map/ppermute | solution.py:287
  25.5 1.6 %collective-permute-start.10 = (bf16[32,768]{1,0:T(8,128)(2,1)S(1)}, bf16[32,768]{1,0:T(8,128)(2,1)S(1)}, u32[]{:S(2)}, u32[]{:S(2)}) collective-permute-start(bf16[32,768]{1,0:T(8,128)(2,1)S(1)} %get-tuple-element.27), channel_id=1, source_target_pairs={{0,2},{1,3},{2,0},{3,1},{4,6},{5,7},{6,4},{7,5},{8,10},{9,11},{10,... | collective-permute-start | bytes 147464 | tf_op jit(solution)/shard_map/ppermute | solution.py:287
  28.7 1.6 %collective-permute-start.7 = (bf16[32,768]{1,0:T(8,128)(2,1)S(1)}, bf16[32,768]{1,0:T(8,128)(2,1)S(1)}, u32[]{:S(2)}, u32[]{:S(2)}) collective-permute-start(bf16[32,768]{1,0:T(8,128)(2,1)S(1)} %get-tuple-element.24), channel_id=1, source_target_pairs={{0,2},{1,3},{2,0},{3,1},{4,6},{5,7},{6,4},{7,5},{8,10},{9,11},{10,... | collective-permute-start | bytes 147464 | tf_op jit(solution)/shard_map/ppermute | solution.py:287
  30.8 2.4 %collective-permute-start.17 = (bf16[32,768]{1,0:T(8,128)(2,1)S(1)}, bf16[32,768]{1,0:T(8,128)(2,1)S(1)}, u32[]{:S(2)}, u32[]{:S(2)}) collective-permute-start(bf16[32,768]{1,0:T(8,128)(2,1)S(1)} %add.2.refs_4_.refs_1_), channel_id=1, source_target_pairs={{0,12},{4,8},{8,4},{12,0},{1,13},{5,9},{9,5},{13,1},{2,14},{6,10},... | collective-permute-start | bytes 147464 | tf_op jit(solution)/shard_map/ppermute | solution.py:287
  33.2 2.0 %collective-permute-start.15 = (bf16[32,768]{1,0:T(8,128)(2,1)S(1)}, bf16[32,768]{1,0:T(8,128)(2,1)S(1)}, u32[]{:S(2)}, u32[]{:S(2)}) collective-permute-start(bf16[32,768]{1,0:T(8,128)(2,1)S(1)} %add.2.refs_4_.refs_1_), channel_id=1, source_target_pairs={{0,4},{4,0},{8,12},{12,8},{1,5},{5,1},{9,13},{13,9},{2,6},{6,2},{1... | collective-permute-start | bytes 147464 | tf_op jit(solution)/shard_map/ppermute | solution.py:287
  35.3 2.4 %collective-permute-start.14 = (bf16[32,768]{1,0:T(8,128)(2,1)S(1)}, bf16[32,768]{1,0:T(8,128)(2,1)S(1)}, u32[]{:S(2)}, u32[]{:S(2)}) collective-permute-start(bf16[32,768]{1,0:T(8,128)(2,1)S(1)} %add.3.refs_5_.refs_1_), channel_id=1, source_target_pairs={{0,12},{4,8},{8,4},{12,0},{1,13},{5,9},{9,5},{13,1},{2,14},{6,10},... | collective-permute-start | bytes 147464 | tf_op jit(solution)/shard_map/ppermute | solution.py:287
  37.7 2.0 %collective-permute-start.12 = (bf16[32,768]{1,0:T(8,128)(2,1)S(1)}, bf16[32,768]{1,0:T(8,128)(2,1)S(1)}, u32[]{:S(2)}, u32[]{:S(2)}) collective-permute-start(bf16[32,768]{1,0:T(8,128)(2,1)S(1)} %add.3.refs_5_.refs_1_), channel_id=1, source_target_pairs={{0,4},{4,0},{8,12},{12,8},{1,5},{5,1},{9,13},{13,9},{2,6},{6,2},{1... | collective-permute-start | bytes 147464 | tf_op jit(solution)/shard_map/ppermute | solution.py:287
  40.0 1.4 %collective-permute-start.18 = (bf16[32,3072]{1,0:T(8,128)(2,1)S(1)}, bf16[32,3072]{1,0:T(8,128)(2,1)S(1)}, u32[]{:S(2)}, u32[]{:S(2)}) collective-permute-start(bf16[32,3072]{1,0:T(8,128)(2,1)S(1)} %norm.2.refs_5_.refs_0_), channel_id=1, source_target_pairs={{0,2},{1,3},{2,0},{3,1},{4,6},{5,7},{6,4},{7,5},{8,10},{9,11},{10,... | collective-permute-start | bytes 589832 | tf_op jit(solution)/shard_map/ppermute | solution.py:287
  41.4 1.6 %collective-permute-done.13.refs_3_ = bf16[32,768]{1,0:T(8,128)(2,1)S(1)} collective-permute-done((bf16[32,768]{1,0:T(8,128)(2,1)S(1)}, bf16[32,768]{1,0:T(8,128)(2,1)S(1)}, u32[]{:S(2)}, u32[]{:S(2)}) %collective-permute-start.13) | collective-permute-done | bytes 49184 | tf_op jit(solution)/shard_map/ppermute | solution.py:287
  43.3 1.4 %collective-permute-start.20 = (bf16[32,3072]{1,0:T(8,128)(2,1)S(1)}, bf16[32,3072]{1,0:T(8,128)(2,1)S(1)}, u32[]{:S(2)}, u32[]{:S(2)}) collective-permute-start(bf16[32,3072]{1,0:T(8,128)(2,1)S(1)} %norm.3.refs_2_.refs_0_), channel_id=1, source_target_pairs={{0,2},{1,3},{2,0},{3,1},{4,6},{5,7},{6,4},{7,5},{8,10},{9,11},{10,... | collective-permute-start | bytes 589832 | tf_op jit(solution)/shard_map/ppermute | solution.py:287
  45.0 3.4 %load_up.1.refs_2_.refs_4_ = bf16[1344,3072]{1,0:T(8,128)(2,1)S(1)} custom-call(bf16[1344,3072]{1,0:T(8,128)(2,1)} %bitcast.13, f32[4,64,128]{2,1,0:T(8,128)S(1)} %gates.1.refs_1_.refs_0_.gate_ref), custom_call_target="tpu_custom_call" | custom-call | flops 1024 | bytes 1024 | tf_op jit(solution)/shard_map/load_up/pallas_call | solution.py:39
  48.5 1.8 %collective-permute-done.20.refs_1_ = bf16[32,3072]{1,0:T(8,128)(2,1)S(1)} collective-permute-done((bf16[32,3072]{1,0:T(8,128)(2,1)S(1)}, bf16[32,3072]{1,0:T(8,128)(2,1)S(1)}, u32[]{:S(2)}, u32[]{:S(2)}) %collective-permute-start.20) | collective-permute-done | bytes 196640 | tf_op jit(solution)/shard_map/ppermute | solution.py:287
  50.8 1.9 %load_down.1.refs_5_.down_ref.refs_1_ = bf16[512,3072]{1,0:T(8,128)(2,1)S(1)} custom-call(bf16[1344,3072]{1,0:T(8,128)(2,1)} %bitcast.11, bf16[2,32,3072]{2,1,0:T(8,128)(2,1)S(1)} %pair.3.refs_1_.refs_2_), custom_call_target="tpu_custom_call" | custom-call | flops 1024 | bytes 1024 | tf_op jit(solution)/shard_map/load_down/pallas_call | solution.py:39
  52.8 4.5 %lift.1 = (bf16[256,1344]{1,0:T(8,128)(2,1)S(1)}, bf16[2,128,768]{2,1,0:T(8,128)(2,1)S(1)}, bf16[2,128,768]{2,1,0:T(8,128)(2,1)S(1)}, bf16[832,3072]{1,0:T(8,128)(2,1)S(1)}) custom-call(bf16[2,32,3072]{2,1,0:T(8,128)(2,1)S(1)} %pair.2.refs_2_.refs_0_, bf16[2,32,3072]{2,1,0:T(8,128)(2,1)S(1)} %collective-permute-done.19.refs_1_, ...), custom_call_target="tpu_custom_call" | custom-call | flops 1024 | bytes 1024 | tf_op jit(solution)/shard_map/lift/pallas_call | solution.py:392
  62.0 2.2 %collective-permute-done.24.refs_0_ = bf16[64,768]{1,0:T(8,128)(2,1)S(1)} collective-permute-done((bf16[64,768]{1,0:T(8,128)(2,1)S(1)}, bf16[64,768]{1,0:T(8,128)(2,1)S(1)}, u32[]{:S(2)}, u32[]{:S(2)}) %collective-permute-start.24) | collective-permute-done | bytes 98336 | tf_op jit(solution)/shard_map/ppermute | solution.py:287
  64.3 2.0 %collective-permute-start.27 = (bf16[64,768]{1,0:T(8,128)(2,1)S(1)}, bf16[64,768]{1,0:T(8,128)(2,1)S(1)}, u32[]{:S(2)}, u32[]{:S(2)}) collective-permute-start(bf16[64,768]{1,0:T(8,128)(2,1)S(1)} %split.3.refs_2_), channel_id=1, source_target_pairs={{0,12},{4,8},{8,4},{12,0},{1,13},{5,9},{9,5},{13,1},{2,14},{6,10},... | collective-permute-start | bytes 294920 | tf_op jit(solution)/shard_map/ppermute | solution.py:287
  66.4 2.4 %collective-permute-start.26 = (bf16[64,768]{1,0:T(8,128)(2,1)S(1)}, bf16[64,768]{1,0:T(8,128)(2,1)S(1)}, u32[]{:S(2)}, u32[]{:S(2)}) collective-permute-start(bf16[64,768]{1,0:T(8,128)(2,1)S(1)} %get-tuple-element.34), channel_id=1, source_target_pairs={{0,2},{1,3},{2,0},{3,1},{4,6},{5,7},{6,4},{7,5},{8,10},{9,11},{10,... | collective-permute-start | bytes 294920 | tf_op jit(solution)/shard_map/ppermute | solution.py:287
  68.9 2.7 %collective-permute-done.27.refs_1_ = bf16[64,768]{1,0:T(8,128)(2,1)S(1)} collective-permute-done((bf16[64,768]{1,0:T(8,128)(2,1)S(1)}, bf16[64,768]{1,0:T(8,128)(2,1)S(1)}, u32[]{:S(2)}, u32[]{:S(2)}) %collective-permute-start.27) | collective-permute-done | bytes 98336 | tf_op jit(solution)/shard_map/ppermute | solution.py:287
  71.7 1.7 %collective-permute-done.25.refs_2_ = bf16[64,768]{1,0:T(8,128)(2,1)S(1)} collective-permute-done((bf16[64,768]{1,0:T(8,128)(2,1)S(1)}, bf16[64,768]{1,0:T(8,128)(2,1)S(1)}, u32[]{:S(2)}, u32[]{:S(2)}) %collective-permute-start.25) | collective-permute-done | bytes 98336 | tf_op jit(solution)/shard_map/ppermute | solution.py:287
  74.9 3.3 %collective-permute-done.29.refs_0_ = bf16[64,768]{1,0:T(8,128)(2,1)S(1)} collective-permute-done((bf16[64,768]{1,0:T(8,128)(2,1)S(1)}, bf16[64,768]{1,0:T(8,128)(2,1)S(1)}, u32[]{:S(2)}, u32[]{:S(2)}) %collective-permute-start.29) | collective-permute-done | bytes 98336 | tf_op jit(solution)/shard_map/ppermute | solution.py:287
  (77 shorter events, 15.3 us)
Async XLA Ops:
  6.3 13.4 %collective-permute-start.5 = (bf16[32,1536]{1,0:T(8,128)(2,1)S(1)}, bf16[32,1536]{1,0:T(8,128)(2,1)S(1)}, u32[]{:S(2)}, u32[]{:S(2)}) collective-permute-start(bf16[32,1536]{1,0:T(8,128)(2,1)S(1)} %attend.2.after_ref.refs_0_), channel_id=1, source_target_pairs={{0,12},{4,8},{8,4},{12,0},{1,13},{5,9},{9,5},{13,1},{2,14},{6,10},... | collective-permute-start | bytes 294920 | tf_op jit(solution)/shard_map/ppermute | solution.py:287
  11.5 13.4 %collective-permute-start.4 = (bf16[32,1536]{1,0:T(8,128)(2,1)S(1)}, bf16[32,1536]{1,0:T(8,128)(2,1)S(1)}, u32[]{:S(2)}, u32[]{:S(2)}) collective-permute-start(bf16[32,1536]{1,0:T(8,128)(2,1)S(1)} %attend.2.after_ref.refs_0_), channel_id=1, source_target_pairs={{0,8},{4,12},{8,0},{12,4},{1,9},{5,13},{9,1},{13,5},{2,10},{6,14},... | collective-permute-start | bytes 294920 | tf_op jit(solution)/shard_map/ppermute | solution.py:287
  11.5 13.4 %collective-permute-start.3 = (bf16[32,1536]{1,0:T(8,128)(2,1)S(1)}, bf16[32,1536]{1,0:T(8,128)(2,1)S(1)}, u32[]{:S(2)}, u32[]{:S(2)}) collective-permute-start(bf16[32,1536]{1,0:T(8,128)(2,1)S(1)} %attend.2.after_ref.refs_0_), channel_id=1, source_target_pairs={{0,4},{4,0},{8,12},{12,8},{1,5},{5,1},{9,13},{13,9},{2,6},{6,2},{1... | collective-permute-start | bytes 294920 | tf_op jit(solution)/shard_map/ppermute | solution.py:287
  15.9 11.1 %collective-permute-start.2 = (bf16[32,1536]{1,0:T(8,128)(2,1)S(1)}, bf16[32,1536]{1,0:T(8,128)(2,1)S(1)}, u32[]{:S(2)}, u32[]{:S(2)}) collective-permute-start(bf16[32,1536]{1,0:T(8,128)(2,1)S(1)} %attend.3.refs_5_.refs_0_), channel_id=1, source_target_pairs={{0,12},{4,8},{8,4},{12,0},{1,13},{5,9},{9,5},{13,1},{2,14},{6,10},... | collective-permute-start | bytes 294920 | tf_op jit(solution)/shard_map/ppermute | solution.py:287
  19.7 8.4 %collective-permute-start.1 = (bf16[32,1536]{1,0:T(8,128)(2,1)S(1)}, bf16[32,1536]{1,0:T(8,128)(2,1)S(1)}, u32[]{:S(2)}, u32[]{:S(2)}) collective-permute-start(bf16[32,1536]{1,0:T(8,128)(2,1)S(1)} %attend.3.refs_5_.refs_0_), channel_id=1, source_target_pairs={{0,8},{4,12},{8,0},{12,4},{1,9},{5,13},{9,1},{13,5},{2,10},{6,14},... | collective-permute-start | bytes 294920 | tf_op jit(solution)/shard_map/ppermute | solution.py:287
  19.7 8.4 %collective-permute-start = (bf16[32,1536]{1,0:T(8,128)(2,1)S(1)}, bf16[32,1536]{1,0:T(8,128)(2,1)S(1)}, u32[]{:S(2)}, u32[]{:S(2)}) collective-permute-start(bf16[32,1536]{1,0:T(8,128)(2,1)S(1)} %attend.3.refs_5_.refs_0_), channel_id=1, source_target_pairs={{0,4},{4,0},{8,12},{12,8},{1,5},{5,1},{9,13},{13,9},{2,6},{6,2},{1... | collective-permute-start | bytes 294920 | tf_op jit(solution)/shard_map/ppermute | solution.py:287
  25.4 4.9 %collective-permute-start.9 = (bf16[32,768]{1,0:T(8,128)(2,1)S(1)}, bf16[32,768]{1,0:T(8,128)(2,1)S(1)}, u32[]{:S(2)}, u32[]{:S(2)}) collective-permute-start(bf16[32,768]{1,0:T(8,128)(2,1)S(1)} %get-tuple-element.26), channel_id=1, source_target_pairs={{0,1},{1,0},{2,3},{3,2},{4,5},{5,4},{6,7},{7,6},{8,9},{9,8},{10,11... | collective-permute-start | bytes 147464 | tf_op jit(solution)/shard_map/ppermute | solution.py:287
  25.5 5.1 %collective-permute-start.10 = (bf16[32,768]{1,0:T(8,128)(2,1)S(1)}, bf16[32,768]{1,0:T(8,128)(2,1)S(1)}, u32[]{:S(2)}, u32[]{:S(2)}) collective-permute-start(bf16[32,768]{1,0:T(8,128)(2,1)S(1)} %get-tuple-element.27), channel_id=1, source_target_pairs={{0,2},{1,3},{2,0},{3,1},{4,6},{5,7},{6,4},{7,5},{8,10},{9,11},{10,... | collective-permute-start | bytes 147464 | tf_op jit(solution)/shard_map/ppermute | solution.py:287
  28.7 6.5 %collective-permute-start.7 = (bf16[32,768]{1,0:T(8,128)(2,1)S(1)}, bf16[32,768]{1,0:T(8,128)(2,1)S(1)}, u32[]{:S(2)}, u32[]{:S(2)}) collective-permute-start(bf16[32,768]{1,0:T(8,128)(2,1)S(1)} %get-tuple-element.24), channel_id=1, source_target_pairs={{0,2},{1,3},{2,0},{3,1},{4,6},{5,7},{6,4},{7,5},{8,10},{9,11},{10,... | collective-permute-start | bytes 147464 | tf_op jit(solution)/shard_map/ppermute | solution.py:287
  30.3 4.9 %collective-permute-start.8 = (bf16[32,768]{1,0:T(8,128)(2,1)S(1)}, bf16[32,768]{1,0:T(8,128)(2,1)S(1)}, u32[]{:S(2)}, u32[]{:S(2)}) collective-permute-start(bf16[32,768]{1,0:T(8,128)(2,1)S(1)} %get-tuple-element.25), channel_id=1, source_target_pairs={{0,3},{1,2},{2,1},{3,0},{4,7},{5,6},{6,5},{7,4},{8,11},{9,10},{10,... | collective-permute-start | bytes 147464 | tf_op jit(solution)/shard_map/ppermute | solution.py:287
  30.8 7.0 %collective-permute-start.17 = (bf16[32,768]{1,0:T(8,128)(2,1)S(1)}, bf16[32,768]{1,0:T(8,128)(2,1)S(1)}, u32[]{:S(2)}, u32[]{:S(2)}) collective-permute-start(bf16[32,768]{1,0:T(8,128)(2,1)S(1)} %add.2.refs_4_.refs_1_), channel_id=1, source_target_pairs={{0,12},{4,8},{8,4},{12,0},{1,13},{5,9},{9,5},{13,1},{2,14},{6,10},... | collective-permute-start | bytes 147464 | tf_op jit(solution)/shard_map/ppermute | solution.py:287
  33.2 6.5 %collective-permute-start.16 = (bf16[32,768]{1,0:T(8,128)(2,1)S(1)}, bf16[32,768]{1,0:T(8,128)(2,1)S(1)}, u32[]{:S(2)}, u32[]{:S(2)}) collective-permute-start(bf16[32,768]{1,0:T(8,128)(2,1)S(1)} %add.2.refs_4_.refs_1_), channel_id=1, source_target_pairs={{0,8},{4,12},{8,0},{12,4},{1,9},{5,13},{9,1},{13,5},{2,10},{6,14},... | collective-permute-start | bytes 147464 | tf_op jit(solution)/shard_map/ppermute | solution.py:287
  33.2 6.5 %collective-permute-start.15 = (bf16[32,768]{1,0:T(8,128)(2,1)S(1)}, bf16[32,768]{1,0:T(8,128)(2,1)S(1)}, u32[]{:S(2)}, u32[]{:S(2)}) collective-permute-start(bf16[32,768]{1,0:T(8,128)(2,1)S(1)} %add.2.refs_4_.refs_1_), channel_id=1, source_target_pairs={{0,4},{4,0},{8,12},{12,8},{1,5},{5,1},{9,13},{13,9},{2,6},{6,2},{1... | collective-permute-start | bytes 147464 | tf_op jit(solution)/shard_map/ppermute | solution.py:287
  35.3 6.2 %collective-permute-start.14 = (bf16[32,768]{1,0:T(8,128)(2,1)S(1)}, bf16[32,768]{1,0:T(8,128)(2,1)S(1)}, u32[]{:S(2)}, u32[]{:S(2)}) collective-permute-start(bf16[32,768]{1,0:T(8,128)(2,1)S(1)} %add.3.refs_5_.refs_1_), channel_id=1, source_target_pairs={{0,12},{4,8},{8,4},{12,0},{1,13},{5,9},{9,5},{13,1},{2,14},{6,10},... | collective-permute-start | bytes 147464 | tf_op jit(solution)/shard_map/ppermute | solution.py:287
  37.7 5.3 %collective-permute-start.13 = (bf16[32,768]{1,0:T(8,128)(2,1)S(1)}, bf16[32,768]{1,0:T(8,128)(2,1)S(1)}, u32[]{:S(2)}, u32[]{:S(2)}) collective-permute-start(bf16[32,768]{1,0:T(8,128)(2,1)S(1)} %add.3.refs_5_.refs_1_), channel_id=1, source_target_pairs={{0,8},{4,12},{8,0},{12,4},{1,9},{5,13},{9,1},{13,5},{2,10},{6,14},... | collective-permute-start | bytes 147464 | tf_op jit(solution)/shard_map/ppermute | solution.py:287
  37.7 5.3 %collective-permute-start.12 = (bf16[32,768]{1,0:T(8,128)(2,1)S(1)}, bf16[32,768]{1,0:T(8,128)(2,1)S(1)}, u32[]{:S(2)}, u32[]{:S(2)}) collective-permute-start(bf16[32,768]{1,0:T(8,128)(2,1)S(1)} %add.3.refs_5_.refs_1_), channel_id=1, source_target_pairs={{0,4},{4,0},{8,12},{12,8},{1,5},{5,1},{9,13},{13,9},{2,6},{6,2},{1... | collective-permute-start | bytes 147464 | tf_op jit(solution)/shard_map/ppermute | solution.py:287
  40.0 8.4 %collective-permute-start.18 = (bf16[32,3072]{1,0:T(8,128)(2,1)S(1)}, bf16[32,3072]{1,0:T(8,128)(2,1)S(1)}, u32[]{:S(2)}, u32[]{:S(2)}) collective-permute-start(bf16[32,3072]{1,0:T(8,128)(2,1)S(1)} %norm.2.refs_5_.refs_0_), channel_id=1, source_target_pairs={{0,2},{1,3},{2,0},{3,1},{4,6},{5,7},{6,4},{7,5},{8,10},{9,11},{10,... | collective-permute-start | bytes 589832 | tf_op jit(solution)/shard_map/ppermute | solution.py:287
  43.3 6.9 %collective-permute-start.20 = (bf16[32,3072]{1,0:T(8,128)(2,1)S(1)}, bf16[32,3072]{1,0:T(8,128)(2,1)S(1)}, u32[]{:S(2)}, u32[]{:S(2)}) collective-permute-start(bf16[32,3072]{1,0:T(8,128)(2,1)S(1)} %norm.3.refs_2_.refs_0_), channel_id=1, source_target_pairs={{0,2},{1,3},{2,0},{3,1},{4,6},{5,7},{6,4},{7,5},{8,10},{9,11},{10,... | collective-permute-start | bytes 589832 | tf_op jit(solution)/shard_map/ppermute | solution.py:287
  57.3 9.0 %collective-permute-start.23 = (bf16[2,128,768]{2,1,0:T(8,128)(2,1)S(1)}, bf16[2,128,768]{2,1,0:T(8,128)(2,1)S(1)}, u32[]{:S(2)}, u32[]{:S(2)}) collective-permute-start(bf16[2,128,768]{2,1,0:T(8,128)(2,1)S(1)} %get-tuple-element.32), channel_id=1, source_target_pairs={{0,1},{1,0},{2,3},{3,2},{4,5},{5,4},{6,7},{7,6},{8,9},{9,8},{10,11... | collective-permute-start | bytes 1179656 | tf_op jit(solution)/shard_map/ppermute | solution.py:287
  59.1 5.2 %collective-permute-start.24 = (bf16[64,768]{1,0:T(8,128)(2,1)S(1)}, bf16[64,768]{1,0:T(8,128)(2,1)S(1)}, u32[]{:S(2)}, u32[]{:S(2)}) collective-permute-start(bf16[64,768]{1,0:T(8,128)(2,1)S(1)} %turn.3.refs_2_), channel_id=1, source_target_pairs={{0,2},{1,3},{2,0},{3,1},{4,6},{5,7},{6,4},{7,5},{8,10},{9,11},{10,... | collective-permute-start | bytes 294920 | tf_op jit(solution)/shard_map/ppermute | solution.py:287
  61.1 7.7 %collective-permute-start.28 = (bf16[64,768]{1,0:T(8,128)(2,1)S(1)}, bf16[64,768]{1,0:T(8,128)(2,1)S(1)}, u32[]{:S(2)}, u32[]{:S(2)}) collective-permute-start(bf16[64,768]{1,0:T(8,128)(2,1)S(1)} %turn.4.refs_3_), channel_id=1, source_target_pairs={{0,2},{1,3},{2,0},{3,1},{4,6},{5,7},{6,4},{7,5},{8,10},{9,11},{10,... | collective-permute-start | bytes 294920 | tf_op jit(solution)/shard_map/ppermute | solution.py:287
  64.3 7.4 %collective-permute-start.27 = (bf16[64,768]{1,0:T(8,128)(2,1)S(1)}, bf16[64,768]{1,0:T(8,128)(2,1)S(1)}, u32[]{:S(2)}, u32[]{:S(2)}) collective-permute-start(bf16[64,768]{1,0:T(8,128)(2,1)S(1)} %split.3.refs_2_), channel_id=1, source_target_pairs={{0,12},{4,8},{8,4},{12,0},{1,13},{5,9},{9,5},{13,1},{2,14},{6,10},... | collective-permute-start | bytes 294920 | tf_op jit(solution)/shard_map/ppermute | solution.py:287
  66.4 5.3 %collective-permute-start.26 = (bf16[64,768]{1,0:T(8,128)(2,1)S(1)}, bf16[64,768]{1,0:T(8,128)(2,1)S(1)}, u32[]{:S(2)}, u32[]{:S(2)}) collective-permute-start(bf16[64,768]{1,0:T(8,128)(2,1)S(1)} %get-tuple-element.34), channel_id=1, source_target_pairs={{0,2},{1,3},{2,0},{3,1},{4,6},{5,7},{6,4},{7,5},{8,10},{9,11},{10,... | collective-permute-start | bytes 294920 | tf_op jit(solution)/shard_map/ppermute | solution.py:287
  68.9 6.0 %collective-permute-start.30 = (bf16[64,768]{1,0:T(8,128)(2,1)S(1)}, bf16[64,768]{1,0:T(8,128)(2,1)S(1)}, u32[]{:S(2)}, u32[]{:S(2)}) collective-permute-start(bf16[64,768]{1,0:T(8,128)(2,1)S(1)} %split.4.refs_2_), channel_id=1, source_target_pairs={{0,8},{4,12},{8,0},{12,4},{1,9},{5,13},{9,1},{13,5},{2,10},{6,14},... | collective-permute-start | bytes 294920 | tf_op jit(solution)/shard_map/ppermute | solution.py:287
  (11 other events, 153.1 us)

commit v9 on v6

--- a/solution.py
+++ b/solution.py
@@ -61,8 +61,8 @@
             sems.at[kind, step],
         )
 
-    for step in range(steps):
-        for kind in range(2):
+    for kind in range(2):
+        for step in range(steps):
             fetch(step, kind).start()
     q_rows[...] = jnp.zeros_like(q_rows)
     for head in range(heads):
@@ -70,7 +70,8 @@
             begin : begin + rows, head * HD : (head + 1) * HD
         ].astype(F32)
     place = lax.broadcasted_iota(jnp.int32, (slots, context), 1).astype(F32)
-    for step in range(steps):
+
+    def score(step):
         fetch(step, 0).wait()
         for k in range(batch):
             row = step * batch + k
@@ -84,34 +85,39 @@
             )
             here = slice(k * slots, (k + 1) * slots)
             seen = place < small_ref[whole, spans].astype(F32)
-            scores[here, :] = jnp.where(seen, cached * scale, -jnp.inf)
+            scores[step % 2, here, :] = jnp.where(seen, cached * scale, -jnp.inf)
             fresh_key = small_ref[whole, fresh[0]].astype(F32)
-            own_scores[here, :] = jnp.broadcast_to(
+            own_scores[step % 2, here, :] = jnp.broadcast_to(
                 jnp.sum(mine * fresh_key, axis=1, keepdims=True) * scale, (slots, HD)
             )
-        cached = scores[...]
-        own = own_scores[:, :1]
+
+    score(0)
+    for step in range(steps):
+        if step + 1 < steps:
+            score(step + 1)
+        cached = scores[step % 2]
+        own = own_scores[step % 2, :, :1]
         largest = jnp.maximum(jnp.max(cached, axis=1, keepdims=True), own)
         lifted = jnp.exp(cached - largest)
         own_lifted = jnp.exp(own - largest)
         total = jnp.sum(lifted, axis=1, keepdims=True) + own_lifted
-        probs[...] = (lifted / total).astype(BF16)
-        own_probs[...] = jnp.broadcast_to(
-            (own_lifted / total).astype(BF16).astype(F32), own_probs.shape
+        probs[step % 2] = (lifted / total).astype(BF16)
+        own_probs[step % 2] = jnp.broadcast_to(
+            (own_lifted / total).astype(BF16).astype(F32), own_probs.shape[1:]
         )
         fetch(step, 1).wait()
         for k in range(batch):
             row = step * batch + k
             whole = slice(begin + row, begin + row + 1)
             here = slice(k * slots, (k + 1) * slots)
-            weighted = jnp.dot(probs[here, :], values[row], preferred_element_type=F32)
+            weighted = jnp.dot(probs[step % 2, here, :], values[row], preferred_element_type=F32)
             fresh_value = small_ref[whole, fresh[1]].astype(F32)
-            total = weighted + own_probs[here, :1] * fresh_value
+            total = weighted + own_probs[step % 2, here, :1] * fresh_value
             for g in range(kv_heads):
-                mixed[g, here, :] = total[:, g * HD : (g + 1) * HD]
+                mixed[step % 2, g, here, :] = total[:, g * HD : (g + 1) * HD]
         for head in range(heads):
             out_ref[step * batch : (step + 1) * batch, head * HD : (head + 1) * HD] = mixed[
-                head // group, pl.ds(head, batch, stride=slots), :
+                step % 2, head // group, pl.ds(head, batch, stride=slots), :
             ].astype(BF16)
 
 
@@ -136,11 +142,11 @@
             pltpu.VMEM((rows, context, width), BF16),
             pltpu.VMEM((rows, context, width), BF16),
             pltpu.VMEM((kv_heads, rows * slots, HD), F32),
-            pltpu.VMEM((batch * slots, context), F32),
-            pltpu.VMEM((batch * slots, HD), F32),
-            pltpu.VMEM((batch * slots, context), BF16),
-            pltpu.VMEM((batch * slots, HD), F32),
-            pltpu.VMEM((kv_heads, batch * slots, HD), F32),
+            pltpu.VMEM((2, batch * slots, context), F32),
+            pltpu.VMEM((2, batch * slots, HD), F32),
+            pltpu.VMEM((2, batch * slots, context), BF16),
+            pltpu.VMEM((2, batch * slots, HD), F32),
+            pltpu.VMEM((2, kv_heads, batch * slots, HD), F32),
             pltpu.SemaphoreType.DMA((2, rows // batch)),
         ],
         compiler_params=pltpu.CompilerParams(vmem_limit_bytes=50 * MIB),
@@ -223,8 +229,8 @@
         for t, shard in enumerate(by_distance(*shards[2 * c : 2 * c + 2])):
             first = pl.multiple_of(((lax.axis_index("ta") ^ t) * chunks + c) * rows, rows)
             held[pl.ds(first, rows), :] = shard[...]
-    for first in range(0, hidden, 2 * HD):
-        last = min(first + 2 * HD, hidden)
+    for first in range(0, hidden, 6 * HD):
+        last = min(first + 6 * HD, hidden)
         raised = lax.dot_general(
             up_ref[first:last, :], held[...], (((1,), (1,)), ((), ())), preferred_element_type=F32
         )
@@ -378,13 +384,13 @@
             )(normed[c], trade(normed[c], "ta", 2))
         )
     blocks = [block for pair in pairs for block in (pair, trade(pair, "ta", 1))]
-    cut = -(-hidden_share // (4 * HD)) * 2 * HD
+    cut = hidden_share // (4 * HD) * 2 * HD
     part = local_call(
         functools.partial(load_kernel, cut),
         shape((cut, model), BF16),
         [ANYWHERE],
         [pltpu.SemaphoreType.DMA],
-        vmem=42,
+        vmem=46,
         name="load_down",
         after=pairs[-1],
     )(w_down[0])

time: 77.8 us -> 76.6 us (0.985)
  Pallas kernels: 22 us -> 20.2 us
    pallas_call x2, Pallas kernels: 7.63 us -> 6.48 us  [attend(): pl.pallas_call(functools.partial(attend_kernel, kv_heads, heads // kv_hea...]
  transfers between devices with their start and end apart: 31 -> 31, of which waited for: 12 -> 12; matrix products, arithmetic and copies ran while one was open for 0% -> 0% of each run, Pallas kernels for 17% -> 16%
where the time goes in v9:
time: 76.6 us; the launch traced here: 76.3 us
  starting transfers between devices  34.1 us (45%)
  Pallas kernels  20.2 us (26%)
  waiting for transfers between devices  19 us (25%)
  other arithmetic  1.61 us (2%)
  local copies, waits for them, and re-layouts  1.1 us (1%)
    ppermute x31, starting transfers between devices, trade(): return lax.ppermute(array, axis, [(k, k ^ turn) for k in range(count)])  34.1 us
    ppermute x31, waiting for transfers between devices, trade(): return lax.ppermute(array, axis, [(k, k ^ turn) for k in range(count)])  19 us
    pallas_call x17, Pallas kernels, local_call(): return call if after is None else lambda *args: call(*args, after)  7.95 us
    pallas_call x2, Pallas kernels, attend(): pl.pallas_call(functools.partial(attend_kernel, kv_heads, heads // kv_hea...  6.48 us
    pallas_call x1, Pallas kernels, every_row_body(): local_call(functools.partial(lift_kernel, chunks), [shape((all_rows, hidd...  4.27 us
  transfers between devices with their start and end apart: 31, of which 12 were waited for; matrix products, arithmetic and copies ran while one was open for 0% of the time, Pallas kernels for 16%

profile of v9, /device:TPU:0, one launch (start us, length us, event | category | flops | bytes accessed | tf_op | source)
XLA Modules:
  0.0 76.3 jit_solution(9135190446812420342)
XLA Ops:
  2.5 3.2 %attend.2.after_ref.refs_0_ = bf16[32,1536]{1,0:T(8,128)(2,1)S(1)} custom-call(bf16[64,2304]{1,0:T(8,128)(2,1)S(1)} %pad_maximum_fusion.small_ref.after_ref, bf16[2,64,192,256]{3,2,1,0:T(8,128)(2,1)} %cache_ref.3, bf16[64,2304]{1,0:T(8,128)(2,1)S(1)} %pad_maximum_fusion.small_ref.after_ref), custom_call_target="tpu_custom_call" | custom-call | flops 1024 | bytes 1024 | tf_op jit(solution)/shard_map/attend/pallas_call | solution.py:136
  5.8 5.1 %collective-permute-start.5 = (bf16[32,1536]{1,0:T(8,128)(2,1)S(1)}, bf16[32,1536]{1,0:T(8,128)(2,1)S(1)}, u32[]{:S(2)}, u32[]{:S(2)}) collective-permute-start(bf16[32,1536]{1,0:T(8,128)(2,1)S(1)} %attend.2.after_ref.refs_0_), channel_id=1, source_target_pairs={{0,12},{4,8},{8,4},{12,0},{1,13},{5,9},{9,5},{13,1},{2,14},{6,10},... | collective-permute-start | bytes 294920 | tf_op jit(solution)/shard_map/ppermute | solution.py:293
  11.5 3.2 %attend.3.refs_5_.refs_0_ = bf16[32,1536]{1,0:T(8,128)(2,1)S(1)} custom-call(bf16[64,2304]{1,0:T(8,128)(2,1)S(1)} %pad_maximum_fusion.small_ref.after_ref, bf16[2,64,192,256]{3,2,1,0:T(8,128)(2,1)} %cache_ref.3, bf16[32,1536]{1,0:T(8,128)(2,1)S(1)} %attend.2.after_ref.refs_0_), custom_call_target="tpu_custom_call" | custom-call | flops 1024 | bytes 1024 | tf_op jit(solution)/shard_map/attend/pallas_call | solution.py:136
  14.8 3.8 %collective-permute-start.2 = (bf16[32,1536]{1,0:T(8,128)(2,1)S(1)}, bf16[32,1536]{1,0:T(8,128)(2,1)S(1)}, u32[]{:S(2)}, u32[]{:S(2)}) collective-permute-start(bf16[32,1536]{1,0:T(8,128)(2,1)S(1)} %attend.3.refs_5_.refs_0_), channel_id=1, source_target_pairs={{0,12},{4,8},{8,4},{12,0},{1,13},{5,9},{9,5},{13,1},{2,14},{6,10},... | collective-permute-start | bytes 294920 | tf_op jit(solution)/shard_map/ppermute | solution.py:293
  19.2 5.1 %collective-permute-done.4.refs_2_ = bf16[32,1536]{1,0:T(8,128)(2,1)S(1)} collective-permute-done((bf16[32,1536]{1,0:T(8,128)(2,1)S(1)}, bf16[32,1536]{1,0:T(8,128)(2,1)S(1)}, u32[]{:S(2)}, u32[]{:S(2)}) %collective-permute-start.4) | collective-permute-done | bytes 98336 | tf_op jit(solution)/shard_map/ppermute | solution.py:293
  24.9 1.6 %collective-permute-start.10 = (bf16[32,768]{1,0:T(8,128)(2,1)S(1)}, bf16[32,768]{1,0:T(8,128)(2,1)S(1)}, u32[]{:S(2)}, u32[]{:S(2)}) collective-permute-start(bf16[32,768]{1,0:T(8,128)(2,1)S(1)} %get-tuple-element.27), channel_id=1, source_target_pairs={{0,2},{1,3},{2,0},{3,1},{4,6},{5,7},{6,4},{7,5},{8,10},{9,11},{10,... | collective-permute-start | bytes 147464 | tf_op jit(solution)/shard_map/ppermute | solution.py:293
  28.2 1.6 %collective-permute-start.7 = (bf16[32,768]{1,0:T(8,128)(2,1)S(1)}, bf16[32,768]{1,0:T(8,128)(2,1)S(1)}, u32[]{:S(2)}, u32[]{:S(2)}) collective-permute-start(bf16[32,768]{1,0:T(8,128)(2,1)S(1)} %get-tuple-element.24), channel_id=1, source_target_pairs={{0,2},{1,3},{2,0},{3,1},{4,6},{5,7},{6,4},{7,5},{8,10},{9,11},{10,... | collective-permute-start | bytes 147464 | tf_op jit(solution)/shard_map/ppermute | solution.py:293
  30.2 2.4 %collective-permute-start.17 = (bf16[32,768]{1,0:T(8,128)(2,1)S(1)}, bf16[32,768]{1,0:T(8,128)(2,1)S(1)}, u32[]{:S(2)}, u32[]{:S(2)}) collective-permute-start(bf16[32,768]{1,0:T(8,128)(2,1)S(1)} %add.2.refs_4_.refs_1_), channel_id=1, source_target_pairs={{0,12},{4,8},{8,4},{12,0},{1,13},{5,9},{9,5},{13,1},{2,14},{6,10},... | collective-permute-start | bytes 147464 | tf_op jit(solution)/shard_map/ppermute | solution.py:293
  32.6 2.0 %collective-permute-start.15 = (bf16[32,768]{1,0:T(8,128)(2,1)S(1)}, bf16[32,768]{1,0:T(8,128)(2,1)S(1)}, u32[]{:S(2)}, u32[]{:S(2)}) collective-permute-start(bf16[32,768]{1,0:T(8,128)(2,1)S(1)} %add.2.refs_4_.refs_1_), channel_id=1, source_target_pairs={{0,4},{4,0},{8,12},{12,8},{1,5},{5,1},{9,13},{13,9},{2,6},{6,2},{1... | collective-permute-start | bytes 147464 | tf_op jit(solution)/shard_map/ppermute | solution.py:293
  34.7 2.4 %collective-permute-start.14 = (bf16[32,768]{1,0:T(8,128)(2,1)S(1)}, bf16[32,768]{1,0:T(8,128)(2,1)S(1)}, u32[]{:S(2)}, u32[]{:S(2)}) collective-permute-start(bf16[32,768]{1,0:T(8,128)(2,1)S(1)} %add.3.refs_5_.refs_1_), channel_id=1, source_target_pairs={{0,12},{4,8},{8,4},{12,0},{1,13},{5,9},{9,5},{13,1},{2,14},{6,10},... | collective-permute-start | bytes 147464 | tf_op jit(solution)/shard_map/ppermute | solution.py:293
  37.1 2.0 %collective-permute-start.12 = (bf16[32,768]{1,0:T(8,128)(2,1)S(1)}, bf16[32,768]{1,0:T(8,128)(2,1)S(1)}, u32[]{:S(2)}, u32[]{:S(2)}) collective-permute-start(bf16[32,768]{1,0:T(8,128)(2,1)S(1)} %add.3.refs_5_.refs_1_), channel_id=1, source_target_pairs={{0,4},{4,0},{8,12},{12,8},{1,5},{5,1},{9,13},{13,9},{2,6},{6,2},{1... | collective-permute-start | bytes 147464 | tf_op jit(solution)/shard_map/ppermute | solution.py:293
  39.4 1.4 %collective-permute-start.18 = (bf16[32,3072]{1,0:T(8,128)(2,1)S(1)}, bf16[32,3072]{1,0:T(8,128)(2,1)S(1)}, u32[]{:S(2)}, u32[]{:S(2)}) collective-permute-start(bf16[32,3072]{1,0:T(8,128)(2,1)S(1)} %norm.2.refs_5_.refs_0_), channel_id=1, source_target_pairs={{0,2},{1,3},{2,0},{3,1},{4,6},{5,7},{6,4},{7,5},{8,10},{9,11},{10,... | collective-permute-start | bytes 589832 | tf_op jit(solution)/shard_map/ppermute | solution.py:293
  40.9 1.6 %collective-permute-done.13.refs_3_ = bf16[32,768]{1,0:T(8,128)(2,1)S(1)} collective-permute-done((bf16[32,768]{1,0:T(8,128)(2,1)S(1)}, bf16[32,768]{1,0:T(8,128)(2,1)S(1)}, u32[]{:S(2)}, u32[]{:S(2)}) %collective-permute-start.13) | collective-permute-done | bytes 49184 | tf_op jit(solution)/shard_map/ppermute | solution.py:293
  42.7 1.4 %collective-permute-start.20 = (bf16[32,3072]{1,0:T(8,128)(2,1)S(1)}, bf16[32,3072]{1,0:T(8,128)(2,1)S(1)}, u32[]{:S(2)}, u32[]{:S(2)}) collective-permute-start(bf16[32,3072]{1,0:T(8,128)(2,1)S(1)} %norm.3.refs_2_.refs_0_), channel_id=1, source_target_pairs={{0,2},{1,3},{2,0},{3,1},{4,6},{5,7},{6,4},{7,5},{8,10},{9,11},{10,... | collective-permute-start | bytes 589832 | tf_op jit(solution)/shard_map/ppermute | solution.py:293
  44.5 3.4 %load_up.1.refs_2_.refs_4_ = bf16[1344,3072]{1,0:T(8,128)(2,1)S(1)} custom-call(bf16[1344,3072]{1,0:T(8,128)(2,1)} %bitcast.13, f32[4,64,128]{2,1,0:T(8,128)S(1)} %gates.1.refs_1_.gate_ref), custom_call_target="tpu_custom_call" | custom-call | flops 1024 | bytes 1024 | tf_op jit(solution)/shard_map/load_up/pallas_call | solution.py:39
  47.9 1.8 %collective-permute-done.20.refs_1_ = bf16[32,3072]{1,0:T(8,128)(2,1)S(1)} collective-permute-done((bf16[32,3072]{1,0:T(8,128)(2,1)S(1)}, bf16[32,3072]{1,0:T(8,128)(2,1)S(1)}, u32[]{:S(2)}, u32[]{:S(2)}) %collective-permute-start.20) | collective-permute-done | bytes 196640 | tf_op jit(solution)/shard_map/ppermute | solution.py:293
  50.2 1.9 %load_down.1.refs_5_.down_ref.refs_1_ = bf16[512,3072]{1,0:T(8,128)(2,1)S(1)} custom-call(bf16[1344,3072]{1,0:T(8,128)(2,1)} %bitcast.11, bf16[2,32,3072]{2,1,0:T(8,128)(2,1)S(1)} %pair.3.refs_1_.refs_2_), custom_call_target="tpu_custom_call" | custom-call | flops 1024 | bytes 1024 | tf_op jit(solution)/shard_map/load_down/pallas_call | solution.py:39
  52.2 4.3 %lift.1 = (bf16[256,1344]{1,0:T(8,128)(2,1)S(1)}, bf16[2,128,768]{2,1,0:T(8,128)(2,1)S(1)}, bf16[2,128,768]{2,1,0:T(8,128)(2,1)S(1)}, bf16[832,3072]{1,0:T(8,128)(2,1)S(1)}) custom-call(bf16[2,32,3072]{2,1,0:T(8,128)(2,1)S(1)} %pair.2.refs_2_.refs_0_, bf16[2,32,3072]{2,1,0:T(8,128)(2,1)S(1)} %collective-permute-done.19.refs_1_, ...), custom_call_target="tpu_custom_call" | custom-call | flops 1024 | bytes 1024 | tf_op jit(solution)/shard_map/lift/pallas_call | solution.py:398
  58.3 1.3 %collective-permute-start.27 = (bf16[64,768]{1,0:T(8,128)(2,1)S(1)}, bf16[64,768]{1,0:T(8,128)(2,1)S(1)}, u32[]{:S(2)}, u32[]{:S(2)}) collective-permute-start(bf16[64,768]{1,0:T(8,128)(2,1)S(1)} %turn.3.refs_2_), channel_id=1, source_target_pairs={{0,2},{1,3},{2,0},{3,1},{4,6},{5,7},{6,4},{7,5},{8,10},{9,11},{10,... | collective-permute-start | bytes 294920 | tf_op jit(solution)/shard_map/ppermute | solution.py:293
  60.5 1.3 %collective-permute-start.25 = (bf16[64,768]{1,0:T(8,128)(2,1)S(1)}, bf16[64,768]{1,0:T(8,128)(2,1)S(1)}, u32[]{:S(2)}, u32[]{:S(2)}) collective-permute-start(bf16[64,768]{1,0:T(8,128)(2,1)S(1)} %get-tuple-element.34), channel_id=1, source_target_pairs={{0,2},{1,3},{2,0},{3,1},{4,6},{5,7},{6,4},{7,5},{8,10},{9,11},{10,... | collective-permute-start | bytes 294920 | tf_op jit(solution)/shard_map/ppermute | solution.py:293
  64.0 2.3 %collective-permute-start.30 = (bf16[64,768]{1,0:T(8,128)(2,1)S(1)}, bf16[64,768]{1,0:T(8,128)(2,1)S(1)}, u32[]{:S(2)}, u32[]{:S(2)}) collective-permute-start(bf16[64,768]{1,0:T(8,128)(2,1)S(1)} %split.3.refs_3_), channel_id=1, source_target_pairs={{0,12},{4,8},{8,4},{12,0},{1,13},{5,9},{9,5},{13,1},{2,14},{6,10},... | collective-permute-start | bytes 294920 | tf_op jit(solution)/shard_map/ppermute | solution.py:293
  66.9 1.2 %collective-permute-done.25.refs_3_ = bf16[64,768]{1,0:T(8,128)(2,1)S(1)} collective-permute-done((bf16[64,768]{1,0:T(8,128)(2,1)S(1)}, bf16[64,768]{1,0:T(8,128)(2,1)S(1)}, u32[]{:S(2)}, u32[]{:S(2)}) %collective-permute-start.25) | collective-permute-done | bytes 98336 | tf_op jit(solution)/shard_map/ppermute | solution.py:293
  68.2 1.3 %collective-permute-done.24.refs_2_ = bf16[64,768]{1,0:T(8,128)(2,1)S(1)} collective-permute-done((bf16[64,768]{1,0:T(8,128)(2,1)S(1)}, bf16[64,768]{1,0:T(8,128)(2,1)S(1)}, u32[]{:S(2)}, u32[]{:S(2)}) %collective-permute-start.24) | collective-permute-done | bytes 98336 | tf_op jit(solution)/shard_map/ppermute | solution.py:293
  70.5 3.9 %collective-permute-done.29.refs_0_ = bf16[64,768]{1,0:T(8,128)(2,1)S(1)} collective-permute-done((bf16[64,768]{1,0:T(8,128)(2,1)S(1)}, bf16[64,768]{1,0:T(8,128)(2,1)S(1)}, u32[]{:S(2)}, u32[]{:S(2)}) %collective-permute-start.29) | collective-permute-done | bytes 98336 | tf_op jit(solution)/shard_map/ppermute | solution.py:293
  (77 shorter events, 16.6 us)
Async XLA Ops:
  5.8 12.8 %collective-permute-start.5 = (bf16[32,1536]{1,0:T(8,128)(2,1)S(1)}, bf16[32,1536]{1,0:T(8,128)(2,1)S(1)}, u32[]{:S(2)}, u32[]{:S(2)}) collective-permute-start(bf16[32,1536]{1,0:T(8,128)(2,1)S(1)} %attend.2.after_ref.refs_0_), channel_id=1, source_target_pairs={{0,12},{4,8},{8,4},{12,0},{1,13},{5,9},{9,5},{13,1},{2,14},{6,10},... | collective-permute-start | bytes 294920 | tf_op jit(solution)/shard_map/ppermute | solution.py:293
  10.9 13.4 %collective-permute-start.4 = (bf16[32,1536]{1,0:T(8,128)(2,1)S(1)}, bf16[32,1536]{1,0:T(8,128)(2,1)S(1)}, u32[]{:S(2)}, u32[]{:S(2)}) collective-permute-start(bf16[32,1536]{1,0:T(8,128)(2,1)S(1)} %attend.2.after_ref.refs_0_), channel_id=1, source_target_pairs={{0,8},{4,12},{8,0},{12,4},{1,9},{5,13},{9,1},{13,5},{2,10},{6,14},... | collective-permute-start | bytes 294920 | tf_op jit(solution)/shard_map/ppermute | solution.py:293
  10.9 13.4 %collective-permute-start.3 = (bf16[32,1536]{1,0:T(8,128)(2,1)S(1)}, bf16[32,1536]{1,0:T(8,128)(2,1)S(1)}, u32[]{:S(2)}, u32[]{:S(2)}) collective-permute-start(bf16[32,1536]{1,0:T(8,128)(2,1)S(1)} %attend.2.after_ref.refs_0_), channel_id=1, source_target_pairs={{0,4},{4,0},{8,12},{12,8},{1,5},{5,1},{9,13},{13,9},{2,6},{6,2},{1... | collective-permute-start | bytes 294920 | tf_op jit(solution)/shard_map/ppermute | solution.py:293
  14.8 11.7 %collective-permute-start.2 = (bf16[32,1536]{1,0:T(8,128)(2,1)S(1)}, bf16[32,1536]{1,0:T(8,128)(2,1)S(1)}, u32[]{:S(2)}, u32[]{:S(2)}) collective-permute-start(bf16[32,1536]{1,0:T(8,128)(2,1)S(1)} %attend.3.refs_5_.refs_0_), channel_id=1, source_target_pairs={{0,12},{4,8},{8,4},{12,0},{1,13},{5,9},{9,5},{13,1},{2,14},{6,10},... | collective-permute-start | bytes 294920 | tf_op jit(solution)/shard_map/ppermute | solution.py:293
  18.6 9.0 %collective-permute-start.1 = (bf16[32,1536]{1,0:T(8,128)(2,1)S(1)}, bf16[32,1536]{1,0:T(8,128)(2,1)S(1)}, u32[]{:S(2)}, u32[]{:S(2)}) collective-permute-start(bf16[32,1536]{1,0:T(8,128)(2,1)S(1)} %attend.3.refs_5_.refs_0_), channel_id=1, source_target_pairs={{0,8},{4,12},{8,0},{12,4},{1,9},{5,13},{9,1},{13,5},{2,10},{6,14},... | collective-permute-start | bytes 294920 | tf_op jit(solution)/shard_map/ppermute | solution.py:293
  18.6 9.0 %collective-permute-start = (bf16[32,1536]{1,0:T(8,128)(2,1)S(1)}, bf16[32,1536]{1,0:T(8,128)(2,1)S(1)}, u32[]{:S(2)}, u32[]{:S(2)}) collective-permute-start(bf16[32,1536]{1,0:T(8,128)(2,1)S(1)} %attend.3.refs_5_.refs_0_), channel_id=1, source_target_pairs={{0,4},{4,0},{8,12},{12,8},{1,5},{5,1},{9,13},{13,9},{2,6},{6,2},{1... | collective-permute-start | bytes 294920 | tf_op jit(solution)/shard_map/ppermute | solution.py:293
  24.9 5.1 %collective-permute-start.10 = (bf16[32,768]{1,0:T(8,128)(2,1)S(1)}, bf16[32,768]{1,0:T(8,128)(2,1)S(1)}, u32[]{:S(2)}, u32[]{:S(2)}) collective-permute-start(bf16[32,768]{1,0:T(8,128)(2,1)S(1)} %get-tuple-element.27), channel_id=1, source_target_pairs={{0,2},{1,3},{2,0},{3,1},{4,6},{5,7},{6,4},{7,5},{8,10},{9,11},{10,... | collective-permute-start | bytes 147464 | tf_op jit(solution)/shard_map/ppermute | solution.py:293
  28.2 6.5 %collective-permute-start.7 = (bf16[32,768]{1,0:T(8,128)(2,1)S(1)}, bf16[32,768]{1,0:T(8,128)(2,1)S(1)}, u32[]{:S(2)}, u32[]{:S(2)}) collective-permute-start(bf16[32,768]{1,0:T(8,128)(2,1)S(1)} %get-tuple-element.24), channel_id=1, source_target_pairs={{0,2},{1,3},{2,0},{3,1},{4,6},{5,7},{6,4},{7,5},{8,10},{9,11},{10,... | collective-permute-start | bytes 147464 | tf_op jit(solution)/shard_map/ppermute | solution.py:293
  29.7 4.9 %collective-permute-start.8 = (bf16[32,768]{1,0:T(8,128)(2,1)S(1)}, bf16[32,768]{1,0:T(8,128)(2,1)S(1)}, u32[]{:S(2)}, u32[]{:S(2)}) collective-permute-start(bf16[32,768]{1,0:T(8,128)(2,1)S(1)} %get-tuple-element.25), channel_id=1, source_target_pairs={{0,3},{1,2},{2,1},{3,0},{4,7},{5,6},{6,5},{7,4},{8,11},{9,10},{10,... | collective-permute-start | bytes 147464 | tf_op jit(solution)/shard_map/ppermute | solution.py:293
  30.2 6.9 %collective-permute-start.17 = (bf16[32,768]{1,0:T(8,128)(2,1)S(1)}, bf16[32,768]{1,0:T(8,128)(2,1)S(1)}, u32[]{:S(2)}, u32[]{:S(2)}) collective-permute-start(bf16[32,768]{1,0:T(8,128)(2,1)S(1)} %add.2.refs_4_.refs_1_), channel_id=1, source_target_pairs={{0,12},{4,8},{8,4},{12,0},{1,13},{5,9},{9,5},{13,1},{2,14},{6,10},... | collective-permute-start | bytes 147464 | tf_op jit(solution)/shard_map/ppermute | solution.py:293
  32.6 6.5 %collective-permute-start.16 = (bf16[32,768]{1,0:T(8,128)(2,1)S(1)}, bf16[32,768]{1,0:T(8,128)(2,1)S(1)}, u32[]{:S(2)}, u32[]{:S(2)}) collective-permute-start(bf16[32,768]{1,0:T(8,128)(2,1)S(1)} %add.2.refs_4_.refs_1_), channel_id=1, source_target_pairs={{0,8},{4,12},{8,0},{12,4},{1,9},{5,13},{9,1},{13,5},{2,10},{6,14},... | collective-permute-start | bytes 147464 | tf_op jit(solution)/shard_map/ppermute | solution.py:293
  32.6 6.5 %collective-permute-start.15 = (bf16[32,768]{1,0:T(8,128)(2,1)S(1)}, bf16[32,768]{1,0:T(8,128)(2,1)S(1)}, u32[]{:S(2)}, u32[]{:S(2)}) collective-permute-start(bf16[32,768]{1,0:T(8,128)(2,1)S(1)} %add.2.refs_4_.refs_1_), channel_id=1, source_target_pairs={{0,4},{4,0},{8,12},{12,8},{1,5},{5,1},{9,13},{13,9},{2,6},{6,2},{1... | collective-permute-start | bytes 147464 | tf_op jit(solution)/shard_map/ppermute | solution.py:293
  34.7 6.2 %collective-permute-start.14 = (bf16[32,768]{1,0:T(8,128)(2,1)S(1)}, bf16[32,768]{1,0:T(8,128)(2,1)S(1)}, u32[]{:S(2)}, u32[]{:S(2)}) collective-permute-start(bf16[32,768]{1,0:T(8,128)(2,1)S(1)} %add.3.refs_5_.refs_1_), channel_id=1, source_target_pairs={{0,12},{4,8},{8,4},{12,0},{1,13},{5,9},{9,5},{13,1},{2,14},{6,10},... | collective-permute-start | bytes 147464 | tf_op jit(solution)/shard_map/ppermute | solution.py:293
  37.1 5.3 %collective-permute-start.13 = (bf16[32,768]{1,0:T(8,128)(2,1)S(1)}, bf16[32,768]{1,0:T(8,128)(2,1)S(1)}, u32[]{:S(2)}, u32[]{:S(2)}) collective-permute-start(bf16[32,768]{1,0:T(8,128)(2,1)S(1)} %add.3.refs_5_.refs_1_), channel_id=1, source_target_pairs={{0,8},{4,12},{8,0},{12,4},{1,9},{5,13},{9,1},{13,5},{2,10},{6,14},... | collective-permute-start | bytes 147464 | tf_op jit(solution)/shard_map/ppermute | solution.py:293
  37.1 5.3 %collective-permute-start.12 = (bf16[32,768]{1,0:T(8,128)(2,1)S(1)}, bf16[32,768]{1,0:T(8,128)(2,1)S(1)}, u32[]{:S(2)}, u32[]{:S(2)}) collective-permute-start(bf16[32,768]{1,0:T(8,128)(2,1)S(1)} %add.3.refs_5_.refs_1_), channel_id=1, source_target_pairs={{0,4},{4,0},{8,12},{12,8},{1,5},{5,1},{9,13},{13,9},{2,6},{6,2},{1... | collective-permute-start | bytes 147464 | tf_op jit(solution)/shard_map/ppermute | solution.py:293
  39.4 8.4 %collective-permute-start.18 = (bf16[32,3072]{1,0:T(8,128)(2,1)S(1)}, bf16[32,3072]{1,0:T(8,128)(2,1)S(1)}, u32[]{:S(2)}, u32[]{:S(2)}) collective-permute-start(bf16[32,3072]{1,0:T(8,128)(2,1)S(1)} %norm.2.refs_5_.refs_0_), channel_id=1, source_target_pairs={{0,2},{1,3},{2,0},{3,1},{4,6},{5,7},{6,4},{7,5},{8,10},{9,11},{10,... | collective-permute-start | bytes 589832 | tf_op jit(solution)/shard_map/ppermute | solution.py:293
  42.7 6.9 %collective-permute-start.20 = (bf16[32,3072]{1,0:T(8,128)(2,1)S(1)}, bf16[32,3072]{1,0:T(8,128)(2,1)S(1)}, u32[]{:S(2)}, u32[]{:S(2)}) collective-permute-start(bf16[32,3072]{1,0:T(8,128)(2,1)S(1)} %norm.3.refs_2_.refs_0_), channel_id=1, source_target_pairs={{0,2},{1,3},{2,0},{3,1},{4,6},{5,7},{6,4},{7,5},{8,10},{9,11},{10,... | collective-permute-start | bytes 589832 | tf_op jit(solution)/shard_map/ppermute | solution.py:293
  58.3 5.7 %collective-permute-start.27 = (bf16[64,768]{1,0:T(8,128)(2,1)S(1)}, bf16[64,768]{1,0:T(8,128)(2,1)S(1)}, u32[]{:S(2)}, u32[]{:S(2)}) collective-permute-start(bf16[64,768]{1,0:T(8,128)(2,1)S(1)} %turn.3.refs_2_), channel_id=1, source_target_pairs={{0,2},{1,3},{2,0},{3,1},{4,6},{5,7},{6,4},{7,5},{8,10},{9,11},{10,... | collective-permute-start | bytes 294920 | tf_op jit(solution)/shard_map/ppermute | solution.py:293
  59.6 6.8 %collective-permute-start.26 = (bf16[64,768]{1,0:T(8,128)(2,1)S(1)}, bf16[64,768]{1,0:T(8,128)(2,1)S(1)}, u32[]{:S(2)}, u32[]{:S(2)}) collective-permute-start(bf16[64,768]{1,0:T(8,128)(2,1)S(1)} %turn.4.refs_2_), channel_id=1, source_target_pairs={{0,2},{1,3},{2,0},{3,1},{4,6},{5,7},{6,4},{7,5},{8,10},{9,11},{10,... | collective-permute-start | bytes 294920 | tf_op jit(solution)/shard_map/ppermute | solution.py:293
  60.5 7.7 %collective-permute-start.25 = (bf16[64,768]{1,0:T(8,128)(2,1)S(1)}, bf16[64,768]{1,0:T(8,128)(2,1)S(1)}, u32[]{:S(2)}, u32[]{:S(2)}) collective-permute-start(bf16[64,768]{1,0:T(8,128)(2,1)S(1)} %get-tuple-element.34), channel_id=1, source_target_pairs={{0,2},{1,3},{2,0},{3,1},{4,6},{5,7},{6,4},{7,5},{8,10},{9,11},{10,... | collective-permute-start | bytes 294920 | tf_op jit(solution)/shard_map/ppermute | solution.py:293
  61.8 7.7 %collective-permute-start.24 = (bf16[64,768]{1,0:T(8,128)(2,1)S(1)}, bf16[64,768]{1,0:T(8,128)(2,1)S(1)}, u32[]{:S(2)}, u32[]{:S(2)}) collective-permute-start(bf16[64,768]{1,0:T(8,128)(2,1)S(1)} %get-tuple-element.33.refs_3_), channel_id=1, source_target_pairs={{0,2},{1,3},{2,0},{3,1},{4,6},{5,7},{6,4},{7,5},{8,10},{9,11},{10,... | collective-permute-start | bytes 294920 | tf_op jit(solution)/shard_map/ppermute | solution.py:293
  64.0 6.5 %collective-permute-start.30 = (bf16[64,768]{1,0:T(8,128)(2,1)S(1)}, bf16[64,768]{1,0:T(8,128)(2,1)S(1)}, u32[]{:S(2)}, u32[]{:S(2)}) collective-permute-start(bf16[64,768]{1,0:T(8,128)(2,1)S(1)} %split.3.refs_3_), channel_id=1, source_target_pairs={{0,12},{4,8},{8,4},{12,0},{1,13},{5,9},{9,5},{13,1},{2,14},{6,10},... | collective-permute-start | bytes 294920 | tf_op jit(solution)/shard_map/ppermute | solution.py:293
  66.4 8.0 %collective-permute-start.29 = (bf16[64,768]{1,0:T(8,128)(2,1)S(1)}, bf16[64,768]{1,0:T(8,128)(2,1)S(1)}, u32[]{:S(2)}, u32[]{:S(2)}) collective-permute-start(bf16[64,768]{1,0:T(8,128)(2,1)S(1)} %split.4.refs_4_), channel_id=1, source_target_pairs={{0,8},{4,12},{8,0},{12,4},{1,9},{5,13},{9,1},{13,5},{2,10},{6,14},... | collective-permute-start | bytes 294920 | tf_op jit(solution)/shard_map/ppermute | solution.py:293
  69.6 6.0 %collective-permute-start.28 = (bf16[64,768]{1,0:T(8,128)(2,1)S(1)}, bf16[64,768]{1,0:T(8,128)(2,1)S(1)}, u32[]{:S(2)}, u32[]{:S(2)}) collective-permute-start(bf16[64,768]{1,0:T(8,128)(2,1)S(1)} %get-tuple-element.35), channel_id=1, source_target_pairs={{0,4},{4,0},{8,12},{12,8},{1,5},{5,1},{9,13},{13,9},{2,6},{6,2},{1... | collective-permute-start | bytes 294920 | tf_op jit(solution)/shard_map/ppermute | solution.py:293
  (11 other events, 152.6 us)

commit v10 on v9

--- a/solution.py
+++ b/solution.py
@@ -160,6 +160,10 @@
     out_ref[1] = other_ref[...]
 
 
+def pass_kernel(source_ref, out_ref):
+    out_ref[...] = source_ref[...]
+
+
 def gate_kernel(ids_ref, gates_ref, gate_ref):
     parts, rows, lanes = gate_ref.shape
     ids = ids_ref[pl.ds(pl.multiple_of(lax.axis_index("gx") * rows, rows), rows), :]
@@ -320,7 +324,14 @@
         parts = {0: array, **{s: trade(array, axis, s) for s in order}}
         return [parts[s] for s in range(len(parts))]
 
-    shards = [spread(part, "gx") for part in attended]
+    two = trade(attended[0], "gx", 2)
+    onward = local_call(
+        pass_kernel, shape(two.shape, BF16), [VMEM], name="pass", after=attended[1]
+    )(two)
+    shards = [
+        [attended[0], trade(attended[0], "gx", 1), two, trade(onward, "gx", 1)],
+        spread(attended[1], "gx"),
+    ]
     pieces, hidden = [], []
     for c in range(chunks):
         pieces.append(
@@ -384,13 +395,13 @@
             )(normed[c], trade(normed[c], "ta", 2))
         )
     blocks = [block for pair in pairs for block in (pair, trade(pair, "ta", 1))]
-    cut = hidden_share // (4 * HD) * 2 * HD
+    cut = 2 * HD
     part = local_call(
         functools.partial(load_kernel, cut),
         shape((cut, model), BF16),
         [ANYWHERE],
         [pltpu.SemaphoreType.DMA],
-        vmem=46,
+        vmem=48,
         name="load_down",
         after=pairs[-1],
     )(w_down[0])

time: 76.6 us -> 77.3 us (level)
  starting transfers between devices: 34.1 us -> 35.3 us
    ppermute x31, starting transfers between devices: 34.1 us -> 35.3 us  [trade(): return lax.ppermute(array, axis, [(k, k ^ turn) for k in range(count)])]
    pallas_call x17 -> x18, Pallas kernels: 7.95 us -> 7.49 us  [local_call(): return call if after is None else lambda *args: call(*args, after)]
  transfers between devices with their start and end apart: 31 -> 31, of which waited for: 12 -> 12; matrix products, arithmetic and copies ran while one was open for 0% -> 0% of each run, Pallas kernels for 16% -> 15%
where the time goes in v10:
time: 77.3 us; the launch traced here: 77 us
  starting transfers between devices  35.3 us (46%)
  Pallas kernels  20.4 us (26%)
  waiting for transfers between devices  18.3 us (24%)
  other arithmetic  1.61 us (2%)
  local copies, waits for them, and re-layouts  1.1 us (1%)
    ppermute x31, starting transfers between devices, trade(): return lax.ppermute(array, axis, [(k, k ^ turn) for k in range(count)])  35.3 us
    ppermute x31, waiting for transfers between devices, trade(): return lax.ppermute(array, axis, [(k, k ^ turn) for k in range(count)])  18.3 us
    pallas_call x18, Pallas kernels, local_call(): return call if after is None else lambda *args: call(*args, after)  7.49 us
    pallas_call x2, Pallas kernels, attend(): pl.pallas_call(functools.partial(attend_kernel, kv_heads, heads // kv_hea...  6.48 us
    pallas_call x1, Pallas kernels, every_row_body(): local_call(functools.partial(lift_kernel, chunks), [shape((all_rows, hidd...  4.86 us
  transfers between devices with their start and end apart: 31, of which 12 were waited for; matrix products, arithmetic and copies ran while one was open for 0% of the time, Pallas kernels for 15%

profile of v10, /device:TPU:0, one launch (start us, length us, event | category | flops | bytes accessed | tf_op | source)
XLA Modules:
  0.0 77.0 jit_solution(15523631480853938188)
XLA Ops:
  2.5 3.2 %attend.2.after_ref.refs_0_ = bf16[32,1536]{1,0:T(8,128)(2,1)S(1)} custom-call(bf16[64,2304]{1,0:T(8,128)(2,1)S(1)} %pad_maximum_fusion.small_ref.after_ref, bf16[2,64,192,256]{3,2,1,0:T(8,128)(2,1)} %cache_ref.3, bf16[64,2304]{1,0:T(8,128)(2,1)S(1)} %pad_maximum_fusion.small_ref.after_ref), custom_call_target="tpu_custom_call" | custom-call | flops 1024 | bytes 1024 | tf_op jit(solution)/shard_map/attend/pallas_call | solution.py:136
  5.8 4.1 %collective-permute-start.4 = (bf16[32,1536]{1,0:T(8,128)(2,1)S(1)}, bf16[32,1536]{1,0:T(8,128)(2,1)S(1)}, u32[]{:S(2)}, u32[]{:S(2)}) collective-permute-start(bf16[32,1536]{1,0:T(8,128)(2,1)S(1)} %attend.2.after_ref.refs_0_), channel_id=1, source_target_pairs={{0,8},{4,12},{8,0},{12,4},{1,9},{5,13},{9,1},{13,5},{2,10},{6,14},... | collective-permute-start | bytes 294920 | tf_op jit(solution)/shard_map/ppermute | solution.py:297
  9.9 1.6 %collective-permute-start.3 = (bf16[32,1536]{1,0:T(8,128)(2,1)S(1)}, bf16[32,1536]{1,0:T(8,128)(2,1)S(1)}, u32[]{:S(2)}, u32[]{:S(2)}) collective-permute-start(bf16[32,1536]{1,0:T(8,128)(2,1)S(1)} %attend.2.after_ref.refs_0_), channel_id=1, source_target_pairs={{0,4},{4,0},{8,12},{12,8},{1,5},{5,1},{9,13},{13,9},{2,6},{6,2},{1... | collective-permute-start | bytes 294920 | tf_op jit(solution)/shard_map/ppermute | solution.py:297
  11.4 3.2 %attend.3.refs_1_.refs_5_.refs_0_ = bf16[32,1536]{1,0:T(8,128)(2,1)S(1)} custom-call(bf16[64,2304]{1,0:T(8,128)(2,1)S(1)} %pad_maximum_fusion.small_ref.after_ref, bf16[2,64,192,256]{3,2,1,0:T(8,128)(2,1)} %cache_ref.3, bf16[32,1536]{1,0:T(8,128)(2,1)S(1)} %attend.2.after_ref.refs_0_), custom_call_target="tpu_custom_call" | custom-call | flops 1024 | bytes 1024 | tf_op jit(solution)/shard_map/attend/pallas_call | solution.py:136
  15.5 2.9 %collective-permute-start.2 = (bf16[32,1536]{1,0:T(8,128)(2,1)S(1)}, bf16[32,1536]{1,0:T(8,128)(2,1)S(1)}, u32[]{:S(2)}, u32[]{:S(2)}) collective-permute-start(bf16[32,1536]{1,0:T(8,128)(2,1)S(1)} %attend.3.refs_1_.refs_5_.refs_0_), channel_id=1, source_target_pairs={{0,12},{4,8},{8,4},{12,0},{1,13},{5,9},{9,5},{13,1},{2,14},{6,10},... | collective-permute-start | bytes 294920 | tf_op jit(solution)/shard_map/ppermute | solution.py:297
  20.5 1.5 %collective-permute-start.10 = (bf16[32,768]{1,0:T(8,128)(2,1)S(1)}, bf16[32,768]{1,0:T(8,128)(2,1)S(1)}, u32[]{:S(2)}, u32[]{:S(2)}) collective-permute-start(bf16[32,768]{1,0:T(8,128)(2,1)S(1)} %get-tuple-element.27), channel_id=1, source_target_pairs={{0,2},{1,3},{2,0},{3,1},{4,6},{5,7},{6,4},{7,5},{8,10},{9,11},{10,... | collective-permute-start | bytes 147464 | tf_op jit(solution)/shard_map/ppermute | solution.py:297
  22.1 2.1 %collective-permute-done.2.refs_3_ = bf16[32,1536]{1,0:T(8,128)(2,1)S(1)} collective-permute-done((bf16[32,1536]{1,0:T(8,128)(2,1)S(1)}, bf16[32,1536]{1,0:T(8,128)(2,1)S(1)}, u32[]{:S(2)}, u32[]{:S(2)}) %collective-permute-start.2) | collective-permute-done | bytes 98336 | tf_op jit(solution)/shard_map/ppermute | solution.py:297
  24.2 3.8 %collective-permute-done.1.refs_2_ = bf16[32,1536]{1,0:T(8,128)(2,1)S(1)} collective-permute-done((bf16[32,1536]{1,0:T(8,128)(2,1)S(1)}, bf16[32,1536]{1,0:T(8,128)(2,1)S(1)}, u32[]{:S(2)}, u32[]{:S(2)}) %collective-permute-start.1) | collective-permute-done | bytes 98336 | tf_op jit(solution)/shard_map/ppermute | solution.py:297
  28.5 1.6 %collective-permute-start.7 = (bf16[32,768]{1,0:T(8,128)(2,1)S(1)}, bf16[32,768]{1,0:T(8,128)(2,1)S(1)}, u32[]{:S(2)}, u32[]{:S(2)}) collective-permute-start(bf16[32,768]{1,0:T(8,128)(2,1)S(1)} %get-tuple-element.24), channel_id=1, source_target_pairs={{0,2},{1,3},{2,0},{3,1},{4,6},{5,7},{6,4},{7,5},{8,10},{9,11},{10,... | collective-permute-start | bytes 147464 | tf_op jit(solution)/shard_map/ppermute | solution.py:297
  30.4 2.7 %collective-permute-start.17 = (bf16[32,768]{1,0:T(8,128)(2,1)S(1)}, bf16[32,768]{1,0:T(8,128)(2,1)S(1)}, u32[]{:S(2)}, u32[]{:S(2)}) collective-permute-start(bf16[32,768]{1,0:T(8,128)(2,1)S(1)} %add.2.refs_4_.refs_1_), channel_id=1, source_target_pairs={{0,12},{4,8},{8,4},{12,0},{1,13},{5,9},{9,5},{13,1},{2,14},{6,10},... | collective-permute-start | bytes 147464 | tf_op jit(solution)/shard_map/ppermute | solution.py:297
  33.2 1.7 %collective-permute-start.15 = (bf16[32,768]{1,0:T(8,128)(2,1)S(1)}, bf16[32,768]{1,0:T(8,128)(2,1)S(1)}, u32[]{:S(2)}, u32[]{:S(2)}) collective-permute-start(bf16[32,768]{1,0:T(8,128)(2,1)S(1)} %add.2.refs_4_.refs_1_), channel_id=1, source_target_pairs={{0,4},{4,0},{8,12},{12,8},{1,5},{5,1},{9,13},{13,9},{2,6},{6,2},{1... | collective-permute-start | bytes 147464 | tf_op jit(solution)/shard_map/ppermute | solution.py:297
  34.9 2.7 %collective-permute-start.14 = (bf16[32,768]{1,0:T(8,128)(2,1)S(1)}, bf16[32,768]{1,0:T(8,128)(2,1)S(1)}, u32[]{:S(2)}, u32[]{:S(2)}) collective-permute-start(bf16[32,768]{1,0:T(8,128)(2,1)S(1)} %add.3.refs_5_.refs_1_), channel_id=1, source_target_pairs={{0,12},{4,8},{8,4},{12,0},{1,13},{5,9},{9,5},{13,1},{2,14},{6,10},... | collective-permute-start | bytes 147464 | tf_op jit(solution)/shard_map/ppermute | solution.py:297
  37.7 1.7 %collective-permute-start.12 = (bf16[32,768]{1,0:T(8,128)(2,1)S(1)}, bf16[32,768]{1,0:T(8,128)(2,1)S(1)}, u32[]{:S(2)}, u32[]{:S(2)}) collective-permute-start(bf16[32,768]{1,0:T(8,128)(2,1)S(1)} %add.3.refs_5_.refs_1_), channel_id=1, source_target_pairs={{0,4},{4,0},{8,12},{12,8},{1,5},{5,1},{9,13},{13,9},{2,6},{6,2},{1... | collective-permute-start | bytes 147464 | tf_op jit(solution)/shard_map/ppermute | solution.py:297
  39.7 1.6 %collective-permute-start.18 = (bf16[32,3072]{1,0:T(8,128)(2,1)S(1)}, bf16[32,3072]{1,0:T(8,128)(2,1)S(1)}, u32[]{:S(2)}, u32[]{:S(2)}) collective-permute-start(bf16[32,3072]{1,0:T(8,128)(2,1)S(1)} %norm.2.refs_5_.refs_0_), channel_id=1, source_target_pairs={{0,2},{1,3},{2,0},{3,1},{4,6},{5,7},{6,4},{7,5},{8,10},{9,11},{10,... | collective-permute-start | bytes 589832 | tf_op jit(solution)/shard_map/ppermute | solution.py:297
  41.2 1.6 %collective-permute-done.13.refs_3_ = bf16[32,768]{1,0:T(8,128)(2,1)S(1)} collective-permute-done((bf16[32,768]{1,0:T(8,128)(2,1)S(1)}, bf16[32,768]{1,0:T(8,128)(2,1)S(1)}, u32[]{:S(2)}, u32[]{:S(2)}) %collective-permute-start.13) | collective-permute-done | bytes 49184 | tf_op jit(solution)/shard_map/ppermute | solution.py:297
  43.1 1.6 %collective-permute-start.20 = (bf16[32,3072]{1,0:T(8,128)(2,1)S(1)}, bf16[32,3072]{1,0:T(8,128)(2,1)S(1)}, u32[]{:S(2)}, u32[]{:S(2)}) collective-permute-start(bf16[32,3072]{1,0:T(8,128)(2,1)S(1)} %norm.3.refs_2_.refs_0_), channel_id=1, source_target_pairs={{0,2},{1,3},{2,0},{3,1},{4,6},{5,7},{6,4},{7,5},{8,10},{9,11},{10,... | collective-permute-start | bytes 589832 | tf_op jit(solution)/shard_map/ppermute | solution.py:297
  45.0 3.4 %load_up.1.refs_2_.refs_4_ = bf16[1344,3072]{1,0:T(8,128)(2,1)S(1)} custom-call(bf16[1344,3072]{1,0:T(8,128)(2,1)} %bitcast.13, f32[4,64,128]{2,1,0:T(8,128)S(1)} %gates.1.refs_1_.gate_ref), custom_call_target="tpu_custom_call" | custom-call | flops 1024 | bytes 1024 | tf_op jit(solution)/shard_map/load_up/pallas_call | solution.py:39
  48.4 1.4 %collective-permute-done.20.refs_1_ = bf16[32,3072]{1,0:T(8,128)(2,1)S(1)} collective-permute-done((bf16[32,3072]{1,0:T(8,128)(2,1)S(1)}, bf16[32,3072]{1,0:T(8,128)(2,1)S(1)}, u32[]{:S(2)}, u32[]{:S(2)}) %collective-permute-start.20) | collective-permute-done | bytes 196640 | tf_op jit(solution)/shard_map/ppermute | solution.py:297
  50.4 1.4 %load_down.1.refs_5_.down_ref.refs_1_ = bf16[256,3072]{1,0:T(8,128)(2,1)S(1)} custom-call(bf16[1344,3072]{1,0:T(8,128)(2,1)} %bitcast.11, bf16[2,32,3072]{2,1,0:T(8,128)(2,1)S(1)} %pair.3.refs_1_.refs_2_), custom_call_target="tpu_custom_call" | custom-call | flops 1024 | bytes 1024 | tf_op jit(solution)/shard_map/load_down/pallas_call | solution.py:39
  52.2 4.9 %lift.1 = (bf16[256,1344]{1,0:T(8,128)(2,1)S(1)}, bf16[2,128,768]{2,1,0:T(8,128)(2,1)S(1)}, bf16[2,128,768]{2,1,0:T(8,128)(2,1)S(1)}, bf16[1088,3072]{1,0:T(8,128)(2,1)S(1)}) custom-call(bf16[2,32,3072]{2,1,0:T(8,128)(2,1)S(1)} %pair.2.refs_2_.refs_0_, bf16[2,32,3072]{2,1,0:T(8,128)(2,1)S(1)} %collective-permute-done.19.refs_1_, ...), custom_call_target="tpu_custom_call" | custom-call | flops 1024 | bytes 1024 | tf_op jit(solution)/shard_map/lift/pallas_call | solution.py:409
  58.9 1.4 %collective-permute-start.27 = (bf16[64,768]{1,0:T(8,128)(2,1)S(1)}, bf16[64,768]{1,0:T(8,128)(2,1)S(1)}, u32[]{:S(2)}, u32[]{:S(2)}) collective-permute-start(bf16[64,768]{1,0:T(8,128)(2,1)S(1)} %turn.3.refs_2_), channel_id=1, source_target_pairs={{0,2},{1,3},{2,0},{3,1},{4,6},{5,7},{6,4},{7,5},{8,10},{9,11},{10,... | collective-permute-start | bytes 294920 | tf_op jit(solution)/shard_map/ppermute | solution.py:297
  61.1 1.4 %collective-permute-start.25 = (bf16[64,768]{1,0:T(8,128)(2,1)S(1)}, bf16[64,768]{1,0:T(8,128)(2,1)S(1)}, u32[]{:S(2)}, u32[]{:S(2)}) collective-permute-start(bf16[64,768]{1,0:T(8,128)(2,1)S(1)} %get-tuple-element.34), channel_id=1, source_target_pairs={{0,2},{1,3},{2,0},{3,1},{4,6},{5,7},{6,4},{7,5},{8,10},{9,11},{10,... | collective-permute-start | bytes 294920 | tf_op jit(solution)/shard_map/ppermute | solution.py:297
  64.6 2.7 %collective-permute-start.30 = (bf16[64,768]{1,0:T(8,128)(2,1)S(1)}, bf16[64,768]{1,0:T(8,128)(2,1)S(1)}, u32[]{:S(2)}, u32[]{:S(2)}) collective-permute-start(bf16[64,768]{1,0:T(8,128)(2,1)S(1)} %split.3.refs_3_), channel_id=1, source_target_pairs={{0,12},{4,8},{8,4},{12,0},{1,13},{5,9},{9,5},{13,1},{2,14},{6,10},... | collective-permute-start | bytes 294920 | tf_op jit(solution)/shard_map/ppermute | solution.py:297
  71.1 3.9 %collective-permute-done.29.refs_0_ = bf16[64,768]{1,0:T(8,128)(2,1)S(1)} collective-permute-done((bf16[64,768]{1,0:T(8,128)(2,1)S(1)}, bf16[64,768]{1,0:T(8,128)(2,1)S(1)}, u32[]{:S(2)}, u32[]{:S(2)}) %collective-permute-start.29) | collective-permute-done | bytes 98336 | tf_op jit(solution)/shard_map/ppermute | solution.py:297
  (78 shorter events, 18.6 us)
Async XLA Ops:
  5.8 8.9 %collective-permute-start.4 = (bf16[32,1536]{1,0:T(8,128)(2,1)S(1)}, bf16[32,1536]{1,0:T(8,128)(2,1)S(1)}, u32[]{:S(2)}, u32[]{:S(2)}) collective-permute-start(bf16[32,1536]{1,0:T(8,128)(2,1)S(1)} %attend.2.after_ref.refs_0_), channel_id=1, source_target_pairs={{0,8},{4,12},{8,0},{12,4},{1,9},{5,13},{9,1},{13,5},{2,10},{6,14},... | collective-permute-start | bytes 294920 | tf_op jit(solution)/shard_map/ppermute | solution.py:297
  9.9 10.1 %collective-permute-start.3 = (bf16[32,1536]{1,0:T(8,128)(2,1)S(1)}, bf16[32,1536]{1,0:T(8,128)(2,1)S(1)}, u32[]{:S(2)}, u32[]{:S(2)}) collective-permute-start(bf16[32,1536]{1,0:T(8,128)(2,1)S(1)} %attend.2.after_ref.refs_0_), channel_id=1, source_target_pairs={{0,4},{4,0},{8,12},{12,8},{1,5},{5,1},{9,13},{13,9},{2,6},{6,2},{1... | collective-permute-start | bytes 294920 | tf_op jit(solution)/shard_map/ppermute | solution.py:297
  14.7 5.2 %collective-permute-start.5 = (bf16[32,1536]{1,0:T(8,128)(2,1)S(1)}, bf16[32,1536]{1,0:T(8,128)(2,1)S(1)}, u32[]{:S(2)}, u32[]{:S(2)}) collective-permute-start(bf16[32,1536]{1,0:T(8,128)(2,1)S(1)} %pass.1), channel_id=1, source_target_pairs={{0,4},{4,0},{8,12},{12,8},{1,5},{5,1},{9,13},{13,9},{2,6},{6,2},{1... | collective-permute-start | bytes 294920 | tf_op jit(solution)/shard_map/ppermute | solution.py:297
  15.5 8.7 %collective-permute-start.2 = (bf16[32,1536]{1,0:T(8,128)(2,1)S(1)}, bf16[32,1536]{1,0:T(8,128)(2,1)S(1)}, u32[]{:S(2)}, u32[]{:S(2)}) collective-permute-start(bf16[32,1536]{1,0:T(8,128)(2,1)S(1)} %attend.3.refs_1_.refs_5_.refs_0_), channel_id=1, source_target_pairs={{0,12},{4,8},{8,4},{12,0},{1,13},{5,9},{9,5},{13,1},{2,14},{6,10},... | collective-permute-start | bytes 294920 | tf_op jit(solution)/shard_map/ppermute | solution.py:297
  18.5 9.5 %collective-permute-start.1 = (bf16[32,1536]{1,0:T(8,128)(2,1)S(1)}, bf16[32,1536]{1,0:T(8,128)(2,1)S(1)}, u32[]{:S(2)}, u32[]{:S(2)}) collective-permute-start(bf16[32,1536]{1,0:T(8,128)(2,1)S(1)} %attend.3.refs_1_.refs_5_.refs_0_), channel_id=1, source_target_pairs={{0,8},{4,12},{8,0},{12,4},{1,9},{5,13},{9,1},{13,5},{2,10},{6,14},... | collective-permute-start | bytes 294920 | tf_op jit(solution)/shard_map/ppermute | solution.py:297
  18.9 9.0 %collective-permute-start = (bf16[32,1536]{1,0:T(8,128)(2,1)S(1)}, bf16[32,1536]{1,0:T(8,128)(2,1)S(1)}, u32[]{:S(2)}, u32[]{:S(2)}) collective-permute-start(bf16[32,1536]{1,0:T(8,128)(2,1)S(1)} %attend.3.refs_1_.refs_5_.refs_0_), channel_id=1, source_target_pairs={{0,4},{4,0},{8,12},{12,8},{1,5},{5,1},{9,13},{13,9},{2,6},{6,2},{1... | collective-permute-start | bytes 294920 | tf_op jit(solution)/shard_map/ppermute | solution.py:297
  20.4 9.7 %collective-permute-start.9 = (bf16[32,768]{1,0:T(8,128)(2,1)S(1)}, bf16[32,768]{1,0:T(8,128)(2,1)S(1)}, u32[]{:S(2)}, u32[]{:S(2)}) collective-permute-start(bf16[32,768]{1,0:T(8,128)(2,1)S(1)} %get-tuple-element.26), channel_id=1, source_target_pairs={{0,1},{1,0},{2,3},{3,2},{4,5},{5,4},{6,7},{7,6},{8,9},{9,8},{10,11... | collective-permute-start | bytes 147464 | tf_op jit(solution)/shard_map/ppermute | solution.py:297
  20.5 9.9 %collective-permute-start.10 = (bf16[32,768]{1,0:T(8,128)(2,1)S(1)}, bf16[32,768]{1,0:T(8,128)(2,1)S(1)}, u32[]{:S(2)}, u32[]{:S(2)}) collective-permute-start(bf16[32,768]{1,0:T(8,128)(2,1)S(1)} %get-tuple-element.27), channel_id=1, source_target_pairs={{0,2},{1,3},{2,0},{3,1},{4,6},{5,7},{6,4},{7,5},{8,10},{9,11},{10,... | collective-permute-start | bytes 147464 | tf_op jit(solution)/shard_map/ppermute | solution.py:297
  24.2 6.2 %collective-permute-start.11 = (bf16[32,768]{1,0:T(8,128)(2,1)S(1)}, bf16[32,768]{1,0:T(8,128)(2,1)S(1)}, u32[]{:S(2)}, u32[]{:S(2)}) collective-permute-start(bf16[32,768]{1,0:T(8,128)(2,1)S(1)} %get-tuple-element.28), channel_id=1, source_target_pairs={{0,3},{1,2},{2,1},{3,0},{4,7},{5,6},{6,5},{7,4},{8,11},{9,10},{10,... | collective-permute-start | bytes 147464 | tf_op jit(solution)/shard_map/ppermute | solution.py:297
  28.5 6.4 %collective-permute-start.7 = (bf16[32,768]{1,0:T(8,128)(2,1)S(1)}, bf16[32,768]{1,0:T(8,128)(2,1)S(1)}, u32[]{:S(2)}, u32[]{:S(2)}) collective-permute-start(bf16[32,768]{1,0:T(8,128)(2,1)S(1)} %get-tuple-element.24), channel_id=1, source_target_pairs={{0,2},{1,3},{2,0},{3,1},{4,6},{5,7},{6,4},{7,5},{8,10},{9,11},{10,... | collective-permute-start | bytes 147464 | tf_op jit(solution)/shard_map/ppermute | solution.py:297
  30.4 7.2 %collective-permute-start.17 = (bf16[32,768]{1,0:T(8,128)(2,1)S(1)}, bf16[32,768]{1,0:T(8,128)(2,1)S(1)}, u32[]{:S(2)}, u32[]{:S(2)}) collective-permute-start(bf16[32,768]{1,0:T(8,128)(2,1)S(1)} %add.2.refs_4_.refs_1_), channel_id=1, source_target_pairs={{0,12},{4,8},{8,4},{12,0},{1,13},{5,9},{9,5},{13,1},{2,14},{6,10},... | collective-permute-start | bytes 147464 | tf_op jit(solution)/shard_map/ppermute | solution.py:297
  33.2 6.2 %collective-permute-start.16 = (bf16[32,768]{1,0:T(8,128)(2,1)S(1)}, bf16[32,768]{1,0:T(8,128)(2,1)S(1)}, u32[]{:S(2)}, u32[]{:S(2)}) collective-permute-start(bf16[32,768]{1,0:T(8,128)(2,1)S(1)} %add.2.refs_4_.refs_1_), channel_id=1, source_target_pairs={{0,8},{4,12},{8,0},{12,4},{1,9},{5,13},{9,1},{13,5},{2,10},{6,14},... | collective-permute-start | bytes 147464 | tf_op jit(solution)/shard_map/ppermute | solution.py:297
  33.2 6.2 %collective-permute-start.15 = (bf16[32,768]{1,0:T(8,128)(2,1)S(1)}, bf16[32,768]{1,0:T(8,128)(2,1)S(1)}, u32[]{:S(2)}, u32[]{:S(2)}) collective-permute-start(bf16[32,768]{1,0:T(8,128)(2,1)S(1)} %add.2.refs_4_.refs_1_), channel_id=1, source_target_pairs={{0,4},{4,0},{8,12},{12,8},{1,5},{5,1},{9,13},{13,9},{2,6},{6,2},{1... | collective-permute-start | bytes 147464 | tf_op jit(solution)/shard_map/ppermute | solution.py:297
  34.9 6.3 %collective-permute-start.14 = (bf16[32,768]{1,0:T(8,128)(2,1)S(1)}, bf16[32,768]{1,0:T(8,128)(2,1)S(1)}, u32[]{:S(2)}, u32[]{:S(2)}) collective-permute-start(bf16[32,768]{1,0:T(8,128)(2,1)S(1)} %add.3.refs_5_.refs_1_), channel_id=1, source_target_pairs={{0,12},{4,8},{8,4},{12,0},{1,13},{5,9},{9,5},{13,1},{2,14},{6,10},... | collective-permute-start | bytes 147464 | tf_op jit(solution)/shard_map/ppermute | solution.py:297
  37.7 5.2 %collective-permute-start.13 = (bf16[32,768]{1,0:T(8,128)(2,1)S(1)}, bf16[32,768]{1,0:T(8,128)(2,1)S(1)}, u32[]{:S(2)}, u32[]{:S(2)}) collective-permute-start(bf16[32,768]{1,0:T(8,128)(2,1)S(1)} %add.3.refs_5_.refs_1_), channel_id=1, source_target_pairs={{0,8},{4,12},{8,0},{12,4},{1,9},{5,13},{9,1},{13,5},{2,10},{6,14},... | collective-permute-start | bytes 147464 | tf_op jit(solution)/shard_map/ppermute | solution.py:297
  39.7 8.7 %collective-permute-start.18 = (bf16[32,3072]{1,0:T(8,128)(2,1)S(1)}, bf16[32,3072]{1,0:T(8,128)(2,1)S(1)}, u32[]{:S(2)}, u32[]{:S(2)}) collective-permute-start(bf16[32,3072]{1,0:T(8,128)(2,1)S(1)} %norm.2.refs_5_.refs_0_), channel_id=1, source_target_pairs={{0,2},{1,3},{2,0},{3,1},{4,6},{5,7},{6,4},{7,5},{8,10},{9,11},{10,... | collective-permute-start | bytes 589832 | tf_op jit(solution)/shard_map/ppermute | solution.py:297
  43.1 6.7 %collective-permute-start.20 = (bf16[32,3072]{1,0:T(8,128)(2,1)S(1)}, bf16[32,3072]{1,0:T(8,128)(2,1)S(1)}, u32[]{:S(2)}, u32[]{:S(2)}) collective-permute-start(bf16[32,3072]{1,0:T(8,128)(2,1)S(1)} %norm.3.refs_2_.refs_0_), channel_id=1, source_target_pairs={{0,2},{1,3},{2,0},{3,1},{4,6},{5,7},{6,4},{7,5},{8,10},{9,11},{10,... | collective-permute-start | bytes 589832 | tf_op jit(solution)/shard_map/ppermute | solution.py:297
  58.9 5.7 %collective-permute-start.27 = (bf16[64,768]{1,0:T(8,128)(2,1)S(1)}, bf16[64,768]{1,0:T(8,128)(2,1)S(1)}, u32[]{:S(2)}, u32[]{:S(2)}) collective-permute-start(bf16[64,768]{1,0:T(8,128)(2,1)S(1)} %turn.3.refs_2_), channel_id=1, source_target_pairs={{0,2},{1,3},{2,0},{3,1},{4,6},{5,7},{6,4},{7,5},{8,10},{9,11},{10,... | collective-permute-start | bytes 294920 | tf_op jit(solution)/shard_map/ppermute | solution.py:297
  60.3 7.0 %collective-permute-start.26 = (bf16[64,768]{1,0:T(8,128)(2,1)S(1)}, bf16[64,768]{1,0:T(8,128)(2,1)S(1)}, u32[]{:S(2)}, u32[]{:S(2)}) collective-permute-start(bf16[64,768]{1,0:T(8,128)(2,1)S(1)} %turn.4.refs_2_), channel_id=1, source_target_pairs={{0,2},{1,3},{2,0},{3,1},{4,6},{5,7},{6,4},{7,5},{8,10},{9,11},{10,... | collective-permute-start | bytes 294920 | tf_op jit(solution)/shard_map/ppermute | solution.py:297
  61.1 7.7 %collective-permute-start.25 = (bf16[64,768]{1,0:T(8,128)(2,1)S(1)}, bf16[64,768]{1,0:T(8,128)(2,1)S(1)}, u32[]{:S(2)}, u32[]{:S(2)}) collective-permute-start(bf16[64,768]{1,0:T(8,128)(2,1)S(1)} %get-tuple-element.34), channel_id=1, source_target_pairs={{0,2},{1,3},{2,0},{3,1},{4,6},{5,7},{6,4},{7,5},{8,10},{9,11},{10,... | collective-permute-start | bytes 294920 | tf_op jit(solution)/shard_map/ppermute | solution.py:297
  62.5 7.6 %collective-permute-start.24 = (bf16[64,768]{1,0:T(8,128)(2,1)S(1)}, bf16[64,768]{1,0:T(8,128)(2,1)S(1)}, u32[]{:S(2)}, u32[]{:S(2)}) collective-permute-start(bf16[64,768]{1,0:T(8,128)(2,1)S(1)} %get-tuple-element.33.refs_3_), channel_id=1, source_target_pairs={{0,2},{1,3},{2,0},{3,1},{4,6},{5,7},{6,4},{7,5},{8,10},{9,11},{10,... | collective-permute-start | bytes 294920 | tf_op jit(solution)/shard_map/ppermute | solution.py:297
  64.6 6.5 %collective-permute-start.30 = (bf16[64,768]{1,0:T(8,128)(2,1)S(1)}, bf16[64,768]{1,0:T(8,128)(2,1)S(1)}, u32[]{:S(2)}, u32[]{:S(2)}) collective-permute-start(bf16[64,768]{1,0:T(8,128)(2,1)S(1)} %split.3.refs_3_), channel_id=1, source_target_pairs={{0,12},{4,8},{8,4},{12,0},{1,13},{5,9},{9,5},{13,1},{2,14},{6,10},... | collective-permute-start | bytes 294920 | tf_op jit(solution)/shard_map/ppermute | solution.py:297
  67.4 7.7 %collective-permute-start.29 = (bf16[64,768]{1,0:T(8,128)(2,1)S(1)}, bf16[64,768]{1,0:T(8,128)(2,1)S(1)}, u32[]{:S(2)}, u32[]{:S(2)}) collective-permute-start(bf16[64,768]{1,0:T(8,128)(2,1)S(1)} %split.4.refs_4_), channel_id=1, source_target_pairs={{0,8},{4,12},{8,0},{12,4},{1,9},{5,13},{9,1},{13,5},{2,10},{6,14},... | collective-permute-start | bytes 294920 | tf_op jit(solution)/shard_map/ppermute | solution.py:297
  70.2 6.1 %collective-permute-start.28 = (bf16[64,768]{1,0:T(8,128)(2,1)S(1)}, bf16[64,768]{1,0:T(8,128)(2,1)S(1)}, u32[]{:S(2)}, u32[]{:S(2)}) collective-permute-start(bf16[64,768]{1,0:T(8,128)(2,1)S(1)} %get-tuple-element.35), channel_id=1, source_target_pairs={{0,4},{4,0},{8,12},{12,8},{1,5},{5,1},{9,13},{13,9},{2,6},{6,2},{1... | collective-permute-start | bytes 294920 | tf_op jit(solution)/shard_map/ppermute | solution.py:297
  (11 other events, 150.3 us)

commit v11 on v9

--- a/solution.py
+++ b/solution.py
@@ -229,12 +229,10 @@
         for t, shard in enumerate(by_distance(*shards[2 * c : 2 * c + 2])):
             first = pl.multiple_of(((lax.axis_index("ta") ^ t) * chunks + c) * rows, rows)
             held[pl.ds(first, rows), :] = shard[...]
-    for first in range(0, hidden, 6 * HD):
-        last = min(first + 6 * HD, hidden)
-        raised = lax.dot_general(
-            up_ref[first:last, :], held[...], (((1,), (1,)), ((), ())), preferred_element_type=F32
-        )
-        active_ref[:, first:last] = (raised / (1.0 + jnp.exp(-raised))).T.astype(BF16)
+    raised = lax.dot_general(
+        up_ref[...], held[...], (((1,), (1,)), ((), ())), preferred_element_type=F32
+    )
+    active_ref[...] = (raised / (1.0 + jnp.exp(-raised))).T.astype(BF16)
     copy.wait()
     mine = lax.axis_index("gx") // 2
     for k in range(2):

time: 76.6 us -> 78.8 us (1.029)
  Pallas kernels: 20.2 us -> 22.4 us
    pallas_call x1, Pallas kernels: 4.27 us -> 6.48 us  [every_row_body(): local_call(functools.partial(lift_kernel, chunks), [shape((all_rows, hidd...]
  transfers between devices with their start and end apart: 31 -> 31, of which waited for: 12 -> 12; matrix products, arithmetic and copies ran while one was open for 0% -> 0% of each run, Pallas kernels for 16% -> 15%
where the time goes in v11:
time: 78.8 us; the launch traced here: 78.5 us
  starting transfers between devices  34.1 us (43%)
  Pallas kernels  22.4 us (28%)
  waiting for transfers between devices  19 us (24%)
  other arithmetic  1.61 us (2%)
  local copies, waits for them, and re-layouts  1.1 us (1%)
    ppermute x31, starting transfers between devices, trade(): return lax.ppermute(array, axis, [(k, k ^ turn) for k in range(count)])  34.1 us
    ppermute x31, waiting for transfers between devices, trade(): return lax.ppermute(array, axis, [(k, k ^ turn) for k in range(count)])  19 us
    pallas_call x17, Pallas kernels, local_call(): return call if after is None else lambda *args: call(*args, after)  7.95 us
    pallas_call x1, Pallas kernels, every_row_body(): local_call(functools.partial(lift_kernel, chunks), [shape((all_rows, hidd...  6.48 us
    pallas_call x2, Pallas kernels, attend(): pl.pallas_call(functools.partial(attend_kernel, kv_heads, heads // kv_hea...  6.48 us
  transfers between devices with their start and end apart: 31, of which 12 were waited for; matrix products, arithmetic and copies ran while one was open for 0% of the time, Pallas kernels for 15%

profile of v11, /device:TPU:0, one launch (start us, length us, event | category | flops | bytes accessed | tf_op | source)
XLA Modules:
  0.0 78.5 jit_solution(15258038739606539016)
XLA Ops:
  2.5 3.2 %attend.2.after_ref.refs_0_ = bf16[32,1536]{1,0:T(8,128)(2,1)S(1)} custom-call(bf16[64,2304]{1,0:T(8,128)(2,1)S(1)} %pad_maximum_fusion.small_ref.after_ref, bf16[2,64,192,256]{3,2,1,0:T(8,128)(2,1)} %cache_ref.3, bf16[64,2304]{1,0:T(8,128)(2,1)S(1)} %pad_maximum_fusion.small_ref.after_ref), custom_call_target="tpu_custom_call" | custom-call | flops 1024 | bytes 1024 | tf_op jit(solution)/shard_map/attend/pallas_call | solution.py:136
  5.8 5.1 %collective-permute-start.5 = (bf16[32,1536]{1,0:T(8,128)(2,1)S(1)}, bf16[32,1536]{1,0:T(8,128)(2,1)S(1)}, u32[]{:S(2)}, u32[]{:S(2)}) collective-permute-start(bf16[32,1536]{1,0:T(8,128)(2,1)S(1)} %attend.2.after_ref.refs_0_), channel_id=1, source_target_pairs={{0,12},{4,8},{8,4},{12,0},{1,13},{5,9},{9,5},{13,1},{2,14},{6,10},... | collective-permute-start | bytes 294920 | tf_op jit(solution)/shard_map/ppermute | solution.py:291
  11.5 3.2 %attend.3.refs_5_.refs_0_ = bf16[32,1536]{1,0:T(8,128)(2,1)S(1)} custom-call(bf16[64,2304]{1,0:T(8,128)(2,1)S(1)} %pad_maximum_fusion.small_ref.after_ref, bf16[2,64,192,256]{3,2,1,0:T(8,128)(2,1)} %cache_ref.3, bf16[32,1536]{1,0:T(8,128)(2,1)S(1)} %attend.2.after_ref.refs_0_), custom_call_target="tpu_custom_call" | custom-call | flops 1024 | bytes 1024 | tf_op jit(solution)/shard_map/attend/pallas_call | solution.py:136
  14.8 3.8 %collective-permute-start.2 = (bf16[32,1536]{1,0:T(8,128)(2,1)S(1)}, bf16[32,1536]{1,0:T(8,128)(2,1)S(1)}, u32[]{:S(2)}, u32[]{:S(2)}) collective-permute-start(bf16[32,1536]{1,0:T(8,128)(2,1)S(1)} %attend.3.refs_5_.refs_0_), channel_id=1, source_target_pairs={{0,12},{4,8},{8,4},{12,0},{1,13},{5,9},{9,5},{13,1},{2,14},{6,10},... | collective-permute-start | bytes 294920 | tf_op jit(solution)/shard_map/ppermute | solution.py:291
  19.2 5.1 %collective-permute-done.4.refs_2_ = bf16[32,1536]{1,0:T(8,128)(2,1)S(1)} collective-permute-done((bf16[32,1536]{1,0:T(8,128)(2,1)S(1)}, bf16[32,1536]{1,0:T(8,128)(2,1)S(1)}, u32[]{:S(2)}, u32[]{:S(2)}) %collective-permute-start.4) | collective-permute-done | bytes 98336 | tf_op jit(solution)/shard_map/ppermute | solution.py:291
  24.9 1.6 %collective-permute-start.10 = (bf16[32,768]{1,0:T(8,128)(2,1)S(1)}, bf16[32,768]{1,0:T(8,128)(2,1)S(1)}, u32[]{:S(2)}, u32[]{:S(2)}) collective-permute-start(bf16[32,768]{1,0:T(8,128)(2,1)S(1)} %get-tuple-element.27), channel_id=1, source_target_pairs={{0,2},{1,3},{2,0},{3,1},{4,6},{5,7},{6,4},{7,5},{8,10},{9,11},{10,... | collective-permute-start | bytes 147464 | tf_op jit(solution)/shard_map/ppermute | solution.py:291
  28.2 1.6 %collective-permute-start.7 = (bf16[32,768]{1,0:T(8,128)(2,1)S(1)}, bf16[32,768]{1,0:T(8,128)(2,1)S(1)}, u32[]{:S(2)}, u32[]{:S(2)}) collective-permute-start(bf16[32,768]{1,0:T(8,128)(2,1)S(1)} %get-tuple-element.24), channel_id=1, source_target_pairs={{0,2},{1,3},{2,0},{3,1},{4,6},{5,7},{6,4},{7,5},{8,10},{9,11},{10,... | collective-permute-start | bytes 147464 | tf_op jit(solution)/shard_map/ppermute | solution.py:291
  30.2 2.4 %collective-permute-start.17 = (bf16[32,768]{1,0:T(8,128)(2,1)S(1)}, bf16[32,768]{1,0:T(8,128)(2,1)S(1)}, u32[]{:S(2)}, u32[]{:S(2)}) collective-permute-start(bf16[32,768]{1,0:T(8,128)(2,1)S(1)} %add.2.refs_4_.refs_1_), channel_id=1, source_target_pairs={{0,12},{4,8},{8,4},{12,0},{1,13},{5,9},{9,5},{13,1},{2,14},{6,10},... | collective-permute-start | bytes 147464 | tf_op jit(solution)/shard_map/ppermute | solution.py:291
  32.6 2.0 %collective-permute-start.15 = (bf16[32,768]{1,0:T(8,128)(2,1)S(1)}, bf16[32,768]{1,0:T(8,128)(2,1)S(1)}, u32[]{:S(2)}, u32[]{:S(2)}) collective-permute-start(bf16[32,768]{1,0:T(8,128)(2,1)S(1)} %add.2.refs_4_.refs_1_), channel_id=1, source_target_pairs={{0,4},{4,0},{8,12},{12,8},{1,5},{5,1},{9,13},{13,9},{2,6},{6,2},{1... | collective-permute-start | bytes 147464 | tf_op jit(solution)/shard_map/ppermute | solution.py:291
  34.7 2.4 %collective-permute-start.14 = (bf16[32,768]{1,0:T(8,128)(2,1)S(1)}, bf16[32,768]{1,0:T(8,128)(2,1)S(1)}, u32[]{:S(2)}, u32[]{:S(2)}) collective-permute-start(bf16[32,768]{1,0:T(8,128)(2,1)S(1)} %add.3.refs_5_.refs_1_), channel_id=1, source_target_pairs={{0,12},{4,8},{8,4},{12,0},{1,13},{5,9},{9,5},{13,1},{2,14},{6,10},... | collective-permute-start | bytes 147464 | tf_op jit(solution)/shard_map/ppermute | solution.py:291
  37.1 2.0 %collective-permute-start.12 = (bf16[32,768]{1,0:T(8,128)(2,1)S(1)}, bf16[32,768]{1,0:T(8,128)(2,1)S(1)}, u32[]{:S(2)}, u32[]{:S(2)}) collective-permute-start(bf16[32,768]{1,0:T(8,128)(2,1)S(1)} %add.3.refs_5_.refs_1_), channel_id=1, source_target_pairs={{0,4},{4,0},{8,12},{12,8},{1,5},{5,1},{9,13},{13,9},{2,6},{6,2},{1... | collective-permute-start | bytes 147464 | tf_op jit(solution)/shard_map/ppermute | solution.py:291
  39.4 1.4 %collective-permute-start.18 = (bf16[32,3072]{1,0:T(8,128)(2,1)S(1)}, bf16[32,3072]{1,0:T(8,128)(2,1)S(1)}, u32[]{:S(2)}, u32[]{:S(2)}) collective-permute-start(bf16[32,3072]{1,0:T(8,128)(2,1)S(1)} %norm.2.refs_5_.refs_0_), channel_id=1, source_target_pairs={{0,2},{1,3},{2,0},{3,1},{4,6},{5,7},{6,4},{7,5},{8,10},{9,11},{10,... | collective-permute-start | bytes 589832 | tf_op jit(solution)/shard_map/ppermute | solution.py:291
  40.9 1.6 %collective-permute-done.13.refs_3_ = bf16[32,768]{1,0:T(8,128)(2,1)S(1)} collective-permute-done((bf16[32,768]{1,0:T(8,128)(2,1)S(1)}, bf16[32,768]{1,0:T(8,128)(2,1)S(1)}, u32[]{:S(2)}, u32[]{:S(2)}) %collective-permute-start.13) | collective-permute-done | bytes 49184 | tf_op jit(solution)/shard_map/ppermute | solution.py:291
  42.7 1.4 %collective-permute-start.20 = (bf16[32,3072]{1,0:T(8,128)(2,1)S(1)}, bf16[32,3072]{1,0:T(8,128)(2,1)S(1)}, u32[]{:S(2)}, u32[]{:S(2)}) collective-permute-start(bf16[32,3072]{1,0:T(8,128)(2,1)S(1)} %norm.3.refs_2_.refs_0_), channel_id=1, source_target_pairs={{0,2},{1,3},{2,0},{3,1},{4,6},{5,7},{6,4},{7,5},{8,10},{9,11},{10,... | collective-permute-start | bytes 589832 | tf_op jit(solution)/shard_map/ppermute | solution.py:291
  44.5 3.4 %load_up.1.refs_2_.refs_4_ = bf16[1344,3072]{1,0:T(8,128)(2,1)S(1)} custom-call(bf16[1344,3072]{1,0:T(8,128)(2,1)} %bitcast.13, f32[4,64,128]{2,1,0:T(8,128)S(1)} %gates.1.refs_1_.gate_ref), custom_call_target="tpu_custom_call" | custom-call | flops 1024 | bytes 1024 | tf_op jit(solution)/shard_map/load_up/pallas_call | solution.py:39
  47.9 1.8 %collective-permute-done.20.refs_1_ = bf16[32,3072]{1,0:T(8,128)(2,1)S(1)} collective-permute-done((bf16[32,3072]{1,0:T(8,128)(2,1)S(1)}, bf16[32,3072]{1,0:T(8,128)(2,1)S(1)}, u32[]{:S(2)}, u32[]{:S(2)}) %collective-permute-start.20) | collective-permute-done | bytes 196640 | tf_op jit(solution)/shard_map/ppermute | solution.py:291
  50.2 1.9 %load_down.1.refs_5_.down_ref.refs_1_ = bf16[512,3072]{1,0:T(8,128)(2,1)S(1)} custom-call(bf16[1344,3072]{1,0:T(8,128)(2,1)} %bitcast.11, bf16[2,32,3072]{2,1,0:T(8,128)(2,1)S(1)} %pair.3.refs_1_.refs_2_), custom_call_target="tpu_custom_call" | custom-call | flops 1024 | bytes 1024 | tf_op jit(solution)/shard_map/load_down/pallas_call | solution.py:39
  52.2 6.5 %lift.1 = (bf16[256,1344]{1,0:T(8,128)(2,1)S(1)}, bf16[2,128,768]{2,1,0:T(8,128)(2,1)S(1)}, bf16[2,128,768]{2,1,0:T(8,128)(2,1)S(1)}, bf16[832,3072]{1,0:T(8,128)(2,1)S(1)}) custom-call(bf16[2,32,3072]{2,1,0:T(8,128)(2,1)S(1)} %pair.2.refs_2_.refs_0_, bf16[2,32,3072]{2,1,0:T(8,128)(2,1)S(1)} %collective-permute-done.19.refs_1_, ...), custom_call_target="tpu_custom_call" | custom-call | flops 1024 | bytes 1024 | tf_op jit(solution)/shard_map/lift/pallas_call | solution.py:396
  60.5 1.3 %collective-permute-start.27 = (bf16[64,768]{1,0:T(8,128)(2,1)S(1)}, bf16[64,768]{1,0:T(8,128)(2,1)S(1)}, u32[]{:S(2)}, u32[]{:S(2)}) collective-permute-start(bf16[64,768]{1,0:T(8,128)(2,1)S(1)} %turn.3.refs_2_), channel_id=1, source_target_pairs={{0,2},{1,3},{2,0},{3,1},{4,6},{5,7},{6,4},{7,5},{8,10},{9,11},{10,... | collective-permute-start | bytes 294920 | tf_op jit(solution)/shard_map/ppermute | solution.py:291
  62.7 1.3 %collective-permute-start.25 = (bf16[64,768]{1,0:T(8,128)(2,1)S(1)}, bf16[64,768]{1,0:T(8,128)(2,1)S(1)}, u32[]{:S(2)}, u32[]{:S(2)}) collective-permute-start(bf16[64,768]{1,0:T(8,128)(2,1)S(1)} %get-tuple-element.34), channel_id=1, source_target_pairs={{0,2},{1,3},{2,0},{3,1},{4,6},{5,7},{6,4},{7,5},{8,10},{9,11},{10,... | collective-permute-start | bytes 294920 | tf_op jit(solution)/shard_map/ppermute | solution.py:291
  66.2 2.3 %collective-permute-start.30 = (bf16[64,768]{1,0:T(8,128)(2,1)S(1)}, bf16[64,768]{1,0:T(8,128)(2,1)S(1)}, u32[]{:S(2)}, u32[]{:S(2)}) collective-permute-start(bf16[64,768]{1,0:T(8,128)(2,1)S(1)} %split.3.refs_3_), channel_id=1, source_target_pairs={{0,12},{4,8},{8,4},{12,0},{1,13},{5,9},{9,5},{13,1},{2,14},{6,10},... | collective-permute-start | bytes 294920 | tf_op jit(solution)/shard_map/ppermute | solution.py:291
  69.2 1.2 %collective-permute-done.25.refs_3_ = bf16[64,768]{1,0:T(8,128)(2,1)S(1)} collective-permute-done((bf16[64,768]{1,0:T(8,128)(2,1)S(1)}, bf16[64,768]{1,0:T(8,128)(2,1)S(1)}, u32[]{:S(2)}, u32[]{:S(2)}) %collective-permute-start.25) | collective-permute-done | bytes 98336 | tf_op jit(solution)/shard_map/ppermute | solution.py:291
  70.4 1.3 %collective-permute-done.24.refs_2_ = bf16[64,768]{1,0:T(8,128)(2,1)S(1)} collective-permute-done((bf16[64,768]{1,0:T(8,128)(2,1)S(1)}, bf16[64,768]{1,0:T(8,128)(2,1)S(1)}, u32[]{:S(2)}, u32[]{:S(2)}) %collective-permute-start.24) | collective-permute-done | bytes 98336 | tf_op jit(solution)/shard_map/ppermute | solution.py:291
  72.7 3.9 %collective-permute-done.29.refs_0_ = bf16[64,768]{1,0:T(8,128)(2,1)S(1)} collective-permute-done((bf16[64,768]{1,0:T(8,128)(2,1)S(1)}, bf16[64,768]{1,0:T(8,128)(2,1)S(1)}, u32[]{:S(2)}, u32[]{:S(2)}) %collective-permute-start.29) | collective-permute-done | bytes 98336 | tf_op jit(solution)/shard_map/ppermute | solution.py:291
  (77 shorter events, 16.5 us)
Async XLA Ops:
  5.8 12.8 %collective-permute-start.5 = (bf16[32,1536]{1,0:T(8,128)(2,1)S(1)}, bf16[32,1536]{1,0:T(8,128)(2,1)S(1)}, u32[]{:S(2)}, u32[]{:S(2)}) collective-permute-start(bf16[32,1536]{1,0:T(8,128)(2,1)S(1)} %attend.2.after_ref.refs_0_), channel_id=1, source_target_pairs={{0,12},{4,8},{8,4},{12,0},{1,13},{5,9},{9,5},{13,1},{2,14},{6,10},... | collective-permute-start | bytes 294920 | tf_op jit(solution)/shard_map/ppermute | solution.py:291
  10.9 13.4 %collective-permute-start.4 = (bf16[32,1536]{1,0:T(8,128)(2,1)S(1)}, bf16[32,1536]{1,0:T(8,128)(2,1)S(1)}, u32[]{:S(2)}, u32[]{:S(2)}) collective-permute-start(bf16[32,1536]{1,0:T(8,128)(2,1)S(1)} %attend.2.after_ref.refs_0_), channel_id=1, source_target_pairs={{0,8},{4,12},{8,0},{12,4},{1,9},{5,13},{9,1},{13,5},{2,10},{6,14},... | collective-permute-start | bytes 294920 | tf_op jit(solution)/shard_map/ppermute | solution.py:291
  10.9 13.4 %collective-permute-start.3 = (bf16[32,1536]{1,0:T(8,128)(2,1)S(1)}, bf16[32,1536]{1,0:T(8,128)(2,1)S(1)}, u32[]{:S(2)}, u32[]{:S(2)}) collective-permute-start(bf16[32,1536]{1,0:T(8,128)(2,1)S(1)} %attend.2.after_ref.refs_0_), channel_id=1, source_target_pairs={{0,4},{4,0},{8,12},{12,8},{1,5},{5,1},{9,13},{13,9},{2,6},{6,2},{1... | collective-permute-start | bytes 294920 | tf_op jit(solution)/shard_map/ppermute | solution.py:291
  14.8 11.7 %collective-permute-start.2 = (bf16[32,1536]{1,0:T(8,128)(2,1)S(1)}, bf16[32,1536]{1,0:T(8,128)(2,1)S(1)}, u32[]{:S(2)}, u32[]{:S(2)}) collective-permute-start(bf16[32,1536]{1,0:T(8,128)(2,1)S(1)} %attend.3.refs_5_.refs_0_), channel_id=1, source_target_pairs={{0,12},{4,8},{8,4},{12,0},{1,13},{5,9},{9,5},{13,1},{2,14},{6,10},... | collective-permute-start | bytes 294920 | tf_op jit(solution)/shard_map/ppermute | solution.py:291
  18.6 9.0 %collective-permute-start.1 = (bf16[32,1536]{1,0:T(8,128)(2,1)S(1)}, bf16[32,1536]{1,0:T(8,128)(2,1)S(1)}, u32[]{:S(2)}, u32[]{:S(2)}) collective-permute-start(bf16[32,1536]{1,0:T(8,128)(2,1)S(1)} %attend.3.refs_5_.refs_0_), channel_id=1, source_target_pairs={{0,8},{4,12},{8,0},{12,4},{1,9},{5,13},{9,1},{13,5},{2,10},{6,14},... | collective-permute-start | bytes 294920 | tf_op jit(solution)/shard_map/ppermute | solution.py:291
  18.6 9.0 %collective-permute-start = (bf16[32,1536]{1,0:T(8,128)(2,1)S(1)}, bf16[32,1536]{1,0:T(8,128)(2,1)S(1)}, u32[]{:S(2)}, u32[]{:S(2)}) collective-permute-start(bf16[32,1536]{1,0:T(8,128)(2,1)S(1)} %attend.3.refs_5_.refs_0_), channel_id=1, source_target_pairs={{0,4},{4,0},{8,12},{12,8},{1,5},{5,1},{9,13},{13,9},{2,6},{6,2},{1... | collective-permute-start | bytes 294920 | tf_op jit(solution)/shard_map/ppermute | solution.py:291
  24.9 5.1 %collective-permute-start.10 = (bf16[32,768]{1,0:T(8,128)(2,1)S(1)}, bf16[32,768]{1,0:T(8,128)(2,1)S(1)}, u32[]{:S(2)}, u32[]{:S(2)}) collective-permute-start(bf16[32,768]{1,0:T(8,128)(2,1)S(1)} %get-tuple-element.27), channel_id=1, source_target_pairs={{0,2},{1,3},{2,0},{3,1},{4,6},{5,7},{6,4},{7,5},{8,10},{9,11},{10,... | collective-permute-start | bytes 147464 | tf_op jit(solution)/shard_map/ppermute | solution.py:291
  28.2 6.5 %collective-permute-start.7 = (bf16[32,768]{1,0:T(8,128)(2,1)S(1)}, bf16[32,768]{1,0:T(8,128)(2,1)S(1)}, u32[]{:S(2)}, u32[]{:S(2)}) collective-permute-start(bf16[32,768]{1,0:T(8,128)(2,1)S(1)} %get-tuple-element.24), channel_id=1, source_target_pairs={{0,2},{1,3},{2,0},{3,1},{4,6},{5,7},{6,4},{7,5},{8,10},{9,11},{10,... | collective-permute-start | bytes 147464 | tf_op jit(solution)/shard_map/ppermute | solution.py:291
  29.7 4.9 %collective-permute-start.8 = (bf16[32,768]{1,0:T(8,128)(2,1)S(1)}, bf16[32,768]{1,0:T(8,128)(2,1)S(1)}, u32[]{:S(2)}, u32[]{:S(2)}) collective-permute-start(bf16[32,768]{1,0:T(8,128)(2,1)S(1)} %get-tuple-element.25), channel_id=1, source_target_pairs={{0,3},{1,2},{2,1},{3,0},{4,7},{5,6},{6,5},{7,4},{8,11},{9,10},{10,... | collective-permute-start | bytes 147464 | tf_op jit(solution)/shard_map/ppermute | solution.py:291
  30.2 6.9 %collective-permute-start.17 = (bf16[32,768]{1,0:T(8,128)(2,1)S(1)}, bf16[32,768]{1,0:T(8,128)(2,1)S(1)}, u32[]{:S(2)}, u32[]{:S(2)}) collective-permute-start(bf16[32,768]{1,0:T(8,128)(2,1)S(1)} %add.2.refs_4_.refs_1_), channel_id=1, source_target_pairs={{0,12},{4,8},{8,4},{12,0},{1,13},{5,9},{9,5},{13,1},{2,14},{6,10},... | collective-permute-start | bytes 147464 | tf_op jit(solution)/shard_map/ppermute | solution.py:291
  32.6 6.5 %collective-permute-start.16 = (bf16[32,768]{1,0:T(8,128)(2,1)S(1)}, bf16[32,768]{1,0:T(8,128)(2,1)S(1)}, u32[]{:S(2)}, u32[]{:S(2)}) collective-permute-start(bf16[32,768]{1,0:T(8,128)(2,1)S(1)} %add.2.refs_4_.refs_1_), channel_id=1, source_target_pairs={{0,8},{4,12},{8,0},{12,4},{1,9},{5,13},{9,1},{13,5},{2,10},{6,14},... | collective-permute-start | bytes 147464 | tf_op jit(solution)/shard_map/ppermute | solution.py:291
  32.6 6.5 %collective-permute-start.15 = (bf16[32,768]{1,0:T(8,128)(2,1)S(1)}, bf16[32,768]{1,0:T(8,128)(2,1)S(1)}, u32[]{:S(2)}, u32[]{:S(2)}) collective-permute-start(bf16[32,768]{1,0:T(8,128)(2,1)S(1)} %add.2.refs_4_.refs_1_), channel_id=1, source_target_pairs={{0,4},{4,0},{8,12},{12,8},{1,5},{5,1},{9,13},{13,9},{2,6},{6,2},{1... | collective-permute-start | bytes 147464 | tf_op jit(solution)/shard_map/ppermute | solution.py:291
  34.7 6.2 %collective-permute-start.14 = (bf16[32,768]{1,0:T(8,128)(2,1)S(1)}, bf16[32,768]{1,0:T(8,128)(2,1)S(1)}, u32[]{:S(2)}, u32[]{:S(2)}) collective-permute-start(bf16[32,768]{1,0:T(8,128)(2,1)S(1)} %add.3.refs_5_.refs_1_), channel_id=1, source_target_pairs={{0,12},{4,8},{8,4},{12,0},{1,13},{5,9},{9,5},{13,1},{2,14},{6,10},... | collective-permute-start | bytes 147464 | tf_op jit(solution)/shard_map/ppermute | solution.py:291
  37.1 5.3 %collective-permute-start.13 = (bf16[32,768]{1,0:T(8,128)(2,1)S(1)}, bf16[32,768]{1,0:T(8,128)(2,1)S(1)}, u32[]{:S(2)}, u32[]{:S(2)}) collective-permute-start(bf16[32,768]{1,0:T(8,128)(2,1)S(1)} %add.3.refs_5_.refs_1_), channel_id=1, source_target_pairs={{0,8},{4,12},{8,0},{12,4},{1,9},{5,13},{9,1},{13,5},{2,10},{6,14},... | collective-permute-start | bytes 147464 | tf_op jit(solution)/shard_map/ppermute | solution.py:291
  37.1 5.3 %collective-permute-start.12 = (bf16[32,768]{1,0:T(8,128)(2,1)S(1)}, bf16[32,768]{1,0:T(8,128)(2,1)S(1)}, u32[]{:S(2)}, u32[]{:S(2)}) collective-permute-start(bf16[32,768]{1,0:T(8,128)(2,1)S(1)} %add.3.refs_5_.refs_1_), channel_id=1, source_target_pairs={{0,4},{4,0},{8,12},{12,8},{1,5},{5,1},{9,13},{13,9},{2,6},{6,2},{1... | collective-permute-start | bytes 147464 | tf_op jit(solution)/shard_map/ppermute | solution.py:291
  39.4 8.4 %collective-permute-start.18 = (bf16[32,3072]{1,0:T(8,128)(2,1)S(1)}, bf16[32,3072]{1,0:T(8,128)(2,1)S(1)}, u32[]{:S(2)}, u32[]{:S(2)}) collective-permute-start(bf16[32,3072]{1,0:T(8,128)(2,1)S(1)} %norm.2.refs_5_.refs_0_), channel_id=1, source_target_pairs={{0,2},{1,3},{2,0},{3,1},{4,6},{5,7},{6,4},{7,5},{8,10},{9,11},{10,... | collective-permute-start | bytes 589832 | tf_op jit(solution)/shard_map/ppermute | solution.py:291
  42.7 6.9 %collective-permute-start.20 = (bf16[32,3072]{1,0:T(8,128)(2,1)S(1)}, bf16[32,3072]{1,0:T(8,128)(2,1)S(1)}, u32[]{:S(2)}, u32[]{:S(2)}) collective-permute-start(bf16[32,3072]{1,0:T(8,128)(2,1)S(1)} %norm.3.refs_2_.refs_0_), channel_id=1, source_target_pairs={{0,2},{1,3},{2,0},{3,1},{4,6},{5,7},{6,4},{7,5},{8,10},{9,11},{10,... | collective-permute-start | bytes 589832 | tf_op jit(solution)/shard_map/ppermute | solution.py:291
  60.5 5.7 %collective-permute-start.27 = (bf16[64,768]{1,0:T(8,128)(2,1)S(1)}, bf16[64,768]{1,0:T(8,128)(2,1)S(1)}, u32[]{:S(2)}, u32[]{:S(2)}) collective-permute-start(bf16[64,768]{1,0:T(8,128)(2,1)S(1)} %turn.3.refs_2_), channel_id=1, source_target_pairs={{0,2},{1,3},{2,0},{3,1},{4,6},{5,7},{6,4},{7,5},{8,10},{9,11},{10,... | collective-permute-start | bytes 294920 | tf_op jit(solution)/shard_map/ppermute | solution.py:291
  61.8 6.8 %collective-permute-start.26 = (bf16[64,768]{1,0:T(8,128)(2,1)S(1)}, bf16[64,768]{1,0:T(8,128)(2,1)S(1)}, u32[]{:S(2)}, u32[]{:S(2)}) collective-permute-start(bf16[64,768]{1,0:T(8,128)(2,1)S(1)} %turn.4.refs_2_), channel_id=1, source_target_pairs={{0,2},{1,3},{2,0},{3,1},{4,6},{5,7},{6,4},{7,5},{8,10},{9,11},{10,... | collective-permute-start | bytes 294920 | tf_op jit(solution)/shard_map/ppermute | solution.py:291
  62.7 7.7 %collective-permute-start.25 = (bf16[64,768]{1,0:T(8,128)(2,1)S(1)}, bf16[64,768]{1,0:T(8,128)(2,1)S(1)}, u32[]{:S(2)}, u32[]{:S(2)}) collective-permute-start(bf16[64,768]{1,0:T(8,128)(2,1)S(1)} %get-tuple-element.34), channel_id=1, source_target_pairs={{0,2},{1,3},{2,0},{3,1},{4,6},{5,7},{6,4},{7,5},{8,10},{9,11},{10,... | collective-permute-start | bytes 294920 | tf_op jit(solution)/shard_map/ppermute | solution.py:291
  64.0 7.7 %collective-permute-start.24 = (bf16[64,768]{1,0:T(8,128)(2,1)S(1)}, bf16[64,768]{1,0:T(8,128)(2,1)S(1)}, u32[]{:S(2)}, u32[]{:S(2)}) collective-permute-start(bf16[64,768]{1,0:T(8,128)(2,1)S(1)} %get-tuple-element.33.refs_3_), channel_id=1, source_target_pairs={{0,2},{1,3},{2,0},{3,1},{4,6},{5,7},{6,4},{7,5},{8,10},{9,11},{10,... | collective-permute-start | bytes 294920 | tf_op jit(solution)/shard_map/ppermute | solution.py:291
  66.2 6.5 %collective-permute-start.30 = (bf16[64,768]{1,0:T(8,128)(2,1)S(1)}, bf16[64,768]{1,0:T(8,128)(2,1)S(1)}, u32[]{:S(2)}, u32[]{:S(2)}) collective-permute-start(bf16[64,768]{1,0:T(8,128)(2,1)S(1)} %split.3.refs_3_), channel_id=1, source_target_pairs={{0,12},{4,8},{8,4},{12,0},{1,13},{5,9},{9,5},{13,1},{2,14},{6,10},... | collective-permute-start | bytes 294920 | tf_op jit(solution)/shard_map/ppermute | solution.py:291
  68.6 8.0 %collective-permute-start.29 = (bf16[64,768]{1,0:T(8,128)(2,1)S(1)}, bf16[64,768]{1,0:T(8,128)(2,1)S(1)}, u32[]{:S(2)}, u32[]{:S(2)}) collective-permute-start(bf16[64,768]{1,0:T(8,128)(2,1)S(1)} %split.4.refs_4_), channel_id=1, source_target_pairs={{0,8},{4,12},{8,0},{12,4},{1,9},{5,13},{9,1},{13,5},{2,10},{6,14},... | collective-permute-start | bytes 294920 | tf_op jit(solution)/shard_map/ppermute | solution.py:291
  71.8 6.0 %collective-permute-start.28 = (bf16[64,768]{1,0:T(8,128)(2,1)S(1)}, bf16[64,768]{1,0:T(8,128)(2,1)S(1)}, u32[]{:S(2)}, u32[]{:S(2)}) collective-permute-start(bf16[64,768]{1,0:T(8,128)(2,1)S(1)} %get-tuple-element.35), channel_id=1, source_target_pairs={{0,4},{4,0},{8,12},{12,8},{1,5},{5,1},{9,13},{13,9},{2,6},{6,2},{1... | collective-permute-start | bytes 294920 | tf_op jit(solution)/shard_map/ppermute | solution.py:291
  (11 other events, 152.6 us)
